TPU v7x, 32 devices: a whole 2x2x4 slice. The times are simulated.
32 devices in a mesh: seq: 4 (over z), wsh: 8 (over y, x, core).
Axes of the slice: x: 2, y: 2, z: 4, core: 2. Of those that a mesh axis runs over, the one named last changes fastest.
Arguments:
- inputs: bfloat16 [8, 2048, 1536], P('wsh', 'seq'), may hold values from -6 to 6
- cotangent: bfloat16 [8, 2048, 1536], P('wsh', 'seq'), may hold values from -6 to 6
- w_in: float32 [1536, 6400], P('wsh'), may hold values from -0.15625 to 0.15625
- w_dt: float32 [1536, 48], P('wsh'), may hold values from -0.15625 to 0.15625
- w_out: float32 [3072, 1536], P('wsh'), may hold values from -0.109375 to 0.109375
- gain_pre: float32 [1536], P('wsh'), may hold values from 0.5 to 1.5
- gain_norm: float32 [3072], P('wsh'), may hold values from 0.5 to 1.5
- conv_param: float32 [5, 3328], P(None, 'wsh'), may hold values from -0.5 to 0.5
- head_param: float32 [3, 48], P(None, 'wsh'), may hold values from -6.5 to 3, as said below
- first_w_in: float32 [1536, 6400], P('wsh')
- second_w_in: float32 [1536, 6400], P('wsh'), as said below
- first_w_dt: float32 [1536, 48], P('wsh')
- second_w_dt: float32 [1536, 48], P('wsh'), as said below
- first_w_out: float32 [3072, 1536], P('wsh')
- second_w_out: float32 [3072, 1536], P('wsh'), as said below
- first_gain_pre: float32 [1536], P('wsh')
- second_gain_pre: float32 [1536], P('wsh'), as said below
- first_gain_norm: float32 [3072], P('wsh')
- second_gain_norm: float32 [3072], P('wsh'), as said below
- first_conv: float32 [5, 3328], P(None, 'wsh')
- second_conv: float32 [5, 3328], P(None, 'wsh'), as said below
- first_head: float32 [3, 48], P(None, 'wsh')
- second_head: float32 [3, 48], P(None, 'wsh'), as said below
Outputs:
- block_out: bfloat16 [8, 2048, 1536], P('wsh', 'seq')
- input_grad: float32 [8, 2048, 1536], P('wsh', 'seq')
- grad_w_in: float32 [1536, 6400], P('wsh')
- grad_w_dt: float32 [1536, 48], P('wsh')
- grad_w_out: float32 [3072, 1536], P('wsh')
- grad_gain_pre: float32 [1536], P('wsh')
- grad_gain_norm: float32 [3072], P('wsh')
- grad_conv: float32 [5, 3328], P(None, 'wsh')
- grad_head: float32 [3, 48], P(None, 'wsh')
- next_w_in: float32 [1536, 6400], P('wsh')
- next_w_dt: float32 [1536, 48], P('wsh')
- next_w_out: float32 [3072, 1536], P('wsh')
- next_gain_pre: float32 [1536], P('wsh')
- next_gain_norm: float32 [3072], P('wsh')
- next_conv: float32 [5, 3328], P(None, 'wsh')
- next_head: float32 [3, 48], P(None, 'wsh')
- next_first_w_in: float32 [1536, 6400], P('wsh')
- next_second_w_in: float32 [1536, 6400], P('wsh')
- next_first_w_dt: float32 [1536, 48], P('wsh')
- next_second_w_dt: float32 [1536, 48], P('wsh')
- next_first_w_out: float32 [3072, 1536], P('wsh')
- next_second_w_out: float32 [3072, 1536], P('wsh')
- next_first_gain_pre: float32 [1536], P('wsh')
- next_second_gain_pre: float32 [1536], P('wsh')
- next_first_gain_norm: float32 [3072], P('wsh')
- next_second_gain_norm: float32 [3072], P('wsh')
- next_first_conv: float32 [5, 3328], P(None, 'wsh')
- next_second_conv: float32 [5, 3328], P(None, 'wsh')
- next_first_head: float32 [3, 48], P(None, 'wsh')
- next_second_head: float32 [3, 48], P(None, 'wsh')
Inputs may be any that keep to these rules, and one draw needn't show every extreme that they name: `head_param`: row 0 lies between 0 and log 16, row 1 between -6.5 and -2.5, row 2 between 0.5 and 1.5. `second_w_in`: Positive. `second_w_dt`: Positive. `second_w_out`: Positive. `second_gain_pre`: Positive. `second_gain_norm`: Positive. `second_conv`: Positive. `second_head`: Positive.
All inputs are finite; a program needn't handle non-finite values.
Results may differ from a plain program's by a relative error of at most 0.014.
The roundings to bfloat16 on the way count: a program that leaves them out, or rounds other values in their place, can miss the bound.
Values may be sent and summed in bfloat16 or wider, within the bound.
A program may use at most 256 MiB of HBM per device.

v0:
```python
import jax
import jax.numpy as jnp
from jax import lax
from jax.sharding import PartitionSpec as P

D = 1536
HEADS = 48
HEAD_DIM = 64
STATE = 128
CONV_WIDTH = 4
SPAN = 256
STEP = 2
INNER = 3072
CONV_CH = 3328


norm_eps = 1e-05
beta_one = 0.9
beta_two = 0.999
adam_eps = 1e-08
rate_matrix = 0.01
rate_gain = 0.4
rate_conv = 0.1
rate_head = 1.0
weight_decay = 0.1
highest = lax.Precision.HIGHEST


def segment_sums(log_rates):
    length = log_rates.shape[-1]
    row_ids = jnp.arange(length)[:, None]
    col_ids = jnp.arange(length)[None, :]
    spread = jnp.where(row_ids > col_ids, log_rates[..., :, None], jnp.zeros((), log_rates.dtype))
    partial_sums = jnp.cumsum(spread, axis=-2)
    return jnp.where(row_ids >= col_ids, partial_sums, jnp.full((), -jnp.inf, log_rates.dtype))


def state_space(values, step_sizes, decay_rate, in_map, out_map):
    length, head_count, head_width = values.shape
    blocks = length // SPAN
    log_rates = (step_sizes * decay_rate).reshape(blocks, SPAN, head_count).transpose(2, 0, 1)
    inflow = (values * step_sizes[:, :, None]).reshape(blocks, SPAN, head_count, head_width)
    in_blocks = in_map.reshape(blocks, SPAN, -1)
    out_blocks = out_map.reshape(blocks, SPAN, -1)
    running = jnp.cumsum(log_rates, axis=-1)
    within = jnp.exp(segment_sums(log_rates))
    intersection = jnp.einsum("cln,csn->cls", out_blocks, in_blocks, precision=highest)
    mixing = within * intersection[None]
    diagonal = jnp.einsum("hcls,cshp->clhp", mixing, inflow, precision=highest)
    tail_decay = jnp.exp(running[:, :, -1:] - running)
    weighted = inflow * tail_decay.transpose(1, 2, 0)[..., None]
    end_states = jnp.einsum("csn,cshp->chpn", in_blocks, weighted, precision=highest)
    totals = jnp.concatenate([jnp.zeros((head_count, 1), running.dtype), running[:, :, -1]], axis=1)
    across = jnp.exp(segment_sums(totals))
    starts = jnp.concatenate(
        [jnp.zeros((1,) + end_states.shape[1:], end_states.dtype), end_states], axis=0
    )
    carried = jnp.einsum("hzc,chpn->zhpn", across, starts, precision=highest)[:-1]
    entering = jnp.exp(running).transpose(1, 2, 0)[..., None]
    offdiag = jnp.einsum("cln,chpn->clhp", out_blocks, carried, precision=highest) * entering
    return (diagonal + offdiag).reshape(length, head_count, head_width)


def single_head(in_map, out_map, items):
    head_vals, head_steps, head_rate = items
    result = state_space(
        head_vals[:, None, :], head_steps[:, None], head_rate[None], in_map, out_map
    )
    return result[:, 0, :]


def state_space_heads(values, step_sizes, decay_rate, in_map, out_map):
    checked = jax.checkpoint(single_head)

    def per_head(items):
        return checked(in_map, out_map, items)

    outputs = lax.map(per_head, (values.transpose(1, 0, 2), step_sizes.T, decay_rate))
    return outputs.transpose(1, 0, 2)


def convolve(signal, kernel):
    length = signal.shape[0]
    padded = jnp.pad(signal, ((CONV_WIDTH - 1, 0), (0, 0)))
    summed = jnp.broadcast_to(kernel[CONV_WIDTH], signal.shape)
    for offset in range(CONV_WIDTH):
        summed = summed + padded[offset : offset + length] * kernel[offset]
    return jax.nn.silu(summed)


def pre_norm(tokens_in, gain_vals):
    inv_rms = lax.rsqrt(jnp.mean(tokens_in * tokens_in, axis=-1, keepdims=True) + norm_eps)
    return tokens_in * inv_rms * gain_vals


def out_norm(scanned_vals, gate_vals, gain_vals):
    gated_vals = scanned_vals * jax.nn.silu(gate_vals)
    return (
        gated_vals
        * lax.rsqrt(jnp.mean(gated_vals * gated_vals, axis=-1, keepdims=True) + norm_eps)
        * gain_vals
    )


def head_side(signal_part, step_part, map_part, conv_part, conv_maps, head_part):
    length = signal_part.shape[0]
    head_count = step_part.shape[1]
    head_inputs = convolve(signal_part, conv_part).reshape(length, head_count, HEAD_DIM)
    map_vals = convolve(map_part, conv_maps)
    step_sizes = jax.nn.softplus(step_part + head_part[1])
    decay_rate = -jnp.exp(head_part[0])
    scanned = state_space_heads(
        head_inputs, step_sizes, decay_rate, map_vals[:, :STATE], map_vals[:, STATE:]
    )
    scanned = scanned + head_part[2][None, :, None] * head_inputs
    return scanned.reshape(length, head_count * HEAD_DIM)


def contract_rows(left_side, right_side):
    return lax.dot_general(
        left_side, right_side, (((0,), (0,)), ((), ())), preferred_element_type=jnp.float32
    )


def contract_cols(left_side, right_side):
    return lax.dot_general(
        left_side, right_side, (((1,), (1,)), ((), ())), preferred_element_type=jnp.float32
    )


def adam_update(weights, gradient, first_moment, second_moment, step_rate, decay_amount):
    next_first = beta_one * first_moment + (1.0 - beta_one) * gradient
    next_second = beta_two * second_moment + (1.0 - beta_two) * gradient * gradient
    corrected = (
        next_first
        / (1.0 - beta_one**STEP)
        / (jnp.sqrt(next_second / (1.0 - beta_two**STEP)) + adam_eps)
    )
    return (weights - step_rate * (corrected + decay_amount * weights), next_first, next_second)


def shards(
    inputs,
    cotangent,
    w_in,
    w_dt,
    w_out,
    gain_pre,
    gain_norm,
    conv_param,
    head_param,
    first_w_in,
    second_w_in,
    first_w_dt,
    second_w_dt,
    first_w_out,
    second_w_out,
    first_gain_pre,
    second_gain_pre,
    first_gain_norm,
    second_gain_norm,
    first_conv,
    second_conv,
    first_head,
    second_head,
):
    wsh_count = lax.axis_size("wsh")
    seq_index = lax.axis_index("seq")
    wsh_index = lax.axis_index("wsh")
    low_type = jnp.bfloat16
    full_type = jnp.float32
    full_in, full_dt, full_out, full_gpre, full_gnorm, full_conv, full_head = (
        lax.all_gather(w_in.astype(low_type), "wsh", axis=0, tiled=True),
        lax.all_gather(w_dt.astype(low_type), "wsh", axis=0, tiled=True),
        lax.all_gather(w_out.astype(low_type), "wsh", axis=0, tiled=True),
        lax.all_gather(gain_pre.astype(low_type), "wsh", axis=0, tiled=True),
        lax.all_gather(gain_norm.astype(low_type), "wsh", axis=0, tiled=True),
        lax.all_gather(conv_param.astype(low_type), "wsh", axis=1, tiled=True),
        lax.all_gather(head_param.astype(low_type), "wsh", axis=1, tiled=True),
    )
    tokens_in = inputs[0].astype(full_type)
    cot_low = cotangent[0]
    normed, norm_pull = jax.vjp(pre_norm, tokens_in, full_gpre.astype(full_type))
    normed_low = normed.astype(low_type)
    projected = jnp.dot(normed_low, full_in, preferred_element_type=full_type)
    raw_step = jnp.dot(normed_low, full_dt, preferred_element_type=full_type).astype(low_type)
    gate_vals = projected[:, :INNER]
    signal_low = projected[:, INNER:].astype(low_type)
    head_signal, head_step = (
        lax.all_to_all(signal_low[:, :INNER], "seq", split_axis=1, concat_axis=0, tiled=True),
        lax.all_to_all(raw_step, "seq", split_axis=1, concat_axis=0, tiled=True),
    )
    all_maps = lax.all_gather(signal_low[:, INNER:], "seq", axis=0, tiled=True)
    inner_local = head_signal.shape[1]
    heads_local = head_step.shape[1]
    conv_local = lax.dynamic_slice_in_dim(
        full_conv, seq_index * inner_local, inner_local, 1
    ).astype(full_type)
    conv_maps = full_conv[:, INNER:].astype(full_type)
    head_local = lax.dynamic_slice_in_dim(
        full_head, seq_index * heads_local, heads_local, 1
    ).astype(full_type)
    scanned, head_pull = jax.vjp(
        head_side,
        head_signal.astype(full_type),
        head_step.astype(full_type),
        all_maps.astype(full_type),
        conv_local,
        conv_maps,
        head_local,
    )
    back_vals = lax.all_to_all(
        scanned.astype(low_type), "seq", split_axis=0, concat_axis=1, tiled=True
    )
    normed_out, out_pull = jax.vjp(
        out_norm, back_vals.astype(full_type), gate_vals, full_gnorm.astype(full_type)
    )
    out_low = normed_out.astype(low_type)
    branch = jnp.dot(out_low, full_out, preferred_element_type=full_type)
    block_out = (tokens_in + branch).astype(low_type)[None]
    grad_normed_out = contract_cols(cot_low, full_out)
    grad_vals, grad_gate, part_gnorm = out_pull(grad_normed_out)
    grad_head_vals = lax.all_to_all(
        grad_vals.astype(low_type), "seq", split_axis=1, concat_axis=0, tiled=True
    )
    grad_signal_h, grad_step_h, grad_maps, grad_conv_local, grad_conv_maps, grad_head_local = (
        head_pull(grad_head_vals.astype(full_type))
    )
    grad_signal, grad_step = (
        lax.all_to_all(
            grad_signal_h.astype(low_type), "seq", split_axis=0, concat_axis=1, tiled=True
        ),
        lax.all_to_all(
            grad_step_h.astype(low_type), "seq", split_axis=0, concat_axis=1, tiled=True
        ),
    )
    grad_maps_tok = (
        lax.psum_scatter(grad_maps.astype(jnp.bfloat16), "seq", scatter_dimension=0, tiled=True)
        .astype(jnp.float32)
        .astype(low_type)
    )
    grad_projected = jnp.concatenate(
        [grad_gate.astype(low_type), grad_signal, grad_maps_tok], axis=1
    )
    grad_normed = contract_cols(grad_projected, full_in) + contract_cols(grad_step, full_dt)
    grad_tokens, part_gpre = norm_pull(grad_normed)
    input_grad = (cot_low.astype(full_type) + grad_tokens)[None]
    part_dt = contract_rows(normed_low, grad_step)
    conv_inner = lax.dynamic_update_slice_in_dim(
        jnp.zeros((CONV_WIDTH + 1, INNER), full_type), grad_conv_local, seq_index * inner_local, 1
    )
    part_conv = jnp.concatenate([conv_inner, grad_conv_maps], axis=1)
    part_head = lax.dynamic_update_slice_in_dim(
        jnp.zeros((3, HEADS), full_type), grad_head_local, seq_index * heads_local, 1
    )
    sum_dt, sum_gpre, sum_gnorm, sum_conv, sum_head = lax.psum(
        (part_dt, part_gpre, part_gnorm, part_conv, part_head), ("seq", "wsh")
    )
    rows_model = D // wsh_count
    rows_inner = INNER // wsh_count
    cols_conv = CONV_CH // wsh_count
    cols_head = HEADS // wsh_count
    grad_dt = lax.dynamic_slice_in_dim(sum_dt, wsh_index * rows_model, rows_model, 0)
    grad_gpre = lax.dynamic_slice_in_dim(sum_gpre, wsh_index * rows_model, rows_model, 0)
    grad_gnorm = lax.dynamic_slice_in_dim(sum_gnorm, wsh_index * rows_inner, rows_inner, 0)
    grad_conv = lax.dynamic_slice_in_dim(sum_conv, wsh_index * cols_conv, cols_conv, 1)
    grad_head = lax.dynamic_slice_in_dim(sum_head, wsh_index * cols_head, cols_head, 1)
    part_in = lax.psum_scatter(
        contract_rows(normed_low, grad_projected).astype(jnp.bfloat16),
        "wsh",
        scatter_dimension=0,
        tiled=True,
    ).astype(jnp.float32)
    part_out = lax.psum_scatter(
        contract_rows(out_low, cot_low).astype(jnp.bfloat16), "wsh", scatter_dimension=0, tiled=True
    ).astype(jnp.float32)
    grad_in, grad_out = lax.psum((part_in, part_out), "seq")
    params = (w_in, w_dt, w_out, gain_pre, gain_norm, conv_param, head_param)
    gradients = (grad_in, grad_dt, grad_out, grad_gpre, grad_gnorm, grad_conv, grad_head)
    firsts = (
        first_w_in,
        first_w_dt,
        first_w_out,
        first_gain_pre,
        first_gain_norm,
        first_conv,
        first_head,
    )
    seconds = (
        second_w_in,
        second_w_dt,
        second_w_out,
        second_gain_pre,
        second_gain_norm,
        second_conv,
        second_head,
    )
    step_rates = (rate_matrix, rate_matrix, rate_matrix, rate_gain, rate_gain, rate_conv, rate_head)
    decays = (weight_decay, weight_decay, weight_decay, 0.0, 0.0, 0.0, 0.0)
    updated = [
        adam_update(weights, gradient, first_moment, second_moment, step_rate, decay_amount)
        for weights, gradient, first_moment, second_moment, step_rate, decay_amount in zip(
            params, gradients, firsts, seconds, step_rates, decays
        )
    ]
    new_params = tuple((entry[0] for entry in updated))
    moments = []
    for entry in updated:
        moments.append(entry[1])
        moments.append(entry[2])
    return (block_out, input_grad) + gradients + new_params + tuple(moments)


def solution(mesh):
    in_specs = (
        P("wsh", "seq", None),
        P("wsh", "seq", None),
        P("wsh", None),
        P("wsh", None),
        P("wsh", None),
        P("wsh"),
        P("wsh"),
        P(None, "wsh"),
        P(None, "wsh"),
        P("wsh", None),
        P("wsh", None),
        P("wsh", None),
        P("wsh", None),
        P("wsh", None),
        P("wsh", None),
        P("wsh"),
        P("wsh"),
        P("wsh"),
        P("wsh"),
        P(None, "wsh"),
        P(None, "wsh"),
        P(None, "wsh"),
        P(None, "wsh"),
    )
    out_specs = (
        P("wsh", "seq", None),
        P("wsh", "seq", None),
        P("wsh", None),
        P("wsh", None),
        P("wsh", None),
        P("wsh"),
        P("wsh"),
        P(None, "wsh"),
        P(None, "wsh"),
        P("wsh", None),
        P("wsh", None),
        P("wsh", None),
        P("wsh"),
        P("wsh"),
        P(None, "wsh"),
        P(None, "wsh"),
        P("wsh", None),
        P("wsh", None),
        P("wsh", None),
        P("wsh", None),
        P("wsh", None),
        P("wsh", None),
        P("wsh"),
        P("wsh"),
        P("wsh"),
        P("wsh"),
        P(None, "wsh"),
        P(None, "wsh"),
        P(None, "wsh"),
        P(None, "wsh"),
    )
    return jax.shard_map(shards, mesh=mesh, in_specs=in_specs, out_specs=out_specs, check_vma=False)
```

profile of v0, /device:TPU:0, one launch (start us, length us, event | category | flops | bytes accessed | tf_op | source)
XLA Modules:
  0.0 3477.5 jit_solution(14757523629349529342)
XLA Ops:
  13.1 15.2 all-reduce.30
  29.3 87.1 %all-gather.8.cloned.1.call-done = bf16[1536,6400]{1,0:T(8,128)(2,1)} async-done(((bf16[192,6400]{1,0:T(8,128)(2,1)}), bf16[1536,6400]{1,0:T(8,128)(2,1)}) %all-gather.8.cloned.1.call-update) | async-done | bytes 19660816 | tf_op jit(solution)/shard_map/all_gather | solution.py:173
  116.4 17.6 fusion.175
  137.5 9.2 all-gather.1
  166.4 8.3 all-gather
  174.8 9.1 all-gather.2
  193.2 42.7 %all-to-all-done = bf16[512,4,768]{2,0,1:T(8,128)(2,1)} async-done(((bf16[512,4,768]{2,0,1:T(8,128)(2,1)}), bf16[512,4,768]{2,0,1:T(8,128)(2,1)}, u32[]{:S(2)}, u32[]{:S(2)}) %all-to-all-start) | async-done | bytes 3145760 | tf_op jit(solution)/shard_map/all_to_all | solution.py:190
  238.4 6.7 fusion.109
  245.0 6.6 copy.291
  255.0 1372.2 %while.35 = (s32[]{:T(128)}, f32[12,2048,64]{1,2,0:T(8,128)}, f32[12,2048,64]{1,2,0:T(8,128)}, f32[12,2048]{1,0:T(8,128)}, f32[12]{0:T(128)}, /*index=5*/f32[1,8...) while((s32[]{:T(128)}, f32[12,2048,64]{1,2,0:T(8,128)}, ...), condition=%wide.region_7.8_spmd.clone, body=%wide.region_1.7_spmd.clone.sunk | while | flops 882750464 | bytes 37226728 | solution.py:78
  258.9 97.2 %fusion.270 = f32[1,8,256,2,128]{2,1,4,3,0:T(8,128)S(1)} fusion(f32[1,8,256,2,128]{2,1,4,3,0:T(8,128)S(1)} %bitcast.772), kind=kOutput, calls=%fused_computation.339.clone.1 | output fusion | flops 66584576 | bytes 4194304 | tf_op jit(solution)/shard_map/reduce-window.16
  373.2 97.2 %fusion.270 = f32[1,8,256,2,128]{2,1,4,3,0:T(8,128)S(1)} fusion(f32[1,8,256,2,128]{2,1,4,3,0:T(8,128)S(1)} %bitcast.772), kind=kOutput, calls=%fused_computation.339.clone.1 | output fusion | flops 66584576 | bytes 4194304 | tf_op jit(solution)/shard_map/reduce-window.16
  487.6 97.2 %fusion.270 = f32[1,8,256,2,128]{2,1,4,3,0:T(8,128)S(1)} fusion(f32[1,8,256,2,128]{2,1,4,3,0:T(8,128)S(1)} %bitcast.772), kind=kOutput, calls=%fused_computation.339.clone.1 | output fusion | flops 66584576 | bytes 4194304 | tf_op jit(solution)/shard_map/reduce-window.16
  602.0 97.2 %fusion.270 = f32[1,8,256,2,128]{2,1,4,3,0:T(8,128)S(1)} fusion(f32[1,8,256,2,128]{2,1,4,3,0:T(8,128)S(1)} %bitcast.772), kind=kOutput, calls=%fused_computation.339.clone.1 | output fusion | flops 66584576 | bytes 4194304 | tf_op jit(solution)/shard_map/reduce-window.16
  716.3 97.2 %fusion.270 = f32[1,8,256,2,128]{2,1,4,3,0:T(8,128)S(1)} fusion(f32[1,8,256,2,128]{2,1,4,3,0:T(8,128)S(1)} %bitcast.772), kind=kOutput, calls=%fused_computation.339.clone.1 | output fusion | flops 66584576 | bytes 4194304 | tf_op jit(solution)/shard_map/reduce-window.16
  830.7 97.2 %fusion.270 = f32[1,8,256,2,128]{2,1,4,3,0:T(8,128)S(1)} fusion(f32[1,8,256,2,128]{2,1,4,3,0:T(8,128)S(1)} %bitcast.772), kind=kOutput, calls=%fused_computation.339.clone.1 | output fusion | flops 66584576 | bytes 4194304 | tf_op jit(solution)/shard_map/reduce-window.16
  945.0 97.2 %fusion.270 = f32[1,8,256,2,128]{2,1,4,3,0:T(8,128)S(1)} fusion(f32[1,8,256,2,128]{2,1,4,3,0:T(8,128)S(1)} %bitcast.772), kind=kOutput, calls=%fused_computation.339.clone.1 | output fusion | flops 66584576 | bytes 4194304 | tf_op jit(solution)/shard_map/reduce-window.16
  1059.4 97.2 %fusion.270 = f32[1,8,256,2,128]{2,1,4,3,0:T(8,128)S(1)} fusion(f32[1,8,256,2,128]{2,1,4,3,0:T(8,128)S(1)} %bitcast.772), kind=kOutput, calls=%fused_computation.339.clone.1 | output fusion | flops 66584576 | bytes 4194304 | tf_op jit(solution)/shard_map/reduce-window.16
  1173.8 97.2 %fusion.270 = f32[1,8,256,2,128]{2,1,4,3,0:T(8,128)S(1)} fusion(f32[1,8,256,2,128]{2,1,4,3,0:T(8,128)S(1)} %bitcast.772), kind=kOutput, calls=%fused_computation.339.clone.1 | output fusion | flops 66584576 | bytes 4194304 | tf_op jit(solution)/shard_map/reduce-window.16
  1288.1 97.2 %fusion.270 = f32[1,8,256,2,128]{2,1,4,3,0:T(8,128)S(1)} fusion(f32[1,8,256,2,128]{2,1,4,3,0:T(8,128)S(1)} %bitcast.772), kind=kOutput, calls=%fused_computation.339.clone.1 | output fusion | flops 66584576 | bytes 4194304 | tf_op jit(solution)/shard_map/reduce-window.16
  1402.5 97.2 %fusion.270 = f32[1,8,256,2,128]{2,1,4,3,0:T(8,128)S(1)} fusion(f32[1,8,256,2,128]{2,1,4,3,0:T(8,128)S(1)} %bitcast.772), kind=kOutput, calls=%fused_computation.339.clone.1 | output fusion | flops 66584576 | bytes 4194304 | tf_op jit(solution)/shard_map/reduce-window.16
  1516.8 97.2 %fusion.270 = f32[1,8,256,2,128]{2,1,4,3,0:T(8,128)S(1)} fusion(f32[1,8,256,2,128]{2,1,4,3,0:T(8,128)S(1)} %bitcast.772), kind=kOutput, calls=%fused_computation.339.clone.1 | output fusion | flops 66584576 | bytes 4194304 | tf_op jit(solution)/shard_map/reduce-window.16
  1627.2 7.9 fusion.107
  1635.1 6.5 convert_element_type.170
  1650.7 7.7 all-gather.3
  1658.3 62.5 %all-to-all-done.2 = bf16[4,512,768]{1,2,0:T(8,128)(2,1)} async-done(((bf16[4,512,768]{1,2,0:T(8,128)(2,1)}), bf16[4,512,768]{1,2,0:T(8,128)(2,1)}, u32[]{:S(2)}, u32[]{:S(2)}) %all-to-all-start.2) | async-done | bytes 3145760 | tf_op jit(solution)/shard_map/all_to_all | solution.py:212
  1720.9 5.4 convert_element_type.203
  1726.2 6.5 copy.305
  1732.8 7.4 multiply_reduce_fusion.9
  1740.3 11.8 multiply_reduce_fusion.7
  1752.2 8.6 fusion.102
  1767.4 70.2 %all-to-all-done.3 = bf16[512,4,768]{2,0,1:T(8,128)(2,1)} async-done(((bf16[512,4,768]{2,0,1:T(8,128)(2,1)}), bf16[512,4,768]{2,0,1:T(8,128)(2,1)}, u32[]{:S(2)}, u32[]{:S(2)}) %all-to-all-start.3) | async-done | bytes 3145760 | tf_op jit(solution)/shard_map/all_to_all | solution.py:223
  1837.6 5.1 convert_bitcast_fusion.1
  1842.7 7.8 copy.298
  1850.5 8.5 reshape.1693
  1863.7 943.4 %while.36 = (s32[]{:T(128)}, f32[2048,128]{1,0:T(8,128)}, f32[2048,128]{1,0:T(8,128)}, f32[12,2048,64]{1,2,0:T(8,128)}, f32[12,2048]{1,0:T(8,128)}, /*index=5*/f...) while((s32[]{:T(128)}, f32[2048,128]{1,0:T(8,128)}, ...), condition=%wide.region_28.29_spmd.clone, body=%wide.region_10.28_spmd.clone.sunk | while | flops 4596381696 | bytes 194722736 | solution.py:78
  1924.5 5.5 fusion.314
  1942.2 5.1 fusion.316
  2000.8 5.5 fusion.314
  2077.2 5.5 fusion.314
  2153.5 5.5 fusion.314
  2229.8 5.5 fusion.314
  2306.2 5.5 fusion.314
  2382.5 5.5 fusion.314
  2458.8 5.5 fusion.314
  2535.1 5.5 fusion.314
  2611.5 5.5 fusion.314
  2687.8 5.5 fusion.314
  2764.1 5.5 fusion.314
  2812.5 5.8 multiply_reduce_fusion.13
  2820.7 9.4 bitcast_add_fusion.7
  2830.1 6.6 copy.299
  2836.7 16.6 multiply_reduce_fusion.6
  2855.6 10.0 convolution_convert_fusion.1
  2866.3 5.6 broadcast_multiply_fusion.5
  2876.0 76.2 %all_to_all.87 = bf16[4,512,768]{2,1,0:T(8,128)(2,1)S(1)} all-to-all(bf16[4,512,768]{2,1,0:T(8,128)(2,1)S(1)} %bitcast.800), channel_id=1, replica_groups=mesh['seq'=4,'wsh'=8] {'seq'}, dimensions={0} | all-to-all | bytes 6291456 | tf_op jit(solution)/shard_map/all_to_all | solution.py:230
  2954.3 16.8 convolution_convert_fusion
  2971.1 11.3 fusion.127
  2991.9 19.9 fusion.119
  3011.8 41.2 %all-reduce.31 = (f32[1536]{0:T(1024)S(1)}, f32[3072]{0:T(1024)S(1)}, f32[3,48]{1,0:T(4,128)S(1)}) all-reduce(f32[1536]{0:T(1024)S(1)} %get-tuple-element.479, f32[3072]{0:T(1024)S(1)} %copy-done.70, f32[3,48]{1,0:T(4,128)S(1)} %dynamic_update_slice.42), channel_id=1, replica_groups=mesh['seq'=4,'wsh'=8] {'seq','wsh'}, use_global_device_ids=true, to_apply=%region_37.38 | all-reduce | flops 4752 | bytes 38016 | tf_op jit(solution)/shard_map/psum | solution.py:256
  3060.0 9.2 reduce-scatter.8.cloned.1.call-done
  3069.2 133.3 %reduce-scatter.6.cloned.1.call-done = bf16[192,6400]{1,0:T(8,128)(2,1)} async-done(((bf16[1536,6400]{1,0:T(8,128)(2,1)}), bf16[192,6400]{1,0:T(8,128)(2,1)}) %reduce-scatter.6.cloned.1.call-update) | async-done | bytes 2457616 | tf_op jit(solution)/shard_map/reduce_scatter | solution.py:268
  3202.5 248.9 %all-reduce.38 = (f32[192,6400]{1,0:T(8,128)}, f32[384,1536]{1,0:T(8,128)S(1)}) all-reduce(bf16[192,6400]{1,0:T(8,128)(2,1)} %reduce-scatter.6.cloned.1.call-done, bf16[384,1536]{1,0:T(8,128)(2,1)} %reduce-scatter.8.cloned.1.call-done), channel_id=1, replica_groups=mesh['seq'=4,'wsh'=8] {'seq'}, use_global_device_ids=true, to_apply=%region_32.33 | all-reduce | flops 1818624 | bytes 10911744 | tf_op jit(solution)/shard_map/psum | solution.py:277
  3451.5 14.4 multiply_subtract_fusion
  (2483 shorter events, 1143.6 us)
Async XLA Ops:
  7.2 21.1 copy-start.35
  7.2 109.2 %all-gather.8.cloned.1.call-start = ((), (), s32[]{:S(2)}) async-start(), calls=%async_computation.9 | async-start | bytes 22118400 | tf_op jit(solution)/shard_map/all_gather | solution.py:173
  11.5 174.4 %all-gather.10.cloned.1.call-start = ((), (), s32[]{:S(2)}) async-start(), calls=%async_computation.10 | async-start | bytes 1310720 | tf_op jit(solution)/shard_map/all_gather | solution.py:193
  28.3 118.6 %copy-start.64 = (f32[1536]{0:T(1024)}, f32[1536]{0:T(1024)S(1)}, u32[]{:S(2)}) copy-start(f32[1536]{0:T(1024)S(1)} %convert_element_type.154) | copy-start | bytes 18436
  29.3 117.7 %copy-start.79 = (f32[512]{0:T(512)}, f32[512]{0:T(512)S(1)}, u32[]{:S(2)}) copy-start(f32[512]{0:T(512)S(1)} %fusion.150) | copy-start | bytes 6148
  29.3 108.2 %copy-start.45 = (f32[192,48]{0,1:T(8,128)S(1)}, f32[192,48]{0,1:T(8,128)}, u32[]{:S(2)}) copy-start(f32[192,48]{0,1:T(8,128)} %param.30) | copy-start | bytes 110596
  148.3 12.0 all-to-all-start.1
  160.3 75.6 %all-to-all-start = ((bf16[512,4,768]{2,0,1:T(8,128)(2,1)}), bf16[512,4,768]{2,0,1:T(8,128)(2,1)}, u32[]{:S(2)}, u32[]{:S(2)}) async-start(bf16[512,4,768]{2,0,1:T(8,128)(2,1)} %bitcast.801), calls=%async_computation | async-start | bytes 6291456 | tf_op jit(solution)/shard_map/all_to_all | solution.py:190
  165.1 9.7 copy-start.85
  165.1 1575.1 %all-gather.12.cloned.1.call-start = ((), (), s32[]{:S(2)}) async-start(), calls=%async_computation.11 | async-start | bytes 10616832 | tf_op jit(solution)/shard_map/all_gather | solution.py:175
  184.2 54.1 %copy-start.56 = (f32[768]{0:T(1024)}, f32[768]{0:T(1024)S(1)}, u32[]{:S(2)}) copy-start(f32[768]{0:T(1024)S(1)} %get-tuple-element.490) | copy-start | bytes 9220
  184.2 54.1 %copy-start.58 = (f32[768]{0:T(1024)}, f32[768]{0:T(1024)S(1)}, u32[]{:S(2)}) copy-start(f32[768]{0:T(1024)S(1)} %get-tuple-element.491) | copy-start | bytes 9220
  184.2 54.1 %copy-start.60 = (f32[768]{0:T(1024)}, f32[768]{0:T(1024)S(1)}, u32[]{:S(2)}) copy-start(f32[768]{0:T(1024)S(1)} %get-tuple-element.492) | copy-start | bytes 9220
  184.2 54.1 %copy-start.62 = (f32[768]{0:T(1024)}, f32[768]{0:T(1024)S(1)}, u32[]{:S(2)}) copy-start(f32[768]{0:T(1024)S(1)} %get-tuple-element.493) | copy-start | bytes 9220
  184.8 1442.5 %copy-start.87 = (f32[12]{0:T(128)}, f32[12]{0:T(128)S(1)}, u32[]{:S(2)}) copy-start(f32[12]{0:T(128)S(1)} %get-tuple-element.613) | copy-start | bytes 148
  1645.8 75.0 %all-to-all-start.2 = ((bf16[4,512,768]{1,2,0:T(8,128)(2,1)}), bf16[4,512,768]{1,2,0:T(8,128)(2,1)}, u32[]{:S(2)}, u32[]{:S(2)}) async-start(bf16[4,512,768]{1,2,0:T(8,128)(2,1)} %copy.295), calls=%async_computation.2 | async-start | bytes 6291456 | tf_op jit(solution)/shard_map/all_to_all | solution.py:212
  1658.3 93.8 %copy-start.52 = (f32[8,1,384]{2,1,0:T(1,128)}, f32[8,1,384]{2,1,0:T(1,128)S(1)}, u32[]{:S(2)}) copy-start(f32[8,1,384]{2,1,0:T(1,128)S(1)} %convert_element_type.206) | copy-start | bytes 36868
  1740.2 11.9 copy-start.81
  1740.3 11.9 slice-start
  1740.3 11.9 slice-start.4
  1740.3 11.9 slice-start.1
  1740.3 11.9 slice-start.5
  1762.7 74.9 %all-to-all-start.3 = ((bf16[512,4,768]{2,0,1:T(8,128)(2,1)}), bf16[512,4,768]{2,0,1:T(8,128)(2,1)}, u32[]{:S(2)}, u32[]{:S(2)}) async-start(bf16[512,4,768]{2,0,1:T(8,128)(2,1)} %bitcast.802), calls=%async_computation.3 | async-start | bytes 6291456 | tf_op jit(solution)/shard_map/all_to_all | solution.py:223
  1882.8 23.2 copy-start
  1948.3 9.6 copy-start.101
  1959.1 23.1 copy-start
  2035.5 23.1 copy-start
  2101.0 9.6 copy-start.101
  2111.8 23.1 copy-start
  2177.3 9.6 copy-start.101
  2188.1 23.1 copy-start
  2264.5 23.1 copy-start
  2340.8 23.1 copy-start
  2417.1 23.1 copy-start
  2493.4 23.1 copy-start
  2558.9 9.6 copy-start.101
  2569.7 23.1 copy-start
  2646.1 23.1 copy-start
  2722.4 23.1 copy-start
  2809.1 45.1 %all-to-all-start.5 = ((bf16[4,512,12]{1,2,0:T(8,128)(2,1)}), bf16[4,512,12]{1,2,0:T(8,128)(2,1)S(1)}, u32[]{:S(2)}, u32[]{:S(2)}) async-start(bf16[4,512,12]{1,2,0:T(8,128)(2,1)} %copy.302), calls=%async_computation.6 | async-start | bytes 131072 | tf_op jit(solution)/shard_map/all_to_all | solution.py:233
  2812.4 141.9 %reduce-scatter.4.cloned.1.call-start = ((), (), s32[]{:S(2)}) async-start(), calls=%async_computation.12 | async-start | bytes 1310720 | tf_op jit(solution)/shard_map/reduce_scatter | solution.py:238
  2820.7 168.0 %all-reduce.37.cloned.1.call-start = ((), (), s32[]{:S(2)}) async-start(), calls=%async_computation.15 | async-start | bytes 802816 | tf_op jit(solution)/shard_map/psum | solution.py:256
  2836.7 17.4 copy-start.36
  2836.7 17.4 copy-start.65
  2836.7 17.4 copy-start.80
  2855.5 213.6 %reduce-scatter.8.cloned.1.call-start = ((), (), s32[]{:S(2)}) async-start(), calls=%async_computation.14 | async-start | bytes 10616832 | tf_op jit(solution)/shard_map/reduce_scatter | solution.py:274
  2865.7 336.9 %reduce-scatter.6.cloned.1.call-start = ((), (), s32[]{:S(2)}) async-start(), calls=%async_computation.13 | async-start | bytes 22118400 | tf_op jit(solution)/shard_map/reduce_scatter | solution.py:268
  2971.1 11.3 slice-start.2
  2971.1 11.3 slice-start.3
  2991.8 20.0 copy-start.70
  2991.8 61.2 %copy-start.67 = (f32[512]{0:T(512)S(1)}, f32[512]{0:T(512)}, u32[]{:S(2)}) copy-start(f32[512]{0:T(512)} %copy-done.66) | copy-start | bytes 6148
  2991.8 61.2 %copy-start.96 = (f32[192]{0:T(256)S(1)}, f32[192]{0:T(256)}, u32[]{:S(2)}) copy-start(f32[192]{0:T(256)} %param.32) | copy-start | bytes 2308
  2991.8 61.2 %copy-start.97 = (f32[192]{0:T(256)S(1)}, f32[192]{0:T(256)}, u32[]{:S(2)}) copy-start(f32[192]{0:T(256)} %param.42) | copy-start | bytes 2308
  2991.8 61.2 %copy-start.98 = (f32[192]{0:T(256)S(1)}, f32[192]{0:T(256)}, u32[]{:S(2)}) copy-start(f32[192]{0:T(256)} %param.43) | copy-start | bytes 2308
  2991.8 61.9 %copy-start.84 = (f32[384]{0:T(512)S(1)}, f32[384]{0:T(512)}, u32[]{:S(2)}) copy-start(f32[384]{0:T(512)} %param.33) | copy-start | bytes 4612
  2991.8 61.9 %copy-start.91 = (f32[384]{0:T(512)S(1)}, f32[384]{0:T(512)}, u32[]{:S(2)}) copy-start(f32[384]{0:T(512)} %param.44) | copy-start | bytes 4612
  2991.9 61.9 %copy-start.92 = (f32[384]{0:T(512)S(1)}, f32[384]{0:T(512)}, u32[]{:S(2)}) copy-start(f32[384]{0:T(512)} %param.45) | copy-start | bytes 4612
  2991.9 62.5 %copy-start.86 = (f32[3,6]{1,0:T(4,128)S(1)}, f32[3,6]{1,0:T(4,128)}, u32[]{:S(2)}) copy-start(f32[3,6]{1,0:T(4,128)} %param.35) | copy-start | bytes 220
  2991.9 62.5 %copy-start.93 = (f32[3,6]{1,0:T(4,128)S(1)}, f32[3,6]{1,0:T(4,128)}, u32[]{:S(2)}) copy-start(f32[3,6]{1,0:T(4,128)} %param.48) | copy-start | bytes 220
  2991.9 62.5 %copy-start.94 = (f32[3,6]{1,0:T(4,128)S(1)}, f32[3,6]{1,0:T(4,128)}, u32[]{:S(2)}) copy-start(f32[3,6]{1,0:T(4,128)} %param.49) | copy-start | bytes 220
  3451.4 14.4 copy-start.40
  3451.4 14.4 copy-start.33
  3451.5 14.4 copy-start.38
  3451.5 14.5 copy-start.39
  (454 other events, 1718.6 us)
Sparse Core Ops, SparseCore 0:
  11.6 104.7 all-gather.7
  137.6 29.8 all-gather.9
  170.0 57.6 all-gather.11
  2820.8 27.2 reduce-scatter.3
  2855.7 132.1 all-reduce.36
  2991.2 77.8 reduce-scatter.7
  3072.8 129.6 reduce-scatter.5
where the time goes:
time: 3490 us; the launch traced here: 3480 us
  other arithmetic  1610 us (46%)
  matrix products  573 us (16%)
  blocking collectives  416 us (12%)
  waiting for transfers between devices  409 us (12%)
  local copies, waits for them, and re-layouts  393 us (11%)
  loops' own time  36.5 us (1%)
    another operation x182, other arithmetic  1320 us
    psum x1, blocking collectives, shards(): grad_in, grad_out = lax.psum((part_in, part_out), 'seq')  249 us
    dot_general x37, matrix products, state_space(): jnp.einsum('cln,csn->cls', out_blocks, in_blocks, precision=highest)  144 us
    reduce_scatter x1, waiting for transfers between devices, shards(): lax.psum_scatter(contract_rows(normed_low, grad_projected).astype(jnp.bfl...  133 us
    while x936, local copies, waits for them, and re-layouts  115 us
    dot_general x36, matrix products, state_space(): diagonal = jnp.einsum('hcls,cshp->clhp', mixing, inflow, precision=highest)  112 us
    dot_general x48, matrix products, state_space(): jnp.einsum('csn,cshp->chpn', in_blocks, weighted, precision=highest)  109 us
    all_gather x1, waiting for transfers between devices, shards(): lax.all_gather(w_in.astype(low_type), 'wsh', axis=0, tiled=True)  87.1 us
  transfers between devices with their start and end apart: 12, of which 7 were waited for; matrix products, arithmetic and copies ran while one was open for 45% of the time, Pallas kernels for 0%

commit v1 on v0

v1 whole, which is shorter than its diff:
```python
import functools

import jax
import jax.numpy as jnp
from jax import lax
from jax.experimental import pallas as pl
from jax.experimental.pallas import tpu as pltpu
from jax.sharding import PartitionSpec as P

D = 1536
HEADS = 48
HEAD_DIM = 64
STATE = 128
CONV_WIDTH = 4
STEP = 2
INNER = 3072
CONV_CH = 3328
BLOCK = 128
LANES = 128
WIDE = 256
HALO = 16
GROUPS = INNER // WIDE
PACK = CONV_CH + LANES
LOG2E = 1.4426950408889634
VMEM_LIMIT = 56 * 1024 * 1024

norm_eps = 1e-05
beta_one = 0.9
beta_two = 0.999
adam_eps = 1e-08
rate_matrix = 0.01
rate_gain = 0.4
rate_conv = 0.1
rate_head = 1.0
weight_decay = 0.1
highest = lax.Precision.HIGHEST
low_type = jnp.bfloat16
full_type = jnp.float32


def dot(left_side, right_side, dims=((1,), (0,)), precision=None):
    return lax.dot_general(
        left_side, right_side, (dims, ((), ())), precision=precision, preferred_element_type=full_type
    )


def dot_nt(left_side, right_side):
    return dot(left_side, right_side, ((1,), (1,)))


def sigmoid(vals):
    return 0.5 * jnp.tanh(0.5 * vals) + 0.5


def lane_ids(shape):
    return lax.broadcasted_iota(jnp.int32, shape, len(shape) - 1)


def widen(vals, first=0):
    left = lane_ids((vals.shape[0], LANES)) < HEAD_DIM
    pairs = [
        jnp.where(left, vals[:, first + i : first + i + 1], vals[:, first + i + 1 : first + i + 2])
        for i in (0, 2)
    ]
    return jnp.concatenate(pairs, axis=1)


def to_front(vals, step):
    return pltpu.roll(vals, lax.rem(LANES - 4 * step, LANES), 1)


def head_rows(ref, step):
    eight = ref[pl.ds(pl.multiple_of(8 * (step // 2), 8), 8), :]
    return pltpu.roll(eight, 4 * lax.rem(step, 2), 0)


def step_terms(raw, head):
    shifted = raw + head[1:2]
    small = jnp.exp(-jnp.abs(shifted))
    log_part = jnp.where(
        small < 0.01, small * (1.0 - small * (0.5 - small * (1.0 / 3.0))), jnp.log(1.0 + small)
    )
    step_sizes = jnp.maximum(shifted, 0.0) + log_part
    slope = jnp.where(shifted >= 0.0, 1.0, small) / (1.0 + small)
    return step_sizes, slope, -jnp.exp(head[0:1])


def convolve(sig, conv, rows):
    total = conv[4:5] + conv[0:1] * sig[HALO - 3 : HALO - 3 + rows, :]
    for k in range(1, CONV_WIDTH):
        total = total + conv[k : k + 1] * sig[HALO - 3 + k : HALO - 3 + k + rows, :]
    return total


def triangle(lower):
    rows = lax.broadcasted_iota(jnp.int32, (BLOCK, BLOCK), 0)
    cols = lax.broadcasted_iota(jnp.int32, (BLOCK, BLOCK), 1)
    return rows >= cols if lower else rows <= cols


def states_kernel(
    sig_ref, maps_ref, raw_ref, conv_ref, conv_maps_ref, head_ref,
    x_ref, bc_ref, run_ref, lag_ref, run_t_ref, lag_t_ref, enter_ref, enter_all_ref, tail_ref, offs_ref,
    states_ref, send_ref,
    sig, in_t,
):
    step = pl.program_id(0)
    rows = x_ref.shape[0]
    blocks = rows // BLOCK

    @pl.when(step == 0)
    def _():
        sig[...] = maps_ref[...].astype(full_type)
        pre = convolve(sig, conv_maps_ref[...], rows)
        maps = pre * sigmoid(pre)
        bc_ref[...] = maps
        in_t[...] = maps[:, :STATE].T.astype(low_type)
        step_sizes, _, rate = step_terms(raw_ref[HALO:, :].astype(full_type), head_ref[...])
        rates = step_sizes * rate * LOG2E
        log_steps = jnp.log2(step_sizes)
        lower = jnp.where(triangle(True), 1.0, 0.0)
        offset = jnp.zeros((1, LANES), full_type)
        offs_ref[...] = jnp.zeros(offs_ref.shape, full_type)
        for c in range(blocks):
            at = slice(c * BLOCK, (c + 1) * BLOCK)
            run = dot(lower, rates[at], precision=highest)
            lag = run - log_steps[at]
            run_ref[at, :] = run
            lag_ref[at, :] = lag
            run_t_ref[:, at] = run.T
            lag_t_ref[:, at] = lag.T
            enter_ref[at, :] = jnp.exp2(run)
            enter_all_ref[at, :] = jnp.exp2(run + offset)
            tail_ref[at, :] = jnp.exp2(run[BLOCK - 1 : BLOCK] - lag)
            offs_ref[c : c + 1, :] = offset
            offset = offset + run[BLOCK - 1 : BLOCK]
        offs_ref[blocks : blocks + 1, :] = offset

    sig[...] = sig_ref[...].astype(full_type)
    pre = convolve(sig, conv_ref[...], rows)
    x = pre * sigmoid(pre)
    x_ref[...] = x
    tail = to_front(tail_ref[...], step)
    last = to_front(offs_ref[...], step)
    state = jnp.zeros((STATE, WIDE), full_type)
    for c in range(blocks):
        at = slice(c * BLOCK, (c + 1) * BLOCK)
        weighted = (x[at] * widen(tail[at])).astype(low_type)
        fade = jnp.exp2(widen(last[c + 1 : c + 2] - last[c : c + 1]))
        state = state * fade + dot(in_t[:, at], weighted)
        states_ref[c] = state.astype(low_type)
    send_ref[:STATE, :] = state.astype(low_type)
    total = widen(last[blocks : blocks + 1])
    high = total.astype(low_type).astype(full_type)
    ids = lax.broadcasted_iota(jnp.int32, (16, WIDE), 0)
    extra = jnp.where(ids == 0, high, jnp.where(ids == 1, total - high, 0.0))
    send_ref[STATE:, :] = extra.astype(low_type)


def outputs_kernel(x_ref, bc_ref, run_ref, lag_t_ref, enter_ref, states_ref, head_ref, y_ref, inter):
    step = pl.program_id(0)
    rows = x_ref.shape[0]
    blocks = rows // BLOCK
    lower = triangle(True)

    @pl.when(step == 0)
    def _():
        for c in range(blocks):
            at = slice(c * BLOCK, (c + 1) * BLOCK)
            maps = bc_ref[at, :].astype(low_type)
            inter[c] = dot_nt(maps[:, STATE:], maps[:, :STATE])

    run = to_front(run_ref[...], step)
    enter = to_front(enter_ref[...], step)
    lag_rows = head_rows(lag_t_ref, step)
    skip = widen(to_front(head_ref[...], step)[2:3])
    left = lane_ids((BLOCK, LANES)) < HEAD_DIM
    for c in range(blocks):
        at = slice(c * BLOCK, (c + 1) * BLOCK)
        x = x_ref[at, :]
        parts = []
        for pair in range(2):
            mixes = []
            for i in range(2):
                h = 2 * pair + i
                lag_row = lag_rows[h : h + 1, at]
                power = jnp.where(lower, run[at, h : h + 1] - lag_row, -1e30)
                mixes.append((jnp.exp2(power) * inter[c]).astype(low_type))
            half = x[:, pair * LANES : (pair + 1) * LANES].astype(low_type)
            zero = jnp.zeros_like(half)
            stacked = jnp.concatenate([jnp.where(left, half, zero), jnp.where(left, zero, half)], axis=0)
            parts.append(dot(jnp.concatenate(mixes, axis=1), stacked))
        y = jnp.concatenate(parts, axis=1) + skip * x
        if c > 0:
            out_map = bc_ref[at, STATE:].astype(low_type)
            y = y + widen(enter[at]) * dot(out_map, states_ref[c - 1])
        y_ref[at, :] = y


def norm_kernel(
    y_ref, gate_ref, back_ref, gain_ref, bc_ref, enter_ref, state_ref,
    normed_ref, grad_y_ref, grad_gate_ref, grad_gain_ref, grad_state_ref,
    gated, low_y,
):
    step = pl.program_id(0)
    rows = y_ref.shape[0]

    @pl.when(step == 0)
    def _():
        grad_gain_ref[...] = jnp.zeros(grad_gain_ref.shape, full_type)
        grad_state_ref[...] = jnp.zeros(grad_state_ref.shape, full_type)

    out_map = bc_ref[:, STATE:]
    out_low = out_map.astype(low_type)
    out_t = out_map.T.astype(low_type)
    squares = jnp.zeros((rows, WIDE), full_type)
    cross = jnp.zeros((rows, WIDE), full_type)
    for j in range(GROUPS):
        at = slice(j * WIDE, (j + 1) * WIDE)
        enter = widen(enter_ref[...], 4 * j)
        y = y_ref[:, at] + enter * dot(out_low, state_ref[:, at])
        y_low = y.astype(low_type)
        low_y[:, at] = y_low
        gate = gate_ref[:, at]
        vals = y_low.astype(full_type) * (gate * sigmoid(gate))
        gated[:, at] = vals
        squares = squares + vals * vals
        cross = cross + vals * (back_ref[:, at] * gain_ref[0:1, at])
    inv = lax.rsqrt(jnp.sum(squares, axis=1, keepdims=True) * (1.0 / INNER) + norm_eps)
    pull = inv * inv * inv * (jnp.sum(cross, axis=1, keepdims=True) * (1.0 / INNER))
    for j in range(GROUPS):
        at = slice(j * WIDE, (j + 1) * WIDE)
        gain = gain_ref[0:1, at]
        back = back_ref[:, at]
        vals = gated[:, at]
        scaled = vals * inv
        normed_ref[:, at] = (scaled * gain).astype(low_type)
        grad_gain_ref[0:1, at] += jnp.sum(back * scaled, axis=0, keepdims=True)
        grad_vals = back * gain * inv - vals * pull
        gate = gate_ref[:, at]
        sig = sigmoid(gate)
        silu = gate * sig
        grad_y = (grad_vals * silu).astype(low_type)
        grad_y_ref[:, at] = grad_y
        slope = sig + silu * (1.0 - sig)
        grad_gate_ref[:, at] = (grad_vals * low_y[:, at].astype(full_type) * slope).astype(low_type)
        enter = widen(enter_ref[...], 4 * j)
        grad_state_ref[:, at] += dot(out_t, (grad_y.astype(full_type) * enter).astype(low_type))


def backward_kernel(
    sig_ref, raw_ref, conv_ref, head_ref, grad_y_ref, bc_ref,
    lag_ref, run_t_ref, enter_ref, tail_ref, offs_ref, states_ref, state_in_ref, grad_in_ref,
    grad_sig_ref, edge_ref, last_ref, grad_conv_ref, grad_skip_ref, grad_head_ref,
    sig, padded, inter, grad_inter, grad_maps, out_t, run_rows, run_cols, run_ends, weighs,
):
    step = pl.program_id(0)
    rows = grad_y_ref.shape[0]
    blocks = rows // BLOCK
    upper = triangle(False)

    @pl.when(step == 0)
    def _():
        for c in range(blocks):
            at = slice(c * BLOCK, (c + 1) * BLOCK)
            maps = bc_ref[at, :].astype(low_type)
            inter[c] = dot_nt(maps[:, :STATE], maps[:, STATE:])
            out_t[:, at] = bc_ref[at, STATE:].T.astype(low_type)
        grad_inter[...] = jnp.zeros(grad_inter.shape, full_type)
        grad_maps[...] = jnp.zeros(grad_maps.shape, full_type)
        run_rows[...] = jnp.zeros(run_rows.shape, full_type)
        run_cols[...] = jnp.zeros(run_cols.shape, full_type)
        run_ends[...] = jnp.zeros(run_ends.shape, full_type)
        weighs[...] = jnp.zeros(weighs.shape, full_type)
        padded[...] = jnp.zeros(padded.shape, full_type)

    def conv_back(grad_pre):
        conv = conv_ref[...]
        grad_sig = conv[3:4] * padded[HALO : HALO + rows, :]
        edge = conv[3:4] * padded[8:HALO, :]
        for k in range(3):
            grad_sig = grad_sig + conv[k : k + 1] * padded[HALO + 3 - k : HALO + 3 - k + rows, :]
            edge = edge + conv[k : k + 1] * padded[11 - k : 19 - k, :]
        grad_sig_ref[...] = grad_sig.astype(low_type)
        edge_ref[...] = edge
        last_ref[...] = grad_sig[rows - 16 :]
        sums = [
            jnp.sum(grad_pre * sig[HALO - 3 + k : HALO - 3 + k + rows, :], axis=0, keepdims=True)
            for k in range(CONV_WIDTH)
        ]
        sums.append(jnp.sum(grad_pre, axis=0, keepdims=True))
        sums.append(jnp.zeros((3, WIDE), full_type))
        grad_conv_ref[...] = jnp.concatenate(sums, axis=0)

    @pl.when(step < GROUPS)
    def _():
        sig[...] = sig_ref[...].astype(full_type)
        lag = to_front(lag_ref[...], step)
        run_all = head_rows(run_t_ref, step)
        enter = to_front(enter_ref[...], step)
        tail = to_front(tail_ref[...], step)
        offs = to_front(offs_ref[...], step)
        skip = widen(to_front(head_ref[...], step)[2:3])
        left = lane_ids((BLOCK, LANES)) < HEAD_DIM
        heads_of = lax.broadcasted_iota(jnp.int32, (WIDE, LANES), 0) // HEAD_DIM + 4 * step
        picks = jnp.where(heads_of == lane_ids((WIDE, LANES)), 1.0, 0.0).astype(low_type)
        state_in = state_in_ref[...].astype(full_type)
        grad_state = grad_in_ref[...].astype(full_type)
        grad_skip = jnp.zeros((1, WIDE), full_type)
        pre_all = convolve(sig, conv_ref[...], rows)

        def head_sums(vals):
            high = vals.astype(low_type)
            rest = (vals - high.astype(full_type)).astype(low_type)
            return dot(high, picks) + dot(rest, picks)

        for c in reversed(range(blocks)):
            at = slice(c * BLOCK, (c + 1) * BLOCK)
            pre = pre_all[at]
            gate = sigmoid(pre)
            x = pre * gate
            x_low = x.astype(low_type)
            x_round = x_low.astype(full_type)
            grad_y = grad_y_ref[at, :]
            grad_y_full = grad_y.astype(full_type)
            in_map = bc_ref[at, :STATE].astype(low_type)
            out_map = bc_ref[at, STATE:].astype(low_type)
            tail_c = widen(tail[at])
            enter_c = widen(enter[at])
            entering = state_in * jnp.exp2(widen(offs[c : c + 1]))
            if c > 0:
                entering = entering + states_ref[c - 1].astype(full_type)
            leaving = states_ref[c].astype(full_type) + state_in * jnp.exp2(widen(offs[c + 1 : c + 2]))
            entering_low = entering.astype(low_type)
            grad_low = grad_state.astype(low_type)
            ends = jnp.sum(grad_state * leaving, axis=0, keepdims=True)
            run_ends[c : c + 1, :] += head_sums(jnp.concatenate([ends, jnp.zeros((7, WIDE), full_type)], axis=0))[0:1]
            grad_x = tail_c * dot(in_map, grad_low)
            grad_maps[at, :STATE] += dot_nt((x * tail_c).astype(low_type), grad_low)
            swept = grad_y_full * enter_c
            swept_low = swept.astype(low_type)
            through = swept * dot(out_map, entering_low)
            grad_maps[at, STATE:] += dot_nt(swept_low, entering_low)
            fade = jnp.exp2(widen(offs[c + 1 : c + 2] - offs[c : c + 1]))
            grad_state = grad_state * fade + dot(out_t[:, at], swept_low)
            parts = []
            sums = []
            for pair in range(2):
                half = slice(pair * LANES, (pair + 1) * LANES)
                grad_half = grad_y[:, half]
                zero = jnp.zeros_like(grad_half)
                stacked = jnp.concatenate(
                    [jnp.where(left, grad_half, zero), jnp.where(left, zero, grad_half)], axis=0
                )
                cross = dot_nt(x_low[:, half], stacked)
                mixes = []
                for i in range(2):
                    h = 2 * pair + i
                    run_row = run_all[h : h + 1, at]
                    power = jnp.where(upper, run_row - lag[at, h : h + 1], -1e30)
                    decay = jnp.exp2(power)
                    mix = (decay * inter[c]).astype(low_type)
                    mixes.append(mix)
                    cross_h = cross[:, i * LANES : (i + 1) * LANES]
                    grad_inter[c] += cross_h * decay
                    sums.append(jnp.sum(cross_h * mix.astype(full_type), axis=0, keepdims=True))
                parts.append(dot(jnp.concatenate(mixes, axis=1), stacked))
            sums.append(jnp.zeros((4, BLOCK), full_type))
            run_rows[pl.ds(pl.multiple_of(8 * step, 8), 8), at] = jnp.concatenate(sums, axis=0)
            grad_x = grad_x + jnp.concatenate(parts, axis=1)
            weigh = head_sums(x_round * grad_x)
            weighs[at, :] += weigh
            run_cols[at, :] += head_sums(through) - weigh
            grad_skip = grad_skip + jnp.sum(grad_y_full * x, axis=0, keepdims=True)
            grad_x = grad_x + skip * grad_y_full
            padded[HALO + c * BLOCK : HALO + (c + 1) * BLOCK, :] = grad_x * (gate + x * (1.0 - gate))
        grad_skip_ref[...] = jnp.broadcast_to(grad_skip, grad_skip_ref.shape)
        conv_back(padded[HALO : HALO + rows, :])

    @pl.when(step == GROUPS)
    def _():
        sig[...] = sig_ref[...].astype(full_type)
        pre_all = convolve(sig, conv_ref[...], rows)
        for c in range(blocks):
            at = slice(c * BLOCK, (c + 1) * BLOCK)
            maps = bc_ref[at, :].astype(low_type)
            grad_block = grad_inter[c]
            grad_bc = grad_maps[at, :] + jnp.concatenate(
                [
                    dot(grad_block.astype(low_type), maps[:, STATE:]),
                    dot(grad_block.T.astype(low_type), maps[:, :STATE]),
                ],
                axis=1,
            )
            pre = pre_all[at]
            gate = sigmoid(pre)
            padded[HALO + c * BLOCK : HALO + (c + 1) * BLOCK, :] = grad_bc * (gate + pre * gate * (1.0 - gate))
        conv_back(padded[HALO : HALO + rows, :])

    @pl.when(step == GROUPS + 1)
    def _():
        head = head_ref[...]
        step_sizes, slope, rate = step_terms(raw_ref[HALO:, :].astype(full_type), head)
        ratio = jnp.where(step_sizes > 1e-30, slope / jnp.maximum(step_sizes, 1e-30), 1.0)
        used = lane_ids((BLOCK, LANES)) < HEADS
        later = jnp.where(upper, 1.0, 0.0)
        rate_sum = jnp.zeros((1, LANES), full_type)
        bias_sum = jnp.zeros((1, LANES), full_type)
        for c in range(blocks):
            at = slice(c * BLOCK, (c + 1) * BLOCK)
            by_head = [run_rows[8 * j : 8 * j + 4, at] for j in range(GROUPS)]
            by_head.append(jnp.zeros((LANES - HEADS, BLOCK), full_type))
            grad_run = jnp.concatenate(by_head, axis=0).T + run_cols[at, :]
            grad_rates = dot(later, grad_run, precision=highest) + run_ends[c : c + 1, :]
            grad_raw = slope[at] * rate * grad_rates + ratio[at] * weighs[at, :]
            grad_raw = jnp.where(used, grad_raw, 0.0)
            grad_sig_ref[at, :LANES] = grad_raw.astype(low_type)
            grad_sig_ref[at, LANES:] = jnp.zeros((BLOCK, LANES), low_type)
            rate_sum = rate_sum + jnp.sum(grad_rates * step_sizes[at], axis=0, keepdims=True)
            bias_sum = bias_sum + jnp.sum(grad_raw, axis=0, keepdims=True)
        grad_head_ref[...] = jnp.concatenate(
            [rate_sum * rate, bias_sum, jnp.zeros((6, LANES), full_type)], axis=0
        )


def run_states(packed, conv, head):
    rows = packed.shape[0] - HALO
    blocks = rows // BLOCK
    whole = lambda shape: pl.BlockSpec(shape, lambda j: (0,) * len(shape))
    small = jax.ShapeDtypeStruct((rows, LANES), full_type)
    small_t = jax.ShapeDtypeStruct((LANES, rows), full_type)
    return pl.pallas_call(
        states_kernel,
        grid=(GROUPS,),
        in_specs=[
            pl.BlockSpec((rows + HALO, WIDE), lambda j: (0, j)),
            pl.BlockSpec((rows + HALO, WIDE), lambda j: (0, GROUPS)),
            pl.BlockSpec((rows + HALO, LANES), lambda j: (0, CONV_CH // LANES)),
            pl.BlockSpec((8, WIDE), lambda j: (0, j)),
            pl.BlockSpec((8, WIDE), lambda j: (0, GROUPS)),
            whole((8, LANES)),
        ],
        out_specs=[
            pl.BlockSpec((rows, WIDE), lambda j: (0, j)),
            whole((rows, WIDE)),
            whole((rows, LANES)),
            whole((rows, LANES)),
            whole((LANES, rows)),
            whole((LANES, rows)),
            whole((rows, LANES)),
            whole((rows, LANES)),
            whole((rows, LANES)),
            whole((16, LANES)),
            pl.BlockSpec((blocks, STATE, WIDE), lambda j: (0, 0, j)),
            pl.BlockSpec((STATE + 16, WIDE), lambda j: (0, j)),
        ],
        out_shape=[
            jax.ShapeDtypeStruct((rows, INNER), full_type),
            jax.ShapeDtypeStruct((rows, WIDE), full_type),
            small, small, small_t, small_t, small, small, small,
            jax.ShapeDtypeStruct((16, LANES), full_type),
            jax.ShapeDtypeStruct((blocks, STATE, INNER), low_type),
            jax.ShapeDtypeStruct((STATE + 16, INNER), low_type),
        ],
        scratch_shapes=[
            pltpu.VMEM((rows + HALO, WIDE), full_type),
            pltpu.VMEM((STATE, rows), low_type),
        ],
        compiler_params=pltpu.CompilerParams(vmem_limit_bytes=VMEM_LIMIT),
        cost_estimate=pl.CostEstimate(flops=10**9, bytes_accessed=15 * 10**6, transcendentals=10**6),
        name="scan_states",
    )(packed, packed, packed, conv, conv, head)


def run_outputs(x, bc, run, lag_t, enter, states, head):
    rows = x.shape[0]
    blocks = rows // BLOCK
    whole = lambda shape: pl.BlockSpec(shape, lambda j: (0,) * len(shape))
    return pl.pallas_call(
        outputs_kernel,
        grid=(GROUPS,),
        in_specs=[
            pl.BlockSpec((rows, WIDE), lambda j: (0, j)),
            whole((rows, WIDE)),
            whole((rows, LANES)),
            whole((LANES, rows)),
            whole((rows, LANES)),
            pl.BlockSpec((blocks, STATE, WIDE), lambda j: (0, 0, j)),
            whole((8, LANES)),
        ],
        out_specs=pl.BlockSpec((rows, WIDE), lambda j: (0, j)),
        out_shape=jax.ShapeDtypeStruct((rows, INNER), full_type),
        scratch_shapes=[pltpu.VMEM((blocks, BLOCK, BLOCK), full_type)],
        compiler_params=pltpu.CompilerParams(vmem_limit_bytes=VMEM_LIMIT),
        cost_estimate=pl.CostEstimate(flops=10**10, bytes_accessed=15 * 10**6, transcendentals=3 * 10**6),
        name="scan_outputs",
    )(x, bc, run, lag_t, enter, states, head)


def run_norm(y, gate, back, gain, bc, enter, state):
    rows = y.shape[0]
    part = BLOCK
    by_rows = lambda cols: pl.BlockSpec((part, cols), lambda i: (i, 0))
    whole = lambda shape: pl.BlockSpec(shape, lambda i: (0,) * len(shape))
    return pl.pallas_call(
        norm_kernel,
        grid=(rows // part,),
        in_specs=[
            by_rows(INNER), by_rows(INNER), by_rows(INNER), whole((8, INNER)),
            by_rows(WIDE), by_rows(LANES), whole((STATE, INNER)),
        ],
        out_specs=[by_rows(INNER), by_rows(INNER), by_rows(INNER), whole((8, INNER)), whole((STATE, INNER))],
        out_shape=[
            jax.ShapeDtypeStruct((rows, INNER), low_type),
            jax.ShapeDtypeStruct((rows, INNER), low_type),
            jax.ShapeDtypeStruct((rows, INNER), low_type),
            jax.ShapeDtypeStruct((8, INNER), full_type),
            jax.ShapeDtypeStruct((STATE, INNER), full_type),
        ],
        scratch_shapes=[pltpu.VMEM((part, INNER), full_type), pltpu.VMEM((part, INNER), low_type)],
        compiler_params=pltpu.CompilerParams(vmem_limit_bytes=VMEM_LIMIT),
        cost_estimate=pl.CostEstimate(flops=10**9, bytes_accessed=30 * 10**6, transcendentals=3 * 10**6),
        name="gated_norm",
    )(y, gate, back, gain, bc, enter, state)


def run_backward(packed, conv, head, grad_y, bc, lag, run_t, enter, tail, offs, states, state_in, grad_in):
    rows = grad_y.shape[0]
    blocks = rows // BLOCK
    whole = lambda shape: pl.BlockSpec(shape, lambda j: (0,) * len(shape))
    most = lambda j, top: jnp.minimum(j, top)
    return pl.pallas_call(
        backward_kernel,
        grid=(GROUPS + 2,),
        in_specs=[
            pl.BlockSpec((rows + HALO, WIDE), lambda j: (0, most(j, GROUPS))),
            pl.BlockSpec((rows + HALO, LANES), lambda j: (0, CONV_CH // LANES)),
            pl.BlockSpec((8, WIDE), lambda j: (0, most(j, GROUPS))),
            whole((8, LANES)),
            pl.BlockSpec((rows, WIDE), lambda j: (0, most(j, GROUPS - 1))),
            whole((rows, WIDE)),
            whole((rows, LANES)),
            whole((LANES, rows)),
            whole((rows, LANES)),
            whole((rows, LANES)),
            whole((16, LANES)),
            pl.BlockSpec((blocks, STATE, WIDE), lambda j: (0, 0, most(j, GROUPS - 1))),
            pl.BlockSpec((STATE, WIDE), lambda j: (0, most(j, GROUPS - 1))),
            pl.BlockSpec((STATE, WIDE), lambda j: (0, most(j, GROUPS - 1))),
        ],
        out_specs=[
            pl.BlockSpec((rows, WIDE), lambda j: (0, j)),
            pl.BlockSpec((8, WIDE), lambda j: (0, most(j, GROUPS))),
            pl.BlockSpec((16, WIDE), lambda j: (0, most(j, GROUPS))),
            pl.BlockSpec((8, WIDE), lambda j: (0, most(j, GROUPS))),
            pl.BlockSpec((8, WIDE), lambda j: (0, most(j, GROUPS - 1))),
            whole((8, LANES)),
        ],
        out_shape=[
            jax.ShapeDtypeStruct((rows, PACK), low_type),
            jax.ShapeDtypeStruct((8, CONV_CH), full_type),
            jax.ShapeDtypeStruct((16, CONV_CH), full_type),
            jax.ShapeDtypeStruct((8, CONV_CH), full_type),
            jax.ShapeDtypeStruct((8, INNER), full_type),
            jax.ShapeDtypeStruct((8, LANES), full_type),
        ],
        scratch_shapes=[
            pltpu.VMEM((rows + HALO, WIDE), full_type),
            pltpu.VMEM((rows + 2 * HALO, WIDE), full_type),
            pltpu.VMEM((blocks, BLOCK, BLOCK), full_type),
            pltpu.VMEM((blocks, BLOCK, BLOCK), full_type),
            pltpu.VMEM((rows, WIDE), full_type),
            pltpu.VMEM((STATE, rows), low_type),
            pltpu.VMEM((LANES, rows), full_type),
            pltpu.VMEM((rows, LANES), full_type),
            pltpu.VMEM((8, LANES), full_type),
            pltpu.VMEM((rows, LANES), full_type),
        ],
        compiler_params=pltpu.CompilerParams(vmem_limit_bytes=VMEM_LIMIT),
        cost_estimate=pl.CostEstimate(flops=2 * 10**10, bytes_accessed=20 * 10**6, transcendentals=5 * 10**6),
        name="scan_backward",
    )(packed, packed, conv, head, grad_y, bc, lag, run_t, enter, tail, offs, states, state_in, grad_in)


def adam_update(weights, gradient, first_moment, second_moment, step_rate, decay_amount):
    next_first = beta_one * first_moment + (1.0 - beta_one) * gradient
    next_second = beta_two * second_moment + (1.0 - beta_two) * gradient * gradient
    corrected = (
        next_first
        / (1.0 - beta_one**STEP)
        / (jnp.sqrt(next_second / (1.0 - beta_two**STEP)) + adam_eps)
    )
    return (weights - step_rate * (corrected + decay_amount * weights), next_first, next_second)


def pad_rows(vals, rows):
    return jnp.pad(vals, ((0, rows - vals.shape[0]), (0, 0)))


def shards(
    inputs, cotangent, w_in, w_dt, w_out, gain_pre, gain_norm, conv_param, head_param,
    first_w_in, second_w_in, first_w_dt, second_w_dt, first_w_out, second_w_out,
    first_gain_pre, second_gain_pre, first_gain_norm, second_gain_norm,
    first_conv, second_conv, first_head, second_head,
):
    wsh_count = lax.axis_size("wsh")
    seq_count = lax.axis_size("seq")
    seq_index = lax.axis_index("seq")
    wsh_index = lax.axis_index("wsh")
    rows_model = D // wsh_count
    rows_inner = INNER // wsh_count
    cols_conv = CONV_CH // wsh_count
    cols_head = HEADS // wsh_count
    flat = jnp.concatenate(
        [gain_pre, gain_norm, conv_param.reshape(-1), head_param.reshape(-1)]
    ).astype(low_type)
    count = flat.shape[0]
    flat = jnp.pad(flat, (0, -count % LANES))
    small = lax.all_gather(flat, "wsh", axis=0)
    part_sig = jnp.concatenate(
        [w_in[:, INNER:].astype(low_type), w_dt.astype(low_type), jnp.zeros((rows_model, LANES - HEADS), low_type)],
        axis=1,
    )
    full_sig = lax.all_gather(part_sig, "wsh", axis=0, tiled=True)
    full_gate = lax.all_gather(w_in[:, :INNER].astype(low_type), "wsh", axis=0, tiled=True)
    full_out = lax.all_gather(w_out.astype(low_type), "wsh", axis=0, tiled=True)
    small = small.astype(full_type)
    ends = [rows_model, rows_model + rows_inner, rows_model + rows_inner + 5 * cols_conv]
    gain_in = small[:, : ends[0]].reshape(-1)
    gain_out = small[:, ends[0] : ends[1]].reshape(1, -1)
    conv = small[:, ends[1] : ends[2]].reshape(wsh_count, 5, cols_conv).transpose(1, 0, 2).reshape(5, CONV_CH)
    head = small[:, ends[2] : ends[2] + 3 * cols_head].reshape(wsh_count, 3, cols_head)
    head = head.transpose(1, 0, 2).reshape(3, HEADS)
    conv = pad_rows(conv, 8)
    head = jnp.pad(head, ((0, 5), (0, LANES - HEADS)))
    tokens_low = inputs[0]
    cot_low = cotangent[0]
    rows = tokens_low.shape[0]
    before = lax.ppermute(tokens_low[rows - HALO :], "seq", [(i, i + 1) for i in range(seq_count - 1)])
    tokens = jnp.concatenate([before, tokens_low], axis=0).astype(full_type)
    inv_rms = lax.rsqrt(jnp.mean(tokens * tokens, axis=-1, keepdims=True) + norm_eps)
    normed_all = (tokens * inv_rms * gain_in).astype(low_type)
    packed = dot(normed_all, full_sig).astype(low_type)
    tokens = tokens[HALO:]
    inv_rms = inv_rms[HALO:]
    normed = normed_all[HALO:]
    x, bc, run, lag, run_t, lag_t, enter, enter_all, tail, offs, states, send = run_states(packed, conv, head)
    gathered = lax.all_gather(send, "seq", axis=0)
    y = run_outputs(x, bc, run, lag_t, enter, states, head)
    gate_vals = dot(normed, full_gate)
    back = dot_nt(cot_low, full_out)
    totals = gathered[:, STATE].astype(full_type) + gathered[:, STATE + 1].astype(full_type)
    state_in = jnp.zeros((STATE, INNER), full_type)
    for z in range(seq_count - 1):
        between = jnp.zeros((INNER,), full_type)
        for other in range(z + 1, seq_count - 1):
            between = between + jnp.where(other < seq_index, totals[other], 0.0)
        state_in = state_in + jnp.where(z < seq_index, jnp.exp2(between), 0.0) * gathered[z, :STATE].astype(full_type)
    state_in = state_in.astype(low_type)
    gain_rows = jnp.broadcast_to(gain_out, (8, INNER))
    normed_out, grad_y, grad_gate, part_gnorm, grad_state = run_norm(
        y, gate_vals, back, gain_rows, bc, enter_all, state_in
    )
    grad_states = lax.all_gather(grad_state.astype(low_type), "seq", axis=0)
    block_out = (tokens + dot(normed_out, full_out)).astype(low_type)[None]
    part_out = lax.psum_scatter(
        dot(normed_out, cot_low, ((0,), (0,))).astype(low_type), "wsh", scatter_dimension=0, tiled=True
    )
    part_gate = lax.psum_scatter(
        dot(normed, grad_gate, ((0,), (0,))).astype(low_type), "wsh", scatter_dimension=0, tiled=True
    )
    grad_normed = dot_nt(grad_gate, full_gate)
    grad_in = jnp.zeros((STATE, INNER), full_type)
    for z in range(1, seq_count):
        between = jnp.zeros((INNER,), full_type)
        for other in range(1, z):
            between = between + jnp.where(other > seq_index, totals[other], 0.0)
        grad_in = grad_in + jnp.where(z > seq_index, jnp.exp2(between), 0.0) * grad_states[z].astype(full_type)
    grad_in = grad_in.astype(low_type)
    grad_pack, edge, last, part_conv, part_skip, part_head = run_backward(
        packed, conv, head, grad_y, bc, lag, run_t, enter, tail, offs, states, state_in, grad_in
    )
    after = lax.ppermute(edge, "seq", [(i, i - 1) for i in range(1, seq_count)])
    fixed = jnp.concatenate([last[:8], last[8:] + after], axis=0).astype(low_type)
    grad_pack = lax.dynamic_update_slice(grad_pack, fixed, (rows - 16, 0))
    part_sig = lax.psum_scatter(
        dot(normed, grad_pack, ((0,), (0,))).astype(low_type), "wsh", scatter_dimension=0, tiled=True
    )
    grad_normed = grad_normed + dot_nt(grad_pack, full_sig)
    scaled = tokens * inv_rms
    part_gpre = jnp.sum(grad_normed * scaled, axis=0)
    pulled = grad_normed * gain_in
    grad_tokens = inv_rms * (pulled - scaled * jnp.mean(pulled * scaled, axis=-1, keepdims=True))
    input_grad = (cot_low.astype(full_type) + grad_tokens)[None]
    skip_sums = part_skip[0].reshape(HEADS, HEAD_DIM).sum(axis=1)
    small_sums = lax.psum(
        jnp.concatenate(
            [part_gpre, part_gnorm[0], part_conv[:5].reshape(-1), part_head[0, :HEADS], part_head[1, :HEADS], skip_sums]
        ),
        ("seq", "wsh"),
    )
    cuts = [D, D + INNER, D + INNER + 5 * CONV_CH]
    grad_gpre = lax.dynamic_slice_in_dim(small_sums[: cuts[0]], wsh_index * rows_model, rows_model, 0)
    grad_gnorm = lax.dynamic_slice_in_dim(small_sums[cuts[0] : cuts[1]], wsh_index * rows_inner, rows_inner, 0)
    grad_conv = lax.dynamic_slice_in_dim(
        small_sums[cuts[1] : cuts[2]].reshape(5, CONV_CH), wsh_index * cols_conv, cols_conv, 1
    )
    grad_head = lax.dynamic_slice_in_dim(
        small_sums[cuts[2] :].reshape(3, HEADS), wsh_index * cols_head, cols_head, 1
    )
    grad_out, sum_gate, sum_sig = (
        lax.psum(part.astype(full_type), "seq") for part in (part_out, part_gate, part_sig)
    )
    grad_in_w = jnp.concatenate([sum_gate, sum_sig[:, :CONV_CH]], axis=1)
    grad_dt = sum_sig[:, CONV_CH : CONV_CH + HEADS]
    params = (w_in, w_dt, w_out, gain_pre, gain_norm, conv_param, head_param)
    gradients = (grad_in_w, grad_dt, grad_out, grad_gpre, grad_gnorm, grad_conv, grad_head)
    firsts = (first_w_in, first_w_dt, first_w_out, first_gain_pre, first_gain_norm, first_conv, first_head)
    seconds = (second_w_in, second_w_dt, second_w_out, second_gain_pre, second_gain_norm, second_conv, second_head)
    step_rates = (rate_matrix, rate_matrix, rate_matrix, rate_gain, rate_gain, rate_conv, rate_head)
    decays = (weight_decay, weight_decay, weight_decay, 0.0, 0.0, 0.0, 0.0)
    updated = [adam_update(*items) for items in zip(params, gradients, firsts, seconds, step_rates, decays)]
    new_params = tuple(entry[0] for entry in updated)
    moments = []
    for entry in updated:
        moments.append(entry[1])
        moments.append(entry[2])
    return (block_out, input_grad) + gradients + new_params + tuple(moments)


def solution(mesh):
    rows, vec, cols = P("wsh", None), P("wsh"), P(None, "wsh")
    tokens = P("wsh", "seq", None)
    params = (rows, rows, rows, vec, vec, cols, cols)
    moments = tuple(spec for spec in params for _ in range(2))
    in_specs = (tokens, tokens) + params + moments
    out_specs = (tokens, tokens) + params + params + moments
    return jax.shard_map(shards, mesh=mesh, in_specs=in_specs, out_specs=out_specs, check_vma=False)
```

time: 3490 us -> 1170 us (0.34)
  other arithmetic: 1610 us -> 50.3 us
  matrix products: 573 us -> 93.1 us
  local copies, waits for them, and re-layouts: 393 us -> 67.9 us
  waiting for transfers between devices: 409 us -> 523 us
  blocking collectives: 416 us -> 315 us
  Pallas kernels: 0 us -> 94.7 us
  loops' own time: 36.5 us -> 0 us
    another operation x218 -> x6, other arithmetic: 1320 us -> 3.57 us
    dot_general x226 -> x9, matrix products: 573 us -> 93.1 us  [dot(): lax.dot_general(left_side, right_side, (dims, ((), ())), precision=precis...]
    all_to_all x5 -> x0, waiting for transfers between devices: 179 us -> none  [the longest x1 70.2 us: shards(): lax.all_to_all(grad_vals.astype(low_type), 'seq', split_axis=1, concat_ax...]
    unnamed x7 -> x11, waiting for transfers between devices: 0.11 us -> 162 us
    all_gather x3 -> x5, waiting for transfers between devices: 87.1 us -> 225 us  [the longest x1 50.7 us: shards(): full_out = lax.all_gather(w_out.astype(low_type), 'wsh', axis=0, tiled=True)]
    while x936 -> x0, local copies, waits for them, and re-layouts: 115 us -> none
    pallas_call x0 -> x4, Pallas kernels: none -> 94.7 us  [the longest x1 46.2 us: run_backward(): pl.pallas_call(backward_kernel, grid=(GROUPS + 2,), in_specs=[pl.BlockSpe...]
    mul x88 -> x0, other arithmetic: 76.6 us -> none  [the longest x36 34.1 us: state_space(): step_sizes * decay_rate]
  transfers between devices with their start and end apart: 12 -> 11, of which waited for: 7 -> 10; matrix products, arithmetic and copies ran while one was open for 45% -> 11% of each run, Pallas kernels for 0% -> 3%
where the time goes in v1:
time: 1170 us
  waiting for transfers between devices  523 us (45%)
  blocking collectives  315 us (27%)
  Pallas kernels  94.7 us (8%)
  matrix products  93.1 us (8%)
  local copies, waits for them, and re-layouts  67.9 us (6%)
  other arithmetic  50.3 us (4%)
  between operations  14.5 us (1%)
    psum x1, blocking collectives, shards(): lax.psum(part.astype(full_type), 'seq')  305 us
    unnamed x11, waiting for transfers between devices  162 us
    dot_general x9, matrix products, dot(): lax.dot_general(left_side, right_side, (dims, ((), ())), precision=precis...  93.1 us
    reduce_scatter x1, waiting for transfers between devices, shards(): lax.psum_scatter(dot(normed_out, cot_low, ((0,), (0,))).astype(low_type),...  78.4 us
    psum x1, waiting for transfers between devices, shards(): lax.psum(jnp.concatenate([part_gpre, part_gnorm[0], part_conv[:5].reshape...  56.3 us
    all_gather x1, waiting for transfers between devices, shards(): full_out = lax.all_gather(w_out.astype(low_type), 'wsh', axis=0, tiled=True)  50.7 us
    all_gather x1, waiting for transfers between devices, shards(): grad_states = lax.all_gather(grad_state.astype(low_type), 'seq', axis=0)  49.1 us
    unnamed x65, local copies, waits for them, and re-layouts  48.8 us
  transfers between devices with their start and end apart: 11, of which 10 were waited for; matrix products, arithmetic and copies ran while one was open for 11% of the time, Pallas kernels for 3%

profile of v1, /device:TPU:0, one launch (start us, length us, event | category | flops | bytes accessed | tf_op | source)
XLA Modules:
  0.0 1166.1 jit_solution(11052439994530441074)
XLA Ops:
  7.3 2.6 convert.33
  9.9 1.1 slice.151
  11.2 3.2 concatenate.22
  14.5 1.1 slice.155
  15.7 2.9 convert_element_type.106
  18.8 4.9 collective-permute-start
  24.0 9.4 all-gather.3
  36.2 45.1 %all-gather.10.cloned.1.call-done = bf16[1536,3456]{1,0:T(8,128)(2,1)} async-done(((bf16[192,3456]{1,0:T(8,128)(2,1)}), bf16[1536,3456]{1,0:T(8,128)(2,1)}) %all-gather.10.cloned.1.call-update) | async-done | bytes 10616848 | tf_op jit(solution)/shard_map/all_gather | solution.py:624
  81.3 11.4 convolution_convert_fusion.3.sig_ref.maps_ref.raw_ref
  92.7 15.7 %scan_states.1 = (f32[512,3072]{1,0:T(8,128)}, f32[512,256]{1,0:T(8,128)}, f32[512,128]{1,0:T(8,128)}, f32[512,128]{1,0:T(8,128)}, f32[128,512]{1,0:T(8,128)}, /...) custom-call(bf16[528,3456]{1,0:T(8,128)(2,1)} %convolution_convert_f, ...), custom_call_target="tpu_custom_call" | custom-call | flops 1000000000 | bytes 15000000 | tf_op jit(solution)/shard_map/scan_states/pallas_call | solution.py:432
  108.9 33.7 %all-gather.12.cloned.1.call-done = bf16[1536,3072]{1,0:T(8,128)(2,1)} async-done(((bf16[192,3072]{1,0:T(8,128)(2,1)}), bf16[1536,3072]{1,0:T(8,128)(2,1)}) %all-gather.12.cloned.1.call-update) | async-done | bytes 9437200 | tf_op jit(solution)/shard_map/all_gather | solution.py:625
  142.6 10.6 fusion.14.gate_ref
  153.2 50.7 %all-gather.14.cloned.1.call-done = bf16[3072,1536]{1,0:T(8,128)(2,1)} async-done(((bf16[384,1536]{1,0:T(8,128)(2,1)}), bf16[3072,1536]{1,0:T(8,128)(2,1)}) %all-gather.14.cloned.1.call-update) | async-done | bytes 9437200 | tf_op jit(solution)/shard_map/all_gather | solution.py:626
  203.9 9.8 fusion.8.back_ref
  213.8 15.9 %scan_outputs.1.y_ref = f32[512,3072]{1,0:T(8,128)} custom-call(f32[512,3072]{1,0:T(8,128)} %get-tuple-element.53.x_ref, f32[512,256]{1,0:T(8,128)} %get-tuple-element.54.bc_ref, f32[512,128]{1,0:T(8,128)} %get-tuple-element.55.run_ref, f32[128,512]{1,0:T(8,128)} %get-tuple-element.56.lag_t_ref, f32[512,128]{1,0:T(8,128)} %get-tuple-element.57.enter_ref, ...), custom_call_target="tpu_custom_call" | custom-call | flops 10000000000 | bytes 15000000 | tf_op jit(solution)/shard_map/scan_outputs/pallas_call | solution.py:479
  229.6 46.3 %all-gather.16.cloned.1.call-done = bf16[576,3072]{1,0:T(8,128)(2,1)} async-done(((bf16[144,3072]{1,0:T(8,128)(2,1)}), bf16[576,3072]{1,0:T(8,128)(2,1)}) %all-gather.16.cloned.1.call-update) | async-done | bytes 3538960 | tf_op jit(solution)/shard_map/all_gather | solution.py:648
  276.0 1.1 fusion.17
  277.1 2.9 fusion.6.state_ref.state_in_ref
  280.7 17.0 %gated_norm.1 = (bf16[512,3072]{1,0:T(8,128)(2,1)}, bf16[512,3072]{1,0:T(8,128)(2,1)}, bf16[512,3072]{1,0:T(8,128)(2,1)}, f32[8,3072]{1,0:T(8,128)}, f32[128,3072]{1,0:T(8,128)}) custom-call(f32[512,3072]{1,0:T(8,128)} %scan_outputs.1.y_ref, f32[512,3072]{1,0:T(8,128)} %fusion.14.gate_ref, f32[512,3072]{1,0:T(8,128)} %fusion.8.back_ref, ...), custom_call_target="tpu_custom_call" | custom-call | flops 1000000000 | bytes 30000000 | tf_op jit(solution)/shard_map/gated_norm/pallas_call | solution.py:505
  297.7 2.4 convert_element_type.117
  300.8 2.1 maximum_convert_fusion
  302.9 0.9 slice.137
  303.8 9.5 fusion.33
  313.3 49.1 %all-gather.18.cloned.1.call-done = bf16[512,3072]{1,0:T(8,128)(2,1)} async-done(((bf16[128,3072]{1,0:T(8,128)(2,1)}), bf16[512,3072]{1,0:T(8,128)(2,1)}) %all-gather.18.cloned.1.call-update) | async-done | bytes 3145744 | tf_op jit(solution)/shard_map/all_gather | solution.py:664
  362.4 2.9 fusion.11.grad_in_ref
  365.3 46.2 %scan_backward.1 = (bf16[512,3456]{1,0:T(8,128)(2,1)}, f32[8,3328]{1,0:T(8,128)}, f32[16,3328]{1,0:T(8,128)}, f32[8,3328]{1,0:T(8,128)}, f32[8,3072]{1,0:T(8,128)}, /*index=5*/f32[8,128]{1,0:T(8,128)}) custom-call(bf16[528,3456]{1,0:T(8,128)(2,1)} %convolution_convert_fusion.3.sig_ref.maps_ref.raw_ref, ...), custom_call_target="tpu_custom_call" | custom-call | flops 20000000000 | bytes 20000000 | tf_op jit(solution)/shard_map/scan_backward/pallas_call | solution.py:532
  411.5 1.3 collective-permute-start.1
  412.8 0.9 slice.224
  413.7 0.9 reshape.163
  414.7 0.8 slice_bitcast_fusion.3
  415.4 0.9 slice_reduce_fusion
  416.5 1.8 collective-permute-done.1
  418.3 0.9 add_convert_fusion
  419.9 11.7 %multiply_reduce_fusion.1 = (f32[1536]{0:T(1024)S(1)}, f32[512]{0:T(512)S(1)}, f32[512,1536]{1,0:T(8,128)}) fusion(f32[528,1536]{1,0:T(8,128)S(1)} %copy-done.1, f32[512]{0:T(512)S(1)} %slice.129, f32[1536]{0:T(1024)S(1)} %mul.362, f32[512,1536]{1,0:T(8,128)} %fusion.33, bf16[512,3456]{1,0:T(8,128)(2,1)} %maximum_dynamic-update-slice_fusion, ...), kind=kOutput, calls=%fused_computation.14 | convolution fusion | flops 5441320960 | bytes 23609344 | tf_op jit(solution)/shard_map/dot_general | solution.py:42
  431.6 0.7 concatenate.25
  432.5 9.5 convolution_convert_fusion.2
  442.1 9.4 convolution_convert_fusion.1
  451.5 10.8 convolution_convert_fusion
  462.3 6.4 copy.105
  468.8 6.4 copy.102
  475.1 6.3 copy.103
  481.5 10.4 fusion.2
  492.0 2.5 add_bitcast_fusion
  494.6 56.3 %all-reduce.7.cloned.1.call-done = f32[21392]{0:T(1024)} async-done(((f32[21392]{0:T(1024)}), f32[21392]{0:T(1024)}) %all-reduce.7.cloned.1.call-update) | async-done | bytes 85584 | tf_op jit(solution)/shard_map/psum | solution.py:696
  550.8 0.9 slice.172
  551.7 0.7 slice.173
  552.5 0.7 slice.171
  553.2 0.7 slice.170
  554.6 0.7 multiply_subtract_fusion.4
  556.0 0.7 multiply_subtract_fusion.3
  556.7 76.0 %reduce-scatter.10.cloned.1.call-done = bf16[192,3072]{1,0:T(8,128)(2,1)} async-done(((bf16[1536,3072]{1,0:T(8,128)(2,1)}), bf16[192,3072]{1,0:T(8,128)(2,1)}) %reduce-scatter.10.cloned.1.call-update) | async-done | bytes 1179664
  632.8 1.6 copy.111
  634.4 78.4 %reduce-scatter.8.cloned.1.call-done = bf16[384,1536]{1,0:T(8,128)(2,1)} async-done(((bf16[3072,1536]{1,0:T(8,128)(2,1)}), bf16[384,1536]{1,0:T(8,128)(2,1)}) %reduce-scatter.8.cloned.1.call-update) | async-done | bytes 1179664 | tf_op jit(solution)/shard_map/reduce_scatter | solution.py:666
  712.8 85.7 %reduce-scatter.12.cloned.1.call-done = bf16[192,3456]{1,0:T(8,128)(2,1)} async-done(((bf16[1536,3456]{1,0:T(8,128)(2,1)}), bf16[192,3456]{1,0:T(8,128)(2,1)}) %reduce-scatter.12.cloned.1.call-update) | async-done | bytes 1327120
  798.5 2.5 copy.113
  801.0 305.3 %all-reduce.8 = (f32[192,3456]{0,1:T(8,128)}, f32[192,3072]{0,1:T(8,128)}, f32[384,1536]{1,0:T(8,128)}) all-reduce(bf16[192,3456]{0,1:T(8,128)(2,1)S(1)} %copy.113, bf16[192,3072]{0,1:T(8,128)(2,1)S(1)} %copy.111, bf16[384,1536]{1,0:T(8,128)(2,1)} %reduce-scatter.8.cloned.1.call-done), channel_id=1, replica_groups=mesh['seq'=4,'wsh'=8] {'seq'}, use_global_device_ids=true, to_apply=%region_5.6 | all-reduce | flops 1843200 | bytes 11059200 | tf_op jit(solution)/shard_map/psum | solution.py:712
  1106.3 2.2 slice.168
  1108.5 16.6 %multiply_subtract_fusion = (f32[192,6400]{0,1:T(8,128)}, f32[192,6400]{0,1:T(8,128)}, f32[192,6400]{0,1:T(8,128)}, f32[192,6400]{0,1:T(8,128)}) fusion(f32[192,6400]{0,1:T(8,128)} %copy.105, f32[192,3328]{0,1:T(8,128)S(1)} %slice.168, f32[192,3072]{0,1:T(8,128)} %get-tuple-element.229, f32[192,6400]{0,1:T(8,128)} %copy.102, f32[192,6400]{0,1:T(8,128)} %copy.103), kind=kLoop, calls=%fused_computation.6 | loop fusion | flops 19660800 | bytes 39321600 | tf_op jit(solution)/shard_map/sub | solution.py:593
  1125.1 6.3 copy.106
  1131.4 6.3 copy.107
  1137.7 6.3 copy.108
  1144.0 6.5 copy.109
  1150.5 1.5 multiply_subtract_fusion.2
  1152.0 7.3 multiply_subtract_fusion.1
  (115 shorter events, 8.0 us)
Async XLA Ops:
  7.2 3.8 copy-start.6
  7.2 74.1 %all-gather.10.cloned.1.call-start = ((), (), s32[]{:S(2)}) async-start(), calls=%async_computation.3 | async-start | bytes 11943936 | tf_op jit(solution)/shard_map/all_gather | solution.py:624
  14.5 128.1 %all-gather.12.cloned.1.call-start = ((), (), s32[]{:S(2)}) async-start(), calls=%async_computation.4 | async-start | bytes 10616832 | tf_op jit(solution)/shard_map/all_gather | solution.py:625
  15.6 3.1 copy-start
  15.7 8.0 copy-start.8
  15.7 8.2 copy-start.16
  15.7 8.2 copy-start.14
  15.7 8.2 copy-start.22
  15.7 188.2 %all-gather.14.cloned.1.call-start = ((), (), s32[]{:S(2)}) async-start(), calls=%async_computation.5 | async-start | bytes 10616832 | tf_op jit(solution)/shard_map/all_gather | solution.py:626
  18.7 257.3 %all-gather.16.cloned.1.call-start = ((), (), s32[]{:S(2)}) async-start(), calls=%async_computation.8 | async-start | bytes 4423680 | tf_op jit(solution)/shard_map/all_gather | solution.py:648
  18.8 16.6 %collective-permute-start = (bf16[16,1536]{1,0:T(8,128)(2,1)S(1)}, bf16[16,1536]{1,0:T(8,128)(2,1)S(1)}, u32[]{:S(2)}, u32[]{:S(2)}) collective-permute-start(bf16[16,1536]{1,0:T(8,128)(2,1)S(1)} %slice_bitcast_fusion.2), channel_id=1, source_target_pairs={{0,8},{8,16},{16,24},{1,9},{9,17},{17,25},{2,10},{10,18},{18,26},{... | collective-permute-start | bytes 147464 | tf_op jit(solution)/shard_map/ppermute | solution.py:639
  36.2 106.4 %copy-start.4 = (bf16[528,1536]{1,0:T(8,128)(2,1)}, bf16[528,1536]{1,0:T(8,128)(2,1)S(1)}, u32[]{:S(2)}) copy-start(bf16[528,1536]{1,0:T(8,128)(2,1)S(1)} %multiply_convert_fusion) | copy-start | bytes 4866052
  108.4 254.0 %all-gather.18.cloned.1.call-start = ((), (), s32[]{:S(2)}) async-start(), calls=%async_computation.9 | async-start | bytes 3932160 | tf_op jit(solution)/shard_map/all_gather | solution.py:664
  300.1 250.7 %all-reduce.7.cloned.1.call-start = ((), (), s32[]{:S(2)}) async-start(), calls=%async_computation.7 | async-start | bytes 172032 | tf_op jit(solution)/shard_map/psum | solution.py:696
  300.7 3.1 copy-start.26
  365.3 54.6 %copy-start.1 = (f32[528,1536]{1,0:T(8,128)S(1)}, f32[528,1536]{1,0:T(8,128)}, u32[]{:S(2)}) copy-start(f32[528,1536]{1,0:T(8,128)} %maximum_convert_fusion) | copy-start | bytes 9732100
  411.5 6.8 collective-permute-start.1
  432.3 200.5 %reduce-scatter.10.cloned.1.call-start = ((), (), s32[]{:S(2)}) async-start(), calls=%async_computation.10 | async-start | bytes 10616832
  442.0 270.7 %reduce-scatter.8.cloned.1.call-start = ((), (), s32[]{:S(2)}) async-start(), calls=%async_computation.6 | async-start | bytes 10616832 | tf_op jit(solution)/shard_map/reduce_scatter | solution.py:666
  451.5 347.0 %reduce-scatter.12.cloned.1.call-start = ((), (), s32[]{:S(2)}) async-start(), calls=%async_computation.11 | async-start | bytes 11943936
  481.5 10.4 copy-start.3
  481.5 10.4 copy-start.5
  491.9 62.1 %copy-start.23 = (f32[192]{0:T(256)S(1)}, f32[192]{0:T(256)}, u32[]{:S(2)}) copy-start(f32[192]{0:T(256)} %param.28) | copy-start | bytes 2308
  491.9 62.0 %copy-start.24 = (f32[192]{0:T(256)S(1)}, f32[192]{0:T(256)}, u32[]{:S(2)}) copy-start(f32[192]{0:T(256)} %param.38) | copy-start | bytes 2308
  491.9 62.0 %copy-start.25 = (f32[192]{0:T(256)S(1)}, f32[192]{0:T(256)}, u32[]{:S(2)}) copy-start(f32[192]{0:T(256)} %param.39) | copy-start | bytes 2308
  491.9 62.7 %copy-start.15 = (f32[384]{0:T(512)S(1)}, f32[384]{0:T(512)}, u32[]{:S(2)}) copy-start(f32[384]{0:T(512)} %param.29) | copy-start | bytes 4612
  491.9 62.7 %copy-start.18 = (f32[384]{0:T(512)S(1)}, f32[384]{0:T(512)}, u32[]{:S(2)}) copy-start(f32[384]{0:T(512)} %param.40) | copy-start | bytes 4612
  491.9 62.7 %copy-start.19 = (f32[384]{0:T(512)S(1)}, f32[384]{0:T(512)}, u32[]{:S(2)}) copy-start(f32[384]{0:T(512)} %param.41) | copy-start | bytes 4612
  492.0 63.4 %copy-start.17 = (f32[3,6]{1,0:T(4,128)S(1)}, f32[3,6]{1,0:T(4,128)}, u32[]{:S(2)}) copy-start(f32[3,6]{1,0:T(4,128)} %param.31) | copy-start | bytes 220
  492.0 63.3 %copy-start.20 = (f32[3,6]{1,0:T(4,128)S(1)}, f32[3,6]{1,0:T(4,128)}, u32[]{:S(2)}) copy-start(f32[3,6]{1,0:T(4,128)} %param.44) | copy-start | bytes 220
  492.0 63.3 %copy-start.21 = (f32[3,6]{1,0:T(4,128)S(1)}, f32[3,6]{1,0:T(4,128)}, u32[]{:S(2)}) copy-start(f32[3,6]{1,0:T(4,128)} %param.45) | copy-start | bytes 220
  492.0 64.0 %copy-start.9 = (f32[5,416]{1,0:T(8,128)S(1)}, f32[5,416]{1,0:T(8,128)}, u32[]{:S(2)}) copy-start(f32[5,416]{1,0:T(8,128)} %param.30) | copy-start | bytes 24964
  492.0 64.0 %copy-start.12 = (f32[5,416]{1,0:T(8,128)S(1)}, f32[5,416]{1,0:T(8,128)}, u32[]{:S(2)}) copy-start(f32[5,416]{1,0:T(8,128)} %param.42) | copy-start | bytes 24964
  492.0 64.0 %copy-start.13 = (f32[5,416]{1,0:T(8,128)S(1)}, f32[5,416]{1,0:T(8,128)}, u32[]{:S(2)}) copy-start(f32[5,416]{1,0:T(8,128)} %param.43) | copy-start | bytes 24964
  1144.0 6.5 copy-start.7
  1144.0 6.5 copy-start.10
  1144.0 6.5 copy-start.11
  1144.0 8.0 copy-start.2
Sparse Core Ops, SparseCore 0:
  14.6 66.6 all-gather.9
  83.7 58.8 all-gather.11
  145.1 58.8 all-gather.13
  205.9 69.9 all-gather.15
  300.2 62.0 all-gather.17
  432.4 118.3 all-reduce.6
  554.3 78.3 reduce-scatter.9
  636.3 76.4 reduce-scatter.7
  716.3 82.1 reduce-scatter.11

commit v2 on v1

--- a/solution.py
+++ b/solution.py
@@ -597,6 +597,426 @@
     return jnp.pad(vals, ((0, rows - vals.shape[0]), (0, 0)))
 
 
+def swap(vals, bit, axis="wsh"):
+    return lax.ppermute(vals, axis, [(i, i ^ bit) for i in range(lax.axis_size(axis))])
+
+
+def gather_pieces(own, count, also=None):
+    rows = own.shape[0]
+    far = [1 << b for b in range(1, count.bit_length() - 1)]
+    pieces = [(0, 0, own)]
+    if len(far) == 2:
+        one, two = far
+        half = rows // 2
+        by_one = swap(own, one)
+        by_two = swap(own, two)
+        pieces += [(one, 0, by_one), (two, 0, by_two)]
+        pieces += [(one | two, 0, swap(by_two[:half], one)), (one | two, half, swap(by_one[half:], two))]
+    else:
+        for bit in far:
+            pieces += [(r ^ bit, first, swap(piece, bit)) for r, first, piece in pieces]
+    marks = [piece for _, _, piece in pieces[-2:]]
+    return pieces + [(r ^ 1, first, swap(piece, 1)) for r, first, piece in pieces], marks
+
+
+def piece_kernel(spots, rows, me_ref, left_ref, *refs):
+    sources, out_ref, whole_ref = refs[: len(spots)], refs[len(spots)], refs[len(spots) + 1]
+    for source, (r, first) in zip(sources, spots):
+        start = lax.bitwise_xor(me_ref[0], r) * rows + first
+        whole_ref[pl.ds(pl.multiple_of(start, 16), source.shape[0]), :] = source[...]
+    out_ref[...] = dot(left_ref[...], whole_ref[...]).astype(out_ref.dtype)
+
+
+def multiply_pieces(left, pieces, count, out_type, name):
+    rows, cols = pieces[0][2].shape
+    tile = 512
+    me = jnp.reshape(lax.axis_index("wsh"), (1,)).astype(jnp.int32)
+    spots = [(r, first) for r, first, _ in pieces]
+    return pl.pallas_call(
+        functools.partial(piece_kernel, spots, rows),
+        grid=(pl.cdiv(cols, tile),),
+        in_specs=[pl.BlockSpec(memory_space=pltpu.SMEM), pl.BlockSpec(left.shape, lambda j: (0, 0))]
+        + [pl.BlockSpec((piece.shape[0], tile), lambda j: (0, j)) for _, _, piece in pieces],
+        out_specs=[
+            pl.BlockSpec((left.shape[0], tile), lambda j: (0, j)),
+            pl.BlockSpec((rows * count, tile), lambda j: (0, j)),
+        ],
+        out_shape=[
+            jax.ShapeDtypeStruct((left.shape[0], cols), out_type),
+            jax.ShapeDtypeStruct((rows * count, cols), low_type),
+        ],
+        compiler_params=pltpu.CompilerParams(vmem_limit_bytes=VMEM_LIMIT),
+        cost_estimate=pl.CostEstimate(
+            flops=2 * left.shape[0] * rows * count * cols, bytes_accessed=4 * rows * count * cols, transcendentals=0
+        ),
+        name=name,
+    )(me, left, *[piece for _, _, piece in pieces])
+
+
+def back_kernel(spots, me_ref, left_ref, *refs):
+    sources, out_ref, whole_ref = refs[: len(spots)], refs[len(spots)], refs[len(spots) + 1]
+    step = pl.program_id(0)
+    for r in sorted({r for r, _ in spots}):
+
+        @pl.when(step == r)
+        def _():
+            for source, (other, first) in zip(sources, spots):
+                if other == r:
+                    whole_ref[first : first + source.shape[0], :] = source[...]
+            out_ref[...] = dot_nt(left_ref[...], whole_ref[...])
+
+
+def multiply_back(left, pieces, count, name):
+    rows, cols = pieces[0][2].shape
+    if rows % LANES:
+        whole = jnp.zeros((rows * count, cols), low_type)
+        for r, first, piece in pieces:
+            start = lax.bitwise_xor(lax.axis_index("wsh"), r) * rows + first
+            whole = lax.dynamic_update_slice_in_dim(whole, piece, start, 0)
+        return dot_nt(left, whole), whole
+    me = jnp.reshape(lax.axis_index("wsh"), (1,)).astype(jnp.int32)
+    spots = [(r, first) for r, first, _ in pieces]
+    once = pl.Buffered(1)
+    grid_spec = pltpu.PrefetchScalarGridSpec(
+        num_scalar_prefetch=1,
+        grid=(count,),
+        in_specs=[pl.BlockSpec(left.shape, lambda j, me: (0, 0), pipeline_mode=once)]
+        + [pl.BlockSpec(piece.shape, lambda j, me: (0, 0), pipeline_mode=once) for _, _, piece in pieces],
+        out_specs=[
+            pl.BlockSpec((left.shape[0], rows), lambda j, me: (0, lax.bitwise_xor(me[0], j))),
+            pl.BlockSpec((rows, cols), lambda j, me: (lax.bitwise_xor(me[0], j), 0)),
+        ],
+    )
+    return pl.pallas_call(
+        functools.partial(back_kernel, spots),
+        grid_spec=grid_spec,
+        out_shape=[
+            jax.ShapeDtypeStruct((left.shape[0], rows * count), full_type),
+            jax.ShapeDtypeStruct((rows * count, cols), low_type),
+        ],
+        compiler_params=pltpu.CompilerParams(vmem_limit_bytes=VMEM_LIMIT),
+        cost_estimate=pl.CostEstimate(
+            flops=2 * left.shape[0] * rows * count * cols, bytes_accessed=4 * rows * count * cols, transcendentals=0
+        ),
+        name=name,
+    )(me, left, *[piece for _, _, piece in pieces])
+
+
+def sum_small(vals):
+    for axis in ("wsh", "seq"):
+        bit = 1
+        while bit < lax.axis_size(axis):
+            vals = vals + swap(vals, bit, axis)
+            bit = 2 * bit
+    return vals
+
+
+TILE = 384
+SLACK = 1
+
+
+def part_orders(count):
+    far = [b for b in range(count.bit_length() - 2)]
+    return [far[p:] + far[:p] for p in range(len(far))]
+
+
+def held(order, phase, bits):
+    done = sum(1 << b for b in order[:phase])
+    left = [m for m in range(1 << bits) if m & done == 0]
+    bit = 1 << order[phase]
+    return [m for m in left if m & bit == 0], [m for m in left if m & bit]
+
+
+def reduce_kernel(counts, rights_at, lefts_ref, *refs):
+    wsh_count, seq_count, starts = counts
+    n_rights = len(starts)
+    right_refs, out_ref = refs[:n_rights], refs[n_rights]
+    (tile, stage, pair, *rest) = refs[n_rights + 1 :]
+    orders = part_orders(wsh_count)
+    bits = len(orders)
+    lands, rest = rest[:bits], rest[bits:]
+    from_left, from_right, pair_sems, far_sems, seq_sems, out_sems = rest
+    chunks, blocks, rows, _ = pair.shape
+    part = rows // bits
+    me = lax.axis_index("wsh")
+    z = lax.axis_index("seq")
+    root = seq_count // 2
+    MESH = pl.DeviceIdType.MESH
+
+    barrier = pltpu.get_barrier_semaphore()
+    for b in range(bits + 1):
+        pl.semaphore_signal(barrier, inc=1, device_id={"wsh": lax.bitwise_xor(me, 1 << b)}, device_id_type=MESH)
+
+    @pl.when(z > 0)
+    def _():
+        pl.semaphore_signal(barrier, inc=1, device_id={"seq": z - 1}, device_id_type=MESH)
+
+    @pl.when(z < seq_count - 1)
+    def _():
+        pl.semaphore_signal(barrier, inc=1, device_id={"seq": z + 1}, device_id_type=MESH)
+
+    along = jnp.where(z > 0, 1, 0) + jnp.where(z < seq_count - 1, 1, 0)
+    pl.semaphore_wait(barrier, bits + 1 + along)
+
+    def pair_copy(k):
+        return pltpu.make_async_remote_copy(
+            src_ref=stage.at[lax.rem(k, 2)], dst_ref=pair.at[k],
+            send_sem=pair_sems.at[0, k], recv_sem=pair_sems.at[1, k],
+            device_id={"wsh": lax.bitwise_xor(me, 1)}, device_id_type=MESH,
+        )
+
+    spots = []
+    for q in range(bits):
+        for p, order in enumerate(orders):
+            for i, m in enumerate(held(order, q, bits)[1]):
+                spots.append((q, p, i, m, 2 << order[q]))
+
+    def far_copies(k, phase):
+        return [
+            pltpu.make_async_remote_copy(
+                src_ref=pair.at[k, m, pl.ds(p * part, part)], dst_ref=lands[q].at[k, p, i],
+                send_sem=far_sems.at[0, n, k], recv_sem=far_sems.at[1, n, k],
+                device_id={"wsh": lax.bitwise_xor(me, bit)}, device_id_type=MESH,
+            )
+            for n, (q, p, i, m, bit) in enumerate(spots)
+            if q == phase
+        ]
+
+    def to_right(k, source):
+        return pltpu.make_async_remote_copy(
+            src_ref=source, dst_ref=from_left.at[k],
+            send_sem=seq_sems.at[0, k], recv_sem=seq_sems.at[1, k],
+            device_id={"seq": z + 1}, device_id_type=MESH,
+        )
+
+    def to_left(k, source):
+        return pltpu.make_async_remote_copy(
+            src_ref=source, dst_ref=from_right.at[k],
+            send_sem=seq_sems.at[2, k], recv_sem=seq_sems.at[3, k],
+            device_id={"seq": z - 1}, device_id_type=MESH,
+        )
+
+    def out_copy(k, source):
+        return pltpu.make_async_copy(source, out_ref.at[k], out_sems.at[k])
+
+    def product(k, first):
+        for n, (start, stop, spans) in enumerate(rights_at):
+            @pl.when((k >= start) & (k < stop))
+            def _():
+                col = lax.rem(k - start, spans) * TILE
+                tile[...] = right_refs[n][:, pl.ds(pl.multiple_of(col, LANES), TILE)]
+        left_at = jnp.where(k < rights_at[0][1], 1 + k // rights_at[0][2], 0)
+        half = blocks * rows
+        return dot(lefts_ref[left_at, pl.ds(first * half, half), :], tile[...])
+
+    def begin(k):
+        @pl.when(k >= 2)
+        def _():
+            pair_copy(k - 2).wait_send()
+        vals = product(k, 1)
+        for b in range(blocks):
+            stage[lax.rem(k, 2), b] = vals[b * rows : (b + 1) * rows].astype(low_type)
+        pair_copy(k).start()
+
+    def add_pair(k):
+        vals = product(k, 0)
+        pair_copy(k).wait_recv()
+        for b in range(blocks):
+            total = vals[b * rows : (b + 1) * rows] + pair[k, b].astype(full_type)
+            pair[k, b] = total.astype(low_type)
+        for copy in far_copies(k, 0):
+            copy.start()
+
+    def add_far(k, phase):
+        for copy in far_copies(k, phase):
+            copy.wait_recv()
+        for p, order in enumerate(orders):
+            at = pl.ds(p * part, part)
+            for i, m in enumerate(held(order, phase, bits)[0]):
+                total = pair[k, m, at].astype(full_type) + lands[phase][k, p, i].astype(full_type)
+                pair[k, m, at] = total.astype(low_type)
+        if phase < bits - 1:
+            for copy in far_copies(k, phase + 1):
+                copy.start()
+
+    def add_to(k, land):
+        pair[k, 0] = (pair[k, 0].astype(full_type) + land[k].astype(full_type)).astype(low_type)
+
+    def seq_up(k):
+        mine = pair.at[k, 0]
+
+        @pl.when((z > 0) & (z <= root))
+        def _():
+            to_right(k, mine).wait_recv()
+            add_to(k, from_left)
+
+        @pl.when((z < seq_count - 1) & (z >= root))
+        def _():
+            to_left(k, mine).wait_recv()
+            add_to(k, from_right)
+
+        @pl.when((z < seq_count - 1) & (z <= root))
+        def _():
+            to_right(k, mine).start()
+
+        @pl.when((z > 0) & (z >= root))
+        def _():
+            to_left(k, mine).start()
+
+    def seq_down(k):
+        @pl.when(z == root)
+        def _():
+            out_copy(k, pair.at[k, 0]).start()
+
+        @pl.when(z < root)
+        def _():
+            to_left(k, from_right.at[k]).wait_recv()
+            out_copy(k, from_right.at[k]).start()
+            pl.when(z > 0)(lambda: to_left(k, from_right.at[k]).start())
+
+        @pl.when(z > root)
+        def _():
+            to_right(k, from_left.at[k]).wait_recv()
+            out_copy(k, from_left.at[k]).start()
+            pl.when(z < seq_count - 1)(lambda: to_right(k, from_left.at[k]).start())
+
+    far = jnp.abs(z - root)
+    farthest = max(root, seq_count - 1 - root)
+    stages = [(0, begin), (1, add_pair)] + [(2 + q, functools.partial(add_far, phase=q)) for q in range(bits)]
+    stages += [
+        (2 + bits + SLACK * (farthest - far), seq_up),
+        (3 + bits + SLACK * (farthest + far), seq_down),
+    ]
+    depth = 4 + bits + SLACK * 2 * farthest
+
+    def turn(s, carry):
+        for offset, run in stages:
+            pl.when((s >= offset) & (s < chunks + offset))(lambda run=run, offset=offset: run(s - offset))
+        return carry
+
+    lax.fori_loop(0, chunks + depth, turn, 0)
+
+    def finish(k, carry):
+        for q in range(bits):
+            for copy in far_copies(k, q):
+                copy.wait_send()
+        pl.when(z < seq_count - 1)(lambda: to_right(k, pair.at[k, 0]).wait_send())
+        pl.when(z > 0)(lambda: to_left(k, pair.at[k, 0]).wait_send())
+        out_copy(k, pair.at[k, 0]).wait()
+        return carry
+
+    lax.fori_loop(0, chunks, finish, 0)
+    for k in (chunks - 2, chunks - 1):
+        pair_copy(k).wait_send()
+
+
+def reduce_rows(lefts, out_right, gate_right, sig_right):
+    wsh_count, seq_count = lax.axis_size("wsh"), lax.axis_size("seq")
+    rows = D // wsh_count
+    orders = part_orders(wsh_count)
+    bits = len(orders)
+    n_out, n_gate, n_sig = (right.shape[1] // TILE for right in (out_right, gate_right, sig_right))
+    groups = lefts.shape[0] - 1
+    starts = [0, groups * n_out, groups * n_out + n_gate]
+    chunks = starts[2] + n_sig
+    rights_at = [(0, starts[1], n_out), (starts[1], starts[2], n_gate), (starts[2], chunks, n_sig)]
+    low = lambda *shape: pltpu.VMEM(shape, low_type)
+    dma = pltpu.SemaphoreType.DMA
+    copies = bits * ((1 << bits) - 1)
+    vmem = pl.BlockSpec(memory_space=pltpu.VMEM)
+    return pl.pallas_call(
+        functools.partial(reduce_kernel, (wsh_count, seq_count, starts), rights_at),
+        in_specs=[vmem] * 4,
+        out_specs=pl.BlockSpec(memory_space=pl.ANY),
+        out_shape=jax.ShapeDtypeStruct((chunks, rows, TILE), low_type),
+        scratch_shapes=[
+            low(out_right.shape[0], TILE),
+            low(2, 1 << bits, rows, TILE),
+            low(chunks, 1 << bits, rows, TILE),
+            *[low(chunks, bits, 1 << (bits - 1 - q), rows // bits, TILE) for q in range(bits)],
+            low(chunks, rows, TILE),
+            low(chunks, rows, TILE),
+            dma((2, chunks)),
+            dma((2, copies, chunks)),
+            dma((4, chunks)),
+            dma((chunks,)),
+        ],
+        compiler_params=pltpu.CompilerParams(
+            collective_id=0, has_side_effects=True, vmem_limit_bytes=60 * 1024 * 1024
+        ),
+        cost_estimate=pl.CostEstimate(flops=10**11, bytes_accessed=20 * 10**6, transcendentals=0),
+        name="reduce_gradients",
+    )(lefts, out_right, gate_right, sig_right)
+
+
+def adam_kernel(start, rate, decay, *refs):
+    share_ref, weight_ref, first_ref, second_ref, grad_ref, next_ref, next_first_ref, next_second_ref = refs
+    grad = share_ref[0].astype(full_type)
+    grad_ref[...] = grad
+    next_ref[...], next_first_ref[...], next_second_ref[...] = adam_update(
+        weight_ref[...], grad, first_ref[...], second_ref[...], rate, decay
+    )
+
+
+def adam_chunks(sums, start, weights, first_moment, second_moment, rate, decay, name):
+    all_rows, cols = weights.shape
+    rows = sums.shape[1]
+    tiles = pl.cdiv(cols, TILE)
+    block = pl.BlockSpec((rows, TILE), lambda i, j: (i, j))
+    return pl.pallas_call(
+        functools.partial(adam_kernel, start, rate, decay),
+        grid=(all_rows // rows, tiles),
+        in_specs=[pl.BlockSpec((1, rows, TILE), lambda i, j: (start + i * tiles + j, 0, 0))] + [block] * 3,
+        out_specs=[block] * 4,
+        out_shape=[jax.ShapeDtypeStruct(weights.shape, full_type)] * 4,
+        compiler_params=pltpu.CompilerParams(vmem_limit_bytes=VMEM_LIMIT),
+        cost_estimate=pl.CostEstimate(
+            flops=20 * weights.size, bytes_accessed=30 * weights.size, transcendentals=weights.size
+        ),
+        name=name,
+    )(sums, weights, first_moment, second_moment)
+
+
+def relative_rows(vals, count, groups):
+    size = vals.shape[1] // (count * groups)
+    me = lax.axis_index("wsh")
+    order = [r for r in range(count) if r % 2 == 0] + [r for r in range(count) if r % 2 == 1]
+    turned = vals.T
+    parts = [
+        lax.dynamic_slice_in_dim(turned, (lax.bitwise_xor(me, r) * groups + g) * size, size, 0)
+        for g in range(groups)
+        for r in order
+    ]
+    return jnp.concatenate(parts, axis=0).reshape(groups, count * size, vals.shape[0])
+
+
+def after(vals, *others):
+    return lax.optimization_barrier((vals,) + others)[0]
+
+
+def shift(vals, by):
+    count = lax.axis_size("seq")
+    pairs = [(i, i + by) for i in range(count) if 0 <= i + by < count]
+    return lax.ppermute(vals, "seq", pairs)
+
+
+def carry_states(own, fades, sign):
+    count = lax.axis_size("seq")
+    span, span_fade = own, fades
+    result, fade = None, jnp.zeros_like(fades)
+    reach = 1
+    while reach < count:
+        got, got_fade = shift(span, sign * reach), shift(span_fade, sign * reach)
+        if result is None:
+            result = got
+        else:
+            result = (result.astype(full_type) + jnp.exp2(fade)[None, :] * got.astype(full_type)).astype(low_type)
+        span = (span.astype(full_type) + jnp.exp2(span_fade)[None, :] * got.astype(full_type)).astype(low_type)
+        fade, span_fade = fade + got_fade, span_fade + got_fade
+        reach = 2 * reach
+    return result
+
+
 def shards(
     inputs, cotangent, w_in, w_dt, w_out, gain_pre, gain_norm, conv_param, head_param,
     first_w_in, second_w_in, first_w_dt, second_w_dt, first_w_out, second_w_out,
@@ -616,14 +1036,15 @@
     ).astype(low_type)
     count = flat.shape[0]
     flat = jnp.pad(flat, (0, -count % LANES))
-    small = lax.all_gather(flat, "wsh", axis=0)
     part_sig = jnp.concatenate(
         [w_in[:, INNER:].astype(low_type), w_dt.astype(low_type), jnp.zeros((rows_model, LANES - HEADS), low_type)],
         axis=1,
     )
-    full_sig = lax.all_gather(part_sig, "wsh", axis=0, tiled=True)
-    full_gate = lax.all_gather(w_in[:, :INNER].astype(low_type), "wsh", axis=0, tiled=True)
-    full_out = lax.all_gather(w_out.astype(low_type), "wsh", axis=0, tiled=True)
+    small = lax.all_gather(flat, "wsh", axis=0)
+    part_sig = after(part_sig, small)
+    sig_pieces, marks = gather_pieces(part_sig, wsh_count)
+    gate_pieces, marks = gather_pieces(after(w_in[:, :INNER].astype(low_type), *marks), wsh_count)
+    out_pieces, marks = gather_pieces(after(w_out.astype(low_type), *marks), wsh_count)
     small = small.astype(full_type)
     ends = [rows_model, rows_model + rows_inner, rows_model + rows_inner + 5 * cols_conv]
     gain_in = small[:, : ends[0]].reshape(-1)
@@ -640,52 +1061,29 @@
     tokens = jnp.concatenate([before, tokens_low], axis=0).astype(full_type)
     inv_rms = lax.rsqrt(jnp.mean(tokens * tokens, axis=-1, keepdims=True) + norm_eps)
     normed_all = (tokens * inv_rms * gain_in).astype(low_type)
-    packed = dot(normed_all, full_sig).astype(low_type)
+    packed, full_sig = multiply_pieces(normed_all, sig_pieces, wsh_count, low_type, "project_signal")
     tokens = tokens[HALO:]
     inv_rms = inv_rms[HALO:]
     normed = normed_all[HALO:]
     x, bc, run, lag, run_t, lag_t, enter, enter_all, tail, offs, states, send = run_states(packed, conv, head)
-    gathered = lax.all_gather(send, "seq", axis=0)
+    fades = send[STATE].astype(full_type) + send[STATE + 1].astype(full_type)
+    state_in = carry_states(send[:STATE], fades, 1)
     y = run_outputs(x, bc, run, lag_t, enter, states, head)
-    gate_vals = dot(normed, full_gate)
-    back = dot_nt(cot_low, full_out)
-    totals = gathered[:, STATE].astype(full_type) + gathered[:, STATE + 1].astype(full_type)
-    state_in = jnp.zeros((STATE, INNER), full_type)
-    for z in range(seq_count - 1):
-        between = jnp.zeros((INNER,), full_type)
-        for other in range(z + 1, seq_count - 1):
-            between = between + jnp.where(other < seq_index, totals[other], 0.0)
-        state_in = state_in + jnp.where(z < seq_index, jnp.exp2(between), 0.0) * gathered[z, :STATE].astype(full_type)
-    state_in = state_in.astype(low_type)
+    gate_vals, full_gate = multiply_pieces(normed, gate_pieces, wsh_count, full_type, "project_gate")
+    back, full_out = multiply_back(cot_low, out_pieces, wsh_count, "project_back")
     gain_rows = jnp.broadcast_to(gain_out, (8, INNER))
     normed_out, grad_y, grad_gate, part_gnorm, grad_state = run_norm(
         y, gate_vals, back, gain_rows, bc, enter_all, state_in
     )
-    grad_states = lax.all_gather(grad_state.astype(low_type), "seq", axis=0)
+    grad_in = carry_states(grad_state.astype(low_type), fades, -1)
     block_out = (tokens + dot(normed_out, full_out)).astype(low_type)[None]
-    part_out = lax.psum_scatter(
-        dot(normed_out, cot_low, ((0,), (0,))).astype(low_type), "wsh", scatter_dimension=0, tiled=True
-    )
-    part_gate = lax.psum_scatter(
-        dot(normed, grad_gate, ((0,), (0,))).astype(low_type), "wsh", scatter_dimension=0, tiled=True
-    )
     grad_normed = dot_nt(grad_gate, full_gate)
-    grad_in = jnp.zeros((STATE, INNER), full_type)
-    for z in range(1, seq_count):
-        between = jnp.zeros((INNER,), full_type)
-        for other in range(1, z):
-            between = between + jnp.where(other > seq_index, totals[other], 0.0)
-        grad_in = grad_in + jnp.where(z > seq_index, jnp.exp2(between), 0.0) * grad_states[z].astype(full_type)
-    grad_in = grad_in.astype(low_type)
     grad_pack, edge, last, part_conv, part_skip, part_head = run_backward(
         packed, conv, head, grad_y, bc, lag, run_t, enter, tail, offs, states, state_in, grad_in
     )
-    after = lax.ppermute(edge, "seq", [(i, i - 1) for i in range(1, seq_count)])
-    fixed = jnp.concatenate([last[:8], last[8:] + after], axis=0).astype(low_type)
+    edge_next = lax.ppermute(edge, "seq", [(i, i - 1) for i in range(1, seq_count)])
+    fixed = jnp.concatenate([last[:8], last[8:] + edge_next], axis=0).astype(low_type)
     grad_pack = lax.dynamic_update_slice(grad_pack, fixed, (rows - 16, 0))
-    part_sig = lax.psum_scatter(
-        dot(normed, grad_pack, ((0,), (0,))).astype(low_type), "wsh", scatter_dimension=0, tiled=True
-    )
     grad_normed = grad_normed + dot_nt(grad_pack, full_sig)
     scaled = tokens * inv_rms
     part_gpre = jnp.sum(grad_normed * scaled, axis=0)
@@ -693,12 +1091,10 @@
     grad_tokens = inv_rms * (pulled - scaled * jnp.mean(pulled * scaled, axis=-1, keepdims=True))
     input_grad = (cot_low.astype(full_type) + grad_tokens)[None]
     skip_sums = part_skip[0].reshape(HEADS, HEAD_DIM).sum(axis=1)
-    small_sums = lax.psum(
-        jnp.concatenate(
-            [part_gpre, part_gnorm[0], part_conv[:5].reshape(-1), part_head[0, :HEADS], part_head[1, :HEADS], skip_sums]
-        ),
-        ("seq", "wsh"),
-    )
+    small_parts = [
+        part_gpre, part_gnorm[0], part_conv[:5].reshape(-1), part_head[0, :HEADS], part_head[1, :HEADS], skip_sums
+    ]
+    small_sums = sum_small(jnp.concatenate(small_parts))
     cuts = [D, D + INNER, D + INNER + 5 * CONV_CH]
     grad_gpre = lax.dynamic_slice_in_dim(small_sums[: cuts[0]], wsh_index * rows_model, rows_model, 0)
     grad_gnorm = lax.dynamic_slice_in_dim(small_sums[cuts[0] : cuts[1]], wsh_index * rows_inner, rows_inner, 0)
@@ -708,18 +1104,28 @@
     grad_head = lax.dynamic_slice_in_dim(
         small_sums[cuts[2] :].reshape(3, HEADS), wsh_index * cols_head, cols_head, 1
     )
-    grad_out, sum_gate, sum_sig = (
-        lax.psum(part.astype(full_type), "seq") for part in (part_out, part_gate, part_sig)
+    lefts = jnp.concatenate(
+        [relative_rows(normed, wsh_count, 1), relative_rows(normed_out, wsh_count, INNER // D)], axis=0
     )
-    grad_in_w = jnp.concatenate([sum_gate, sum_sig[:, :CONV_CH]], axis=1)
-    grad_dt = sum_sig[:, CONV_CH : CONV_CH + HEADS]
+    sums = reduce_rows(lefts, cot_low, grad_gate, grad_pack)
+    tiles_out = (INNER // D) * (D // TILE)
+    grad_out, *new_out = adam_chunks(sums, 0, w_out, first_w_out, second_w_out, rate_matrix, weight_decay, "adam_w_out")
+    grad_in_w, *new_in = adam_chunks(
+        sums, tiles_out, w_in, first_w_in, second_w_in, rate_matrix, weight_decay, "adam_w_in"
+    )
+    at_dt = CONV_CH % TILE
+    grad_dt = sums[-1, :, at_dt : at_dt + HEADS].astype(full_type)
     params = (w_in, w_dt, w_out, gain_pre, gain_norm, conv_param, head_param)
     gradients = (grad_in_w, grad_dt, grad_out, grad_gpre, grad_gnorm, grad_conv, grad_head)
     firsts = (first_w_in, first_w_dt, first_w_out, first_gain_pre, first_gain_norm, first_conv, first_head)
     seconds = (second_w_in, second_w_dt, second_w_out, second_gain_pre, second_gain_norm, second_conv, second_head)
     step_rates = (rate_matrix, rate_matrix, rate_matrix, rate_gain, rate_gain, rate_conv, rate_head)
     decays = (weight_decay, weight_decay, weight_decay, 0.0, 0.0, 0.0, 0.0)
-    updated = [adam_update(*items) for items in zip(params, gradients, firsts, seconds, step_rates, decays)]
+    updated = [
+        None if i in (0, 2) else adam_update(*items)
+        for i, items in enumerate(zip(params, gradients, firsts, seconds, step_rates, decays))
+    ]
+    updated[0], updated[2] = new_in, new_out
     new_params = tuple(entry[0] for entry in updated)
     moments = []
     for entry in updated:

time: 1170 us -> 612 us (0.52)
  waiting for transfers between devices: 523 us -> 104 us
  blocking collectives: 315 us -> 10.7 us
  Pallas kernels: 94.7 us -> 328 us
  matrix products: 93.1 us -> 29.5 us
  starting transfers between devices: 7.58 us -> 36.4 us
  other arithmetic: 50.3 us -> 36.7 us
  local copies, waits for them, and re-layouts: 67.9 us -> 55.1 us
  between operations: 14.5 us -> 1.99 us
    psum x1 -> x0, blocking collectives: 305 us -> none  [shards(): lax.psum(part.astype(full_type), 'seq')]
    pallas_call x0 -> x6, Pallas kernels: none -> 234 us  [the longest x1 159 us: reduce_rows(): pl.pallas_call(functools.partial(reduce_kernel, (wsh_count, seq_count, st...]
    all_gather x5 -> x0, waiting for transfers between devices: 225 us -> none  [the longest x1 50.7 us: shards(): full_out = lax.all_gather(w_out.astype(low_type), 'wsh', axis=0, tiled=True)]
    unnamed x11 -> x0, waiting for transfers between devices: 162 us -> none
    ppermute x1 -> x39, waiting for transfers between devices: 1.81 us -> 102 us  [the longest x32 61.8 us: swap(): lax.ppermute(vals, axis, [(i, i ^ bit) for i in range(lax.axis_size(axis))])]
    reduce_scatter x1 -> x0, waiting for transfers between devices: 78.4 us -> none  [shards(): lax.psum_scatter(dot(normed_out, cot_low, ((0,), (0,))).astype(low_type),...]
    dot_general x9 -> x3, matrix products: 93.1 us -> 29.5 us  [dot(): lax.dot_general(left_side, right_side, (dims, ((), ())), precision=precis...]
    psum x1 -> x0, waiting for transfers between devices: 56.3 us -> none  [shards(): lax.psum(jnp.concatenate([part_gpre, part_gnorm[0], part_conv[:5].reshape...]
  transfers between devices with their start and end apart: 11 -> 40, of which waited for: 10 -> 13; matrix products, arithmetic and copies ran while one was open for 11% -> 12% of each run, Pallas kernels for 3% -> 42%
where the time goes in v2:
time: 612 us; the launch traced here: 602 us
  Pallas kernels  328 us (54%)
  waiting for transfers between devices  104 us (17%)
  local copies, waits for them, and re-layouts  55.1 us (9%)
  other arithmetic  36.7 us (6%)
  starting transfers between devices  36.4 us (6%)
  matrix products  29.5 us (5%)
  blocking collectives  10.7 us (2%)
    pallas_call x1, Pallas kernels, reduce_rows(): pl.pallas_call(functools.partial(reduce_kernel, (wsh_count, seq_count, st...  159 us
    ppermute x32, waiting for transfers between devices, swap(): lax.ppermute(vals, axis, [(i, i ^ bit) for i in range(lax.axis_size(axis))])  61.8 us
    pallas_call x1, Pallas kernels, run_backward(): pl.pallas_call(backward_kernel, grid=(GROUPS + 2,), in_specs=[pl.BlockSpe...  46.1 us
    ppermute x6, waiting for transfers between devices, shift(): return lax.ppermute(vals, 'seq', pairs)  38.7 us
    pallas_call x2, Pallas kernels, adam_chunks(): pl.pallas_call(functools.partial(adam_kernel, start, rate, decay), grid=(...  31.3 us
    dot_general x3, matrix products, dot(): lax.dot_general(left_side, right_side, (dims, ((), ())), precision=precis...  29.5 us
    pallas_call x2, Pallas kernels, multiply_pieces(): pl.pallas_call(functools.partial(piece_kernel, spots, rows), grid=(pl.cdi...  28.7 us
    pallas_call x1, Pallas kernels, run_norm(): pl.pallas_call(norm_kernel, grid=(rows // part,), in_specs=[by_rows(INNER...  17 us
  transfers between devices with their start and end apart: 40, of which 13 were waited for; matrix products, arithmetic and copies ran while one was open for 12% of the time, Pallas kernels for 42%

profile of v2, /device:TPU:0, one launch (start us, length us, event | category | flops | bytes accessed | tf_op | source)
XLA Modules:
  0.0 602.4 jit_solution(13131506911608183634)
XLA Ops:
  3.7 10.7 %all-gather.1 = bf16[8,1,2688]{2,1,0:T(2,128)(2,1)S(1)} all-gather(bf16[1,1,2688]{2,1,0:T(2,128)(2,1)S(1)} %reshape.152), channel_id=2, replica_groups=mesh['seq'=4,'wsh'=8] {'wsh'}, dimensions={0}, use_global_device_ids=true | all-gather | bytes 48384 | tf_op jit(solution)/shard_map/all_gather | solution.py:1043
  14.5 2.7 convert.30
  17.1 1.4 copy-done.2
  18.8 1.8 concatenate.28.refs_0_
  20.6 1.5 collective-permute-start.2
  22.6 29.7 %collective-permute-done.2.refs_2_ = bf16[192,3456]{1,0:T(8,128)(2,1)} collective-permute-done((bf16[192,3456]{1,0:T(8,128)(2,1)}, bf16[192,3456]{1,0:T(8,128)(2,1)}, u32[]{:S(2)}, u32[]{:S(2)}) %collective-permute-start.2) | collective-permute-done | bytes 1327136 | tf_op jit(solution)/shard_map/ppermute | solution.py:601
  53.4 1.6 collective-permute-start.3
  55.0 1.1 slice.136
  56.7 3.5 collective-permute-start
  60.3 1.7 collective-permute-done
  62.0 7.9 %collective-permute-done.3.refs_3_ = bf16[96,3456]{1,0:T(8,128)(2,1)S(1)} collective-permute-done((bf16[96,3456]{1,0:T(8,128)(2,1)S(1)}, bf16[96,3456]{1,0:T(8,128)(2,1)S(1)}, u32[]{:S(2)}, u32[]{:S(2)}) %collective-permute-start.3) | collective-permute-done | bytes 663584 | tf_op jit(solution)/shard_map/ppermute | solution.py:601
  70.0 2.4 slice.140.refs_0_
  75.1 1.5 collective-permute-start.11
  77.2 1.6 multiply_convert_fusion.left_ref
  79.6 14.9 %project_signal.1 = (bf16[528,3456]{1,0:T(8,128)(2,1)}, bf16[1536,3456]{1,0:T(8,128)(2,1)}) custom-call(s32[1]{0:T(128)} %bitcast.2.me_ref, bf16[528,1536]{1,0:T(8,128)(2,1)} %multiply_convert_fusion.left_ref, bf16[192,3456]{1,0:T(8,128)(2,1)} %concatenate.28.refs_0_, bf16[192,3456]{1,0:T(8,128)(2,1)} %collective-permute-done.1.refs_1_, ...), custom_call_target="tpu_custom_call" | custom-call | flops 5605687296 | bytes 21233664 | tf_op jit(solution)/shard_map/project_signal/pallas_call | solution.py:635
  94.5 15.7 %scan_states.1 = (f32[512,3072]{1,0:T(8,128)}, f32[512,256]{1,0:T(8,128)}, f32[512,128]{1,0:T(8,128)}, f32[512,128]{1,0:T(8,128)}, f32[128,512]{1,0:T(8,128)}, /...) custom-call(bf16[528,3456]{1,0:T(8,128)(2,1)} %get-tuple-element.71., ...), custom_call_target="tpu_custom_call" | custom-call | flops 1000000000 | bytes 15000000 | tf_op jit(solution)/shard_map/scan_states/pallas_call | solution.py:432
  110.2 1.2 slice.116
  111.4 3.7 collective-permute-start.28
  115.3 1.6 slice.141
  116.9 1.6 collective-permute-start.12
  120.2 12.1 %collective-permute-done.12.refs_3_ = bf16[96,3072]{1,0:T(8,128)(2,1)} collective-permute-done((bf16[96,3072]{1,0:T(8,128)(2,1)S(1)}, bf16[96,3072]{1,0:T(8,128)(2,1)}, u32[]{:S(2)}, u32[]{:S(2)}) %collective-permute-start.12) | collective-permute-done | bytes 589856 | tf_op jit(solution)/shard_map/ppermute | solution.py:601
  132.3 2.4 collective-permute-done.13.refs_4_
  135.2 1.5 collective-permute-start.19
  138.7 5.3 collective-permute-start.30
  144.0 1.5 collective-permute-start.29
  145.5 13.4 %collective-permute-done.29 = f32[3072]{0:T(1024)S(1)} collective-permute-done((f32[3072]{0:T(1024)S(1)}, f32[3072]{0:T(1024)S(1)}, u32[]{:S(2)}, u32[]{:S(2)}) %collective-permute-start.29) | collective-permute-done | bytes 12320 | tf_op jit(solution)/shard_map/ppermute | solution.py:1000
  158.9 2.5 collective-permute-done.20.refs_2_
  163.5 1.2 slice.139.left_ref
  166.7 1.3 collective-permute-start.22
  168.0 16.0 %scan_outputs.1.y_ref = f32[512,3072]{1,0:T(8,128)} custom-call(f32[512,3072]{1,0:T(8,128)} %get-tuple-element.72.x_ref, f32[512,256]{1,0:T(8,128)} %get-tuple-element.73.bc_ref, f32[512,128]{1,0:T(8,128)} %get-tuple-element.74.run_ref, f32[128,512]{1,0:T(8,128)} %get-tuple-element.75.lag_t_ref, f32[512,128]{1,0:T(8,128)} %get-tuple-element.76.enter_ref, ...), custom_call_target="tpu_custom_call" | custom-call | flops 10000000000 | bytes 15000000 | tf_op jit(solution)/shard_map/scan_outputs/pallas_call | solution.py:479
  185.2 2.2 fusion.4.state_ref.state_in_ref
  187.4 13.8 %project_gate.1 = (f32[512,3072]{1,0:T(8,128)}, bf16[1536,3072]{1,0:T(8,128)(2,1)}) custom-call(s32[1]{0:T(128)} %bitcast.2.me_ref, bf16[512,1536]{1,0:T(8,128)(2,1)} %slice.139.left_ref, bf16[192,3072]{1,0:T(8,128)(2,1)} %slice.140.refs_0_, bf16[192,3072]{1,0:T(8,128)(2,1)} %collective-permute-done.10.refs_1_, ...), custom_call_target="tpu_custom_call" | custom-call | flops 4831838208 | bytes 18874368 | tf_op jit(solution)/shard_map/project_gate/pallas_call | solution.py:635
  202.3 14.8 %project_back.1 = (f32[512,3072]{1,0:T(8,128)}, bf16[3072,1536]{1,0:T(8,128)(2,1)}) custom-call(s32[1]{0:T(128)} %bitcast.2.me_ref, bf16[512,1536]{1,0:T(8,128)(2,1)} %bitcast.91, bf16[384,1536]{1,0:T(8,128)(2,1)} %copy-done.10, bf16[384,1536]{1,0:T(8,128)(2,1)} %copy-done.17, bf16[384,1536]{1,0:T(8,128)(2,1)} %copy-done.15, ...), custom_call_target="tpu_custom_call" | custom-call | flops 4831838208 | bytes 18874368 | tf_op jit(solution)/shard_map/project_back/pallas_call | solution.py:690
  217.7 17.0 %gated_norm.1 = (bf16[512,3072]{1,0:T(8,128)(2,1)}, bf16[512,3072]{1,0:T(8,128)(2,1)}, bf16[512,3072]{1,0:T(8,128)(2,1)}, f32[8,3072]{1,0:T(8,128)}, f32[128,3072]{1,0:T(8,128)}) custom-call(f32[512,3072]{1,0:T(8,128)} %scan_outputs.1.y_ref, f32[512,3072]{1,0:T(8,128)} %get-tuple-element.79.gate_ref, f32[512,3072]{1,0:T(8,128)} %get-tuple-element.81.back_ref, ...), custom_call_target="tpu_custom_call" | custom-call | flops 1000000000 | bytes 30000000 | tf_op jit(solution)/shard_map/gated_norm/pallas_call | solution.py:505
  234.7 2.4 convert_element_type.96
  237.1 1.4 collective-permute-start.31
  240.9 2.1 maximum_convert_fusion
  243.0 1.5 collective-permute-start.32
  244.5 1.7 dynamic-slice_bitcast_fusion.16
  246.3 3.6 concatenate.30
  249.9 2.7 copy.94
  252.6 19.1 %collective-permute-done.32 = f32[3072]{0:T(1024)S(1)} collective-permute-done((f32[3072]{0:T(1024)S(1)}, f32[3072]{0:T(1024)S(1)}, u32[]{:S(2)}, u32[]{:S(2)}) %collective-permute-start.32) | collective-permute-done | bytes 12320 | tf_op jit(solution)/shard_map/ppermute | solution.py:1000
  271.7 2.7 fusion.6
  274.4 1.3 collective-permute-start.33
  275.7 10.4 %fusion.1 = bf16[1,512,1536]{2,1,0:T(8,128)(2,1)} fusion(bf16[512,3072]{1,0:T(8,128)(2,1)} %get-tuple-element.84, bf16[3072,1536]{1,0:T(8,128)(2,1)} %get-tuple-element.85, f32[528,1536]{1,0:T(8,128)S(1)} %copy-done.1), kind=kOutput, calls=%fused_computation.10 | convolution fusion | flops 4833411072 | bytes 17301504 | tf_op jit(solution)/shard_map/dot_general | solution.py:42
  287.0 4.2 dynamic-slice_bitcast_fusion
  291.2 6.7 %concatenate.31 = bf16[3072,512]{0,1:T(8,128)(2,1)} concatenate(bf16[192,512]{0,1:T(8,128)(2,1)} %get-tuple-element.268, bf16[192,512]{0,1:T(8,128)(2,1)} %get-tuple-element.267, bf16[192,512]{0,1:T(8,128)(2,1)} %get-tuple-element.266, bf16[192,512]{0,1:T(8,128)(2,1)} %get-tuple-element.265, bf16[192,512]{0,1:T(8,128)(2,1)} %get-tuple-element.264, ...), dimensions={0} | concatenate | bytes 6291456 | tf_op jit(solution)/shard_map/concatenate | solution.py:990
  297.9 4.6 copy.93
  302.6 4.9 pad_maximum_fusion.lefts_ref
  307.5 6.2 %collective-permute-done.33 = bf16[128,3072]{1,0:T(8,128)(2,1)} collective-permute-done((bf16[128,3072]{1,0:T(8,128)(2,1)}, bf16[128,3072]{1,0:T(8,128)(2,1)}, u32[]{:S(2)}, u32[]{:S(2)}) %collective-permute-start.33) | collective-permute-done | bytes 786464 | tf_op jit(solution)/shard_map/ppermute | solution.py:1000
  313.8 2.5 fusion.7.grad_in_ref
  316.3 46.1 %scan_backward.1 = (bf16[512,3456]{1,0:T(8,128)(2,1)}, f32[8,3328]{1,0:T(8,128)}, f32[16,3328]{1,0:T(8,128)}, f32[8,3328]{1,0:T(8,128)}, f32[8,3072]{1,0:T(8,128)}, /*index=5*/f32[8,128]{1,0:T(8,128)}) custom-call(bf16[528,3456]{1,0:T(8,128)(2,1)} %get-tuple-element.71.sig_ref.maps_ref.raw_ref, bf16[528,3456]{1,0:T(8,128)(2,1)} %get-tuple-element.71.sig_ref.maps_ref.raw_ref, ...), custom_call_target="tpu_custom_call" | custom-call | flops 20000000000 | bytes 20000000 | tf_op jit(solution)/shard_map/scan_backward/pallas_call | solution.py:532
  362.4 1.5 collective-permute-start.34
  367.6 1.6 collective-permute-done.34
  370.7 9.8 %fusion.18 = f32[512,1536]{1,0:T(8,128)S(1)} fusion(bf16[512,3456]{1,0:T(8,128)(2,1)} %maximum_dynamic-update-slice_fusion.refs_2_, bf16[1536,3456]{1,0:T(8,128)(2,1)} %get-tuple-element.97), kind=kOutput, calls=%fused_computation.83 | convolution fusion | flops 5435817984 | bytes 17301504 | tf_op jit(solution)/shard_map/dot_general | solution.py:42
  380.6 9.3 %multiply_reduce_fusion.1 = (f32[1536]{0:T(1024)S(1)}, f32[512]{0:T(512)S(1)}, f32[512,1536]{1,0:T(8,128)}) fusion(f32[528,1536]{1,0:T(8,128)S(1)} %copy-done.1, f32[512]{0:T(512)S(1)} %slice.119, f32[1536]{0:T(1024)S(1)} %mul.366, f32[512,1536]{1,0:T(8,128)S(1)} %fusion.18, bf16[512,3072]{1,0:T(8,128)(2,1)S(1)} %copy-done.35, ...), kind=kOutput, calls=%fused_computation.5 | convolution fusion | flops 4837341184 | bytes 22036480 | tf_op jit(solution)/shard_map/dot_general | solution.py:42
  389.9 158.7 %reduce_gradients.1.refs_0_ = bf16[25,192,384]{2,1,0:T(8,128)(2,1)} custom-call(bf16[3,1536,512]{2,1,0:T(8,128)(2,1)} %pad_maximum_fusion.lefts_ref, bf16[512,1536]{1,0:T(8,128)(2,1)} %bitcast.92, bf16[512,3072]{1,0:T(8,128)(2,1)} %get-tuple-element.86.refs_1_, bf16[512,3456]{1,0:T(8,128)(2,1)} %maximum_dynamic-update-slice_fusion.refs_2_), custom_call_target="tpu_custom_call" | custom-call | flops 99999997952 | bytes 20000000 | tf_op jit(solution)/shard_map/reduce_gradients/pallas_call | solution.py:927
  548.7 1.2 collective-permute-start.36
  549.8 3.4 collective-permute-done.36
  553.2 1.1 collective-permute-start.37
  554.4 4.8 add_bitcast_fusion
  560.3 3.5 collective-permute-done.38
  567.5 9.9 %adam_w_out.1 = (f32[384,1536]{1,0:T(8,128)}, f32[384,1536]{1,0:T(8,128)}, f32[384,1536]{1,0:T(8,128)}, f32[384,1536]{1,0:T(8,128)}) custom-call(bf16[25,192,384]{2,1,0:T(8,128)(2,1)} %reduce_gradients.1.refs_0_, f32[384,1536]{1,0:T(8,128)} %refs_1_.3, f32[384,1536]{1,0:T(8,128)} %refs_2_.3, f32[384,1536]{1,0:T(8,128)} %refs_3_.3), custom_call_target="tpu_custom_call" | custom-call | flops 11796480 | bytes 17694720 | tf_op jit(solution)/shard_map/adam_w_out/pallas_call | solution.py:966
  577.6 21.4 %adam_w_in.1 = (f32[192,6400]{1,0:T(8,128)}, f32[192,6400]{1,0:T(8,128)}, f32[192,6400]{1,0:T(8,128)}, f32[192,6400]{1,0:T(8,128)}) custom-call(bf16[25,192,384]{2,1,0:T(8,128)(2,1)} %reduce_gradients.1.refs_0_, f32[192,6400]{1,0:T(8,128)} %refs_1_.2, f32[192,6400]{1,0:T(8,128)} %refs_2_.2, f32[192,6400]{1,0:T(8,128)} %refs_3_.2), custom_call_target="tpu_custom_call" | custom-call | flops 24576000 | bytes 36864000 | tf_op jit(solution)/shard_map/adam_w_in/pallas_call | solution.py:966
  (208 shorter events, 37.3 us)
Async XLA Ops:
  18.7 38.1 %copy-start = (bf16[1,512,1536]{2,1,0:T(8,128)(2,1)S(1)}, bf16[1,512,1536]{2,1,0:T(8,128)(2,1)}, u32[]{:S(2)}) copy-start(bf16[1,512,1536]{2,1,0:T(8,128)(2,1)} %param.23) | copy-start | bytes 4718596
  20.6 31.7 %collective-permute-start.2 = (bf16[192,3456]{1,0:T(8,128)(2,1)}, bf16[192,3456]{1,0:T(8,128)(2,1)}, u32[]{:S(2)}, u32[]{:S(2)}) collective-permute-start(bf16[192,3456]{1,0:T(8,128)(2,1)} %concatenate.28.refs_0_), channel_id=1, source_target_pairs={{0,4},{1,5},{2,6},{3,7},{4,0},{5,1},{6,2},{7,3},{8,12},{9,13},{10,... | collective-permute-start | bytes 3981320 | tf_op jit(solution)/shard_map/ppermute | solution.py:601
  22.1 32.9 %collective-permute-start.1 = (bf16[192,3456]{1,0:T(8,128)(2,1)}, bf16[192,3456]{1,0:T(8,128)(2,1)}, u32[]{:S(2)}, u32[]{:S(2)}) collective-permute-start(bf16[192,3456]{1,0:T(8,128)(2,1)} %concatenate.28.refs_0_), channel_id=1, source_target_pairs={{0,2},{1,3},{2,0},{3,1},{4,6},{5,7},{6,4},{7,5},{8,10},{9,11},{10,... | collective-permute-start | bytes 3981320 | tf_op jit(solution)/shard_map/ppermute | solution.py:601
  22.6 52.5 %collective-permute-start.5 = (bf16[192,3456]{1,0:T(8,128)(2,1)}, bf16[192,3456]{1,0:T(8,128)(2,1)}, u32[]{:S(2)}, u32[]{:S(2)}) collective-permute-start(bf16[192,3456]{1,0:T(8,128)(2,1)} %concatenate.28.refs_0_), channel_id=1, source_target_pairs={{0,1},{1,0},{2,3},{3,2},{4,5},{5,4},{6,7},{7,6},{8,9},{9,8},{10,11... | collective-permute-start | bytes 3981320 | tf_op jit(solution)/shard_map/ppermute | solution.py:601
  53.4 16.4 %collective-permute-start.3 = (bf16[96,3456]{1,0:T(8,128)(2,1)S(1)}, bf16[96,3456]{1,0:T(8,128)(2,1)S(1)}, u32[]{:S(2)}, u32[]{:S(2)}) collective-permute-start(bf16[96,3456]{1,0:T(8,128)(2,1)S(1)} %slice.135), channel_id=1, source_target_pairs={{0,2},{1,3},{2,0},{3,1},{4,6},{5,7},{6,4},{7,5},{8,10},{9,11},{10,... | collective-permute-start | bytes 1990664 | tf_op jit(solution)/shard_map/ppermute | solution.py:601
  56.1 18.5 %collective-permute-start.4 = (bf16[96,3456]{1,0:T(8,128)(2,1)S(1)}, bf16[96,3456]{1,0:T(8,128)(2,1)}, u32[]{:S(2)}, u32[]{:S(2)}) collective-permute-start(bf16[96,3456]{1,0:T(8,128)(2,1)S(1)} %slice.136), channel_id=1, source_target_pairs={{0,4},{1,5},{2,6},{3,7},{4,0},{5,1},{6,2},{7,3},{8,12},{9,13},{10,... | collective-permute-start | bytes 1990664 | tf_op jit(solution)/shard_map/ppermute | solution.py:601
  56.7 5.2 collective-permute-start
  60.2 18.6 %collective-permute-start.6 = (bf16[192,3456]{1,0:T(8,128)(2,1)}, bf16[192,3456]{1,0:T(8,128)(2,1)}, u32[]{:S(2)}, u32[]{:S(2)}) collective-permute-start(bf16[192,3456]{1,0:T(8,128)(2,1)} %collective-permute-done.1.refs_1_), channel_id=1, source_target_pairs={{0,1},{1,0},{2,3},{3,2},{4,5},{5,4},{6,7},{7,6},{8,9},{9,8},{10,11... | collective-permute-start | bytes 3981320 | tf_op jit(solution)/shard_map/ppermute | solution.py:601
  62.0 16.8 %collective-permute-start.7 = (bf16[192,3456]{1,0:T(8,128)(2,1)}, bf16[192,3456]{1,0:T(8,128)(2,1)}, u32[]{:S(2)}, u32[]{:S(2)}) collective-permute-start(bf16[192,3456]{1,0:T(8,128)(2,1)} %collective-permute-done.2.refs_2_), channel_id=1, source_target_pairs={{0,1},{1,0},{2,3},{3,2},{4,5},{5,4},{6,7},{7,6},{8,9},{9,8},{10,11... | collective-permute-start | bytes 3981320 | tf_op jit(solution)/shard_map/ppermute | solution.py:601
  69.9 6.8 %collective-permute-start.8 = (bf16[96,3456]{1,0:T(8,128)(2,1)S(1)}, bf16[96,3456]{1,0:T(8,128)(2,1)}, u32[]{:S(2)}, u32[]{:S(2)}) collective-permute-start(bf16[96,3456]{1,0:T(8,128)(2,1)S(1)} %collective-permute-done.3.refs_3_), channel_id=1, source_target_pairs={{0,1},{1,0},{2,3},{3,2},{4,5},{5,4},{6,7},{7,6},{8,9},{9,8},{10,11... | collective-permute-start | bytes 1990664 | tf_op jit(solution)/shard_map/ppermute | solution.py:601
  74.7 4.1 collective-permute-start.9
  75.1 40.1 %collective-permute-start.11 = (bf16[192,3072]{1,0:T(8,128)(2,1)}, bf16[192,3072]{1,0:T(8,128)(2,1)}, u32[]{:S(2)}, u32[]{:S(2)}) collective-permute-start(bf16[192,3072]{1,0:T(8,128)(2,1)} %slice.140.refs_0_), channel_id=1, source_target_pairs={{0,4},{1,5},{2,6},{3,7},{4,0},{5,1},{6,2},{7,3},{8,12},{9,13},{10,... | collective-permute-start | bytes 3538952 | tf_op jit(solution)/shard_map/ppermute | solution.py:601
  76.6 41.8 %collective-permute-start.10 = (bf16[192,3072]{1,0:T(8,128)(2,1)}, bf16[192,3072]{1,0:T(8,128)(2,1)}, u32[]{:S(2)}, u32[]{:S(2)}) collective-permute-start(bf16[192,3072]{1,0:T(8,128)(2,1)} %slice.140.refs_0_), channel_id=1, source_target_pairs={{0,2},{1,3},{2,0},{3,1},{4,6},{5,7},{6,4},{7,5},{8,10},{9,11},{10,... | collective-permute-start | bytes 3538952 | tf_op jit(solution)/shard_map/ppermute | solution.py:601
  94.5 20.5 %copy-start.3 = (f32[384,1536]{1,0:T(8,128)S(1)}, f32[384,1536]{1,0:T(8,128)}, u32[]{:S(2)}) copy-start(f32[384,1536]{1,0:T(8,128)} %refs_1_.3) | copy-start | bytes 7077892
  111.4 25.4 %collective-permute-start.28 = (bf16[128,3072]{1,0:T(8,128)(2,1)S(1)}, bf16[128,3072]{1,0:T(8,128)(2,1)S(1)}, u32[]{:S(2)}, u32[]{:S(2)}) collective-permute-start(bf16[128,3072]{1,0:T(8,128)(2,1)S(1)} %slice.116), channel_id=1, source_target_pairs={{0,8},{8,16},{16,24},{1,9},{9,17},{17,25},{2,10},{10,18},{18,26},{... | collective-permute-start | bytes 2359304 | tf_op jit(solution)/shard_map/ppermute | solution.py:1000
  115.2 23.6 %copy-start.10 = (bf16[384,1536]{1,0:T(8,128)(2,1)}, bf16[384,1536]{1,0:T(8,128)(2,1)S(1)}, u32[]{:S(2)}) copy-start(bf16[384,1536]{1,0:T(8,128)(2,1)S(1)} %convert_element_type.86.refs_0_) | copy-start | bytes 3538948
  115.2 48.3 %copy-start.5 = (bf16[528,1536]{1,0:T(8,128)(2,1)S(1)}, bf16[528,1536]{1,0:T(8,128)(2,1)}, u32[]{:S(2)}) copy-start(bf16[528,1536]{1,0:T(8,128)(2,1)} %multiply_convert_fusion.left_ref) | copy-start | bytes 4866052
  115.2 50.6 %collective-permute-start.14 = (bf16[192,3072]{1,0:T(8,128)(2,1)}, bf16[192,3072]{1,0:T(8,128)(2,1)}, u32[]{:S(2)}, u32[]{:S(2)}) collective-permute-start(bf16[192,3072]{1,0:T(8,128)(2,1)} %slice.140.refs_0_), channel_id=1, source_target_pairs={{0,1},{1,0},{2,3},{3,2},{4,5},{5,4},{6,7},{7,6},{8,9},{9,8},{10,11... | collective-permute-start | bytes 3538952 | tf_op jit(solution)/shard_map/ppermute | solution.py:601
  116.9 15.4 %collective-permute-start.12 = (bf16[96,3072]{1,0:T(8,128)(2,1)S(1)}, bf16[96,3072]{1,0:T(8,128)(2,1)}, u32[]{:S(2)}, u32[]{:S(2)}) collective-permute-start(bf16[96,3072]{1,0:T(8,128)(2,1)S(1)} %slice.141), channel_id=1, source_target_pairs={{0,2},{1,3},{2,0},{3,1},{4,6},{5,7},{6,4},{7,5},{8,10},{9,11},{10,... | collective-permute-start | bytes 1769480 | tf_op jit(solution)/shard_map/ppermute | solution.py:601
  119.6 15.1 %collective-permute-start.13 = (bf16[96,3072]{1,0:T(8,128)(2,1)S(1)}, bf16[96,3072]{1,0:T(8,128)(2,1)}, u32[]{:S(2)}, u32[]{:S(2)}) collective-permute-start(bf16[96,3072]{1,0:T(8,128)(2,1)S(1)} %slice.142), channel_id=1, source_target_pairs={{0,4},{1,5},{2,6},{3,7},{4,0},{5,1},{6,2},{7,3},{8,12},{9,13},{10,... | collective-permute-start | bytes 1769480 | tf_op jit(solution)/shard_map/ppermute | solution.py:601
  134.7 26.7 %collective-permute-start.20 = (bf16[384,1536]{1,0:T(8,128)(2,1)S(1)}, bf16[384,1536]{1,0:T(8,128)(2,1)S(1)}, u32[]{:S(2)}, u32[]{:S(2)}) collective-permute-start(bf16[384,1536]{1,0:T(8,128)(2,1)S(1)} %convert_element_type.86.refs_0_), channel_id=1, source_target_pairs={{0,4},{1,5},{2,6},{3,7},{4,0},{5,1},{6,2},{7,3},{8,12},{9,13},{10,... | collective-permute-start | bytes 3538952 | tf_op jit(solution)/shard_map/ppermute | solution.py:601
  135.2 26.4 %collective-permute-start.19 = (bf16[384,1536]{1,0:T(8,128)(2,1)S(1)}, bf16[384,1536]{1,0:T(8,128)(2,1)S(1)}, u32[]{:S(2)}, u32[]{:S(2)}) collective-permute-start(bf16[384,1536]{1,0:T(8,128)(2,1)S(1)} %convert_element_type.86.refs_0_), channel_id=1, source_target_pairs={{0,2},{1,3},{2,0},{3,1},{4,6},{5,7},{6,4},{7,5},{8,10},{9,11},{10,... | collective-permute-start | bytes 3538952 | tf_op jit(solution)/shard_map/ppermute | solution.py:601
  138.7 27.1 %collective-permute-start.30 = (bf16[128,3072]{1,0:T(8,128)(2,1)}, bf16[128,3072]{1,0:T(8,128)(2,1)}, u32[]{:S(2)}, u32[]{:S(2)}) collective-permute-start(bf16[128,3072]{1,0:T(8,128)(2,1)} %fusion.3), channel_id=1, source_target_pairs={{0,16},{8,24},{1,17},{9,25},{2,18},{10,26},{3,19},{11,27},{4,20},{... | collective-permute-start | bytes 2359304 | tf_op jit(solution)/shard_map/ppermute | solution.py:1000
  144.0 14.9 %collective-permute-start.29 = (f32[3072]{0:T(1024)S(1)}, f32[3072]{0:T(1024)S(1)}, u32[]{:S(2)}, u32[]{:S(2)}) collective-permute-start(f32[3072]{0:T(1024)S(1)} %bitcast.103), channel_id=1, source_target_pairs={{0,8},{8,16},{16,24},{1,9},{9,17},{17,25},{2,10},{10,18},{18,26},{... | collective-permute-start | bytes 36872 | tf_op jit(solution)/shard_map/ppermute | solution.py:1000
  158.9 7.8 %collective-permute-start.17 = (bf16[96,3072]{1,0:T(8,128)(2,1)}, bf16[96,3072]{1,0:T(8,128)(2,1)}, u32[]{:S(2)}, u32[]{:S(2)}) collective-permute-start(bf16[96,3072]{1,0:T(8,128)(2,1)} %collective-permute-done.12.refs_3_), channel_id=1, source_target_pairs={{0,1},{1,0},{2,3},{3,2},{4,5},{5,4},{6,7},{7,6},{8,9},{9,8},{10,11... | collective-permute-start | bytes 1769480 | tf_op jit(solution)/shard_map/ppermute | solution.py:601
  161.4 22.7 %collective-permute-start.15 = (bf16[192,3072]{1,0:T(8,128)(2,1)}, bf16[192,3072]{1,0:T(8,128)(2,1)}, u32[]{:S(2)}, u32[]{:S(2)}) collective-permute-start(bf16[192,3072]{1,0:T(8,128)(2,1)} %collective-permute-done.10.refs_1_), channel_id=1, source_target_pairs={{0,1},{1,0},{2,3},{3,2},{4,5},{5,4},{6,7},{7,6},{8,9},{9,8},{10,11... | collective-permute-start | bytes 3538952 | tf_op jit(solution)/shard_map/ppermute | solution.py:601
  162.4 22.1 %collective-permute-start.16 = (bf16[192,3072]{1,0:T(8,128)(2,1)}, bf16[192,3072]{1,0:T(8,128)(2,1)}, u32[]{:S(2)}, u32[]{:S(2)}) collective-permute-start(bf16[192,3072]{1,0:T(8,128)(2,1)} %collective-permute-done.11.refs_2_), channel_id=1, source_target_pairs={{0,1},{1,0},{2,3},{3,2},{4,5},{5,4},{6,7},{7,6},{8,9},{9,8},{10,11... | collective-permute-start | bytes 3538952 | tf_op jit(solution)/shard_map/ppermute | solution.py:601
  165.8 18.2 %collective-permute-start.18 = (bf16[96,3072]{1,0:T(8,128)(2,1)}, bf16[96,3072]{1,0:T(8,128)(2,1)}, u32[]{:S(2)}, u32[]{:S(2)}) collective-permute-start(bf16[96,3072]{1,0:T(8,128)(2,1)} %collective-permute-done.13.refs_4_), channel_id=1, source_target_pairs={{0,1},{1,0},{2,3},{3,2},{4,5},{5,4},{6,7},{7,6},{8,9},{9,8},{10,11... | collective-permute-start | bytes 1769480 | tf_op jit(solution)/shard_map/ppermute | solution.py:601
  165.9 18.8 %collective-permute-start.21 = (bf16[192,1536]{1,0:T(8,128)(2,1)S(1)}, bf16[192,1536]{1,0:T(8,128)(2,1)}, u32[]{:S(2)}, u32[]{:S(2)}) collective-permute-start(bf16[192,1536]{1,0:T(8,128)(2,1)S(1)} %slice.143), channel_id=1, source_target_pairs={{0,2},{1,3},{2,0},{3,1},{4,6},{5,7},{6,4},{7,5},{8,10},{9,11},{10,... | collective-permute-start | bytes 1769480 | tf_op jit(solution)/shard_map/ppermute | solution.py:601
  166.7 18.4 %collective-permute-start.22 = (bf16[192,1536]{1,0:T(8,128)(2,1)S(1)}, bf16[192,1536]{1,0:T(8,128)(2,1)}, u32[]{:S(2)}, u32[]{:S(2)}) collective-permute-start(bf16[192,1536]{1,0:T(8,128)(2,1)S(1)} %slice.144), channel_id=1, source_target_pairs={{0,4},{1,5},{2,6},{3,7},{4,0},{5,1},{6,2},{7,3},{8,12},{9,13},{10,... | collective-permute-start | bytes 1769480 | tf_op jit(solution)/shard_map/ppermute | solution.py:601
  168.0 16.0 %copy-start.11 = (bf16[384,1536]{1,0:T(8,128)(2,1)S(1)}, bf16[384,1536]{1,0:T(8,128)(2,1)}, u32[]{:S(2)}) copy-start(bf16[384,1536]{1,0:T(8,128)(2,1)} %copy-done.10) | copy-start | bytes 3538948
  168.0 16.1 %copy-start.19 = (bf16[384,1536]{1,0:T(8,128)(2,1)S(1)}, bf16[384,1536]{1,0:T(8,128)(2,1)}, u32[]{:S(2)}) copy-start(bf16[384,1536]{1,0:T(8,128)(2,1)} %copy-done.17) | copy-start | bytes 3538948
  168.0 17.2 %copy-start.8 = (bf16[128,3072]{1,0:T(8,128)(2,1)S(1)}, bf16[128,3072]{1,0:T(8,128)(2,1)}, u32[]{:S(2)}) copy-start(bf16[128,3072]{1,0:T(8,128)(2,1)} %copy-done.7) | copy-start | bytes 2359300
  184.0 17.3 %collective-permute-start.23 = (bf16[384,1536]{1,0:T(8,128)(2,1)S(1)}, bf16[384,1536]{1,0:T(8,128)(2,1)}, u32[]{:S(2)}, u32[]{:S(2)}) collective-permute-start(bf16[384,1536]{1,0:T(8,128)(2,1)S(1)} %copy-done.11), channel_id=1, source_target_pairs={{0,1},{1,0},{2,3},{3,2},{4,5},{5,4},{6,7},{7,6},{8,9},{9,8},{10,11... | collective-permute-start | bytes 3538952 | tf_op jit(solution)/shard_map/ppermute | solution.py:601
  184.1 17.2 %collective-permute-start.24 = (bf16[384,1536]{1,0:T(8,128)(2,1)S(1)}, bf16[384,1536]{1,0:T(8,128)(2,1)}, u32[]{:S(2)}, u32[]{:S(2)}) collective-permute-start(bf16[384,1536]{1,0:T(8,128)(2,1)S(1)} %copy-done.19), channel_id=1, source_target_pairs={{0,1},{1,0},{2,3},{3,2},{4,5},{5,4},{6,7},{7,6},{8,9},{9,8},{10,11... | collective-permute-start | bytes 3538952 | tf_op jit(solution)/shard_map/ppermute | solution.py:601
  184.6 16.8 %collective-permute-start.25 = (bf16[384,1536]{1,0:T(8,128)(2,1)S(1)}, bf16[384,1536]{1,0:T(8,128)(2,1)}, u32[]{:S(2)}, u32[]{:S(2)}) collective-permute-start(bf16[384,1536]{1,0:T(8,128)(2,1)S(1)} %copy-done.16), channel_id=1, source_target_pairs={{0,1},{1,0},{2,3},{3,2},{4,5},{5,4},{6,7},{7,6},{8,9},{9,8},{10,11... | collective-permute-start | bytes 3538952 | tf_op jit(solution)/shard_map/ppermute | solution.py:601
  184.7 16.6 %collective-permute-start.26 = (bf16[192,1536]{1,0:T(8,128)(2,1)}, bf16[192,1536]{1,0:T(8,128)(2,1)S(1)}, u32[]{:S(2)}, u32[]{:S(2)}) collective-permute-start(bf16[192,1536]{1,0:T(8,128)(2,1)} %collective-permute-done.21.refs_3_), channel_id=1, source_target_pairs={{0,1},{1,0},{2,3},{3,2},{4,5},{5,4},{6,7},{7,6},{8,9},{9,8},{10,11... | collective-permute-start | bytes 1769480 | tf_op jit(solution)/shard_map/ppermute | solution.py:601
  185.1 16.2 %collective-permute-start.27 = (bf16[192,1536]{1,0:T(8,128)(2,1)}, bf16[192,1536]{1,0:T(8,128)(2,1)S(1)}, u32[]{:S(2)}, u32[]{:S(2)}) collective-permute-start(bf16[192,1536]{1,0:T(8,128)(2,1)} %collective-permute-done.22.refs_4_), channel_id=1, source_target_pairs={{0,1},{1,0},{2,3},{3,2},{4,5},{5,4},{6,7},{7,6},{8,9},{9,8},{10,11... | collective-permute-start | bytes 1769480 | tf_op jit(solution)/shard_map/ppermute | solution.py:601
  217.7 21.7 %copy-start.22 = (f32[192,48]{0,1:T(8,128)S(1)}, f32[192,48]{0,1:T(8,128)}, u32[]{:S(2)}) copy-start(f32[192,48]{0,1:T(8,128)} %param.34) | copy-start | bytes 110596
  217.7 22.4 %copy-start.23 = (f32[192,48]{0,1:T(8,128)S(1)}, f32[192,48]{0,1:T(8,128)}, u32[]{:S(2)}) copy-start(f32[192,48]{0,1:T(8,128)} %param.35) | copy-start | bytes 110596
  237.1 34.6 %collective-permute-start.31 = (bf16[128,3072]{1,0:T(8,128)(2,1)}, bf16[128,3072]{1,0:T(8,128)(2,1)}, u32[]{:S(2)}, u32[]{:S(2)}) collective-permute-start(bf16[128,3072]{1,0:T(8,128)(2,1)} %convert_element_type.96), channel_id=1, source_target_pairs={{8,0},{16,8},{24,16},{9,1},{17,9},{25,17},{10,2},{18,10},{26,18},{... | collective-permute-start | bytes 2359304 | tf_op jit(solution)/shard_map/ppermute | solution.py:1000
  243.0 28.7 %collective-permute-start.32 = (f32[3072]{0:T(1024)S(1)}, f32[3072]{0:T(1024)S(1)}, u32[]{:S(2)}, u32[]{:S(2)}) collective-permute-start(f32[3072]{0:T(1024)S(1)} %bitcast.104), channel_id=1, source_target_pairs={{8,0},{16,8},{24,16},{9,1},{17,9},{25,17},{10,2},{18,10},{26,18},{... | collective-permute-start | bytes 36872 | tf_op jit(solution)/shard_map/ppermute | solution.py:1000
  249.9 25.8 %copy-start.1 = (f32[528,1536]{1,0:T(8,128)S(1)}, f32[528,1536]{1,0:T(8,128)}, u32[]{:S(2)}) copy-start(f32[528,1536]{1,0:T(8,128)} %maximum_convert_fusion) | copy-start | bytes 9732100
  274.4 39.3 %collective-permute-start.33 = (bf16[128,3072]{1,0:T(8,128)(2,1)}, bf16[128,3072]{1,0:T(8,128)(2,1)}, u32[]{:S(2)}, u32[]{:S(2)}) collective-permute-start(bf16[128,3072]{1,0:T(8,128)(2,1)} %fusion.6), channel_id=1, source_target_pairs={{16,0},{24,8},{17,1},{25,9},{18,2},{26,10},{19,3},{27,11},{20,4},{... | collective-permute-start | bytes 2359304 | tf_op jit(solution)/shard_map/ppermute | solution.py:1000
  275.7 11.3 %copy-start.6 = (bf16[512,3072]{1,0:T(8,128)(2,1)S(1)}, bf16[512,3072]{1,0:T(8,128)(2,1)}, u32[]{:S(2)}) copy-start(bf16[512,3072]{1,0:T(8,128)(2,1)} %get-tuple-element.84) | copy-start | bytes 9437188
  362.4 6.8 %collective-permute-start.34 = (f32[8,3328]{1,0:T(8,128)}, f32[8,3328]{1,0:T(8,128)S(1)}, u32[]{:S(2)}, u32[]{:S(2)}) collective-permute-start(f32[8,3328]{1,0:T(8,128)} %get-tuple-element.96), channel_id=1, source_target_pairs={{8,0},{16,8},{24,16},{9,1},{17,9},{25,17},{10,2},{18,10},{26,18},{... | collective-permute-start | bytes 319496 | tf_op jit(solution)/shard_map/ppermute | solution.py:1084
  370.7 9.8 %copy-start.35 = (bf16[512,3072]{1,0:T(8,128)(2,1)S(1)}, bf16[512,3072]{1,0:T(8,128)(2,1)}, u32[]{:S(2)}) copy-start(bf16[512,3072]{1,0:T(8,128)(2,1)} %get-tuple-element.86.refs_1_) | copy-start | bytes 9437188
  389.9 158.7 %collective-permute-start.35 = (f32[21392]{0:T(1024)S(1)}, f32[21392]{0:T(1024)S(1)}, u32[]{:S(2)}, u32[]{:S(2)}) collective-permute-start(f32[21392]{0:T(1024)S(1)} %concatenate.33), channel_id=1, source_target_pairs={{0,1},{1,0},{2,3},{3,2},{4,5},{5,4},{6,7},{7,6},{8,9},{9,8},{10,11... | collective-permute-start | bytes 256712 | tf_op jit(solution)/shard_map/ppermute | solution.py:601
  548.7 4.6 collective-permute-start.36
  553.2 6.0 collective-permute-start.37
  559.3 4.6 collective-permute-start.38
  563.8 35.2 %collective-permute-start.39 = (f32[21392]{0:T(1024)S(1)}, f32[21392]{0:T(1024)S(1)}, u32[]{:S(2)}, u32[]{:S(2)}) collective-permute-start(f32[21392]{0:T(1024)S(1)} %add.291), channel_id=1, source_target_pairs={{0,16},{8,24},{16,0},{24,8},{1,17},{9,25},{17,1},{25,9},{2,18},{10... | collective-permute-start | bytes 256712 | tf_op jit(solution)/shard_map/ppermute | solution.py:601
  577.4 21.8 %copy-start.26 = (f32[384]{0:T(512)S(1)}, f32[384]{0:T(512)}, u32[]{:S(2)}) copy-start(f32[384]{0:T(512)} %param.29) | copy-start | bytes 4612
  577.4 21.8 %copy-start.28 = (f32[384]{0:T(512)S(1)}, f32[384]{0:T(512)}, u32[]{:S(2)}) copy-start(f32[384]{0:T(512)} %param.40) | copy-start | bytes 4612
  577.4 21.8 %copy-start.29 = (f32[384]{0:T(512)S(1)}, f32[384]{0:T(512)}, u32[]{:S(2)}) copy-start(f32[384]{0:T(512)} %param.41) | copy-start | bytes 4612
  577.4 22.4 %copy-start.32 = (f32[192]{0:T(256)S(1)}, f32[192]{0:T(256)}, u32[]{:S(2)}) copy-start(f32[192]{0:T(256)} %param.28) | copy-start | bytes 2308
  577.5 22.4 %copy-start.33 = (f32[192]{0:T(256)S(1)}, f32[192]{0:T(256)}, u32[]{:S(2)}) copy-start(f32[192]{0:T(256)} %param.38) | copy-start | bytes 2308
  577.5 22.4 %copy-start.34 = (f32[192]{0:T(256)S(1)}, f32[192]{0:T(256)}, u32[]{:S(2)}) copy-start(f32[192]{0:T(256)} %param.39) | copy-start | bytes 2308
  577.5 23.1 %copy-start.21 = (f32[5,416]{1,0:T(8,128)S(1)}, f32[5,416]{1,0:T(8,128)}, u32[]{:S(2)}) copy-start(f32[5,416]{1,0:T(8,128)} %param.30) | copy-start | bytes 24964
  577.5 23.1 %copy-start.24 = (f32[5,416]{1,0:T(8,128)S(1)}, f32[5,416]{1,0:T(8,128)}, u32[]{:S(2)}) copy-start(f32[5,416]{1,0:T(8,128)} %param.42) | copy-start | bytes 24964
  577.5 23.1 %copy-start.25 = (f32[5,416]{1,0:T(8,128)S(1)}, f32[5,416]{1,0:T(8,128)}, u32[]{:S(2)}) copy-start(f32[5,416]{1,0:T(8,128)} %param.43) | copy-start | bytes 24964
  577.5 23.8 %copy-start.27 = (f32[3,6]{1,0:T(4,128)S(1)}, f32[3,6]{1,0:T(4,128)}, u32[]{:S(2)}) copy-start(f32[3,6]{1,0:T(4,128)} %param.31) | copy-start | bytes 220
  577.5 23.8 %copy-start.30 = (f32[3,6]{1,0:T(4,128)S(1)}, f32[3,6]{1,0:T(4,128)}, u32[]{:S(2)}) copy-start(f32[3,6]{1,0:T(4,128)} %param.44) | copy-start | bytes 220
  577.5 23.7 %copy-start.31 = (f32[3,6]{1,0:T(4,128)S(1)}, f32[3,6]{1,0:T(4,128)}, u32[]{:S(2)}) copy-start(f32[3,6]{1,0:T(4,128)} %param.45) | copy-start | bytes 220
  (16 other events, 55.2 us)

commit v3 on v2

--- a/solution.py
+++ b/solution.py
@@ -20,6 +20,8 @@
 WIDE = 256
 HALO = 16
 GROUPS = INNER // WIDE
+CHAIN_LAG = 2
+AHEAD = 6
 PACK = CONV_CH + LANES
 LOG2E = 1.4426950408889634
 VMEM_LIMIT = 56 * 1024 * 1024
@@ -98,18 +100,43 @@
     return rows >= cols if lower else rows <= cols
 
 
+def greet_along():
+    z = lax.axis_index("seq")
+    seq_count = lax.axis_size("seq")
+    barrier = pltpu.get_barrier_semaphore()
+
+    @pl.when(z > 0)
+    def _():
+        pl.semaphore_signal(barrier, inc=1, device_id={"seq": z - 1}, device_id_type=pl.DeviceIdType.MESH)
+
+    @pl.when(z < seq_count - 1)
+    def _():
+        pl.semaphore_signal(barrier, inc=1, device_id={"seq": z + 1}, device_id_type=pl.DeviceIdType.MESH)
+
+    pl.semaphore_wait(barrier, jnp.where(z > 0, 1, 0) + jnp.where(z < seq_count - 1, 1, 0))
+
+
 def states_kernel(
     sig_ref, maps_ref, raw_ref, conv_ref, conv_maps_ref, head_ref,
     x_ref, bc_ref, run_ref, lag_ref, run_t_ref, lag_t_ref, enter_ref, enter_all_ref, tail_ref, offs_ref,
-    states_ref, send_ref,
-    sig, in_t,
+    states_ref, before_ref,
+    sig, in_t, ends, stage, land, sems,
 ):
     step = pl.program_id(0)
     rows = x_ref.shape[0]
     blocks = rows // BLOCK
+    z = lax.axis_index("seq")
+    seq_count = lax.axis_size("seq")
+
+    def to_next(k):
+        return pltpu.make_async_remote_copy(
+            src_ref=stage.at[k], dst_ref=land.at[k], send_sem=sems.at[0, k], recv_sem=sems.at[1, k],
+            device_id={"seq": z + 1}, device_id_type=pl.DeviceIdType.MESH,
+        )
 
     @pl.when(step == 0)
     def _():
+        greet_along()
         sig[...] = maps_ref[...].astype(full_type)
         pre = convolve(sig, conv_maps_ref[...], rows)
         maps = pre * sigmoid(pre)
@@ -136,25 +163,47 @@
             offset = offset + run[BLOCK - 1 : BLOCK]
         offs_ref[blocks : blocks + 1, :] = offset
 
-    sig[...] = sig_ref[...].astype(full_type)
-    pre = convolve(sig, conv_ref[...], rows)
-    x = pre * sigmoid(pre)
-    x_ref[...] = x
-    tail = to_front(tail_ref[...], step)
-    last = to_front(offs_ref[...], step)
-    state = jnp.zeros((STATE, WIDE), full_type)
-    for c in range(blocks):
-        at = slice(c * BLOCK, (c + 1) * BLOCK)
-        weighted = (x[at] * widen(tail[at])).astype(low_type)
-        fade = jnp.exp2(widen(last[c + 1 : c + 2] - last[c : c + 1]))
-        state = state * fade + dot(in_t[:, at], weighted)
-        states_ref[c] = state.astype(low_type)
-    send_ref[:STATE, :] = state.astype(low_type)
-    total = widen(last[blocks : blocks + 1])
-    high = total.astype(low_type).astype(full_type)
-    ids = lax.broadcasted_iota(jnp.int32, (16, WIDE), 0)
-    extra = jnp.where(ids == 0, high, jnp.where(ids == 1, total - high, 0.0))
-    send_ref[STATE:, :] = extra.astype(low_type)
+    @pl.when(step < GROUPS)
+    def _():
+        sig[...] = sig_ref[...].astype(full_type)
+        pre = convolve(sig, conv_ref[...], rows)
+        x = pre * sigmoid(pre)
+        x_ref[...] = x
+        tail = to_front(tail_ref[...], step)
+        last = to_front(offs_ref[...], step)
+        state = jnp.zeros((STATE, WIDE), full_type)
+        for c in range(blocks):
+            at = slice(c * BLOCK, (c + 1) * BLOCK)
+            weighted = (x[at] * widen(tail[at])).astype(low_type)
+            fade = jnp.exp2(widen(last[c + 1 : c + 2] - last[c : c + 1]))
+            state = state * fade + dot(in_t[:, at], weighted)
+            states_ref[c] = state.astype(low_type)
+        ends[step] = state
+
+    @pl.when(step >= CHAIN_LAG)
+    def _():
+        k = step - CHAIN_LAG
+
+        @pl.when(z == 0)
+        def _():
+            land[k] = jnp.zeros((STATE, WIDE), low_type)
+
+        @pl.when(z > 0)
+        def _():
+            to_next(k).wait_recv()
+
+        before_ref[...] = land[k]
+
+        @pl.when(z < seq_count - 1)
+        def _():
+            fade = jnp.exp2(widen(to_front(offs_ref[...], k)[blocks : blocks + 1]))
+            stage[k] = (ends[k] + fade * land[k].astype(full_type)).astype(low_type)
+            to_next(k).start()
+
+    @pl.when((step == GROUPS + CHAIN_LAG - 1) & (z < seq_count - 1))
+    def _():
+        for k in range(GROUPS):
+            to_next(k).wait_send()
 
 
 def outputs_kernel(x_ref, bc_ref, run_ref, lag_t_ref, enter_ref, states_ref, head_ref, y_ref, inter):
@@ -199,7 +248,7 @@
 
 def norm_kernel(
     y_ref, gate_ref, back_ref, gain_ref, bc_ref, enter_ref, state_ref,
-    normed_ref, grad_y_ref, grad_gate_ref, grad_gain_ref, grad_state_ref,
+    normed_ref, normed_t_ref, grad_y_ref, grad_gate_ref, grad_gain_ref, grad_state_ref,
     gated, low_y,
 ):
     step = pl.program_id(0)
@@ -234,7 +283,9 @@
         back = back_ref[:, at]
         vals = gated[:, at]
         scaled = vals * inv
-        normed_ref[:, at] = (scaled * gain).astype(low_type)
+        normed = (scaled * gain).astype(low_type)
+        normed_ref[:, at] = normed
+        normed_t_ref[at, :] = normed.T
         grad_gain_ref[0:1, at] += jnp.sum(back * scaled, axis=0, keepdims=True)
         grad_vals = back * gain * inv - vals * pull
         gate = gate_ref[:, at]
@@ -249,15 +300,67 @@
 
 
 def backward_kernel(
+    counts, spans, left_rows,
     sig_ref, raw_ref, conv_ref, head_ref, grad_y_ref, bc_ref,
-    lag_ref, run_t_ref, enter_ref, tail_ref, offs_ref, states_ref, state_in_ref, grad_in_ref,
-    grad_sig_ref, edge_ref, last_ref, grad_conv_ref, grad_skip_ref, grad_head_ref,
+    lag_ref, run_t_ref, enter_ref, tail_ref, offs_ref, states_ref, state_in_ref, grad_state_ref,
+    lefts_ref, cot_ref, grad_gate_ref,
+    grad_sig_ref, edge_ref, last_ref, grad_conv_ref, grad_skip_ref, grad_head_ref, sums_ref,
     sig, padded, inter, grad_inter, grad_maps, out_t, run_rows, run_cols, run_ends, weighs,
+    stage, land, chain_sems, *scratch,
 ):
-    step = pl.program_id(0)
+    step = pl.program_id(0) - AHEAD
     rows = grad_y_ref.shape[0]
     blocks = rows // BLOCK
+    z = lax.axis_index("seq")
+    seq_count = counts[1]
+    turns, turn, finish = reduce_turns(
+        *counts, spans, [lefts_ref, *left_rows], [cot_ref, grad_gate_ref], sums_ref, scratch
+    )
+    place = step + AHEAD
+    steps = GROUPS + 2 + AHEAD
+
+    def to_previous(k):
+        return pltpu.make_async_remote_copy(
+            src_ref=stage.at[k], dst_ref=land.at[k], send_sem=chain_sems.at[0, k], recv_sem=chain_sems.at[1, k],
+            device_id={"seq": z - 1}, device_id_type=pl.DeviceIdType.MESH,
+        )
+
+    def chain(k):
+        @pl.when(z == seq_count - 1)
+        def _():
+            land[k] = jnp.zeros((STATE, WIDE), low_type)
+
+        @pl.when(z < seq_count - 1)
+        def _():
+            to_previous(k).wait_recv()
+
+        @pl.when(z > 0)
+        def _():
+            fade = jnp.exp2(widen(to_front(offs_ref[...], k)[blocks : blocks + 1]))
+            own = grad_state_ref[:, pl.ds(pl.multiple_of(k * WIDE, WIDE), WIDE)]
+            stage[k] = (own + fade * land[k].astype(full_type)).astype(low_type)
+            to_previous(k).start()
+
+    @pl.when(place == 0)
+    def _():
+        greet()
+
+    lax.fori_loop(place * turns // steps, (place + 1) * turns // steps, turn, 0)
     upper = triangle(False)
+
+    @pl.when(place < AHEAD)
+    def _():
+        for i in range(GROUPS // AHEAD):
+            chain(place * (GROUPS // AHEAD) + i)
+
+    @pl.when(place == steps - 1)
+    def _():
+        finish()
+
+        @pl.when(z > 0)
+        def _():
+            for k in range(GROUPS):
+                to_previous(k).wait_send()
 
     @pl.when(step == 0)
     def _():
@@ -292,7 +395,7 @@
         sums.append(jnp.zeros((3, WIDE), full_type))
         grad_conv_ref[...] = jnp.concatenate(sums, axis=0)
 
-    @pl.when(step < GROUPS)
+    @pl.when((step >= 0) & (step < GROUPS))
     def _():
         sig[...] = sig_ref[...].astype(full_type)
         lag = to_front(lag_ref[...], step)
@@ -305,7 +408,7 @@
         heads_of = lax.broadcasted_iota(jnp.int32, (WIDE, LANES), 0) // HEAD_DIM + 4 * step
         picks = jnp.where(heads_of == lane_ids((WIDE, LANES)), 1.0, 0.0).astype(low_type)
         state_in = state_in_ref[...].astype(full_type)
-        grad_state = grad_in_ref[...].astype(full_type)
+        grad_state = land[step].astype(full_type)
         grad_skip = jnp.zeros((1, WIDE), full_type)
         pre_all = convolve(sig, conv_ref[...], rows)
 
@@ -426,22 +529,23 @@
 def run_states(packed, conv, head):
     rows = packed.shape[0] - HALO
     blocks = rows // BLOCK
+    last = lambda j: jnp.minimum(j, GROUPS - 1)
     whole = lambda shape: pl.BlockSpec(shape, lambda j: (0,) * len(shape))
     small = jax.ShapeDtypeStruct((rows, LANES), full_type)
     small_t = jax.ShapeDtypeStruct((LANES, rows), full_type)
     return pl.pallas_call(
         states_kernel,
-        grid=(GROUPS,),
+        grid=(GROUPS + CHAIN_LAG,),
         in_specs=[
-            pl.BlockSpec((rows + HALO, WIDE), lambda j: (0, j)),
+            pl.BlockSpec((rows + HALO, WIDE), lambda j: (0, last(j))),
             pl.BlockSpec((rows + HALO, WIDE), lambda j: (0, GROUPS)),
             pl.BlockSpec((rows + HALO, LANES), lambda j: (0, CONV_CH // LANES)),
-            pl.BlockSpec((8, WIDE), lambda j: (0, j)),
+            pl.BlockSpec((8, WIDE), lambda j: (0, last(j))),
             pl.BlockSpec((8, WIDE), lambda j: (0, GROUPS)),
             whole((8, LANES)),
         ],
         out_specs=[
-            pl.BlockSpec((rows, WIDE), lambda j: (0, j)),
+            pl.BlockSpec((rows, WIDE), lambda j: (0, last(j))),
             whole((rows, WIDE)),
             whole((rows, LANES)),
             whole((rows, LANES)),
@@ -451,8 +555,8 @@
             whole((rows, LANES)),
             whole((rows, LANES)),
             whole((16, LANES)),
-            pl.BlockSpec((blocks, STATE, WIDE), lambda j: (0, 0, j)),
-            pl.BlockSpec((STATE + 16, WIDE), lambda j: (0, j)),
+            pl.BlockSpec((blocks, STATE, WIDE), lambda j: (0, 0, last(j))),
+            pl.BlockSpec((STATE, WIDE), lambda j: (0, jnp.maximum(j - CHAIN_LAG, 0))),
         ],
         out_shape=[
             jax.ShapeDtypeStruct((rows, INNER), full_type),
@@ -460,13 +564,17 @@
             small, small, small_t, small_t, small, small, small,
             jax.ShapeDtypeStruct((16, LANES), full_type),
             jax.ShapeDtypeStruct((blocks, STATE, INNER), low_type),
-            jax.ShapeDtypeStruct((STATE + 16, INNER), low_type),
+            jax.ShapeDtypeStruct((STATE, INNER), low_type),
         ],
         scratch_shapes=[
             pltpu.VMEM((rows + HALO, WIDE), full_type),
             pltpu.VMEM((STATE, rows), low_type),
+            pltpu.VMEM((GROUPS, STATE, WIDE), full_type),
+            pltpu.VMEM((GROUPS, STATE, WIDE), low_type),
+            pltpu.VMEM((GROUPS, STATE, WIDE), low_type),
+            pltpu.SemaphoreType.DMA((2, GROUPS)),
         ],
-        compiler_params=pltpu.CompilerParams(vmem_limit_bytes=VMEM_LIMIT),
+        compiler_params=pltpu.CompilerParams(collective_id=1, has_side_effects=True, vmem_limit_bytes=VMEM_LIMIT),
         cost_estimate=pl.CostEstimate(flops=10**9, bytes_accessed=15 * 10**6, transcendentals=10**6),
         name="scan_states",
     )(packed, packed, packed, conv, conv, head)
@@ -509,9 +617,13 @@
             by_rows(INNER), by_rows(INNER), by_rows(INNER), whole((8, INNER)),
             by_rows(WIDE), by_rows(LANES), whole((STATE, INNER)),
         ],
-        out_specs=[by_rows(INNER), by_rows(INNER), by_rows(INNER), whole((8, INNER)), whole((STATE, INNER))],
+        out_specs=[
+            by_rows(INNER), pl.BlockSpec((INNER, part), lambda i: (0, i)), by_rows(INNER), by_rows(INNER),
+            whole((8, INNER)), whole((STATE, INNER)),
+        ],
         out_shape=[
             jax.ShapeDtypeStruct((rows, INNER), low_type),
+            jax.ShapeDtypeStruct((INNER, rows), low_type),
             jax.ShapeDtypeStruct((rows, INNER), low_type),
             jax.ShapeDtypeStruct((rows, INNER), low_type),
             jax.ShapeDtypeStruct((8, INNER), full_type),
@@ -524,37 +636,50 @@
     )(y, gate, back, gain, bc, enter, state)
 
 
-def run_backward(packed, conv, head, grad_y, bc, lag, run_t, enter, tail, offs, states, state_in, grad_in):
+def run_backward(
+    packed, conv, head, grad_y, bc, lag, run_t, enter, tail, offs, states, state_in, grad_state, lefts, cot, grad_gate
+):
     rows = grad_y.shape[0]
     blocks = rows // BLOCK
-    whole = lambda shape: pl.BlockSpec(shape, lambda j: (0,) * len(shape))
-    most = lambda j, top: jnp.minimum(j, top)
+    wsh_count, seq_count = lax.axis_size("wsh"), lax.axis_size("seq")
+    groups = INNER // D
+    n_out, n_gate = cot.shape[1] // TILE, grad_gate.shape[1] // TILE
+    spans = [(0, n_out, groups), (n_out * groups, n_gate, 1)]
+    chunks = n_out * groups + n_gate
+    low_at = lambda j, top: jnp.clip(j - AHEAD, 0, top)
+    once = pl.Buffered(1)
+    whole = lambda shape: pl.BlockSpec(shape, lambda j: (0,) * len(shape), pipeline_mode=once)
+    kept = lambda shape: pl.BlockSpec(shape, lambda j: (0,) * len(shape))
     return pl.pallas_call(
-        backward_kernel,
-        grid=(GROUPS + 2,),
+        functools.partial(backward_kernel, (wsh_count, seq_count), spans, [INNER, D]),
+        grid=(GROUPS + 2 + AHEAD,),
         in_specs=[
-            pl.BlockSpec((rows + HALO, WIDE), lambda j: (0, most(j, GROUPS))),
-            pl.BlockSpec((rows + HALO, LANES), lambda j: (0, CONV_CH // LANES)),
-            pl.BlockSpec((8, WIDE), lambda j: (0, most(j, GROUPS))),
+            pl.BlockSpec((rows + HALO, WIDE), lambda j: (0, low_at(j, GROUPS))),
+            pl.BlockSpec((rows + HALO, LANES), lambda j: (0, CONV_CH // LANES), pipeline_mode=once),
+            pl.BlockSpec((8, WIDE), lambda j: (0, low_at(j, GROUPS))),
             whole((8, LANES)),
-            pl.BlockSpec((rows, WIDE), lambda j: (0, most(j, GROUPS - 1))),
+            pl.BlockSpec((rows, WIDE), lambda j: (0, low_at(j, GROUPS - 1))),
             whole((rows, WIDE)),
             whole((rows, LANES)),
             whole((LANES, rows)),
             whole((rows, LANES)),
             whole((rows, LANES)),
             whole((16, LANES)),
-            pl.BlockSpec((blocks, STATE, WIDE), lambda j: (0, 0, most(j, GROUPS - 1))),
-            pl.BlockSpec((STATE, WIDE), lambda j: (0, most(j, GROUPS - 1))),
-            pl.BlockSpec((STATE, WIDE), lambda j: (0, most(j, GROUPS - 1))),
+            pl.BlockSpec((blocks, STATE, WIDE), lambda j: (0, 0, low_at(j, GROUPS - 1))),
+            pl.BlockSpec((STATE, WIDE), lambda j: (0, low_at(j, GROUPS - 1))),
+            whole((STATE, INNER)),
+            whole(lefts.shape),
+            whole(cot.shape),
+            whole(grad_gate.shape),
         ],
         out_specs=[
-            pl.BlockSpec((rows, WIDE), lambda j: (0, j)),
-            pl.BlockSpec((8, WIDE), lambda j: (0, most(j, GROUPS))),
-            pl.BlockSpec((16, WIDE), lambda j: (0, most(j, GROUPS))),
-            pl.BlockSpec((8, WIDE), lambda j: (0, most(j, GROUPS))),
-            pl.BlockSpec((8, WIDE), lambda j: (0, most(j, GROUPS - 1))),
-            whole((8, LANES)),
+            pl.BlockSpec((rows, WIDE), lambda j: (0, low_at(j, GROUPS + 1))),
+            pl.BlockSpec((8, WIDE), lambda j: (0, low_at(j, GROUPS))),
+            pl.BlockSpec((16, WIDE), lambda j: (0, low_at(j, GROUPS))),
+            pl.BlockSpec((8, WIDE), lambda j: (0, low_at(j, GROUPS))),
+            pl.BlockSpec((8, WIDE), lambda j: (0, low_at(j, GROUPS - 1))),
+            kept((8, LANES)),
+            pl.BlockSpec(memory_space=pl.ANY),
         ],
         out_shape=[
             jax.ShapeDtypeStruct((rows, PACK), low_type),
@@ -563,6 +688,7 @@
             jax.ShapeDtypeStruct((8, CONV_CH), full_type),
             jax.ShapeDtypeStruct((8, INNER), full_type),
             jax.ShapeDtypeStruct((8, LANES), full_type),
+            jax.ShapeDtypeStruct((chunks, D // wsh_count, TILE), low_type),
         ],
         scratch_shapes=[
             pltpu.VMEM((rows + HALO, WIDE), full_type),
@@ -575,11 +701,18 @@
             pltpu.VMEM((rows, LANES), full_type),
             pltpu.VMEM((8, LANES), full_type),
             pltpu.VMEM((rows, LANES), full_type),
+            pltpu.VMEM((GROUPS, STATE, WIDE), low_type),
+            pltpu.VMEM((GROUPS, STATE, WIDE), low_type),
+            pltpu.SemaphoreType.DMA((2, GROUPS)),
+            *reduce_scratch(chunks, rows, wsh_count),
         ],
-        compiler_params=pltpu.CompilerParams(vmem_limit_bytes=VMEM_LIMIT),
-        cost_estimate=pl.CostEstimate(flops=2 * 10**10, bytes_accessed=20 * 10**6, transcendentals=5 * 10**6),
+        compiler_params=pltpu.CompilerParams(collective_id=2, has_side_effects=True, vmem_limit_bytes=VMEM_LIMIT),
+        cost_estimate=pl.CostEstimate(flops=10**11, bytes_accessed=20 * 10**6, transcendentals=5 * 10**6),
         name="scan_backward",
-    )(packed, packed, conv, head, grad_y, bc, lag, run_t, enter, tail, offs, states, state_in, grad_in)
+    )(
+        packed, packed, conv, head, grad_y, bc, lag, run_t, enter, tail, offs, states, state_in, grad_state,
+        lefts, cot, grad_gate,
+    )
 
 
 def adam_update(weights, gradient, first_moment, second_moment, step_rate, decay_amount):
@@ -727,13 +860,31 @@
     return [m for m in left if m & bit == 0], [m for m in left if m & bit]
 
 
-def reduce_kernel(counts, rights_at, lefts_ref, *refs):
-    wsh_count, seq_count, starts = counts
-    n_rights = len(starts)
-    right_refs, out_ref = refs[:n_rights], refs[n_rights]
-    (tile, stage, pair, *rest) = refs[n_rights + 1 :]
+def greet():
+    me, z = lax.axis_index("wsh"), lax.axis_index("seq")
+    seq_count = lax.axis_size("seq")
+    barrier = pltpu.get_barrier_semaphore()
+    mesh_id = pl.DeviceIdType.MESH
+    bits = lax.axis_size("wsh").bit_length() - 1
+    for b in range(bits):
+        pl.semaphore_signal(barrier, inc=1, device_id={"wsh": lax.bitwise_xor(me, 1 << b)}, device_id_type=mesh_id)
+
+    @pl.when(z > 0)
+    def _():
+        pl.semaphore_signal(barrier, inc=1, device_id={"seq": z - 1}, device_id_type=mesh_id)
+
+    @pl.when(z < seq_count - 1)
+    def _():
+        pl.semaphore_signal(barrier, inc=1, device_id={"seq": z + 1}, device_id_type=mesh_id)
+
+    along = jnp.where(z > 0, 1, 0) + jnp.where(z < seq_count - 1, 1, 0)
+    pl.semaphore_wait(barrier, bits + along)
+
+
+def reduce_turns(wsh_count, seq_count, spans, left_refs, right_refs, out_ref, scratch):
     orders = part_orders(wsh_count)
     bits = len(orders)
+    tile, stage, pair, *rest = scratch
     lands, rest = rest[:bits], rest[bits:]
     from_left, from_right, pair_sems, far_sems, seq_sems, out_sems = rest
     chunks, blocks, rows, _ = pair.shape
@@ -741,28 +892,13 @@
     me = lax.axis_index("wsh")
     z = lax.axis_index("seq")
     root = seq_count // 2
-    MESH = pl.DeviceIdType.MESH
-
-    barrier = pltpu.get_barrier_semaphore()
-    for b in range(bits + 1):
-        pl.semaphore_signal(barrier, inc=1, device_id={"wsh": lax.bitwise_xor(me, 1 << b)}, device_id_type=MESH)
-
-    @pl.when(z > 0)
-    def _():
-        pl.semaphore_signal(barrier, inc=1, device_id={"seq": z - 1}, device_id_type=MESH)
-
-    @pl.when(z < seq_count - 1)
-    def _():
-        pl.semaphore_signal(barrier, inc=1, device_id={"seq": z + 1}, device_id_type=MESH)
-
-    along = jnp.where(z > 0, 1, 0) + jnp.where(z < seq_count - 1, 1, 0)
-    pl.semaphore_wait(barrier, bits + 1 + along)
+    mesh_id = pl.DeviceIdType.MESH
 
     def pair_copy(k):
         return pltpu.make_async_remote_copy(
             src_ref=stage.at[lax.rem(k, 2)], dst_ref=pair.at[k],
             send_sem=pair_sems.at[0, k], recv_sem=pair_sems.at[1, k],
-            device_id={"wsh": lax.bitwise_xor(me, 1)}, device_id_type=MESH,
+            device_id={"wsh": lax.bitwise_xor(me, 1)}, device_id_type=mesh_id,
         )
 
     spots = []
@@ -776,7 +912,7 @@
             pltpu.make_async_remote_copy(
                 src_ref=pair.at[k, m, pl.ds(p * part, part)], dst_ref=lands[q].at[k, p, i],
                 send_sem=far_sems.at[0, n, k], recv_sem=far_sems.at[1, n, k],
-                device_id={"wsh": lax.bitwise_xor(me, bit)}, device_id_type=MESH,
+                device_id={"wsh": lax.bitwise_xor(me, bit)}, device_id_type=mesh_id,
             )
             for n, (q, p, i, m, bit) in enumerate(spots)
             if q == phase
@@ -786,44 +922,56 @@
         return pltpu.make_async_remote_copy(
             src_ref=source, dst_ref=from_left.at[k],
             send_sem=seq_sems.at[0, k], recv_sem=seq_sems.at[1, k],
-            device_id={"seq": z + 1}, device_id_type=MESH,
+            device_id={"seq": z + 1}, device_id_type=mesh_id,
         )
 
     def to_left(k, source):
         return pltpu.make_async_remote_copy(
             src_ref=source, dst_ref=from_right.at[k],
             send_sem=seq_sems.at[2, k], recv_sem=seq_sems.at[3, k],
-            device_id={"seq": z - 1}, device_id_type=MESH,
+            device_id={"seq": z - 1}, device_id_type=mesh_id,
         )
 
     def out_copy(k, source):
         return pltpu.make_async_copy(source, out_ref.at[k], out_sems.at[k])
 
-    def product(k, first):
-        for n, (start, stop, spans) in enumerate(rights_at):
-            @pl.when((k >= start) & (k < stop))
+    def take_tile(k):
+        for (start, tiles, groups), right_ref in zip(spans, right_refs):
+
+            @pl.when((k >= start) & (k < start + tiles * groups))
             def _():
-                col = lax.rem(k - start, spans) * TILE
-                tile[...] = right_refs[n][:, pl.ds(pl.multiple_of(col, LANES), TILE)]
-        left_at = jnp.where(k < rights_at[0][1], 1 + k // rights_at[0][2], 0)
-        half = blocks * rows
-        return dot(lefts_ref[left_at, pl.ds(first * half, half), :], tile[...])
+                col = lax.rem(k - start, tiles) * TILE
+                tile[...] = right_ref[:, pl.ds(pl.multiple_of(col, LANES), TILE)]
+
+    def product(k, b, core):
+        owner = lax.bitwise_xor(me, 2 * b + core)
+        if len(left_refs) == 1:
+            group, groups, left_ref = 0, 1, left_refs[0]
+            first = owner * rows
+            return dot(left_ref[pl.ds(pl.multiple_of(first, 16), rows), :], tile[...])
+        first = jnp.zeros((), jnp.int32)
+        base = 0
+        for (start, tiles, groups), left_rows in zip(spans, left_refs[1:]):
+            at = base + (owner * groups + (k - start) // tiles) * rows
+            first = jnp.where((k >= start) & (k < start + tiles * groups), at, first)
+            base += left_rows
+        return dot(left_refs[0][pl.ds(pl.multiple_of(first, 16), rows), :], tile[...])
 
     def begin(k):
         @pl.when(k >= 2)
         def _():
             pair_copy(k - 2).wait_send()
-        vals = product(k, 1)
+
+        take_tile(k)
         for b in range(blocks):
-            stage[lax.rem(k, 2), b] = vals[b * rows : (b + 1) * rows].astype(low_type)
+            stage[lax.rem(k, 2), b] = product(k, b, 1).astype(low_type)
         pair_copy(k).start()
 
     def add_pair(k):
-        vals = product(k, 0)
+        take_tile(k)
         pair_copy(k).wait_recv()
         for b in range(blocks):
-            total = vals[b * rows : (b + 1) * rows] + pair[k, b].astype(full_type)
-            pair[k, b] = total.astype(low_type)
+            pair[k, b] = (product(k, b, 0) + pair[k, b].astype(full_type)).astype(low_type)
         for copy in far_copies(k, 0):
             copy.start()
 
@@ -887,66 +1035,70 @@
         (2 + bits + SLACK * (farthest - far), seq_up),
         (3 + bits + SLACK * (farthest + far), seq_down),
     ]
-    depth = 4 + bits + SLACK * 2 * farthest
+    turns = chunks + 4 + bits + SLACK * 2 * farthest
 
     def turn(s, carry):
         for offset, run in stages:
             pl.when((s >= offset) & (s < chunks + offset))(lambda run=run, offset=offset: run(s - offset))
         return carry
 
-    lax.fori_loop(0, chunks + depth, turn, 0)
-
-    def finish(k, carry):
-        for q in range(bits):
-            for copy in far_copies(k, q):
-                copy.wait_send()
-        pl.when(z < seq_count - 1)(lambda: to_right(k, pair.at[k, 0]).wait_send())
-        pl.when(z > 0)(lambda: to_left(k, pair.at[k, 0]).wait_send())
-        out_copy(k, pair.at[k, 0]).wait()
-        return carry
-
-    lax.fori_loop(0, chunks, finish, 0)
-    for k in (chunks - 2, chunks - 1):
-        pair_copy(k).wait_send()
-
-
-def reduce_rows(lefts, out_right, gate_right, sig_right):
-    wsh_count, seq_count = lax.axis_size("wsh"), lax.axis_size("seq")
+    def finish():
+        def wait_all(k, carry):
+            for q in range(bits):
+                for copy in far_copies(k, q):
+                    copy.wait_send()
+            pl.when(z < seq_count - 1)(lambda: to_right(k, pair.at[k, 0]).wait_send())
+            pl.when(z > 0)(lambda: to_left(k, pair.at[k, 0]).wait_send())
+            out_copy(k, pair.at[k, 0]).wait()
+            return carry
+
+        lax.fori_loop(0, chunks, wait_all, 0)
+        for k in (chunks - 2, chunks - 1):
+            pair_copy(k).wait_send()
+
+    return turns, turn, finish
+
+
+def reduce_scratch(chunks, depth, wsh_count):
     rows = D // wsh_count
-    orders = part_orders(wsh_count)
-    bits = len(orders)
-    n_out, n_gate, n_sig = (right.shape[1] // TILE for right in (out_right, gate_right, sig_right))
-    groups = lefts.shape[0] - 1
-    starts = [0, groups * n_out, groups * n_out + n_gate]
-    chunks = starts[2] + n_sig
-    rights_at = [(0, starts[1], n_out), (starts[1], starts[2], n_gate), (starts[2], chunks, n_sig)]
+    bits = len(part_orders(wsh_count))
     low = lambda *shape: pltpu.VMEM(shape, low_type)
     dma = pltpu.SemaphoreType.DMA
-    copies = bits * ((1 << bits) - 1)
+    return [
+        low(depth, TILE),
+        low(2, 1 << bits, rows, TILE),
+        low(chunks, 1 << bits, rows, TILE),
+        *[low(chunks, bits, 1 << (bits - 1 - q), rows // bits, TILE) for q in range(bits)],
+        low(chunks, rows, TILE),
+        low(chunks, rows, TILE),
+        dma((2, chunks)),
+        dma((2, bits * ((1 << bits) - 1), chunks)),
+        dma((4, chunks)),
+        dma((chunks,)),
+    ]
+
+
+def reduce_kernel(counts, spans, left_ref, right_ref, out_ref, *scratch):
+    greet()
+    turns, turn, finish = reduce_turns(*counts, spans, [left_ref], [right_ref], out_ref, scratch)
+    lax.fori_loop(0, turns, turn, 0)
+    finish()
+
+
+def reduce_rows(left, right):
+    wsh_count, seq_count = lax.axis_size("wsh"), lax.axis_size("seq")
+    chunks = right.shape[1] // TILE
     vmem = pl.BlockSpec(memory_space=pltpu.VMEM)
     return pl.pallas_call(
-        functools.partial(reduce_kernel, (wsh_count, seq_count, starts), rights_at),
-        in_specs=[vmem] * 4,
+        functools.partial(reduce_kernel, (wsh_count, seq_count), [(0, chunks, 1)]),
+        in_specs=[vmem] * 2,
         out_specs=pl.BlockSpec(memory_space=pl.ANY),
-        out_shape=jax.ShapeDtypeStruct((chunks, rows, TILE), low_type),
-        scratch_shapes=[
-            low(out_right.shape[0], TILE),
-            low(2, 1 << bits, rows, TILE),
-            low(chunks, 1 << bits, rows, TILE),
-            *[low(chunks, bits, 1 << (bits - 1 - q), rows // bits, TILE) for q in range(bits)],
-            low(chunks, rows, TILE),
-            low(chunks, rows, TILE),
-            dma((2, chunks)),
-            dma((2, copies, chunks)),
-            dma((4, chunks)),
-            dma((chunks,)),
-        ],
-        compiler_params=pltpu.CompilerParams(
-            collective_id=0, has_side_effects=True, vmem_limit_bytes=60 * 1024 * 1024
-        ),
-        cost_estimate=pl.CostEstimate(flops=10**11, bytes_accessed=20 * 10**6, transcendentals=0),
+        out_shape=jax.ShapeDtypeStruct((chunks, D // wsh_count, TILE), low_type),
+        scratch_shapes=reduce_scratch(chunks, right.shape[0], wsh_count),
+        compiler_params=pltpu.CompilerParams(collective_id=0, has_side_effects=True, vmem_limit_bytes=VMEM_LIMIT),
+        cost_estimate=pl.CostEstimate(flops=5 * 10**10, bytes_accessed=20 * 10**6, transcendentals=0),
         name="reduce_gradients",
-    )(lefts, out_right, gate_right, sig_right)
+    )(left, right)
 
 
 def adam_kernel(start, rate, decay, *refs):
@@ -977,17 +1129,588 @@
     )(sums, weights, first_moment, second_moment)
 
 
-def relative_rows(vals, count, groups):
-    size = vals.shape[1] // (count * groups)
+def after(vals, *others):
+    return lax.optimization_barrier((vals,) + others)[0]
+
+
+TILE = 384
+SLACK = 1
+
+
+def part_orders(count):
+    far = [b for b in range(count.bit_length() - 2)]
+    return [far[p:] + far[:p] for p in range(len(far))]
+
+
+def held(order, phase, bits):
+    done = sum(1 << b for b in order[:phase])
+    left = [m for m in range(1 << bits) if m & done == 0]
+    bit = 1 << order[phase]
+    return [m for m in left if m & bit == 0], [m for m in left if m & bit]
+
+
+def greet():
+    me, z = lax.axis_index("wsh"), lax.axis_index("seq")
+    seq_count = lax.axis_size("seq")
+    barrier = pltpu.get_barrier_semaphore()
+    mesh_id = pl.DeviceIdType.MESH
+    bits = lax.axis_size("wsh").bit_length() - 1
+    for b in range(bits):
+        pl.semaphore_signal(barrier, inc=1, device_id={"wsh": lax.bitwise_xor(me, 1 << b)}, device_id_type=mesh_id)
+
+    @pl.when(z > 0)
+    def _():
+        pl.semaphore_signal(barrier, inc=1, device_id={"seq": z - 1}, device_id_type=mesh_id)
+
+    @pl.when(z < seq_count - 1)
+    def _():
+        pl.semaphore_signal(barrier, inc=1, device_id={"seq": z + 1}, device_id_type=mesh_id)
+
+    along = jnp.where(z > 0, 1, 0) + jnp.where(z < seq_count - 1, 1, 0)
+    pl.semaphore_wait(barrier, bits + along)
+
+
+def reduce_turns(wsh_count, seq_count, spans, left_refs, right_refs, out_ref, scratch):
+    orders = part_orders(wsh_count)
+    bits = len(orders)
+    tile, stage, pair, *rest = scratch
+    lands, rest = rest[:bits], rest[bits:]
+    from_left, from_right, pair_sems, far_sems, seq_sems, out_sems = rest
+    chunks, blocks, rows, _ = pair.shape
+    part = rows // bits
     me = lax.axis_index("wsh")
-    order = [r for r in range(count) if r % 2 == 0] + [r for r in range(count) if r % 2 == 1]
-    turned = vals.T
-    parts = [
-        lax.dynamic_slice_in_dim(turned, (lax.bitwise_xor(me, r) * groups + g) * size, size, 0)
-        for g in range(groups)
-        for r in order
+    z = lax.axis_index("seq")
+    root = seq_count // 2
+    mesh_id = pl.DeviceIdType.MESH
+
+    def pair_copy(k):
+        return pltpu.make_async_remote_copy(
+            src_ref=stage.at[lax.rem(k, 2)], dst_ref=pair.at[k],
+            send_sem=pair_sems.at[0, k], recv_sem=pair_sems.at[1, k],
+            device_id={"wsh": lax.bitwise_xor(me, 1)}, device_id_type=mesh_id,
+        )
+
+    spots = []
+    for q in range(bits):
+        for p, order in enumerate(orders):
+            for i, m in enumerate(held(order, q, bits)[1]):
+                spots.append((q, p, i, m, 2 << order[q]))
+
+    def far_copies(k, phase):
+        return [
+            pltpu.make_async_remote_copy(
+                src_ref=pair.at[k, m, pl.ds(p * part, part)], dst_ref=lands[q].at[k, p, i],
+                send_sem=far_sems.at[0, n, k], recv_sem=far_sems.at[1, n, k],
+                device_id={"wsh": lax.bitwise_xor(me, bit)}, device_id_type=mesh_id,
+            )
+            for n, (q, p, i, m, bit) in enumerate(spots)
+            if q == phase
+        ]
+
+    def to_right(k, source):
+        return pltpu.make_async_remote_copy(
+            src_ref=source, dst_ref=from_left.at[k],
+            send_sem=seq_sems.at[0, k], recv_sem=seq_sems.at[1, k],
+            device_id={"seq": z + 1}, device_id_type=mesh_id,
+        )
+
+    def to_left(k, source):
+        return pltpu.make_async_remote_copy(
+            src_ref=source, dst_ref=from_right.at[k],
+            send_sem=seq_sems.at[2, k], recv_sem=seq_sems.at[3, k],
+            device_id={"seq": z - 1}, device_id_type=mesh_id,
+        )
+
+    def out_copy(k, source):
+        return pltpu.make_async_copy(source, out_ref.at[k], out_sems.at[k])
+
+    def take_tile(k):
+        for (start, tiles, groups), right_ref in zip(spans, right_refs):
+
+            @pl.when((k >= start) & (k < start + tiles * groups))
+            def _():
+                col = lax.rem(k - start, tiles) * TILE
+                tile[...] = right_ref[:, pl.ds(pl.multiple_of(col, LANES), TILE)]
+
+    def product(k, b, core):
+        owner = lax.bitwise_xor(me, 2 * b + core)
+        if len(left_refs) == 1:
+            group, groups, left_ref = 0, 1, left_refs[0]
+            first = owner * rows
+            return dot(left_ref[pl.ds(pl.multiple_of(first, 16), rows), :], tile[...])
+        first = jnp.zeros((), jnp.int32)
+        base = 0
+        for (start, tiles, groups), left_rows in zip(spans, left_refs[1:]):
+            at = base + (owner * groups + (k - start) // tiles) * rows
+            first = jnp.where((k >= start) & (k < start + tiles * groups), at, first)
+            base += left_rows
+        return dot(left_refs[0][pl.ds(pl.multiple_of(first, 16), rows), :], tile[...])
+
+    def begin(k):
+        @pl.when(k >= 2)
+        def _():
+            pair_copy(k - 2).wait_send()
+
+        take_tile(k)
+        for b in range(blocks):
+            stage[lax.rem(k, 2), b] = product(k, b, 1).astype(low_type)
+        pair_copy(k).start()
+
+    def add_pair(k):
+        take_tile(k)
+        pair_copy(k).wait_recv()
+        for b in range(blocks):
+            pair[k, b] = (product(k, b, 0) + pair[k, b].astype(full_type)).astype(low_type)
+        for copy in far_copies(k, 0):
+            copy.start()
+
+    def add_far(k, phase):
+        for copy in far_copies(k, phase):
+            copy.wait_recv()
+        for p, order in enumerate(orders):
+            at = pl.ds(p * part, part)
+            for i, m in enumerate(held(order, phase, bits)[0]):
+                total = pair[k, m, at].astype(full_type) + lands[phase][k, p, i].astype(full_type)
+                pair[k, m, at] = total.astype(low_type)
+        if phase < bits - 1:
+            for copy in far_copies(k, phase + 1):
+                copy.start()
+
+    def add_to(k, land):
+        pair[k, 0] = (pair[k, 0].astype(full_type) + land[k].astype(full_type)).astype(low_type)
+
+    def seq_up(k):
+        mine = pair.at[k, 0]
+
+        @pl.when((z > 0) & (z <= root))
+        def _():
+            to_right(k, mine).wait_recv()
+            add_to(k, from_left)
+
+        @pl.when((z < seq_count - 1) & (z >= root))
+        def _():
+            to_left(k, mine).wait_recv()
+            add_to(k, from_right)
+
+        @pl.when((z < seq_count - 1) & (z <= root))
+        def _():
+            to_right(k, mine).start()
+
+        @pl.when((z > 0) & (z >= root))
+        def _():
+            to_left(k, mine).start()
+
+    def seq_down(k):
+        @pl.when(z == root)
+        def _():
+            out_copy(k, pair.at[k, 0]).start()
+
+        @pl.when(z < root)
+        def _():
+            to_left(k, from_right.at[k]).wait_recv()
+            out_copy(k, from_right.at[k]).start()
+            pl.when(z > 0)(lambda: to_left(k, from_right.at[k]).start())
+
+        @pl.when(z > root)
+        def _():
+            to_right(k, from_left.at[k]).wait_recv()
+            out_copy(k, from_left.at[k]).start()
+            pl.when(z < seq_count - 1)(lambda: to_right(k, from_left.at[k]).start())
+
+    far = jnp.abs(z - root)
+    farthest = max(root, seq_count - 1 - root)
+    stages = [(0, begin), (1, add_pair)] + [(2 + q, functools.partial(add_far, phase=q)) for q in range(bits)]
+    stages += [
+        (2 + bits + SLACK * (farthest - far), seq_up),
+        (3 + bits + SLACK * (farthest + far), seq_down),
     ]
-    return jnp.concatenate(parts, axis=0).reshape(groups, count * size, vals.shape[0])
+    turns = chunks + 4 + bits + SLACK * 2 * farthest
+
+    def turn(s, carry):
+        for offset, run in stages:
+            pl.when((s >= offset) & (s < chunks + offset))(lambda run=run, offset=offset: run(s - offset))
+        return carry
+
+    def finish():
+        def wait_all(k, carry):
+            for q in range(bits):
+                for copy in far_copies(k, q):
+                    copy.wait_send()
+            pl.when(z < seq_count - 1)(lambda: to_right(k, pair.at[k, 0]).wait_send())
+            pl.when(z > 0)(lambda: to_left(k, pair.at[k, 0]).wait_send())
+            out_copy(k, pair.at[k, 0]).wait()
+            return carry
+
+        lax.fori_loop(0, chunks, wait_all, 0)
+        for k in (chunks - 2, chunks - 1):
+            pair_copy(k).wait_send()
+
+    return turns, turn, finish
+
+
+def reduce_scratch(chunks, depth, wsh_count):
+    rows = D // wsh_count
+    bits = len(part_orders(wsh_count))
+    low = lambda *shape: pltpu.VMEM(shape, low_type)
+    dma = pltpu.SemaphoreType.DMA
+    return [
+        low(depth, TILE),
+        low(2, 1 << bits, rows, TILE),
+        low(chunks, 1 << bits, rows, TILE),
+        *[low(chunks, bits, 1 << (bits - 1 - q), rows // bits, TILE) for q in range(bits)],
+        low(chunks, rows, TILE),
+        low(chunks, rows, TILE),
+        dma((2, chunks)),
+        dma((2, bits * ((1 << bits) - 1), chunks)),
+        dma((4, chunks)),
+        dma((chunks,)),
+    ]
+
+
+def reduce_kernel(counts, spans, left_ref, right_ref, out_ref, *scratch):
+    greet()
+    turns, turn, finish = reduce_turns(*counts, spans, [left_ref], [right_ref], out_ref, scratch)
+    lax.fori_loop(0, turns, turn, 0)
+    finish()
+
+
+def reduce_rows(left, right):
+    wsh_count, seq_count = lax.axis_size("wsh"), lax.axis_size("seq")
+    chunks = right.shape[1] // TILE
+    vmem = pl.BlockSpec(memory_space=pltpu.VMEM)
+    return pl.pallas_call(
+        functools.partial(reduce_kernel, (wsh_count, seq_count), [(0, chunks, 1)]),
+        in_specs=[vmem] * 2,
+        out_specs=pl.BlockSpec(memory_space=pl.ANY),
+        out_shape=jax.ShapeDtypeStruct((chunks, D // wsh_count, TILE), low_type),
+        scratch_shapes=reduce_scratch(chunks, right.shape[0], wsh_count),
+        compiler_params=pltpu.CompilerParams(collective_id=0, has_side_effects=True, vmem_limit_bytes=VMEM_LIMIT),
+        cost_estimate=pl.CostEstimate(flops=5 * 10**10, bytes_accessed=20 * 10**6, transcendentals=0),
+        name="reduce_gradients",
+    )(left, right)
+
+
+def adam_kernel(start, rate, decay, *refs):
+    share_ref, weight_ref, first_ref, second_ref, grad_ref, next_ref, next_first_ref, next_second_ref = refs
+    grad = share_ref[0].astype(full_type)
+    grad_ref[...] = grad
+    next_ref[...], next_first_ref[...], next_second_ref[...] = adam_update(
+        weight_ref[...], grad, first_ref[...], second_ref[...], rate, decay
+    )
+
+
+def adam_chunks(sums, start, weights, first_moment, second_moment, rate, decay, name):
+    all_rows, cols = weights.shape
+    rows = sums.shape[1]
+    tiles = pl.cdiv(cols, TILE)
+    block = pl.BlockSpec((rows, TILE), lambda i, j: (i, j))
+    return pl.pallas_call(
+        functools.partial(adam_kernel, start, rate, decay),
+        grid=(all_rows // rows, tiles),
+        in_specs=[pl.BlockSpec((1, rows, TILE), lambda i, j: (start + i * tiles + j, 0, 0))] + [block] * 3,
+        out_specs=[block] * 4,
+        out_shape=[jax.ShapeDtypeStruct(weights.shape, full_type)] * 4,
+        compiler_params=pltpu.CompilerParams(vmem_limit_bytes=VMEM_LIMIT),
+        cost_estimate=pl.CostEstimate(
+            flops=20 * weights.size, bytes_accessed=30 * weights.size, transcendentals=weights.size
+        ),
+        name=name,
+    )(sums, weights, first_moment, second_moment)
+
+
+def after(vals, *others):
+    return lax.optimization_barrier((vals,) + others)[0]
+
+
+def shift(vals, by):
+    count = lax.axis_size("seq")
+    pairs = [(i, i + by) for i in range(count) if 0 <= i + by < count]
+    return lax.ppermute(vals, "seq", pairs)
+
+
+TILE = 384
+SLACK = 1
+
+
+def part_orders(count):
+    far = [b for b in range(count.bit_length() - 2)]
+    return [far[p:] + far[:p] for p in range(len(far))]
+
+
+def held(order, phase, bits):
+    done = sum(1 << b for b in order[:phase])
+    left = [m for m in range(1 << bits) if m & done == 0]
+    bit = 1 << order[phase]
+    return [m for m in left if m & bit == 0], [m for m in left if m & bit]
+
+
+def greet():
+    me, z = lax.axis_index("wsh"), lax.axis_index("seq")
+    seq_count = lax.axis_size("seq")
+    barrier = pltpu.get_barrier_semaphore()
+    mesh_id = pl.DeviceIdType.MESH
+    bits = lax.axis_size("wsh").bit_length() - 1
+    for b in range(bits):
+        pl.semaphore_signal(barrier, inc=1, device_id={"wsh": lax.bitwise_xor(me, 1 << b)}, device_id_type=mesh_id)
+
+    @pl.when(z > 0)
+    def _():
+        pl.semaphore_signal(barrier, inc=1, device_id={"seq": z - 1}, device_id_type=mesh_id)
+
+    @pl.when(z < seq_count - 1)
+    def _():
+        pl.semaphore_signal(barrier, inc=1, device_id={"seq": z + 1}, device_id_type=mesh_id)
+
+    along = jnp.where(z > 0, 1, 0) + jnp.where(z < seq_count - 1, 1, 0)
+    pl.semaphore_wait(barrier, bits + along)
+
+
+def reduce_turns(wsh_count, seq_count, spans, left_refs, right_refs, out_ref, scratch):
+    orders = part_orders(wsh_count)
+    bits = len(orders)
+    tile, stage, pair, *rest = scratch
+    lands, rest = rest[:bits], rest[bits:]
+    from_left, from_right, pair_sems, far_sems, seq_sems, out_sems = rest
+    chunks, blocks, rows, _ = pair.shape
+    part = rows // bits
+    me = lax.axis_index("wsh")
+    z = lax.axis_index("seq")
+    root = seq_count // 2
+    mesh_id = pl.DeviceIdType.MESH
+
+    def pair_copy(k):
+        return pltpu.make_async_remote_copy(
+            src_ref=stage.at[lax.rem(k, 2)], dst_ref=pair.at[k],
+            send_sem=pair_sems.at[0, k], recv_sem=pair_sems.at[1, k],
+            device_id={"wsh": lax.bitwise_xor(me, 1)}, device_id_type=mesh_id,
+        )
+
+    spots = []
+    for q in range(bits):
+        for p, order in enumerate(orders):
+            for i, m in enumerate(held(order, q, bits)[1]):
+                spots.append((q, p, i, m, 2 << order[q]))
+
+    def far_copies(k, phase):
+        return [
+            pltpu.make_async_remote_copy(
+                src_ref=pair.at[k, m, pl.ds(p * part, part)], dst_ref=lands[q].at[k, p, i],
+                send_sem=far_sems.at[0, n, k], recv_sem=far_sems.at[1, n, k],
+                device_id={"wsh": lax.bitwise_xor(me, bit)}, device_id_type=mesh_id,
+            )
+            for n, (q, p, i, m, bit) in enumerate(spots)
+            if q == phase
+        ]
+
+    def to_right(k, source):
+        return pltpu.make_async_remote_copy(
+            src_ref=source, dst_ref=from_left.at[k],
+            send_sem=seq_sems.at[0, k], recv_sem=seq_sems.at[1, k],
+            device_id={"seq": z + 1}, device_id_type=mesh_id,
+        )
+
+    def to_left(k, source):
+        return pltpu.make_async_remote_copy(
+            src_ref=source, dst_ref=from_right.at[k],
+            send_sem=seq_sems.at[2, k], recv_sem=seq_sems.at[3, k],
+            device_id={"seq": z - 1}, device_id_type=mesh_id,
+        )
+
+    def out_copy(k, source):
+        return pltpu.make_async_copy(source, out_ref.at[k], out_sems.at[k])
+
+    def take_tile(k):
+        for (start, tiles, groups), right_ref in zip(spans, right_refs):
+
+            @pl.when((k >= start) & (k < start + tiles * groups))
+            def _():
+                col = lax.rem(k - start, tiles) * TILE
+                tile[...] = right_ref[:, pl.ds(pl.multiple_of(col, LANES), TILE)]
+
+    def product(k, b, core):
+        owner = lax.bitwise_xor(me, 2 * b + core)
+        if len(left_refs) == 1:
+            group, groups, left_ref = 0, 1, left_refs[0]
+            first = owner * rows
+            return dot(left_ref[pl.ds(pl.multiple_of(first, 16), rows), :], tile[...])
+        first = jnp.zeros((), jnp.int32)
+        base = 0
+        for (start, tiles, groups), left_rows in zip(spans, left_refs[1:]):
+            at = base + (owner * groups + (k - start) // tiles) * rows
+            first = jnp.where((k >= start) & (k < start + tiles * groups), at, first)
+            base += left_rows
+        return dot(left_refs[0][pl.ds(pl.multiple_of(first, 16), rows), :], tile[...])
+
+    def begin(k):
+        @pl.when(k >= 2)
+        def _():
+            pair_copy(k - 2).wait_send()
+
+        take_tile(k)
+        for b in range(blocks):
+            stage[lax.rem(k, 2), b] = product(k, b, 1).astype(low_type)
+        pair_copy(k).start()
+
+    def add_pair(k):
+        take_tile(k)
+        pair_copy(k).wait_recv()
+        for b in range(blocks):
+            pair[k, b] = (product(k, b, 0) + pair[k, b].astype(full_type)).astype(low_type)
+        for copy in far_copies(k, 0):
+            copy.start()
+
+    def add_far(k, phase):
+        for copy in far_copies(k, phase):
+            copy.wait_recv()
+        for p, order in enumerate(orders):
+            at = pl.ds(p * part, part)
+            for i, m in enumerate(held(order, phase, bits)[0]):
+                total = pair[k, m, at].astype(full_type) + lands[phase][k, p, i].astype(full_type)
+                pair[k, m, at] = total.astype(low_type)
+        if phase < bits - 1:
+            for copy in far_copies(k, phase + 1):
+                copy.start()
+
+    def add_to(k, land):
+        pair[k, 0] = (pair[k, 0].astype(full_type) + land[k].astype(full_type)).astype(low_type)
+
+    def seq_up(k):
+        mine = pair.at[k, 0]
+
+        @pl.when((z > 0) & (z <= root))
+        def _():
+            to_right(k, mine).wait_recv()
+            add_to(k, from_left)
+
+        @pl.when((z < seq_count - 1) & (z >= root))
+        def _():
+            to_left(k, mine).wait_recv()
+            add_to(k, from_right)
+
+        @pl.when((z < seq_count - 1) & (z <= root))
+        def _():
+            to_right(k, mine).start()
+
+        @pl.when((z > 0) & (z >= root))
+        def _():
+            to_left(k, mine).start()
+
+    def seq_down(k):
+        @pl.when(z == root)
+        def _():
+            out_copy(k, pair.at[k, 0]).start()
+
+        @pl.when(z < root)
+        def _():
+            to_left(k, from_right.at[k]).wait_recv()
+            out_copy(k, from_right.at[k]).start()
+            pl.when(z > 0)(lambda: to_left(k, from_right.at[k]).start())
+
+        @pl.when(z > root)
+        def _():
+            to_right(k, from_left.at[k]).wait_recv()
+            out_copy(k, from_left.at[k]).start()
+            pl.when(z < seq_count - 1)(lambda: to_right(k, from_left.at[k]).start())
+
+    far = jnp.abs(z - root)
+    farthest = max(root, seq_count - 1 - root)
+    stages = [(0, begin), (1, add_pair)] + [(2 + q, functools.partial(add_far, phase=q)) for q in range(bits)]
+    stages += [
+        (2 + bits + SLACK * (farthest - far), seq_up),
+        (3 + bits + SLACK * (farthest + far), seq_down),
+    ]
+    turns = chunks + 4 + bits + SLACK * 2 * farthest
+
+    def turn(s, carry):
+        for offset, run in stages:
+            pl.when((s >= offset) & (s < chunks + offset))(lambda run=run, offset=offset: run(s - offset))
+        return carry
+
+    def finish():
+        def wait_all(k, carry):
+            for q in range(bits):
+                for copy in far_copies(k, q):
+                    copy.wait_send()
+            pl.when(z < seq_count - 1)(lambda: to_right(k, pair.at[k, 0]).wait_send())
+            pl.when(z > 0)(lambda: to_left(k, pair.at[k, 0]).wait_send())
+            out_copy(k, pair.at[k, 0]).wait()
+            return carry
+
+        lax.fori_loop(0, chunks, wait_all, 0)
+        for k in (chunks - 2, chunks - 1):
+            pair_copy(k).wait_send()
+
+    return turns, turn, finish
+
+
+def reduce_scratch(chunks, depth, wsh_count):
+    rows = D // wsh_count
+    bits = len(part_orders(wsh_count))
+    low = lambda *shape: pltpu.VMEM(shape, low_type)
+    dma = pltpu.SemaphoreType.DMA
+    return [
+        low(depth, TILE),
+        low(2, 1 << bits, rows, TILE),
+        low(chunks, 1 << bits, rows, TILE),
+        *[low(chunks, bits, 1 << (bits - 1 - q), rows // bits, TILE) for q in range(bits)],
+        low(chunks, rows, TILE),
+        low(chunks, rows, TILE),
+        dma((2, chunks)),
+        dma((2, bits * ((1 << bits) - 1), chunks)),
+        dma((4, chunks)),
+        dma((chunks,)),
+    ]
+
+
+def reduce_kernel(counts, spans, left_ref, right_ref, out_ref, *scratch):
+    greet()
+    turns, turn, finish = reduce_turns(*counts, spans, [left_ref], [right_ref], out_ref, scratch)
+    lax.fori_loop(0, turns, turn, 0)
+    finish()
+
+
+def reduce_rows(left, right):
+    wsh_count, seq_count = lax.axis_size("wsh"), lax.axis_size("seq")
+    chunks = right.shape[1] // TILE
+    vmem = pl.BlockSpec(memory_space=pltpu.VMEM)
+    return pl.pallas_call(
+        functools.partial(reduce_kernel, (wsh_count, seq_count), [(0, chunks, 1)]),
+        in_specs=[vmem] * 2,
+        out_specs=pl.BlockSpec(memory_space=pl.ANY),
+        out_shape=jax.ShapeDtypeStruct((chunks, D // wsh_count, TILE), low_type),
+        scratch_shapes=reduce_scratch(chunks, right.shape[0], wsh_count),
+        compiler_params=pltpu.CompilerParams(collective_id=0, has_side_effects=True, vmem_limit_bytes=VMEM_LIMIT),
+        cost_estimate=pl.CostEstimate(flops=5 * 10**10, bytes_accessed=20 * 10**6, transcendentals=0),
+        name="reduce_gradients",
+    )(left, right)
+
+
+def adam_kernel(start, rate, decay, *refs):
+    share_ref, weight_ref, first_ref, second_ref, grad_ref, next_ref, next_first_ref, next_second_ref = refs
+    grad = share_ref[0].astype(full_type)
+    grad_ref[...] = grad
+    next_ref[...], next_first_ref[...], next_second_ref[...] = adam_update(
+        weight_ref[...], grad, first_ref[...], second_ref[...], rate, decay
+    )
+
+
+def adam_chunks(sums, start, weights, first_moment, second_moment, rate, decay, name):
+    all_rows, cols = weights.shape
+    rows = sums.shape[1]
+    tiles = pl.cdiv(cols, TILE)
+    block = pl.BlockSpec((rows, TILE), lambda i, j: (i, j))
+    return pl.pallas_call(
+        functools.partial(adam_kernel, start, rate, decay),
+        grid=(all_rows // rows, tiles),
+        in_specs=[pl.BlockSpec((1, rows, TILE), lambda i, j: (start + i * tiles + j, 0, 0))] + [block] * 3,
+        out_specs=[block] * 4,
+        out_shape=[jax.ShapeDtypeStruct(weights.shape, full_type)] * 4,
+        compiler_params=pltpu.CompilerParams(vmem_limit_bytes=VMEM_LIMIT),
+        cost_estimate=pl.CostEstimate(
+            flops=20 * weights.size, bytes_accessed=30 * weights.size, transcendentals=weights.size
+        ),
+        name=name,
+    )(sums, weights, first_moment, second_moment)
 
 
 def after(vals, *others):
@@ -1065,21 +1788,21 @@
     tokens = tokens[HALO:]
     inv_rms = inv_rms[HALO:]
     normed = normed_all[HALO:]
-    x, bc, run, lag, run_t, lag_t, enter, enter_all, tail, offs, states, send = run_states(packed, conv, head)
-    fades = send[STATE].astype(full_type) + send[STATE + 1].astype(full_type)
-    state_in = carry_states(send[:STATE], fades, 1)
+    normed_t = normed.T
+    x, bc, run, lag, run_t, lag_t, enter, enter_all, tail, offs, states, state_in = run_states(packed, conv, head)
     y = run_outputs(x, bc, run, lag_t, enter, states, head)
     gate_vals, full_gate = multiply_pieces(normed, gate_pieces, wsh_count, full_type, "project_gate")
     back, full_out = multiply_back(cot_low, out_pieces, wsh_count, "project_back")
     gain_rows = jnp.broadcast_to(gain_out, (8, INNER))
-    normed_out, grad_y, grad_gate, part_gnorm, grad_state = run_norm(
+    normed_out, normed_out_t, grad_y, grad_gate, part_gnorm, grad_state = run_norm(
         y, gate_vals, back, gain_rows, bc, enter_all, state_in
     )
-    grad_in = carry_states(grad_state.astype(low_type), fades, -1)
     block_out = (tokens + dot(normed_out, full_out)).astype(low_type)[None]
     grad_normed = dot_nt(grad_gate, full_gate)
-    grad_pack, edge, last, part_conv, part_skip, part_head = run_backward(
-        packed, conv, head, grad_y, bc, lag, run_t, enter, tail, offs, states, state_in, grad_in
+    lefts = jnp.concatenate([normed_out_t, normed_t], axis=0)
+    grad_pack, edge, last, part_conv, part_skip, part_head, sums_early = run_backward(
+        packed, conv, head, grad_y, bc, lag, run_t, enter, tail, offs, states, state_in, grad_state,
+        lefts, cot_low, grad_gate,
     )
     edge_next = lax.ppermute(edge, "seq", [(i, i - 1) for i in range(1, seq_count)])
     fixed = jnp.concatenate([last[:8], last[8:] + edge_next], axis=0).astype(low_type)
@@ -1104,17 +1827,15 @@
     grad_head = lax.dynamic_slice_in_dim(
         small_sums[cuts[2] :].reshape(3, HEADS), wsh_index * cols_head, cols_head, 1
     )
-    lefts = jnp.concatenate(
-        [relative_rows(normed, wsh_count, 1), relative_rows(normed_out, wsh_count, INNER // D)], axis=0
+    sums_sig = reduce_rows(normed_t, grad_pack)
+    tiles_out = (INNER // D) * (D // TILE)
+    sums = jnp.concatenate([sums_early[tiles_out:], sums_sig], axis=0)
+    grad_out, *new_out = adam_chunks(
+        sums_early, 0, w_out, first_w_out, second_w_out, rate_matrix, weight_decay, "adam_w_out"
     )
-    sums = reduce_rows(lefts, cot_low, grad_gate, grad_pack)
-    tiles_out = (INNER // D) * (D // TILE)
-    grad_out, *new_out = adam_chunks(sums, 0, w_out, first_w_out, second_w_out, rate_matrix, weight_decay, "adam_w_out")
-    grad_in_w, *new_in = adam_chunks(
-        sums, tiles_out, w_in, first_w_in, second_w_in, rate_matrix, weight_decay, "adam_w_in"
-    )
+    grad_in_w, *new_in = adam_chunks(sums, 0, w_in, first_w_in, second_w_in, rate_matrix, weight_decay, "adam_w_in")
     at_dt = CONV_CH % TILE
-    grad_dt = sums[-1, :, at_dt : at_dt + HEADS].astype(full_type)
+    grad_dt = sums_sig[-1, :, at_dt : at_dt + HEADS].astype(full_type)
     params = (w_in, w_dt, w_out, gain_pre, gain_norm, conv_param, head_param)
     gradients = (grad_in_w, grad_dt, grad_out, grad_gpre, grad_gnorm, grad_conv, grad_head)
     firsts = (first_w_in, first_w_dt, first_w_out, first_gain_pre, first_gain_norm, first_conv, first_head)

time: 612 us -> 612 us (level)
  Pallas kernels: 328 us -> 367 us
  waiting for transfers between devices: 104 us -> 82 us
  starting transfers between devices: 36.4 us -> 23 us
  local copies, waits for them, and re-layouts: 55.1 us -> 61.7 us
    ppermute x6 -> x0, waiting for transfers between devices: 38.7 us -> none  [shift(): return lax.ppermute(vals, 'seq', pairs)]
    pallas_call x3, Pallas kernels: 220 us -> 258 us  [the longest x1 152 us: run_backward(): pl.pallas_call(functools.partial(backward_kernel, (wsh_count, seq_count),...]
    ppermute x32, waiting for transfers between devices: 61.8 us -> 80.9 us  [swap(): lax.ppermute(vals, axis, [(i, i ^ bit) for i in range(lax.axis_size(axis))])]
    concatenate x3 -> x0, local copies, waits for them, and re-layouts: 14.9 us -> none  [relative_rows(): jnp.concatenate(parts, axis=0).reshape(groups, count * size, vals.shape[0])]
    ppermute x6 -> x0, starting transfers between devices: 14.6 us -> none  [shift(): return lax.ppermute(vals, 'seq', pairs)]
    convert_element_type x6 -> x1, other arithmetic: 11.8 us -> 0.01 us  [shards(): grad_dt = sums_sig[-1, :, at_dt:at_dt + HEADS].astype(full_type)]
    unnamed x89 -> x97, local copies, waits for them, and re-layouts: 12 us -> 19.6 us
  transfers between devices with their start and end apart: 40 -> 34, of which waited for: 13 -> 10; matrix products, arithmetic and copies ran while one was open for 12% -> 13% of each run, Pallas kernels for 42% -> 17%
where the time goes in v3:
time: 612 us; the launch traced here: 606 us
  Pallas kernels  367 us (60%)
  waiting for transfers between devices  82 us (13%)
  local copies, waits for them, and re-layouts  61.7 us (10%)
  other arithmetic  30.9 us (5%)
  matrix products  28.4 us (5%)
  starting transfers between devices  23 us (4%)
  blocking collectives  10.7 us (2%)
    pallas_call x1, Pallas kernels, run_backward(): pl.pallas_call(functools.partial(backward_kernel, (wsh_count, seq_count),...  152 us
    ppermute x32, waiting for transfers between devices, swap(): lax.ppermute(vals, axis, [(i, i ^ bit) for i in range(lax.axis_size(axis))])  80.9 us
    pallas_call x1, Pallas kernels, reduce_rows(): pl.pallas_call(functools.partial(reduce_kernel, (wsh_count, seq_count), [...  79.6 us
    pallas_call x2, Pallas kernels, adam_chunks(): pl.pallas_call(functools.partial(adam_kernel, start, rate, decay), grid=(...  31.3 us
    pallas_call x2, Pallas kernels, multiply_pieces(): pl.pallas_call(functools.partial(piece_kernel, spots, rows), grid=(pl.cdi...  28.7 us
    dot_general x3, matrix products, dot(): lax.dot_general(left_side, right_side, (dims, ((), ())), precision=precis...  28.4 us
    pallas_call x1, Pallas kernels, run_states(): pl.pallas_call(states_kernel, grid=(GROUPS + CHAIN_LAG,), in_specs=[pl.Bl...  26.8 us
    unnamed x97, local copies, waits for them, and re-layouts  19.6 us
  transfers between devices with their start and end apart: 34, of which 10 were waited for; matrix products, arithmetic and copies ran while one was open for 13% of the time, Pallas kernels for 17%

profile of v3, /device:TPU:0, one launch (start us, length us, event | category | flops | bytes accessed | tf_op | source)
XLA Modules:
  0.0 605.6 jit_solution(13800975644427696519)
XLA Ops:
  3.7 10.7 %all-gather.1 = bf16[8,1,2688]{2,1,0:T(2,128)(2,1)S(1)} all-gather(bf16[1,1,2688]{2,1,0:T(2,128)(2,1)S(1)} %reshape.139), channel_id=2, replica_groups=mesh['seq'=4,'wsh'=8] {'wsh'}, dimensions={0}, use_global_device_ids=true | all-gather | bytes 48384 | tf_op jit(solution)/shard_map/all_gather | solution.py:1766
  15.1 2.6 convert.30
  17.7 1.1 slice.127
  19.0 3.2 concatenate.25.refs_0_
  22.3 1.5 collective-permute-start.2
  24.3 29.6 %collective-permute-done.2.refs_2_ = bf16[192,3456]{1,0:T(8,128)(2,1)S(1)} collective-permute-done((bf16[192,3456]{1,0:T(8,128)(2,1)}, bf16[192,3456]{1,0:T(8,128)(2,1)S(1)}, u32[]{:S(2)}, u32[]{:S(2)}) %collective-permute-start.2) | collective-permute-done | bytes 1327136 | tf_op jit(solution)/shard_map/ppermute | solution.py:734
  53.9 1.6 collective-permute-start.3
  57.2 13.2 %collective-permute-done.3.refs_3_ = bf16[96,3456]{1,0:T(8,128)(2,1)} collective-permute-done((bf16[96,3456]{1,0:T(8,128)(2,1)S(1)}, bf16[96,3456]{1,0:T(8,128)(2,1)}, u32[]{:S(2)}, u32[]{:S(2)}) %collective-permute-start.3) | collective-permute-done | bytes 663584 | tf_op jit(solution)/shard_map/ppermute | solution.py:734
  70.4 2.3 collective-permute-done.4.refs_4_
  73.3 1.4 collective-permute-start.10
  74.7 24.3 %collective-permute-done.11.refs_2_ = bf16[192,3072]{1,0:T(8,128)(2,1)} collective-permute-done((bf16[192,3072]{1,0:T(8,128)(2,1)S(1)}, bf16[192,3072]{1,0:T(8,128)(2,1)}, u32[]{:S(2)}, u32[]{:S(2)}) %collective-permute-start.11) | collective-permute-done | bytes 1179680 | tf_op jit(solution)/shard_map/ppermute | solution.py:734
  99.0 1.9 slice.134
  101.6 1.9 slice.135
  103.5 1.4 collective-permute-start.13
  104.9 1.7 copy.120
  106.9 3.8 collective-permute-start
  110.7 2.8 convert_element_type.41.refs_0_
  113.9 2.4 collective-permute-done.13.refs_4_
  116.3 1.6 collective-permute-start.20
  120.6 1.3 slice.131
  121.9 1.5 slice.130
  123.4 1.4 slice.138
  124.8 1.5 copy.137
  126.4 1.4 reshape.132
  127.8 1.3 copy.125
  129.9 1.6 reshape.130
  131.5 1.6 copy.124
  133.1 1.6 reshape.131
  135.3 1.5 pad.13.conv_ref.conv_maps_ref
  136.9 1.3 broadcast_in_dim.19
  138.2 1.6 copy.127
  139.8 1.5 copy.133
  141.3 1.5 copy.135
  142.8 1.1 multiply_reduce_fusion
  144.6 2.6 multiply_convert_fusion
  147.9 2.4 slice_bitcast_fusion.3
  150.3 2.2 copy.123.left_ref
  153.1 2.6 copy.126.left_ref
  155.7 2.8 maximum_convert_fusion
  161.8 1.4 collective-permute-start.22
  163.2 14.9 %project_signal.1 = (bf16[528,3456]{1,0:T(8,128)(2,1)}, bf16[1536,3456]{1,0:T(8,128)(2,1)}) custom-call(s32[1]{0:T(128)} %bitcast.2.me_ref, bf16[528,1536]{1,0:T(8,128)(2,1)} %copy.123.left_ref, bf16[192,3456]{1,0:T(8,128)(2,1)} %concatenate.25.refs_0_, bf16[192,3456]{1,0:T(8,128)(2,1)} %copy-done.13, bf16[192,3456]{1,0:T(8,128)(2,1)} %copy-done.12, ...), custom_call_target="tpu_custom_call" | custom-call | flops 5605687296 | bytes 21233664 | tf_op jit(solution)/shard_map/project_signal/pallas_call | solution.py:768
  178.1 26.8 %scan_states.1 = (f32[512,3072]{1,0:T(8,128)}, f32[512,256]{1,0:T(8,128)}, f32[512,128]{1,0:T(8,128)}, f32[512,128]{1,0:T(8,128)}, f32[128,512]{1,0:T(8,128)}, /...) custom-call(bf16[528,3456]{1,0:T(8,128)(2,1)} %get-tuple-element.73., ...), custom_call_target="tpu_custom_call" | custom-call | flops 1000000000 | bytes 15000000 | tf_op jit(solution)/shard_map/scan_states/pallas_call | solution.py:536
  206.1 15.9 %scan_outputs.1.y_ref = f32[512,3072]{1,0:T(8,128)} custom-call(f32[512,3072]{1,0:T(8,128)} %get-tuple-element.74.x_ref, f32[512,256]{1,0:T(8,128)} %get-tuple-element.75.bc_ref, f32[512,128]{1,0:T(8,128)} %get-tuple-element.76.run_ref, f32[128,512]{1,0:T(8,128)} %get-tuple-element.77.lag_t_ref, f32[512,128]{1,0:T(8,128)} %get-tuple-element.78.enter_ref, ...), custom_call_target="tpu_custom_call" | custom-call | flops 10000000000 | bytes 15000000 | tf_op jit(solution)/shard_map/scan_outputs/pallas_call | solution.py:587
  222.0 13.8 %project_gate.1 = (f32[512,3072]{1,0:T(8,128)}, bf16[1536,3072]{1,0:T(8,128)(2,1)}) custom-call(s32[1]{0:T(128)} %bitcast.2.me_ref, bf16[512,1536]{1,0:T(8,128)(2,1)} %copy.126.left_ref, bf16[192,3072]{1,0:T(8,128)(2,1)} %copy-done.8, bf16[192,3072]{1,0:T(8,128)(2,1)} %collective-permute-done.10.refs_1_, bf16[192,3072]{1,0:T(8,128)(2,1)} %collective-permute-done.11.refs_2_, ...), custom_call_target="tpu_custom_call" | custom-call | flops 4831838208 | bytes 18874368 | tf_op jit(solution)/shard_map/project_gate/pallas_call | solution.py:768
  238.0 14.9 %project_back.1 = (f32[512,3072]{1,0:T(8,128)}, bf16[3072,1536]{1,0:T(8,128)(2,1)}) custom-call(s32[1]{0:T(128)} %bitcast.2.me_ref, bf16[512,1536]{1,0:T(8,128)(2,1)} %bitcast.41, bf16[384,1536]{1,0:T(8,128)(2,1)} %convert_element_type.41.refs_0_, bf16[384,1536]{1,0:T(8,128)(2,1)} %collective-permute-done.19.refs_1_, ...), custom_call_target="tpu_custom_call" | custom-call | flops 4831838208 | bytes 18874368 | tf_op jit(solution)/shard_map/project_back/pallas_call | solution.py:823
  253.6 18.2 %gated_norm.1 = (bf16[512,3072]{1,0:T(8,128)(2,1)}, bf16[3072,512]{1,0:T(8,128)(2,1)}, bf16[512,3072]{1,0:T(8,128)(2,1)}, bf16[512,3072]{1,0:T(8,128)(2,1)}, f32[8,3072]{1,0:T(8,128)}, /*index=5*/f32[128,3072]{1,0:T(8,128)}) custom-call(f32[512,3072]{1,0:T(8,128)} %scan_outputs.1.y_ref, f32[512,3072]{1,0:T(8,128)} %get-tuple-element.81.gate_ref, ...), custom_call_target="tpu_custom_call" | custom-call | flops 1000000000 | bytes 30000000 | tf_op jit(solution)/shard_map/gated_norm/pallas_call | solution.py:613
  271.9 4.4 pad_maximum_fusion.lefts_ref
  276.2 151.8 %scan_backward.1 = (bf16[512,3456]{1,0:T(8,128)(2,1)}, f32[8,3328]{1,0:T(8,128)}, f32[16,3328]{1,0:T(8,128)}, f32[8,3328]{1,0:T(8,128)}, f32[8,3072]{1,0:T(8,128...) custom-call(bf16[528,3456]{1,0:T(8,128)(2,1)} %get-tuple-element.73.sig_ref.maps_ref.raw_ref, ...), custom_call_target="tpu_custom_call" | custom-call | flops 99999997952 | bytes 20000000 | tf_op jit(solution)/shard_map/scan_backward/pallas_call | solution.py:653
  428.0 1.3 collective-permute-start.28
  431.9 10.3 %fusion.1 = bf16[1,512,1536]{1,2,0:T(8,128)(2,1)} fusion(bf16[512,3072]{1,0:T(8,128)(2,1)} %get-tuple-element.86, bf16[3072,1536]{1,0:T(8,128)(2,1)} %get-tuple-element.87, f32[528,1536]{0,1:T(8,128)} %maximum_convert_fusion), kind=kOutput, calls=%fused_computation.10 | convolution fusion | flops 4833411072 | bytes 17301504 | tf_op jit(solution)/shard_map/dot_general | solution.py:44
  444.2 1.1 slice.113
  445.4 2.6 copy.138
  447.9 9.9 %adam_w_out.1 = (f32[384,1536]{1,0:T(8,128)}, f32[384,1536]{1,0:T(8,128)}, f32[384,1536]{1,0:T(8,128)}, f32[384,1536]{1,0:T(8,128)}) custom-call(bf16[16,192,384]{2,1,0:T(8,128)(2,1)} %get-tuple-element.101.refs_0_, f32[384,1536]{1,0:T(8,128)} %refs_1_.3, f32[384,1536]{1,0:T(8,128)} %refs_2_.3, f32[384,1536]{1,0:T(8,128)} %refs_3_.3), custom_call_target="tpu_custom_call" | custom-call | flops 11796480 | bytes 17694720 | tf_op jit(solution)/shard_map/adam_w_out/pallas_call | solution.py:1702
  458.6 79.6 %reduce_gradients.1 = bf16[9,192,384]{2,1,0:T(8,128)(2,1)} custom-call(bf16[1536,512]{1,0:T(8,128)(2,1)} %get-tuple-element.255.left_ref, bf16[512,3456]{1,0:T(8,128)(2,1)} %maximum_dynamic-update-slice_fusion.right_ref), custom_call_target="tpu_custom_call" | custom-call | flops 49999998976 | bytes 20000000 | tf_op jit(solution)/shard_map/reduce_gradients/pallas_call | solution.py:1676
  538.2 8.7 %fusion.12 = f32[512,1536]{0,1:T(8,128)S(1)} fusion(bf16[512,3456]{1,0:T(8,128)(2,1)S(1)} %copy-done.32, bf16[1536,3456]{1,0:T(8,128)(2,1)} %get-tuple-element.100), kind=kOutput, calls=%fused_computation.47 | convolution fusion | flops 5435817984 | bytes 17301504 | tf_op jit(solution)/shard_map/dot_general | solution.py:44
  547.0 9.4 %multiply_reduce_fusion.1 = (f32[1536]{0:T(1024)S(1)}, f32[512]{0:T(512)S(1)}, f32[512,1536]{0,1:T(8,128)}) fusion(f32[528,1536]{0,1:T(8,128)S(1)} %copy-done, f32[512]{0:T(512)S(1)} %copy-done.22, f32[1536]{0:T(1024)S(1)} %copy-done.17, f32[512,1536]{0,1:T(8,128)S(1)} %fusion.12, bf16[512,3072]{1,0:T(8,128)(2,1)S(1)} %copy-done.33, ...), kind=kOutput, calls=%fused_computation.5 | convolution fusion | flops 4837341184 | bytes 22036480 | tf_op jit(solution)/shard_map/dot_general | solution.py:44
  556.5 1.3 collective-permute-done.29
  558.6 4.8 add_bitcast_fusion
  563.4 1.4 collective-permute-start.31
  564.9 3.1 collective-permute-done.31
  568.1 4.5 collective-permute-done.32
  573.2 1.7 pad_maximum_fusion.1.refs_0_
  574.9 2.4 copy.139
  580.2 21.4 %adam_w_in.1 = (f32[192,6400]{1,0:T(8,128)}, f32[192,6400]{1,0:T(8,128)}, f32[192,6400]{1,0:T(8,128)}, f32[192,6400]{1,0:T(8,128)}) custom-call(bf16[17,192,384]{2,1,0:T(8,128)(2,1)} %pad_maximum_fusion.1.refs_0_, f32[192,6400]{1,0:T(8,128)} %refs_1_.2, f32[192,6400]{1,0:T(8,128)} %refs_2_.2, f32[192,6400]{1,0:T(8,128)} %refs_3_.2), custom_call_target="tpu_custom_call" | custom-call | flops 24576000 | bytes 36864000 | tf_op jit(solution)/shard_map/adam_w_in/pallas_call | solution.py:1702
  (193 shorter events, 35.1 us)
Async XLA Ops:
  22.3 31.6 %collective-permute-start.2 = (bf16[192,3456]{1,0:T(8,128)(2,1)}, bf16[192,3456]{1,0:T(8,128)(2,1)S(1)}, u32[]{:S(2)}, u32[]{:S(2)}) collective-permute-start(bf16[192,3456]{1,0:T(8,128)(2,1)} %concatenate.25.refs_0_), channel_id=1, source_target_pairs={{0,4},{1,5},{2,6},{3,7},{4,0},{5,1},{6,2},{7,3},{8,12},{9,13},{10,... | collective-permute-start | bytes 3981320 | tf_op jit(solution)/shard_map/ppermute | solution.py:734
  23.7 31.7 %collective-permute-start.1 = (bf16[192,3456]{1,0:T(8,128)(2,1)}, bf16[192,3456]{1,0:T(8,128)(2,1)S(1)}, u32[]{:S(2)}, u32[]{:S(2)}) collective-permute-start(bf16[192,3456]{1,0:T(8,128)(2,1)} %concatenate.25.refs_0_), channel_id=1, source_target_pairs={{0,2},{1,3},{2,0},{3,1},{4,6},{5,7},{6,4},{7,5},{8,10},{9,11},{10,... | collective-permute-start | bytes 3981320 | tf_op jit(solution)/shard_map/ppermute | solution.py:734
  53.9 16.5 %collective-permute-start.3 = (bf16[96,3456]{1,0:T(8,128)(2,1)S(1)}, bf16[96,3456]{1,0:T(8,128)(2,1)}, u32[]{:S(2)}, u32[]{:S(2)}) collective-permute-start(bf16[96,3456]{1,0:T(8,128)(2,1)S(1)} %slice.128), channel_id=1, source_target_pairs={{0,2},{1,3},{2,0},{3,1},{4,6},{5,7},{6,4},{7,5},{8,10},{9,11},{10,... | collective-permute-start | bytes 1990664 | tf_op jit(solution)/shard_map/ppermute | solution.py:734
  56.5 16.2 %collective-permute-start.4 = (bf16[96,3456]{1,0:T(8,128)(2,1)S(1)}, bf16[96,3456]{1,0:T(8,128)(2,1)}, u32[]{:S(2)}, u32[]{:S(2)}) collective-permute-start(bf16[96,3456]{1,0:T(8,128)(2,1)S(1)} %slice.129), channel_id=1, source_target_pairs={{0,4},{1,5},{2,6},{3,7},{4,0},{5,1},{6,2},{7,3},{8,12},{9,13},{10,... | collective-permute-start | bytes 1990664 | tf_op jit(solution)/shard_map/ppermute | solution.py:734
  57.2 46.3 %copy-start.8 = (bf16[192,3072]{1,0:T(8,128)(2,1)}, bf16[192,3072]{1,0:T(8,128)(2,1)S(1)}, u32[]{:S(2)}) copy-start(bf16[192,3072]{1,0:T(8,128)(2,1)S(1)} %slice.133.refs_0_) | copy-start | bytes 3538948
  72.7 26.3 %collective-permute-start.11 = (bf16[192,3072]{1,0:T(8,128)(2,1)S(1)}, bf16[192,3072]{1,0:T(8,128)(2,1)}, u32[]{:S(2)}, u32[]{:S(2)}) collective-permute-start(bf16[192,3072]{1,0:T(8,128)(2,1)S(1)} %slice.133.refs_0_), channel_id=1, source_target_pairs={{0,4},{1,5},{2,6},{3,7},{4,0},{5,1},{6,2},{7,3},{8,12},{9,13},{10,... | collective-permute-start | bytes 3538952 | tf_op jit(solution)/shard_map/ppermute | solution.py:734
  73.3 28.3 %collective-permute-start.10 = (bf16[192,3072]{1,0:T(8,128)(2,1)S(1)}, bf16[192,3072]{1,0:T(8,128)(2,1)}, u32[]{:S(2)}, u32[]{:S(2)}) collective-permute-start(bf16[192,3072]{1,0:T(8,128)(2,1)S(1)} %slice.133.refs_0_), channel_id=1, source_target_pairs={{0,2},{1,3},{2,0},{3,1},{4,6},{5,7},{6,4},{7,5},{8,10},{9,11},{10,... | collective-permute-start | bytes 3538952 | tf_op jit(solution)/shard_map/ppermute | solution.py:734
  74.7 44.7 %collective-permute-start.5 = (bf16[192,3456]{1,0:T(8,128)(2,1)}, bf16[192,3456]{1,0:T(8,128)(2,1)}, u32[]{:S(2)}, u32[]{:S(2)}) collective-permute-start(bf16[192,3456]{1,0:T(8,128)(2,1)} %concatenate.25.refs_0_), channel_id=1, source_target_pairs={{0,1},{1,0},{2,3},{3,2},{4,5},{5,4},{6,7},{7,6},{8,9},{9,8},{10,11... | collective-permute-start | bytes 3981320 | tf_op jit(solution)/shard_map/ppermute | solution.py:734
  100.9 13.0 %collective-permute-start.12 = (bf16[96,3072]{1,0:T(8,128)(2,1)}, bf16[96,3072]{1,0:T(8,128)(2,1)}, u32[]{:S(2)}, u32[]{:S(2)}) collective-permute-start(bf16[96,3072]{1,0:T(8,128)(2,1)} %slice.134), channel_id=1, source_target_pairs={{0,2},{1,3},{2,0},{3,1},{4,6},{5,7},{6,4},{7,5},{8,10},{9,11},{10,... | collective-permute-start | bytes 1769480 | tf_op jit(solution)/shard_map/ppermute | solution.py:734
  103.5 12.7 %collective-permute-start.13 = (bf16[96,3072]{1,0:T(8,128)(2,1)}, bf16[96,3072]{1,0:T(8,128)(2,1)}, u32[]{:S(2)}, u32[]{:S(2)}) collective-permute-start(bf16[96,3072]{1,0:T(8,128)(2,1)} %slice.135), channel_id=1, source_target_pairs={{0,4},{1,5},{2,6},{3,7},{4,0},{5,1},{6,2},{7,3},{8,12},{9,13},{10,... | collective-permute-start | bytes 1769480 | tf_op jit(solution)/shard_map/ppermute | solution.py:734
  106.6 31.6 %copy-start.6 = (bf16[1,512,1536]{2,1,0:T(8,128)(2,1)S(1)}, bf16[1,512,1536]{2,1,0:T(8,128)(2,1)}, u32[]{:S(2)}) copy-start(bf16[1,512,1536]{2,1,0:T(8,128)(2,1)} %param.24) | copy-start | bytes 4718596
  106.6 40.6 %collective-permute-start.6 = (bf16[192,3456]{1,0:T(8,128)(2,1)}, bf16[192,3456]{1,0:T(8,128)(2,1)}, u32[]{:S(2)}, u32[]{:S(2)}) collective-permute-start(bf16[192,3456]{1,0:T(8,128)(2,1)} %copy-done.13), channel_id=1, source_target_pairs={{0,1},{1,0},{2,3},{3,2},{4,5},{5,4},{6,7},{7,6},{8,9},{9,8},{10,11... | collective-permute-start | bytes 3981320 | tf_op jit(solution)/shard_map/ppermute | solution.py:734
  106.9 12.5 %collective-permute-start = (bf16[16,1536]{0,1:T(8,128)(2,1)S(1)}, bf16[16,1536]{0,1:T(8,128)(2,1)S(1)}, u32[]{:S(2)}, u32[]{:S(2)}) collective-permute-start(bf16[16,1536]{0,1:T(8,128)(2,1)S(1)} %slice_bitcast_fusion), channel_id=1, source_target_pairs={{0,8},{8,16},{16,24},{1,9},{9,17},{17,25},{2,10},{10,18},{18,26},{... | collective-permute-start | bytes 147464 | tf_op jit(solution)/shard_map/ppermute | solution.py:1783
  116.3 31.1 %collective-permute-start.20 = (bf16[384,1536]{1,0:T(8,128)(2,1)}, bf16[384,1536]{1,0:T(8,128)(2,1)}, u32[]{:S(2)}, u32[]{:S(2)}) collective-permute-start(bf16[384,1536]{1,0:T(8,128)(2,1)} %convert_element_type.41.refs_0_), channel_id=1, source_target_pairs={{0,4},{1,5},{2,6},{3,7},{4,0},{5,1},{6,2},{7,3},{8,12},{9,13},{10,... | collective-permute-start | bytes 3538952 | tf_op jit(solution)/shard_map/ppermute | solution.py:734
  117.9 29.9 %collective-permute-start.19 = (bf16[384,1536]{1,0:T(8,128)(2,1)}, bf16[384,1536]{1,0:T(8,128)(2,1)}, u32[]{:S(2)}, u32[]{:S(2)}) collective-permute-start(bf16[384,1536]{1,0:T(8,128)(2,1)} %convert_element_type.41.refs_0_), channel_id=1, source_target_pairs={{0,2},{1,3},{2,0},{3,1},{4,6},{5,7},{6,4},{7,5},{8,10},{9,11},{10,... | collective-permute-start | bytes 3538952 | tf_op jit(solution)/shard_map/ppermute | solution.py:734
  119.4 24.6 %copy-start.4 = (bf16[16,1536]{0,1:T(8,128)(2,1)}, bf16[16,1536]{0,1:T(8,128)(2,1)S(1)}, u32[]{:S(2)}) copy-start(bf16[16,1536]{0,1:T(8,128)(2,1)S(1)} %collective-permute-done) | copy-start | bytes 147460
  119.4 24.6 %collective-permute-start.8 = (bf16[96,3456]{1,0:T(8,128)(2,1)}, bf16[96,3456]{1,0:T(8,128)(2,1)}, u32[]{:S(2)}, u32[]{:S(2)}) collective-permute-start(bf16[96,3456]{1,0:T(8,128)(2,1)} %collective-permute-done.3.refs_3_), channel_id=1, source_target_pairs={{0,1},{1,0},{2,3},{3,2},{4,5},{5,4},{6,7},{7,6},{8,9},{9,8},{10,11... | collective-permute-start | bytes 1990664 | tf_op jit(solution)/shard_map/ppermute | solution.py:734
  119.4 24.8 %collective-permute-start.9 = (bf16[96,3456]{1,0:T(8,128)(2,1)}, bf16[96,3456]{1,0:T(8,128)(2,1)}, u32[]{:S(2)}, u32[]{:S(2)}) collective-permute-start(bf16[96,3456]{1,0:T(8,128)(2,1)} %collective-permute-done.4.refs_4_), channel_id=1, source_target_pairs={{0,1},{1,0},{2,3},{3,2},{4,5},{5,4},{6,7},{7,6},{8,9},{9,8},{10,11... | collective-permute-start | bytes 1990664 | tf_op jit(solution)/shard_map/ppermute | solution.py:734
  126.4 18.2 %copy-start.16 = (f32[1536]{0:T(1024)}, f32[1536]{0:T(1024)S(1)}, u32[]{:S(2)}) copy-start(f32[1536]{0:T(1024)S(1)} %mul.234) | copy-start | bytes 18436
  144.0 16.7 %collective-permute-start.7 = (bf16[192,3456]{1,0:T(8,128)(2,1)}, bf16[192,3456]{1,0:T(8,128)(2,1)}, u32[]{:S(2)}, u32[]{:S(2)}) collective-permute-start(bf16[192,3456]{1,0:T(8,128)(2,1)} %copy-done.12), channel_id=1, source_target_pairs={{0,1},{1,0},{2,3},{3,2},{4,5},{5,4},{6,7},{7,6},{8,9},{9,8},{10,11... | collective-permute-start | bytes 3981320 | tf_op jit(solution)/shard_map/ppermute | solution.py:734
  144.1 17.0 %collective-permute-start.14 = (bf16[192,3072]{1,0:T(8,128)(2,1)}, bf16[192,3072]{1,0:T(8,128)(2,1)}, u32[]{:S(2)}, u32[]{:S(2)}) collective-permute-start(bf16[192,3072]{1,0:T(8,128)(2,1)} %copy-done.8), channel_id=1, source_target_pairs={{0,1},{1,0},{2,3},{3,2},{4,5},{5,4},{6,7},{7,6},{8,9},{9,8},{10,11... | collective-permute-start | bytes 3538952 | tf_op jit(solution)/shard_map/ppermute | solution.py:734
  147.2 57.7 %collective-permute-start.15 = (bf16[192,3072]{1,0:T(8,128)(2,1)}, bf16[192,3072]{1,0:T(8,128)(2,1)}, u32[]{:S(2)}, u32[]{:S(2)}) collective-permute-start(bf16[192,3072]{1,0:T(8,128)(2,1)} %collective-permute-done.10.refs_1_), channel_id=1, source_target_pairs={{0,1},{1,0},{2,3},{3,2},{4,5},{5,4},{6,7},{7,6},{8,9},{9,8},{10,11... | collective-permute-start | bytes 3538952 | tf_op jit(solution)/shard_map/ppermute | solution.py:734
  147.4 58.1 %collective-permute-start.16 = (bf16[192,3072]{1,0:T(8,128)(2,1)}, bf16[192,3072]{1,0:T(8,128)(2,1)}, u32[]{:S(2)}, u32[]{:S(2)}) collective-permute-start(bf16[192,3072]{1,0:T(8,128)(2,1)} %collective-permute-done.11.refs_2_), channel_id=1, source_target_pairs={{0,1},{1,0},{2,3},{3,2},{4,5},{5,4},{6,7},{7,6},{8,9},{9,8},{10,11... | collective-permute-start | bytes 3538952 | tf_op jit(solution)/shard_map/ppermute | solution.py:734
  147.8 14.0 %collective-permute-start.17 = (bf16[96,3072]{1,0:T(8,128)(2,1)}, bf16[96,3072]{1,0:T(8,128)(2,1)}, u32[]{:S(2)}, u32[]{:S(2)}) collective-permute-start(bf16[96,3072]{1,0:T(8,128)(2,1)} %collective-permute-done.12.refs_3_), channel_id=1, source_target_pairs={{0,1},{1,0},{2,3},{3,2},{4,5},{5,4},{6,7},{7,6},{8,9},{9,8},{10,11... | collective-permute-start | bytes 1769480 | tf_op jit(solution)/shard_map/ppermute | solution.py:734
  160.7 44.2 %collective-permute-start.18 = (bf16[96,3072]{1,0:T(8,128)(2,1)}, bf16[96,3072]{1,0:T(8,128)(2,1)S(1)}, u32[]{:S(2)}, u32[]{:S(2)}) collective-permute-start(bf16[96,3072]{1,0:T(8,128)(2,1)} %collective-permute-done.13.refs_4_), channel_id=1, source_target_pairs={{0,1},{1,0},{2,3},{3,2},{4,5},{5,4},{6,7},{7,6},{8,9},{9,8},{10,11... | collective-permute-start | bytes 1769480 | tf_op jit(solution)/shard_map/ppermute | solution.py:734
  161.2 44.4 %collective-permute-start.21 = (bf16[192,1536]{1,0:T(8,128)(2,1)S(1)}, bf16[192,1536]{1,0:T(8,128)(2,1)S(1)}, u32[]{:S(2)}, u32[]{:S(2)}) collective-permute-start(bf16[192,1536]{1,0:T(8,128)(2,1)S(1)} %slice.136), channel_id=1, source_target_pairs={{0,2},{1,3},{2,0},{3,1},{4,6},{5,7},{6,4},{7,5},{8,10},{9,11},{10,... | collective-permute-start | bytes 1769480 | tf_op jit(solution)/shard_map/ppermute | solution.py:734
  161.8 44.1 %collective-permute-start.22 = (bf16[192,1536]{1,0:T(8,128)(2,1)S(1)}, bf16[192,1536]{1,0:T(8,128)(2,1)S(1)}, u32[]{:S(2)}, u32[]{:S(2)}) collective-permute-start(bf16[192,1536]{1,0:T(8,128)(2,1)S(1)} %slice.137), channel_id=1, source_target_pairs={{0,4},{1,5},{2,6},{3,7},{4,0},{5,1},{6,2},{7,3},{8,12},{9,13},{10,... | collective-permute-start | bytes 1769480 | tf_op jit(solution)/shard_map/ppermute | solution.py:734
  204.9 17.2 %copy-start.39 = (bf16[96,3072]{1,0:T(8,128)(2,1)}, bf16[96,3072]{1,0:T(8,128)(2,1)S(1)}, u32[]{:S(2)}) copy-start(bf16[96,3072]{1,0:T(8,128)(2,1)S(1)} %collective-permute-done.18.refs_9_) | copy-start | bytes 1769476
  204.9 31.0 %collective-permute-start.23 = (bf16[384,1536]{1,0:T(8,128)(2,1)}, bf16[384,1536]{1,0:T(8,128)(2,1)S(1)}, u32[]{:S(2)}, u32[]{:S(2)}) collective-permute-start(bf16[384,1536]{1,0:T(8,128)(2,1)} %convert_element_type.41.refs_0_), channel_id=1, source_target_pairs={{0,1},{1,0},{2,3},{3,2},{4,5},{5,4},{6,7},{7,6},{8,9},{9,8},{10,11... | collective-permute-start | bytes 3538952 | tf_op jit(solution)/shard_map/ppermute | solution.py:734
  205.0 31.0 %collective-permute-start.24 = (bf16[384,1536]{1,0:T(8,128)(2,1)}, bf16[384,1536]{1,0:T(8,128)(2,1)S(1)}, u32[]{:S(2)}, u32[]{:S(2)}) collective-permute-start(bf16[384,1536]{1,0:T(8,128)(2,1)} %collective-permute-done.19.refs_1_), channel_id=1, source_target_pairs={{0,1},{1,0},{2,3},{3,2},{4,5},{5,4},{6,7},{7,6},{8,9},{9,8},{10,11... | collective-permute-start | bytes 3538952 | tf_op jit(solution)/shard_map/ppermute | solution.py:734
  205.4 30.5 %collective-permute-start.25 = (bf16[384,1536]{1,0:T(8,128)(2,1)}, bf16[384,1536]{1,0:T(8,128)(2,1)S(1)}, u32[]{:S(2)}, u32[]{:S(2)}) collective-permute-start(bf16[384,1536]{1,0:T(8,128)(2,1)} %collective-permute-done.20.refs_2_), channel_id=1, source_target_pairs={{0,1},{1,0},{2,3},{3,2},{4,5},{5,4},{6,7},{7,6},{8,9},{9,8},{10,11... | collective-permute-start | bytes 3538952 | tf_op jit(solution)/shard_map/ppermute | solution.py:734
  205.5 16.5 %copy-start.37 = (bf16[192,1536]{1,0:T(8,128)(2,1)}, bf16[192,1536]{1,0:T(8,128)(2,1)S(1)}, u32[]{:S(2)}) copy-start(bf16[192,1536]{1,0:T(8,128)(2,1)S(1)} %collective-permute-done.21.refs_3_) | copy-start | bytes 1769476
  205.5 30.3 %collective-permute-start.26 = (bf16[192,1536]{1,0:T(8,128)(2,1)S(1)}, bf16[192,1536]{1,0:T(8,128)(2,1)S(1)}, u32[]{:S(2)}, u32[]{:S(2)}) collective-permute-start(bf16[192,1536]{1,0:T(8,128)(2,1)S(1)} %collective-permute-done.21.refs_3_), channel_id=1, source_target_pairs={{0,1},{1,0},{2,3},{3,2},{4,5},{5,4},{6,7},{7,6},{8,9},{9,8},{10,11... | collective-permute-start | bytes 1769480 | tf_op jit(solution)/shard_map/ppermute | solution.py:734
  206.0 16.1 %copy-start.38 = (bf16[192,1536]{1,0:T(8,128)(2,1)}, bf16[192,1536]{1,0:T(8,128)(2,1)S(1)}, u32[]{:S(2)}) copy-start(bf16[192,1536]{1,0:T(8,128)(2,1)S(1)} %collective-permute-done.22.refs_4_) | copy-start | bytes 1769476
  206.0 29.9 %collective-permute-start.27 = (bf16[192,1536]{1,0:T(8,128)(2,1)S(1)}, bf16[192,1536]{1,0:T(8,128)(2,1)S(1)}, u32[]{:S(2)}, u32[]{:S(2)}) collective-permute-start(bf16[192,1536]{1,0:T(8,128)(2,1)S(1)} %collective-permute-done.22.refs_4_), channel_id=1, source_target_pairs={{0,1},{1,0},{2,3},{3,2},{4,5},{5,4},{6,7},{7,6},{8,9},{9,8},{10,11... | collective-permute-start | bytes 1769480 | tf_op jit(solution)/shard_map/ppermute | solution.py:734
  238.0 14.9 %copy-start.19 = (f32[3072]{0:T(1024)S(1)}, f32[3072]{0:T(1024)}, u32[]{:S(2)}) copy-start(f32[3072]{0:T(1024)} %broadcast_in_dim.19) | copy-start | bytes 36868
  253.6 18.2 %copy-start.1 = (bf16[1536,512]{1,0:T(8,128)(2,1)S(1)}, bf16[1536,512]{1,0:T(8,128)(2,1)}, u32[]{:S(2)}) copy-start(bf16[1536,512]{1,0:T(8,128)(2,1)} %get-tuple-element.255.left_ref) | copy-start | bytes 4718596
  428.0 29.9 %collective-permute-start.28 = (f32[8,3328]{1,0:T(8,128)}, f32[8,3328]{1,0:T(8,128)S(1)}, u32[]{:S(2)}, u32[]{:S(2)}) collective-permute-start(f32[8,3328]{1,0:T(8,128)} %get-tuple-element.99), channel_id=1, source_target_pairs={{8,0},{16,8},{24,16},{9,1},{17,9},{25,17},{10,2},{18,10},{26,18},{... | collective-permute-start | bytes 319496 | tf_op jit(solution)/shard_map/ppermute | solution.py:1807
  431.9 12.3 %copy-start.2 = (bf16[16,192,384]{2,1,0:T(8,128)(2,1)S(1)}, bf16[16,192,384]{2,1,0:T(8,128)(2,1)}, u32[]{:S(2)}) copy-start(bf16[16,192,384]{2,1,0:T(8,128)(2,1)} %get-tuple-element.101.refs_0_) | copy-start | bytes 7077892
  447.9 10.0 %copy-start.15 = (f32[16,3328]{1,0:T(8,128)S(1)}, f32[16,3328]{1,0:T(8,128)}, u32[]{:S(2)}) copy-start(f32[16,3328]{1,0:T(8,128)} %get-tuple-element.98) | copy-start | bytes 638980
  458.6 79.6 %copy-start.32 = (bf16[512,3456]{1,0:T(8,128)(2,1)S(1)}, bf16[512,3456]{1,0:T(8,128)(2,1)}, u32[]{:S(2)}) copy-start(bf16[512,3456]{1,0:T(8,128)(2,1)} %maximum_dynamic-update-slice_fusion.right_ref) | copy-start | bytes 10616836
  538.2 8.8 %copy-start = (f32[528,1536]{0,1:T(8,128)S(1)}, f32[528,1536]{0,1:T(8,128)}, u32[]{:S(2)}) copy-start(f32[528,1536]{0,1:T(8,128)} %maximum_convert_fusion) | copy-start | bytes 9732100
  538.2 8.8 %copy-start.17 = (f32[1536]{0:T(1024)S(1)}, f32[1536]{0:T(1024)}, u32[]{:S(2)}) copy-start(f32[1536]{0:T(1024)} %copy-done.16) | copy-start | bytes 18436
  538.2 8.8 %copy-start.22 = (f32[512]{0:T(512)S(1)}, f32[512]{0:T(512)}, u32[]{:S(2)}) copy-start(f32[512]{0:T(512)} %slice.110) | copy-start | bytes 6148
  538.2 8.8 %copy-start.33 = (bf16[512,3072]{1,0:T(8,128)(2,1)S(1)}, bf16[512,3072]{1,0:T(8,128)(2,1)}, u32[]{:S(2)}) copy-start(bf16[512,3072]{1,0:T(8,128)(2,1)} %get-tuple-element.88.grad_gate_ref) | copy-start | bytes 9437188
  556.5 1.3 collective-permute-start.29
  557.8 5.6 collective-permute-start.30
  558.6 6.2 %copy-start.11 = (f32[192,48]{1,0:T(8,128)S(1)}, f32[192,48]{1,0:T(8,128)}, u32[]{:S(2)}) copy-start(f32[192,48]{1,0:T(8,128)} %copy.135) | copy-start | bytes 110596
  558.6 14.6 %copy-start.3 = (bf16[8,192,384]{2,1,0:T(8,128)(2,1)S(1)}, bf16[8,192,384]{2,1,0:T(8,128)(2,1)}, u32[]{:S(2)}) copy-start(bf16[8,192,384]{2,1,0:T(8,128)(2,1)} %slice.113) | copy-start | bytes 3538948
  563.4 4.6 collective-permute-start.31
  568.0 4.6 collective-permute-start.32
  573.2 28.3 %collective-permute-start.33 = (f32[21392]{0:T(1024)}, f32[21392]{0:T(1024)}, u32[]{:S(2)}, u32[]{:S(2)}) collective-permute-start(f32[21392]{0:T(1024)} %add.142), channel_id=1, source_target_pairs={{0,16},{8,24},{16,0},{24,8},{1,17},{9,25},{17,1},{25,9},{2,18},{10... | collective-permute-start | bytes 256712 | tf_op jit(solution)/shard_map/ppermute | solution.py:734
  580.0 22.6 %copy-start.18 = (f32[5,416]{1,0:T(8,128)S(1)}, f32[5,416]{1,0:T(8,128)}, u32[]{:S(2)}) copy-start(f32[5,416]{1,0:T(8,128)} %param.30) | copy-start | bytes 24964
  580.1 22.6 %copy-start.20 = (f32[5,416]{1,0:T(8,128)S(1)}, f32[5,416]{1,0:T(8,128)}, u32[]{:S(2)}) copy-start(f32[5,416]{1,0:T(8,128)} %param.42) | copy-start | bytes 24964
  580.1 22.6 %copy-start.21 = (f32[5,416]{1,0:T(8,128)S(1)}, f32[5,416]{1,0:T(8,128)}, u32[]{:S(2)}) copy-start(f32[5,416]{1,0:T(8,128)} %param.43) | copy-start | bytes 24964
  580.1 23.3 %copy-start.23 = (f32[384]{0:T(512)S(1)}, f32[384]{0:T(512)}, u32[]{:S(2)}) copy-start(f32[384]{0:T(512)} %param.29) | copy-start | bytes 4612
  580.1 23.3 %copy-start.25 = (f32[384]{0:T(512)S(1)}, f32[384]{0:T(512)}, u32[]{:S(2)}) copy-start(f32[384]{0:T(512)} %param.40) | copy-start | bytes 4612
  580.1 23.3 %copy-start.26 = (f32[384]{0:T(512)S(1)}, f32[384]{0:T(512)}, u32[]{:S(2)}) copy-start(f32[384]{0:T(512)} %param.41) | copy-start | bytes 4612
  580.1 24.0 %copy-start.24 = (f32[3,6]{1,0:T(4,128)S(1)}, f32[3,6]{1,0:T(4,128)}, u32[]{:S(2)}) copy-start(f32[3,6]{1,0:T(4,128)} %param.31) | copy-start | bytes 220
  580.1 23.9 %copy-start.27 = (f32[3,6]{1,0:T(4,128)S(1)}, f32[3,6]{1,0:T(4,128)}, u32[]{:S(2)}) copy-start(f32[3,6]{1,0:T(4,128)} %param.44) | copy-start | bytes 220
  580.1 23.9 %copy-start.28 = (f32[3,6]{1,0:T(4,128)S(1)}, f32[3,6]{1,0:T(4,128)}, u32[]{:S(2)}) copy-start(f32[3,6]{1,0:T(4,128)} %param.45) | copy-start | bytes 220
  580.1 24.6 %copy-start.29 = (f32[192]{0:T(256)S(1)}, f32[192]{0:T(256)}, u32[]{:S(2)}) copy-start(f32[192]{0:T(256)} %param.28) | copy-start | bytes 2308
  580.1 24.6 %copy-start.30 = (f32[192]{0:T(256)S(1)}, f32[192]{0:T(256)}, u32[]{:S(2)}) copy-start(f32[192]{0:T(256)} %param.38) | copy-start | bytes 2308
  580.1 24.6 %copy-start.31 = (f32[192]{0:T(256)S(1)}, f32[192]{0:T(256)}, u32[]{:S(2)}) copy-start(f32[192]{0:T(256)} %param.39) | copy-start | bytes 2308
  (12 other events, 35.7 us)

commit v4 on v2

--- a/solution.py
+++ b/solution.py
@@ -20,6 +20,8 @@
 WIDE = 256
 HALO = 16
 GROUPS = INNER // WIDE
+CHAIN_LAG = 2
+AHEAD = 6
 PACK = CONV_CH + LANES
 LOG2E = 1.4426950408889634
 VMEM_LIMIT = 56 * 1024 * 1024
@@ -98,18 +100,43 @@
     return rows >= cols if lower else rows <= cols
 
 
+def greet_along():
+    z = lax.axis_index("seq")
+    seq_count = lax.axis_size("seq")
+    barrier = pltpu.get_barrier_semaphore()
+
+    @pl.when(z > 0)
+    def _():
+        pl.semaphore_signal(barrier, inc=1, device_id={"seq": z - 1}, device_id_type=pl.DeviceIdType.MESH)
+
+    @pl.when(z < seq_count - 1)
+    def _():
+        pl.semaphore_signal(barrier, inc=1, device_id={"seq": z + 1}, device_id_type=pl.DeviceIdType.MESH)
+
+    pl.semaphore_wait(barrier, jnp.where(z > 0, 1, 0) + jnp.where(z < seq_count - 1, 1, 0))
+
+
 def states_kernel(
     sig_ref, maps_ref, raw_ref, conv_ref, conv_maps_ref, head_ref,
     x_ref, bc_ref, run_ref, lag_ref, run_t_ref, lag_t_ref, enter_ref, enter_all_ref, tail_ref, offs_ref,
-    states_ref, send_ref,
-    sig, in_t,
+    states_ref, before_ref,
+    sig, in_t, ends, stage, land, sems,
 ):
     step = pl.program_id(0)
     rows = x_ref.shape[0]
     blocks = rows // BLOCK
+    z = lax.axis_index("seq")
+    seq_count = lax.axis_size("seq")
+
+    def to_next(k):
+        return pltpu.make_async_remote_copy(
+            src_ref=stage.at[k], dst_ref=land.at[k], send_sem=sems.at[0, k], recv_sem=sems.at[1, k],
+            device_id={"seq": z + 1}, device_id_type=pl.DeviceIdType.MESH,
+        )
 
     @pl.when(step == 0)
     def _():
+        greet_along()
         sig[...] = maps_ref[...].astype(full_type)
         pre = convolve(sig, conv_maps_ref[...], rows)
         maps = pre * sigmoid(pre)
@@ -136,25 +163,47 @@
             offset = offset + run[BLOCK - 1 : BLOCK]
         offs_ref[blocks : blocks + 1, :] = offset
 
-    sig[...] = sig_ref[...].astype(full_type)
-    pre = convolve(sig, conv_ref[...], rows)
-    x = pre * sigmoid(pre)
-    x_ref[...] = x
-    tail = to_front(tail_ref[...], step)
-    last = to_front(offs_ref[...], step)
-    state = jnp.zeros((STATE, WIDE), full_type)
-    for c in range(blocks):
-        at = slice(c * BLOCK, (c + 1) * BLOCK)
-        weighted = (x[at] * widen(tail[at])).astype(low_type)
-        fade = jnp.exp2(widen(last[c + 1 : c + 2] - last[c : c + 1]))
-        state = state * fade + dot(in_t[:, at], weighted)
-        states_ref[c] = state.astype(low_type)
-    send_ref[:STATE, :] = state.astype(low_type)
-    total = widen(last[blocks : blocks + 1])
-    high = total.astype(low_type).astype(full_type)
-    ids = lax.broadcasted_iota(jnp.int32, (16, WIDE), 0)
-    extra = jnp.where(ids == 0, high, jnp.where(ids == 1, total - high, 0.0))
-    send_ref[STATE:, :] = extra.astype(low_type)
+    @pl.when(step < GROUPS)
+    def _():
+        sig[...] = sig_ref[...].astype(full_type)
+        pre = convolve(sig, conv_ref[...], rows)
+        x = pre * sigmoid(pre)
+        x_ref[...] = x
+        tail = to_front(tail_ref[...], step)
+        last = to_front(offs_ref[...], step)
+        state = jnp.zeros((STATE, WIDE), full_type)
+        for c in range(blocks):
+            at = slice(c * BLOCK, (c + 1) * BLOCK)
+            weighted = (x[at] * widen(tail[at])).astype(low_type)
+            fade = jnp.exp2(widen(last[c + 1 : c + 2] - last[c : c + 1]))
+            state = state * fade + dot(in_t[:, at], weighted)
+            states_ref[c] = state.astype(low_type)
+        ends[step] = state
+
+    @pl.when(step >= CHAIN_LAG)
+    def _():
+        k = step - CHAIN_LAG
+
+        @pl.when(z == 0)
+        def _():
+            land[k] = jnp.zeros((STATE, WIDE), low_type)
+
+        @pl.when(z > 0)
+        def _():
+            to_next(k).wait_recv()
+
+        before_ref[...] = land[k]
+
+        @pl.when(z < seq_count - 1)
+        def _():
+            fade = jnp.exp2(widen(to_front(offs_ref[...], k)[blocks : blocks + 1]))
+            stage[k] = (ends[k] + fade * land[k].astype(full_type)).astype(low_type)
+            to_next(k).start()
+
+    @pl.when((step == GROUPS + CHAIN_LAG - 1) & (z < seq_count - 1))
+    def _():
+        for k in range(GROUPS):
+            to_next(k).wait_send()
 
 
 def outputs_kernel(x_ref, bc_ref, run_ref, lag_t_ref, enter_ref, states_ref, head_ref, y_ref, inter):
@@ -199,7 +248,7 @@
 
 def norm_kernel(
     y_ref, gate_ref, back_ref, gain_ref, bc_ref, enter_ref, state_ref,
-    normed_ref, grad_y_ref, grad_gate_ref, grad_gain_ref, grad_state_ref,
+    normed_ref, normed_t_ref, grad_y_ref, grad_gate_ref, grad_gain_ref, grad_state_ref,
     gated, low_y,
 ):
     step = pl.program_id(0)
@@ -234,7 +283,9 @@
         back = back_ref[:, at]
         vals = gated[:, at]
         scaled = vals * inv
-        normed_ref[:, at] = (scaled * gain).astype(low_type)
+        normed = (scaled * gain).astype(low_type)
+        normed_ref[:, at] = normed
+        normed_t_ref[at, :] = normed.T
         grad_gain_ref[0:1, at] += jnp.sum(back * scaled, axis=0, keepdims=True)
         grad_vals = back * gain * inv - vals * pull
         gate = gate_ref[:, at]
@@ -249,15 +300,129 @@
 
 
 def backward_kernel(
+    counts, spans,
     sig_ref, raw_ref, conv_ref, head_ref, grad_y_ref, bc_ref,
-    lag_ref, run_t_ref, enter_ref, tail_ref, offs_ref, states_ref, state_in_ref, grad_in_ref,
-    grad_sig_ref, edge_ref, last_ref, grad_conv_ref, grad_skip_ref, grad_head_ref,
+    lag_ref, run_t_ref, enter_ref, tail_ref, offs_ref, states_ref, state_in_ref, grad_state_ref,
+    lefts_ref, cot_ref, grad_gate_ref, full_gate_ref, full_sig_ref,
+    grad_normed_ref, grad_conv_ref, grad_skip_ref, grad_head_ref, sums_ref,
     sig, padded, inter, grad_inter, grad_maps, out_t, run_rows, run_cols, run_ends, weighs,
+    stage, land, chain_sems, grad_pack, lasts, edges, edge_land, edge_sems, grad_normed, weights, weight_sems, done_sems,
+    *scratch,
 ):
-    step = pl.program_id(0)
+    place = pl.program_id(0)
+    step = place - AHEAD
+    steps = GROUPS + 2 + AHEAD
     rows = grad_y_ref.shape[0]
     blocks = rows // BLOCK
+    z = lax.axis_index("seq")
+    seq_count = counts[1]
+    mesh_id = pl.DeviceIdType.MESH
+    first_gate, first_sig = spans[1][0], spans[2][0]
+    chunks = first_sig + spans[2][1]
+
+    def weight_copies(k):
+        slot = lax.rem(k, 2)
+        for ref, first, last in ((full_gate_ref, first_gate, first_sig), (full_sig_ref, first_sig, chunks)):
+            col = pl.multiple_of(jnp.clip(k - first, 0, last - first - 1) * TILE, LANES)
+            copy = pltpu.make_async_copy(ref.at[:, pl.ds(col, TILE)], weights.at[slot], weight_sems.at[slot])
+            yield (k >= first) & (k < last), copy
+
+    def beside(k, tile):
+        for right, copy in weight_copies(k):
+            pl.when(right)(copy.wait)
+        for right, copy in weight_copies(k + 1):
+            pl.when(right)(copy.start)
+
+        @pl.when(k == first_gate)
+        def _():
+            grad_normed[...] = dot_nt(tile[...], weights[lax.rem(k, 2)])
+
+        @pl.when(k > first_gate)
+        def _():
+            grad_normed[...] += dot_nt(tile[...], weights[lax.rem(k, 2)])
+
+    turns, turn, finish = reduce_turns(
+        *counts, spans, lefts_ref, [cot_ref, grad_gate_ref, grad_pack], sums_ref, scratch, beside
+    )
+
+    def to_previous(k):
+        return pltpu.make_async_remote_copy(
+            src_ref=stage.at[k], dst_ref=land.at[k], send_sem=chain_sems.at[0, k], recv_sem=chain_sems.at[1, k],
+            device_id={"seq": z - 1}, device_id_type=mesh_id,
+        )
+
+    def edge_copy(k):
+        return pltpu.make_async_remote_copy(
+            src_ref=edges.at[k], dst_ref=edge_land.at[k], send_sem=edge_sems.at[0, k], recv_sem=edge_sems.at[1, k],
+            device_id={"seq": z - 1}, device_id_type=mesh_id,
+        )
+
+    def chain(k):
+        @pl.when(z == seq_count - 1)
+        def _():
+            land[k] = jnp.zeros((STATE, WIDE), low_type)
+
+        @pl.when(z < seq_count - 1)
+        def _():
+            to_previous(k).wait_recv()
+
+        @pl.when(z > 0)
+        def _():
+            fade = jnp.exp2(widen(to_front(offs_ref[...], k)[blocks : blocks + 1]))
+            own = grad_state_ref[:, pl.ds(pl.multiple_of(k * WIDE, WIDE), WIDE)]
+            stage[k] = (own + fade * land[k].astype(full_type)).astype(low_type)
+            to_previous(k).start()
+
+    def mend(k):
+        @pl.when(z == seq_count - 1)
+        def _():
+            edge_land[k] = jnp.zeros((8, WIDE), full_type)
+
+        @pl.when(z < seq_count - 1)
+        def _():
+            edge_copy(k).wait_recv()
+
+        whole = lasts[k] + jnp.concatenate([jnp.zeros((8, WIDE), full_type), edge_land[k]], axis=0)
+        grad_pack[rows - 16 :, pl.ds(pl.multiple_of(k * WIDE, WIDE), WIDE)] = whole.astype(low_type)
+
+    @pl.when(place == 0)
+    def _():
+        greet()
+
+    @pl.when((step >= 1) & (step <= GROUPS + 1))
+    def _():
+        mend(step - 1)
+
+    early = chunks - 1
+    for i in range(spans[2][1] - 1):
+        at = next(p for p in range(steps) if (p + 1) * early // steps > first_sig + i)
+        assert AHEAD + ((i + 1) * TILE - 1) // WIDE + 1 <= at
+
+    @pl.when(place < steps)
+    def _():
+        lax.fori_loop(place * early // steps, (place + 1) * early // steps, turn, 0)
+
     upper = triangle(False)
+
+    @pl.when(place < AHEAD)
+    def _():
+        for i in range(GROUPS // AHEAD):
+            chain(place * (GROUPS // AHEAD) + i)
+
+    @pl.when(place == steps)
+    def _():
+        lax.fori_loop(early, turns, turn, 0)
+        normed_copy = pltpu.make_async_copy(grad_normed, grad_normed_ref, done_sems.at[0])
+        normed_copy.start()
+        finish()
+        normed_copy.wait()
+
+        @pl.when(z > 0)
+        def _():
+            for k in range(GROUPS):
+                to_previous(k).wait_send()
+            for k in range(GROUPS + 1):
+                edge_copy(k).wait_send()
 
     @pl.when(step == 0)
     def _():
@@ -281,9 +446,14 @@
         for k in range(3):
             grad_sig = grad_sig + conv[k : k + 1] * padded[HALO + 3 - k : HALO + 3 - k + rows, :]
             edge = edge + conv[k : k + 1] * padded[11 - k : 19 - k, :]
-        grad_sig_ref[...] = grad_sig.astype(low_type)
-        edge_ref[...] = edge
-        last_ref[...] = grad_sig[rows - 16 :]
+        grad_pack[:, pl.ds(pl.multiple_of(step * WIDE, WIDE), WIDE)] = grad_sig.astype(low_type)
+        lasts[step] = grad_sig[rows - 16 :]
+
+        @pl.when(z > 0)
+        def _():
+            edges[step] = edge
+            edge_copy(step).start()
+
         sums = [
             jnp.sum(grad_pre * sig[HALO - 3 + k : HALO - 3 + k + rows, :], axis=0, keepdims=True)
             for k in range(CONV_WIDTH)
@@ -292,7 +462,7 @@
         sums.append(jnp.zeros((3, WIDE), full_type))
         grad_conv_ref[...] = jnp.concatenate(sums, axis=0)
 
-    @pl.when(step < GROUPS)
+    @pl.when((step >= 0) & (step < GROUPS))
     def _():
         sig[...] = sig_ref[...].astype(full_type)
         lag = to_front(lag_ref[...], step)
@@ -305,7 +475,7 @@
         heads_of = lax.broadcasted_iota(jnp.int32, (WIDE, LANES), 0) // HEAD_DIM + 4 * step
         picks = jnp.where(heads_of == lane_ids((WIDE, LANES)), 1.0, 0.0).astype(low_type)
         state_in = state_in_ref[...].astype(full_type)
-        grad_state = grad_in_ref[...].astype(full_type)
+        grad_state = land[step].astype(full_type)
         grad_skip = jnp.zeros((1, WIDE), full_type)
         pre_all = convolve(sig, conv_ref[...], rows)
 
@@ -414,8 +584,7 @@
             grad_rates = dot(later, grad_run, precision=highest) + run_ends[c : c + 1, :]
             grad_raw = slope[at] * rate * grad_rates + ratio[at] * weighs[at, :]
             grad_raw = jnp.where(used, grad_raw, 0.0)
-            grad_sig_ref[at, :LANES] = grad_raw.astype(low_type)
-            grad_sig_ref[at, LANES:] = jnp.zeros((BLOCK, LANES), low_type)
+            grad_pack[at, CONV_CH:] = grad_raw.astype(low_type)
             rate_sum = rate_sum + jnp.sum(grad_rates * step_sizes[at], axis=0, keepdims=True)
             bias_sum = bias_sum + jnp.sum(grad_raw, axis=0, keepdims=True)
         grad_head_ref[...] = jnp.concatenate(
@@ -426,22 +595,23 @@
 def run_states(packed, conv, head):
     rows = packed.shape[0] - HALO
     blocks = rows // BLOCK
+    last = lambda j: jnp.minimum(j, GROUPS - 1)
     whole = lambda shape: pl.BlockSpec(shape, lambda j: (0,) * len(shape))
     small = jax.ShapeDtypeStruct((rows, LANES), full_type)
     small_t = jax.ShapeDtypeStruct((LANES, rows), full_type)
     return pl.pallas_call(
         states_kernel,
-        grid=(GROUPS,),
+        grid=(GROUPS + CHAIN_LAG,),
         in_specs=[
-            pl.BlockSpec((rows + HALO, WIDE), lambda j: (0, j)),
+            pl.BlockSpec((rows + HALO, WIDE), lambda j: (0, last(j))),
             pl.BlockSpec((rows + HALO, WIDE), lambda j: (0, GROUPS)),
             pl.BlockSpec((rows + HALO, LANES), lambda j: (0, CONV_CH // LANES)),
-            pl.BlockSpec((8, WIDE), lambda j: (0, j)),
+            pl.BlockSpec((8, WIDE), lambda j: (0, last(j))),
             pl.BlockSpec((8, WIDE), lambda j: (0, GROUPS)),
             whole((8, LANES)),
         ],
         out_specs=[
-            pl.BlockSpec((rows, WIDE), lambda j: (0, j)),
+            pl.BlockSpec((rows, WIDE), lambda j: (0, last(j))),
             whole((rows, WIDE)),
             whole((rows, LANES)),
             whole((rows, LANES)),
@@ -451,8 +621,8 @@
             whole((rows, LANES)),
             whole((rows, LANES)),
             whole((16, LANES)),
-            pl.BlockSpec((blocks, STATE, WIDE), lambda j: (0, 0, j)),
-            pl.BlockSpec((STATE + 16, WIDE), lambda j: (0, j)),
+            pl.BlockSpec((blocks, STATE, WIDE), lambda j: (0, 0, last(j))),
+            pl.BlockSpec((STATE, WIDE), lambda j: (0, jnp.maximum(j - CHAIN_LAG, 0))),
         ],
         out_shape=[
             jax.ShapeDtypeStruct((rows, INNER), full_type),
@@ -460,13 +630,17 @@
             small, small, small_t, small_t, small, small, small,
             jax.ShapeDtypeStruct((16, LANES), full_type),
             jax.ShapeDtypeStruct((blocks, STATE, INNER), low_type),
-            jax.ShapeDtypeStruct((STATE + 16, INNER), low_type),
+            jax.ShapeDtypeStruct((STATE, INNER), low_type),
         ],
         scratch_shapes=[
             pltpu.VMEM((rows + HALO, WIDE), full_type),
             pltpu.VMEM((STATE, rows), low_type),
-        ],
-        compiler_params=pltpu.CompilerParams(vmem_limit_bytes=VMEM_LIMIT),
+            pltpu.VMEM((GROUPS, STATE, WIDE), full_type),
+            pltpu.VMEM((GROUPS, STATE, WIDE), low_type),
+            pltpu.VMEM((GROUPS, STATE, WIDE), low_type),
+            pltpu.SemaphoreType.DMA((2, GROUPS)),
+        ],
+        compiler_params=pltpu.CompilerParams(collective_id=1, has_side_effects=True, vmem_limit_bytes=VMEM_LIMIT),
         cost_estimate=pl.CostEstimate(flops=10**9, bytes_accessed=15 * 10**6, transcendentals=10**6),
         name="scan_states",
     )(packed, packed, packed, conv, conv, head)
@@ -509,9 +683,13 @@
             by_rows(INNER), by_rows(INNER), by_rows(INNER), whole((8, INNER)),
             by_rows(WIDE), by_rows(LANES), whole((STATE, INNER)),
         ],
-        out_specs=[by_rows(INNER), by_rows(INNER), by_rows(INNER), whole((8, INNER)), whole((STATE, INNER))],
+        out_specs=[
+            by_rows(INNER), pl.BlockSpec((INNER, part), lambda i: (0, i)), by_rows(INNER), by_rows(INNER),
+            whole((8, INNER)), whole((STATE, INNER)),
+        ],
         out_shape=[
             jax.ShapeDtypeStruct((rows, INNER), low_type),
+            jax.ShapeDtypeStruct((INNER, rows), low_type),
             jax.ShapeDtypeStruct((rows, INNER), low_type),
             jax.ShapeDtypeStruct((rows, INNER), low_type),
             jax.ShapeDtypeStruct((8, INNER), full_type),
@@ -524,45 +702,60 @@
     )(y, gate, back, gain, bc, enter, state)
 
 
-def run_backward(packed, conv, head, grad_y, bc, lag, run_t, enter, tail, offs, states, state_in, grad_in):
+def run_backward(
+    packed, conv, head, grad_y, bc, lag, run_t, enter, tail, offs, states, state_in, grad_state, lefts, cot, grad_gate,
+    full_gate, full_sig,
+):
     rows = grad_y.shape[0]
     blocks = rows // BLOCK
-    whole = lambda shape: pl.BlockSpec(shape, lambda j: (0,) * len(shape))
-    most = lambda j, top: jnp.minimum(j, top)
+    wsh_count, seq_count = lax.axis_size("wsh"), lax.axis_size("seq")
+    groups = INNER // D
+    n_out, n_gate, n_sig = cot.shape[1] // TILE, grad_gate.shape[1] // TILE, PACK // TILE
+    first_gate, first_sig = n_out * groups, n_out * groups + n_gate
+    spans = [(0, n_out, groups, 0), (first_gate, n_gate, 1, INNER), (first_sig, n_sig, 1, INNER)]
+    chunks = first_sig + n_sig
+    anywhere = pl.BlockSpec(memory_space=pl.ANY)
+    low_at = lambda j, top: jnp.clip(j - AHEAD, 0, top)
+    once = pl.Buffered(1)
+    whole = lambda shape: pl.BlockSpec(shape, lambda j: (0,) * len(shape), pipeline_mode=once)
+    kept = lambda shape: pl.BlockSpec(shape, lambda j: (0,) * len(shape))
     return pl.pallas_call(
-        backward_kernel,
-        grid=(GROUPS + 2,),
+        functools.partial(backward_kernel, (wsh_count, seq_count), spans),
+        grid=(GROUPS + 3 + AHEAD,),
         in_specs=[
-            pl.BlockSpec((rows + HALO, WIDE), lambda j: (0, most(j, GROUPS))),
-            pl.BlockSpec((rows + HALO, LANES), lambda j: (0, CONV_CH // LANES)),
-            pl.BlockSpec((8, WIDE), lambda j: (0, most(j, GROUPS))),
+            pl.BlockSpec((rows + HALO, WIDE), lambda j: (0, low_at(j, GROUPS))),
+            pl.BlockSpec((rows + HALO, LANES), lambda j: (0, CONV_CH // LANES), pipeline_mode=once),
+            pl.BlockSpec((8, WIDE), lambda j: (0, low_at(j, GROUPS))),
             whole((8, LANES)),
-            pl.BlockSpec((rows, WIDE), lambda j: (0, most(j, GROUPS - 1))),
+            pl.BlockSpec((rows, WIDE), lambda j: (0, low_at(j, GROUPS - 1))),
             whole((rows, WIDE)),
             whole((rows, LANES)),
             whole((LANES, rows)),
             whole((rows, LANES)),
             whole((rows, LANES)),
             whole((16, LANES)),
-            pl.BlockSpec((blocks, STATE, WIDE), lambda j: (0, 0, most(j, GROUPS - 1))),
-            pl.BlockSpec((STATE, WIDE), lambda j: (0, most(j, GROUPS - 1))),
-            pl.BlockSpec((STATE, WIDE), lambda j: (0, most(j, GROUPS - 1))),
+            pl.BlockSpec((blocks, STATE, WIDE), lambda j: (0, 0, low_at(j, GROUPS - 1))),
+            pl.BlockSpec((STATE, WIDE), lambda j: (0, low_at(j, GROUPS - 1))),
+            whole((STATE, INNER)),
+            whole(lefts.shape),
+            whole(cot.shape),
+            whole(grad_gate.shape),
+            anywhere,
+            anywhere,
         ],
         out_specs=[
-            pl.BlockSpec((rows, WIDE), lambda j: (0, j)),
-            pl.BlockSpec((8, WIDE), lambda j: (0, most(j, GROUPS))),
-            pl.BlockSpec((16, WIDE), lambda j: (0, most(j, GROUPS))),
-            pl.BlockSpec((8, WIDE), lambda j: (0, most(j, GROUPS))),
-            pl.BlockSpec((8, WIDE), lambda j: (0, most(j, GROUPS - 1))),
-            whole((8, LANES)),
+            anywhere,
+            pl.BlockSpec((8, WIDE), lambda j: (0, low_at(j, GROUPS))),
+            pl.BlockSpec((8, WIDE), lambda j: (0, low_at(j, GROUPS - 1))),
+            kept((8, LANES)),
+            anywhere,
         ],
         out_shape=[
-            jax.ShapeDtypeStruct((rows, PACK), low_type),
-            jax.ShapeDtypeStruct((8, CONV_CH), full_type),
-            jax.ShapeDtypeStruct((16, CONV_CH), full_type),
+            jax.ShapeDtypeStruct((rows, D), full_type),
             jax.ShapeDtypeStruct((8, CONV_CH), full_type),
             jax.ShapeDtypeStruct((8, INNER), full_type),
             jax.ShapeDtypeStruct((8, LANES), full_type),
+            jax.ShapeDtypeStruct((chunks, D // wsh_count, TILE), low_type),
         ],
         scratch_shapes=[
             pltpu.VMEM((rows + HALO, WIDE), full_type),
@@ -575,11 +768,27 @@
             pltpu.VMEM((rows, LANES), full_type),
             pltpu.VMEM((8, LANES), full_type),
             pltpu.VMEM((rows, LANES), full_type),
-        ],
-        compiler_params=pltpu.CompilerParams(vmem_limit_bytes=VMEM_LIMIT),
-        cost_estimate=pl.CostEstimate(flops=2 * 10**10, bytes_accessed=20 * 10**6, transcendentals=5 * 10**6),
+            pltpu.VMEM((GROUPS, STATE, WIDE), low_type),
+            pltpu.VMEM((GROUPS, STATE, WIDE), low_type),
+            pltpu.SemaphoreType.DMA((2, GROUPS)),
+            pltpu.VMEM((rows, PACK), low_type),
+            pltpu.VMEM((GROUPS + 1, 16, WIDE), full_type),
+            pltpu.VMEM((GROUPS + 1, 8, WIDE), full_type),
+            pltpu.VMEM((GROUPS + 1, 8, WIDE), full_type),
+            pltpu.SemaphoreType.DMA((2, GROUPS + 1)),
+            pltpu.VMEM((rows, D), full_type),
+            pltpu.VMEM((2, D, TILE), low_type),
+            pltpu.SemaphoreType.DMA((2,)),
+            pltpu.SemaphoreType.DMA((1,)),
+            *reduce_scratch(chunks, rows, wsh_count),
+        ],
+        compiler_params=pltpu.CompilerParams(collective_id=2, has_side_effects=True, vmem_limit_bytes=61 * 1024 * 1024),
+        cost_estimate=pl.CostEstimate(flops=10**11, bytes_accessed=20 * 10**6, transcendentals=5 * 10**6),
         name="scan_backward",
-    )(packed, packed, conv, head, grad_y, bc, lag, run_t, enter, tail, offs, states, state_in, grad_in)
+    )(
+        packed, packed, conv, head, grad_y, bc, lag, run_t, enter, tail, offs, states, state_in, grad_state,
+        lefts, cot, grad_gate, full_gate, full_sig,
+    )
 
 
 def adam_update(weights, gradient, first_moment, second_moment, step_rate, decay_amount):
@@ -712,6 +921,9 @@
 
 
 TILE = 384
+FAR_LAG = 2
+UP_LAG = 1
+LAND_SLOTS = 10
 SLACK = 1
 
 
@@ -727,42 +939,46 @@
     return [m for m in left if m & bit == 0], [m for m in left if m & bit]
 
 
-def reduce_kernel(counts, rights_at, lefts_ref, *refs):
-    wsh_count, seq_count, starts = counts
-    n_rights = len(starts)
-    right_refs, out_ref = refs[:n_rights], refs[n_rights]
-    (tile, stage, pair, *rest) = refs[n_rights + 1 :]
+def greet():
+    me, z = lax.axis_index("wsh"), lax.axis_index("seq")
+    seq_count = lax.axis_size("seq")
+    barrier = pltpu.get_barrier_semaphore()
+    mesh_id = pl.DeviceIdType.MESH
+    bits = lax.axis_size("wsh").bit_length() - 1
+    for b in range(bits):
+        pl.semaphore_signal(barrier, inc=1, device_id={"wsh": lax.bitwise_xor(me, 1 << b)}, device_id_type=mesh_id)
+
+    @pl.when(z > 0)
+    def _():
+        pl.semaphore_signal(barrier, inc=1, device_id={"seq": z - 1}, device_id_type=mesh_id)
+
+    @pl.when(z < seq_count - 1)
+    def _():
+        pl.semaphore_signal(barrier, inc=1, device_id={"seq": z + 1}, device_id_type=mesh_id)
+
+    along = jnp.where(z > 0, 1, 0) + jnp.where(z < seq_count - 1, 1, 0)
+    pl.semaphore_wait(barrier, bits + along)
+
+
+def reduce_turns(wsh_count, seq_count, spans, left_ref, right_refs, out_ref, scratch, beside):
     orders = part_orders(wsh_count)
     bits = len(orders)
+    tile, stage, pair, *rest = scratch
     lands, rest = rest[:bits], rest[bits:]
     from_left, from_right, pair_sems, far_sems, seq_sems, out_sems = rest
     chunks, blocks, rows, _ = pair.shape
+    slots = lands[0].shape[0]
     part = rows // bits
     me = lax.axis_index("wsh")
     z = lax.axis_index("seq")
     root = seq_count // 2
-    MESH = pl.DeviceIdType.MESH
-
-    barrier = pltpu.get_barrier_semaphore()
-    for b in range(bits + 1):
-        pl.semaphore_signal(barrier, inc=1, device_id={"wsh": lax.bitwise_xor(me, 1 << b)}, device_id_type=MESH)
-
-    @pl.when(z > 0)
-    def _():
-        pl.semaphore_signal(barrier, inc=1, device_id={"seq": z - 1}, device_id_type=MESH)
-
-    @pl.when(z < seq_count - 1)
-    def _():
-        pl.semaphore_signal(barrier, inc=1, device_id={"seq": z + 1}, device_id_type=MESH)
-
-    along = jnp.where(z > 0, 1, 0) + jnp.where(z < seq_count - 1, 1, 0)
-    pl.semaphore_wait(barrier, bits + 1 + along)
+    mesh_id = pl.DeviceIdType.MESH
 
     def pair_copy(k):
         return pltpu.make_async_remote_copy(
             src_ref=stage.at[lax.rem(k, 2)], dst_ref=pair.at[k],
             send_sem=pair_sems.at[0, k], recv_sem=pair_sems.at[1, k],
-            device_id={"wsh": lax.bitwise_xor(me, 1)}, device_id_type=MESH,
+            device_id={"wsh": lax.bitwise_xor(me, 1)}, device_id_type=mesh_id,
         )
 
     spots = []
@@ -774,9 +990,9 @@
     def far_copies(k, phase):
         return [
             pltpu.make_async_remote_copy(
-                src_ref=pair.at[k, m, pl.ds(p * part, part)], dst_ref=lands[q].at[k, p, i],
+                src_ref=pair.at[k, m, pl.ds(p * part, part)], dst_ref=lands[q].at[lax.rem(k, slots), p, i],
                 send_sem=far_sems.at[0, n, k], recv_sem=far_sems.at[1, n, k],
-                device_id={"wsh": lax.bitwise_xor(me, bit)}, device_id_type=MESH,
+                device_id={"wsh": lax.bitwise_xor(me, bit)}, device_id_type=mesh_id,
             )
             for n, (q, p, i, m, bit) in enumerate(spots)
             if q == phase
@@ -786,44 +1002,51 @@
         return pltpu.make_async_remote_copy(
             src_ref=source, dst_ref=from_left.at[k],
             send_sem=seq_sems.at[0, k], recv_sem=seq_sems.at[1, k],
-            device_id={"seq": z + 1}, device_id_type=MESH,
+            device_id={"seq": z + 1}, device_id_type=mesh_id,
         )
 
     def to_left(k, source):
         return pltpu.make_async_remote_copy(
             src_ref=source, dst_ref=from_right.at[k],
             send_sem=seq_sems.at[2, k], recv_sem=seq_sems.at[3, k],
-            device_id={"seq": z - 1}, device_id_type=MESH,
+            device_id={"seq": z - 1}, device_id_type=mesh_id,
         )
 
     def out_copy(k, source):
         return pltpu.make_async_copy(source, out_ref.at[k], out_sems.at[k])
 
-    def product(k, first):
-        for n, (start, stop, spans) in enumerate(rights_at):
-            @pl.when((k >= start) & (k < stop))
+    def take_tile(k):
+        for (start, tiles, groups, _), right_ref in zip(spans, right_refs):
+
+            @pl.when((k >= start) & (k < start + tiles * groups))
             def _():
-                col = lax.rem(k - start, spans) * TILE
-                tile[...] = right_refs[n][:, pl.ds(pl.multiple_of(col, LANES), TILE)]
-        left_at = jnp.where(k < rights_at[0][1], 1 + k // rights_at[0][2], 0)
-        half = blocks * rows
-        return dot(lefts_ref[left_at, pl.ds(first * half, half), :], tile[...])
+                col = lax.rem(k - start, tiles) * TILE
+                tile[...] = right_ref[:, pl.ds(pl.multiple_of(col, LANES), TILE)]
+
+    def product(k, b, core):
+        owner = lax.bitwise_xor(me, 2 * b + core)
+        first = jnp.zeros((), jnp.int32)
+        for start, tiles, groups, base in spans:
+            at = base + (owner * groups + (k - start) // tiles) * rows
+            first = jnp.where((k >= start) & (k < start + tiles * groups), at, first)
+        return dot(left_ref[pl.ds(pl.multiple_of(first, 16), rows), :], tile[...])
 
     def begin(k):
         @pl.when(k >= 2)
         def _():
             pair_copy(k - 2).wait_send()
-        vals = product(k, 1)
+
+        take_tile(k)
         for b in range(blocks):
-            stage[lax.rem(k, 2), b] = vals[b * rows : (b + 1) * rows].astype(low_type)
+            stage[lax.rem(k, 2), b] = product(k, b, 1).astype(low_type)
         pair_copy(k).start()
+        beside(k, tile)
 
     def add_pair(k):
-        vals = product(k, 0)
+        take_tile(k)
         pair_copy(k).wait_recv()
         for b in range(blocks):
-            total = vals[b * rows : (b + 1) * rows] + pair[k, b].astype(full_type)
-            pair[k, b] = total.astype(low_type)
+            pair[k, b] = (product(k, b, 0) + pair[k, b].astype(full_type)).astype(low_type)
         for copy in far_copies(k, 0):
             copy.start()
 
@@ -833,7 +1056,7 @@
         for p, order in enumerate(orders):
             at = pl.ds(p * part, part)
             for i, m in enumerate(held(order, phase, bits)[0]):
-                total = pair[k, m, at].astype(full_type) + lands[phase][k, p, i].astype(full_type)
+                total = pair[k, m, at].astype(full_type) + lands[phase][lax.rem(k, slots), p, i].astype(full_type)
                 pair[k, m, at] = total.astype(low_type)
         if phase < bits - 1:
             for copy in far_copies(k, phase + 1):
@@ -882,71 +1105,52 @@
 
     far = jnp.abs(z - root)
     farthest = max(root, seq_count - 1 - root)
-    stages = [(0, begin), (1, add_pair)] + [(2 + q, functools.partial(add_far, phase=q)) for q in range(bits)]
-    stages += [
-        (2 + bits + SLACK * (farthest - far), seq_up),
-        (3 + bits + SLACK * (farthest + far), seq_down),
+    stages = [(0, begin), (1, add_pair)] + [
+        (1 + FAR_LAG * (q + 1), functools.partial(add_far, phase=q)) for q in range(bits)
     ]
-    depth = 4 + bits + SLACK * 2 * farthest
+    up_at = 1 + FAR_LAG * bits + UP_LAG
+    stages += [(up_at + SLACK * (farthest - far), seq_up), (up_at + 1 + SLACK * (farthest + far), seq_down)]
+    turns = chunks + up_at + 2 + SLACK * 2 * farthest
 
     def turn(s, carry):
         for offset, run in stages:
             pl.when((s >= offset) & (s < chunks + offset))(lambda run=run, offset=offset: run(s - offset))
         return carry
 
-    lax.fori_loop(0, chunks + depth, turn, 0)
-
-    def finish(k, carry):
-        for q in range(bits):
-            for copy in far_copies(k, q):
-                copy.wait_send()
-        pl.when(z < seq_count - 1)(lambda: to_right(k, pair.at[k, 0]).wait_send())
-        pl.when(z > 0)(lambda: to_left(k, pair.at[k, 0]).wait_send())
-        out_copy(k, pair.at[k, 0]).wait()
-        return carry
-
-    lax.fori_loop(0, chunks, finish, 0)
-    for k in (chunks - 2, chunks - 1):
-        pair_copy(k).wait_send()
-
-
-def reduce_rows(lefts, out_right, gate_right, sig_right):
-    wsh_count, seq_count = lax.axis_size("wsh"), lax.axis_size("seq")
+    def finish():
+        def wait_all(k, carry):
+            for q in range(bits):
+                for copy in far_copies(k, q):
+                    copy.wait_send()
+            pl.when(z < seq_count - 1)(lambda: to_right(k, pair.at[k, 0]).wait_send())
+            pl.when(z > 0)(lambda: to_left(k, pair.at[k, 0]).wait_send())
+            out_copy(k, pair.at[k, 0]).wait()
+            return carry
+
+        lax.fori_loop(0, chunks, wait_all, 0)
+        for k in (chunks - 2, chunks - 1):
+            pair_copy(k).wait_send()
+
+    return turns, turn, finish
+
+
+def reduce_scratch(chunks, depth, wsh_count):
     rows = D // wsh_count
-    orders = part_orders(wsh_count)
-    bits = len(orders)
-    n_out, n_gate, n_sig = (right.shape[1] // TILE for right in (out_right, gate_right, sig_right))
-    groups = lefts.shape[0] - 1
-    starts = [0, groups * n_out, groups * n_out + n_gate]
-    chunks = starts[2] + n_sig
-    rights_at = [(0, starts[1], n_out), (starts[1], starts[2], n_gate), (starts[2], chunks, n_sig)]
+    bits = len(part_orders(wsh_count))
     low = lambda *shape: pltpu.VMEM(shape, low_type)
     dma = pltpu.SemaphoreType.DMA
-    copies = bits * ((1 << bits) - 1)
-    vmem = pl.BlockSpec(memory_space=pltpu.VMEM)
-    return pl.pallas_call(
-        functools.partial(reduce_kernel, (wsh_count, seq_count, starts), rights_at),
-        in_specs=[vmem] * 4,
-        out_specs=pl.BlockSpec(memory_space=pl.ANY),
-        out_shape=jax.ShapeDtypeStruct((chunks, rows, TILE), low_type),
-        scratch_shapes=[
-            low(out_right.shape[0], TILE),
-            low(2, 1 << bits, rows, TILE),
-            low(chunks, 1 << bits, rows, TILE),
-            *[low(chunks, bits, 1 << (bits - 1 - q), rows // bits, TILE) for q in range(bits)],
-            low(chunks, rows, TILE),
-            low(chunks, rows, TILE),
-            dma((2, chunks)),
-            dma((2, copies, chunks)),
-            dma((4, chunks)),
-            dma((chunks,)),
-        ],
-        compiler_params=pltpu.CompilerParams(
-            collective_id=0, has_side_effects=True, vmem_limit_bytes=60 * 1024 * 1024
-        ),
-        cost_estimate=pl.CostEstimate(flops=10**11, bytes_accessed=20 * 10**6, transcendentals=0),
-        name="reduce_gradients",
-    )(lefts, out_right, gate_right, sig_right)
+    return [
+        low(depth, TILE),
+        low(2, 1 << bits, rows, TILE),
+        low(chunks, 1 << bits, rows, TILE),
+        *[low(min(chunks, LAND_SLOTS), bits, 1 << (bits - 1 - q), rows // bits, TILE) for q in range(bits)],
+        low(chunks, rows, TILE),
+        low(chunks, rows, TILE),
+        dma((2, chunks)),
+        dma((2, bits * ((1 << bits) - 1), chunks)),
+        dma((4, chunks)),
+        dma((chunks,)),
+    ]
 
 
 def adam_kernel(start, rate, decay, *refs):
@@ -977,44 +1181,8 @@
     )(sums, weights, first_moment, second_moment)
 
 
-def relative_rows(vals, count, groups):
-    size = vals.shape[1] // (count * groups)
-    me = lax.axis_index("wsh")
-    order = [r for r in range(count) if r % 2 == 0] + [r for r in range(count) if r % 2 == 1]
-    turned = vals.T
-    parts = [
-        lax.dynamic_slice_in_dim(turned, (lax.bitwise_xor(me, r) * groups + g) * size, size, 0)
-        for g in range(groups)
-        for r in order
-    ]
-    return jnp.concatenate(parts, axis=0).reshape(groups, count * size, vals.shape[0])
-
-
 def after(vals, *others):
     return lax.optimization_barrier((vals,) + others)[0]
-
-
-def shift(vals, by):
-    count = lax.axis_size("seq")
-    pairs = [(i, i + by) for i in range(count) if 0 <= i + by < count]
-    return lax.ppermute(vals, "seq", pairs)
-
-
-def carry_states(own, fades, sign):
-    count = lax.axis_size("seq")
-    span, span_fade = own, fades
-    result, fade = None, jnp.zeros_like(fades)
-    reach = 1
-    while reach < count:
-        got, got_fade = shift(span, sign * reach), shift(span_fade, sign * reach)
-        if result is None:
-            result = got
-        else:
-            result = (result.astype(full_type) + jnp.exp2(fade)[None, :] * got.astype(full_type)).astype(low_type)
-        span = (span.astype(full_type) + jnp.exp2(span_fade)[None, :] * got.astype(full_type)).astype(low_type)
-        fade, span_fade = fade + got_fade, span_fade + got_fade
-        reach = 2 * reach
-    return result
 
 
 def shards(
@@ -1065,26 +1233,21 @@
     tokens = tokens[HALO:]
     inv_rms = inv_rms[HALO:]
     normed = normed_all[HALO:]
-    x, bc, run, lag, run_t, lag_t, enter, enter_all, tail, offs, states, send = run_states(packed, conv, head)
-    fades = send[STATE].astype(full_type) + send[STATE + 1].astype(full_type)
-    state_in = carry_states(send[:STATE], fades, 1)
+    normed_t = normed.T
+    x, bc, run, lag, run_t, lag_t, enter, enter_all, tail, offs, states, state_in = run_states(packed, conv, head)
     y = run_outputs(x, bc, run, lag_t, enter, states, head)
     gate_vals, full_gate = multiply_pieces(normed, gate_pieces, wsh_count, full_type, "project_gate")
     back, full_out = multiply_back(cot_low, out_pieces, wsh_count, "project_back")
     gain_rows = jnp.broadcast_to(gain_out, (8, INNER))
-    normed_out, grad_y, grad_gate, part_gnorm, grad_state = run_norm(
+    normed_out, normed_out_t, grad_y, grad_gate, part_gnorm, grad_state = run_norm(
         y, gate_vals, back, gain_rows, bc, enter_all, state_in
     )
-    grad_in = carry_states(grad_state.astype(low_type), fades, -1)
     block_out = (tokens + dot(normed_out, full_out)).astype(low_type)[None]
-    grad_normed = dot_nt(grad_gate, full_gate)
-    grad_pack, edge, last, part_conv, part_skip, part_head = run_backward(
-        packed, conv, head, grad_y, bc, lag, run_t, enter, tail, offs, states, state_in, grad_in
+    lefts = jnp.concatenate([normed_out_t, normed_t], axis=0)
+    grad_normed, part_conv, part_skip, part_head, sums = run_backward(
+        packed, conv, head, grad_y, bc, lag, run_t, enter, tail, offs, states, state_in, grad_state,
+        lefts, cot_low, grad_gate, full_gate, full_sig,
     )
-    edge_next = lax.ppermute(edge, "seq", [(i, i - 1) for i in range(1, seq_count)])
-    fixed = jnp.concatenate([last[:8], last[8:] + edge_next], axis=0).astype(low_type)
-    grad_pack = lax.dynamic_update_slice(grad_pack, fixed, (rows - 16, 0))
-    grad_normed = grad_normed + dot_nt(grad_pack, full_sig)
     scaled = tokens * inv_rms
     part_gpre = jnp.sum(grad_normed * scaled, axis=0)
     pulled = grad_normed * gain_in
@@ -1104,10 +1267,6 @@
     grad_head = lax.dynamic_slice_in_dim(
         small_sums[cuts[2] :].reshape(3, HEADS), wsh_index * cols_head, cols_head, 1
     )
-    lefts = jnp.concatenate(
-        [relative_rows(normed, wsh_count, 1), relative_rows(normed_out, wsh_count, INNER // D)], axis=0
-    )
-    sums = reduce_rows(lefts, cot_low, grad_gate, grad_pack)
     tiles_out = (INNER // D) * (D // TILE)
     grad_out, *new_out = adam_chunks(sums, 0, w_out, first_w_out, second_w_out, rate_matrix, weight_decay, "adam_w_out")
     grad_in_w, *new_in = adam_chunks(

time: 612 us -> 549 us (0.90)
  local copies, waits for them, and re-layouts: 55.1 us -> 26.9 us
  matrix products: 29.5 us -> 10.4 us
  Pallas kernels: 328 us -> 346 us
  starting transfers between devices: 36.4 us -> 23.6 us
  other arithmetic: 36.7 us -> 24.9 us
    ppermute x7 -> x0, waiting for transfers between devices: 40.3 us -> none  [the longest x6 38.7 us: shift(): return lax.ppermute(vals, 'seq', pairs)]
    ppermute x32, waiting for transfers between devices: 61.8 us -> 98 us  [swap(): lax.ppermute(vals, axis, [(i, i ^ bit) for i in range(lax.axis_size(axis))])]
    dot_general x3 -> x1, matrix products: 29.5 us -> 10.4 us  [dot(): lax.dot_general(left_side, right_side, (dims, ((), ())), precision=precis...]
    pallas_call x3 -> x2, Pallas kernels: 220 us -> 238 us  [the longest x1 212 us: run_backward(): pl.pallas_call(functools.partial(backward_kernel, (wsh_count, seq_count),...]
    ppermute x7 -> x0, starting transfers between devices: 16.1 us -> none  [the longest x6 14.6 us: shift(): return lax.ppermute(vals, 'seq', pairs)]
    concatenate x3 -> x0, local copies, waits for them, and re-layouts: 14.9 us -> none  [relative_rows(): jnp.concatenate(parts, axis=0).reshape(groups, count * size, vals.shape[0])]
    convert_element_type x5 -> x0, other arithmetic: 11 us -> none  [the longest x2 4.74 us: carry_states(): (result.astype(full_type) + jnp.exp2(fade)[None, :] * got.astype(full_typ...]
  transfers between devices with their start and end apart: 40 -> 33, of which waited for: 13 -> 11; matrix products, arithmetic and copies ran while one was open for 12% -> 7% of each run, Pallas kernels for 42% -> 19%
where the time goes in v4:
time: 549 us; the launch traced here: 543 us
  Pallas kernels  346 us (63%)
  waiting for transfers between devices  98 us (18%)
  local copies, waits for them, and re-layouts  26.9 us (5%)
  other arithmetic  24.9 us (5%)
  starting transfers between devices  23.6 us (4%)
  blocking collectives  10.7 us (2%)
  matrix products  10.4 us (2%)
    pallas_call x1, Pallas kernels, run_backward(): pl.pallas_call(functools.partial(backward_kernel, (wsh_count, seq_count),...  212 us
    ppermute x32, waiting for transfers between devices, swap(): lax.ppermute(vals, axis, [(i, i ^ bit) for i in range(lax.axis_size(axis))])  98 us
    pallas_call x2, Pallas kernels, adam_chunks(): pl.pallas_call(functools.partial(adam_kernel, start, rate, decay), grid=(...  31.3 us
    pallas_call x2, Pallas kernels, multiply_pieces(): pl.pallas_call(functools.partial(piece_kernel, spots, rows), grid=(pl.cdi...  28.7 us
    pallas_call x1, Pallas kernels, run_states(): pl.pallas_call(states_kernel, grid=(GROUPS + CHAIN_LAG,), in_specs=[pl.Bl...  25.9 us
    ppermute x32, starting transfers between devices, swap(): lax.ppermute(vals, axis, [(i, i ^ bit) for i in range(lax.axis_size(axis))])  20.1 us
    pallas_call x1, Pallas kernels, run_norm(): pl.pallas_call(norm_kernel, grid=(rows // part,), in_specs=[by_rows(INNER...  18.2 us
    pallas_call x1, Pallas kernels, run_outputs(): pl.pallas_call(outputs_kernel, grid=(GROUPS,), in_specs=[pl.BlockSpec((ro...  16 us
  transfers between devices with their start and end apart: 33, of which 11 were waited for; matrix products, arithmetic and copies ran while one was open for 7% of the time, Pallas kernels for 19%

profile of v4, /device:TPU:0, one launch (start us, length us, event | category | flops | bytes accessed | tf_op | source)
XLA Modules:
  0.0 542.9 jit_solution(15201713619419411952)
XLA Ops:
  0.7 0.7 convert.21
  1.5 0.7 convert.22
  2.3 0.7 convert.20
  3.7 10.7 %all-gather.1 = bf16[8,1,2688]{2,1,0:T(2,128)(2,1)S(1)} all-gather(bf16[1,1,2688]{2,1,0:T(2,128)(2,1)S(1)} %reshape.139), channel_id=2, replica_groups=mesh['seq'=4,'wsh'=8] {'wsh'}, dimensions={0}, use_global_device_ids=true | all-gather | bytes 48384 | tf_op jit(solution)/shard_map/all_gather | solution.py:1211
  14.5 2.7 convert.23
  17.1 1.4 copy-done.3
  19.3 1.6 collective-permute-start.2
  21.3 29.4 %collective-permute-done.2.refs_2_ = bf16[192,3456]{1,0:T(8,128)(2,1)S(1)} collective-permute-done((bf16[192,3456]{1,0:T(8,128)(2,1)S(1)}, bf16[192,3456]{1,0:T(8,128)(2,1)S(1)}, u32[]{:S(2)}, u32[]{:S(2)}) %collective-permute-start.2) | collective-permute-done | bytes 1327136 | tf_op jit(solution)/shard_map/ppermute | solution.py:810
  50.8 1.6 collective-permute-start.3
  52.3 1.2 slice.115
  53.5 1.3 collective-permute-start.4
  54.8 1.3 slice.119.refs_0_
  56.2 11.2 %collective-permute-done.3.refs_3_ = bf16[96,3456]{1,0:T(8,128)(2,1)} collective-permute-done((bf16[96,3456]{1,0:T(8,128)(2,1)S(1)}, bf16[96,3456]{1,0:T(8,128)(2,1)}, u32[]{:S(2)}, u32[]{:S(2)}) %collective-permute-start.3) | collective-permute-done | bytes 663584 | tf_op jit(solution)/shard_map/ppermute | solution.py:810
  67.4 2.8 collective-permute-done.4.refs_4_
  70.2 0.8 collective-permute-start.11
  71.0 1.2 collective-permute-start.10
  72.2 24.6 %collective-permute-done.11.refs_2_ = bf16[192,3072]{1,0:T(8,128)(2,1)S(1)} collective-permute-done((bf16[192,3072]{1,0:T(8,128)(2,1)S(1)}, bf16[192,3072]{1,0:T(8,128)(2,1)S(1)}, u32[]{:S(2)}, u32[]{:S(2)}) %collective-permute-start.11) | collective-permute-done | bytes 1179680 | tf_op jit(solution)/shard_map/ppermute | solution.py:810
  97.4 2.1 collective-permute-start.13
  99.5 3.5 collective-permute-start
  103.0 1.2 convert_element_type.40.refs_0_
  104.2 5.9 %collective-permute-done.12.refs_3_ = bf16[96,3072]{1,0:T(8,128)(2,1)} collective-permute-done((bf16[96,3072]{1,0:T(8,128)(2,1)S(1)}, bf16[96,3072]{1,0:T(8,128)(2,1)}, u32[]{:S(2)}, u32[]{:S(2)}) %collective-permute-start.12) | collective-permute-done | bytes 589856 | tf_op jit(solution)/shard_map/ppermute | solution.py:810
  110.2 1.7 collective-permute-start.20
  113.4 0.7 copy.95
  115.9 0.7 copy.91
  116.7 0.7 copy.93
  118.4 0.8 copy-done.35
  120.3 15.2 %collective-permute-done.20.refs_2_ = bf16[384,1536]{1,0:T(8,128)(2,1)} collective-permute-done((bf16[384,1536]{1,0:T(8,128)(2,1)}, bf16[384,1536]{1,0:T(8,128)(2,1)}, u32[]{:S(2)}, u32[]{:S(2)}) %collective-permute-start.20) | collective-permute-done | bytes 1179680 | tf_op jit(solution)/shard_map/ppermute | solution.py:810
  135.5 1.4 collective-permute-done.19.refs_1_
  136.9 1.9 slice_bitcast_fusion.3
  138.8 2.7 copy.90
  141.6 2.1 maximum_convert_fusion
  143.7 1.1 slice.122
  144.8 1.1 slice.123
  146.9 1.6 collective-permute-start.22
  148.5 14.8 %project_signal.1 = (bf16[528,3456]{1,0:T(8,128)(2,1)}, bf16[1536,3456]{1,0:T(8,128)(2,1)}) custom-call(s32[1]{0:T(128)} %bitcast.2.me_ref, bf16[528,1536]{1,0:T(8,128)(2,1)} %copy-done.5, bf16[192,3456]{1,0:T(8,128)(2,1)} %copy-done.8, bf16[192,3456]{1,0:T(8,128)(2,1)} %collective-permute-done.1.refs_1_, bf16[192,3456]{1,0:T(8,128)(2,1)} %copy-done.13, ...), custom_call_target="tpu_custom_call" | custom-call | flops 5605687296 | bytes 21233664 | tf_op jit(solution)/shard_map/project_signal/pallas_call | solution.py:844
  163.4 25.9 %scan_states.1 = (f32[512,3072]{1,0:T(8,128)}, f32[512,256]{1,0:T(8,128)}, f32[512,128]{1,0:T(8,128)}, f32[512,128]{1,0:T(8,128)}, f32[128,512]{1,0:T(8,128)}, /...) custom-call(bf16[528,3456]{1,0:T(8,128)(2,1)} %get-tuple-element.71., ...), custom_call_target="tpu_custom_call" | custom-call | flops 1000000000 | bytes 15000000 | tf_op jit(solution)/shard_map/scan_states/pallas_call | solution.py:602
  190.5 16.0 %scan_outputs.1.y_ref = f32[512,3072]{1,0:T(8,128)} custom-call(f32[512,3072]{1,0:T(8,128)} %get-tuple-element.72.x_ref, f32[512,256]{1,0:T(8,128)} %get-tuple-element.73.bc_ref, f32[512,128]{1,0:T(8,128)} %get-tuple-element.74.run_ref, f32[128,512]{1,0:T(8,128)} %get-tuple-element.75.lag_t_ref, f32[512,128]{1,0:T(8,128)} %get-tuple-element.76.enter_ref, ...), custom_call_target="tpu_custom_call" | custom-call | flops 10000000000 | bytes 15000000 | tf_op jit(solution)/shard_map/scan_outputs/pallas_call | solution.py:653
  206.5 13.8 %project_gate.1 = (f32[512,3072]{1,0:T(8,128)}, bf16[1536,3072]{1,0:T(8,128)(2,1)}) custom-call(s32[1]{0:T(128)} %bitcast.2.me_ref, bf16[512,1536]{1,0:T(8,128)(2,1)} %get-tuple-element.252.left_ref, bf16[192,3072]{1,0:T(8,128)(2,1)} %copy-done.9, bf16[192,3072]{1,0:T(8,128)(2,1)} %copy-done.15, bf16[192,3072]{1,0:T(8,128)(2,1)} %copy-done.14, ...), custom_call_target="tpu_custom_call" | custom-call | flops 4831838208 | bytes 18874368 | tf_op jit(solution)/shard_map/project_gate/pallas_call | solution.py:844
  220.4 0.9 copy-done.32
  222.5 14.7 %project_back.1 = (f32[512,3072]{1,0:T(8,128)}, bf16[3072,1536]{1,0:T(8,128)(2,1)}) custom-call(s32[1]{0:T(128)} %bitcast.2.me_ref, bf16[512,1536]{1,0:T(8,128)(2,1)} %bitcast.35, bf16[384,1536]{1,0:T(8,128)(2,1)} %convert_element_type.40.refs_0_, bf16[384,1536]{1,0:T(8,128)(2,1)} %collective-permute-done.19.refs_1_, ...), custom_call_target="tpu_custom_call" | custom-call | flops 4831838208 | bytes 18874368 | tf_op jit(solution)/shard_map/project_back/pallas_call | solution.py:899
  237.9 18.2 %gated_norm.1 = (bf16[512,3072]{1,0:T(8,128)(2,1)}, bf16[3072,512]{1,0:T(8,128)(2,1)}, bf16[512,3072]{1,0:T(8,128)(2,1)}, bf16[512,3072]{1,0:T(8,128)(2,1)}, f32[8,3072]{1,0:T(8,128)}, /*index=5*/f32[128,3072]{1,0:T(8,128)}) custom-call(f32[512,3072]{1,0:T(8,128)} %scan_outputs.1.y_ref, f32[512,3072]{1,0:T(8,128)} %get-tuple-element.79.gate_ref, ...), custom_call_target="tpu_custom_call" | custom-call | flops 1000000000 | bytes 30000000 | tf_op jit(solution)/shard_map/gated_norm/pallas_call | solution.py:679
  256.1 4.4 pad_maximum_fusion.lefts_ref
  260.5 211.7 %scan_backward.1 = (f32[512,1536]{1,0:T(8,128)}, f32[8,3328]{1,0:T(8,128)}, f32[8,3072]{1,0:T(8,128)}, f32[8,128]{1,0:T(8,128)}, bf16[25,192,384]{2,1,0:T(8,128)(2,1)}) custom-call(bf16[528,3456]{1,0:T(8,128)(2,1)} %get-tuple-element.71.sig_ref.maps_ref.raw_ref, bf16[528,3456]{1,0:T(8,128)(2,1)} %get-tuple-element.71.sig_ref.maps_ref.raw_ref, ...), custom_call_target="tpu_custom_call" | custom-call | flops 99999997952 | bytes 20000000 | tf_op jit(solution)/shard_map/scan_backward/pallas_call | solution.py:722
  472.1 0.9 reshape.134
  473.1 0.9 slice_reduce_fusion
  474.2 0.8 slice_bitcast_fusion.1
  474.9 0.9 slice.102
  475.8 3.8 multiply_reduce_fusion.1
  479.7 10.4 %fusion.1 = bf16[1,512,1536]{2,1,0:T(8,128)(2,1)} fusion(bf16[512,3072]{1,0:T(8,128)(2,1)} %get-tuple-element.84, bf16[3072,1536]{1,0:T(8,128)(2,1)} %get-tuple-element.85, f32[528,1536]{1,0:T(8,128)S(1)} %copy-done), kind=kOutput, calls=%fused_computation.9 | convolution fusion | flops 4833411072 | bytes 17301504 | tf_op jit(solution)/shard_map/dot_general | solution.py:44
  490.2 1.5 collective-permute-start.29
  491.7 3.5 collective-permute-done.29
  495.2 1.5 collective-permute-start.30
  496.7 2.5 add_bitcast_fusion
  499.8 0.9 multiply_subtract_fusion
  500.7 3.5 collective-permute-done.31
  504.4 0.8 bitcast_convert_fusion
  505.2 0.7 copy.97
  505.9 0.7 copy.98
  506.6 0.7 copy.99
  507.3 0.7 copy.96
  508.0 9.9 %adam_w_out.1 = (f32[384,1536]{1,0:T(8,128)}, f32[384,1536]{1,0:T(8,128)}, f32[384,1536]{1,0:T(8,128)}, f32[384,1536]{1,0:T(8,128)}) custom-call(bf16[25,192,384]{2,1,0:T(8,128)(2,1)} %get-tuple-element.97.refs_0_, f32[384,1536]{1,0:T(8,128)} %refs_1_.3, f32[384,1536]{1,0:T(8,128)} %refs_2_.3, f32[384,1536]{1,0:T(8,128)} %refs_3_.3), custom_call_target="tpu_custom_call" | custom-call | flops 11796480 | bytes 17694720 | tf_op jit(solution)/shard_map/adam_w_out/pallas_call | solution.py:1170
  518.0 21.4 %adam_w_in.1 = (f32[192,6400]{1,0:T(8,128)}, f32[192,6400]{1,0:T(8,128)}, f32[192,6400]{1,0:T(8,128)}, f32[192,6400]{1,0:T(8,128)}) custom-call(bf16[25,192,384]{2,1,0:T(8,128)(2,1)} %get-tuple-element.97.refs_0_, f32[192,6400]{1,0:T(8,128)} %refs_1_.2, f32[192,6400]{1,0:T(8,128)} %refs_2_.2, f32[192,6400]{1,0:T(8,128)} %refs_3_.2), custom_call_target="tpu_custom_call" | custom-call | flops 24576000 | bytes 36864000 | tf_op jit(solution)/shard_map/adam_w_in/pallas_call | solution.py:1170
  539.7 0.7 multiply_subtract_fusion.1
  540.4 0.7 multiply_subtract_fusion.2
  (181 shorter events, 14.8 us)
Async XLA Ops:
  14.5 4.2 copy-start.16
  19.2 78.1 %copy-start.8 = (bf16[192,3456]{1,0:T(8,128)(2,1)}, bf16[192,3456]{1,0:T(8,128)(2,1)S(1)}, u32[]{:S(2)}) copy-start(bf16[192,3456]{1,0:T(8,128)(2,1)S(1)} %concatenate.18.refs_0_) | copy-start | bytes 3981316
  19.3 31.4 %collective-permute-start.2 = (bf16[192,3456]{1,0:T(8,128)(2,1)S(1)}, bf16[192,3456]{1,0:T(8,128)(2,1)S(1)}, u32[]{:S(2)}, u32[]{:S(2)}) collective-permute-start(bf16[192,3456]{1,0:T(8,128)(2,1)S(1)} %concatenate.18.refs_0_), channel_id=1, source_target_pairs={{0,4},{1,5},{2,6},{3,7},{4,0},{5,1},{6,2},{7,3},{8,12},{9,13},{10,... | collective-permute-start | bytes 3981320 | tf_op jit(solution)/shard_map/ppermute | solution.py:810
  20.8 31.5 %collective-permute-start.1 = (bf16[192,3456]{1,0:T(8,128)(2,1)S(1)}, bf16[192,3456]{1,0:T(8,128)(2,1)}, u32[]{:S(2)}, u32[]{:S(2)}) collective-permute-start(bf16[192,3456]{1,0:T(8,128)(2,1)S(1)} %concatenate.18.refs_0_), channel_id=1, source_target_pairs={{0,2},{1,3},{2,0},{3,1},{4,6},{5,7},{6,4},{7,5},{8,10},{9,11},{10,... | collective-permute-start | bytes 3981320 | tf_op jit(solution)/shard_map/ppermute | solution.py:810
  50.8 48.8 %copy-start.1 = (bf16[1,512,1536]{2,1,0:T(8,128)(2,1)S(1)}, bf16[1,512,1536]{2,1,0:T(8,128)(2,1)}, u32[]{:S(2)}) copy-start(bf16[1,512,1536]{2,1,0:T(8,128)(2,1)} %param.23) | copy-start | bytes 4718596
  50.8 52.3 %copy-start.4 = (f32[384,1536]{1,0:T(8,128)S(1)}, f32[384,1536]{1,0:T(8,128)}, u32[]{:S(2)}) copy-start(f32[384,1536]{1,0:T(8,128)} %refs_1_.3) | copy-start | bytes 7077892
  50.8 16.6 %collective-permute-start.3 = (bf16[96,3456]{1,0:T(8,128)(2,1)S(1)}, bf16[96,3456]{1,0:T(8,128)(2,1)}, u32[]{:S(2)}, u32[]{:S(2)}) collective-permute-start(bf16[96,3456]{1,0:T(8,128)(2,1)S(1)} %slice.114), channel_id=1, source_target_pairs={{0,2},{1,3},{2,0},{3,1},{4,6},{5,7},{6,4},{7,5},{8,10},{9,11},{10,... | collective-permute-start | bytes 1990664 | tf_op jit(solution)/shard_map/ppermute | solution.py:810
  53.5 16.6 %collective-permute-start.4 = (bf16[96,3456]{1,0:T(8,128)(2,1)S(1)}, bf16[96,3456]{1,0:T(8,128)(2,1)}, u32[]{:S(2)}, u32[]{:S(2)}) collective-permute-start(bf16[96,3456]{1,0:T(8,128)(2,1)S(1)} %slice.115), channel_id=1, source_target_pairs={{0,4},{1,5},{2,6},{3,7},{4,0},{5,1},{6,2},{7,3},{8,12},{9,13},{10,... | collective-permute-start | bytes 1990664 | tf_op jit(solution)/shard_map/ppermute | solution.py:810
  56.2 43.3 %copy-start.9 = (bf16[192,3072]{1,0:T(8,128)(2,1)}, bf16[192,3072]{1,0:T(8,128)(2,1)S(1)}, u32[]{:S(2)}) copy-start(bf16[192,3072]{1,0:T(8,128)(2,1)S(1)} %slice.119.refs_0_) | copy-start | bytes 3538948
  70.2 26.6 %collective-permute-start.11 = (bf16[192,3072]{1,0:T(8,128)(2,1)S(1)}, bf16[192,3072]{1,0:T(8,128)(2,1)S(1)}, u32[]{:S(2)}, u32[]{:S(2)}) collective-permute-start(bf16[192,3072]{1,0:T(8,128)(2,1)S(1)} %slice.119.refs_0_), channel_id=1, source_target_pairs={{0,4},{1,5},{2,6},{3,7},{4,0},{5,1},{6,2},{7,3},{8,12},{9,13},{10,... | collective-permute-start | bytes 3538952 | tf_op jit(solution)/shard_map/ppermute | solution.py:810
  71.0 26.3 %collective-permute-start.10 = (bf16[192,3072]{1,0:T(8,128)(2,1)S(1)}, bf16[192,3072]{1,0:T(8,128)(2,1)S(1)}, u32[]{:S(2)}, u32[]{:S(2)}) collective-permute-start(bf16[192,3072]{1,0:T(8,128)(2,1)S(1)} %slice.119.refs_0_), channel_id=1, source_target_pairs={{0,2},{1,3},{2,0},{3,1},{4,6},{5,7},{6,4},{7,5},{8,10},{9,11},{10,... | collective-permute-start | bytes 3538952 | tf_op jit(solution)/shard_map/ppermute | solution.py:810
  72.2 40.0 %collective-permute-start.5 = (bf16[192,3456]{1,0:T(8,128)(2,1)S(1)}, bf16[192,3456]{1,0:T(8,128)(2,1)S(1)}, u32[]{:S(2)}, u32[]{:S(2)}) collective-permute-start(bf16[192,3456]{1,0:T(8,128)(2,1)S(1)} %concatenate.18.refs_0_), channel_id=1, source_target_pairs={{0,1},{1,0},{2,3},{3,2},{4,5},{5,4},{6,7},{7,6},{8,9},{9,8},{10,11... | collective-permute-start | bytes 3981320 | tf_op jit(solution)/shard_map/ppermute | solution.py:810
  96.8 19.1 %copy-start.18 = (f32[192,48]{0,1:T(8,128)S(1)}, f32[192,48]{0,1:T(8,128)}, u32[]{:S(2)}) copy-start(f32[192,48]{0,1:T(8,128)} %param.34) | copy-start | bytes 110596
  96.8 19.8 %copy-start.19 = (f32[192,48]{0,1:T(8,128)S(1)}, f32[192,48]{0,1:T(8,128)}, u32[]{:S(2)}) copy-start(f32[192,48]{0,1:T(8,128)} %param.35) | copy-start | bytes 110596
  96.9 13.2 %collective-permute-start.12 = (bf16[96,3072]{1,0:T(8,128)(2,1)S(1)}, bf16[96,3072]{1,0:T(8,128)(2,1)}, u32[]{:S(2)}, u32[]{:S(2)}) collective-permute-start(bf16[96,3072]{1,0:T(8,128)(2,1)S(1)} %slice.120), channel_id=1, source_target_pairs={{0,2},{1,3},{2,0},{3,1},{4,6},{5,7},{6,4},{7,5},{8,10},{9,11},{10,... | collective-permute-start | bytes 1769480 | tf_op jit(solution)/shard_map/ppermute | solution.py:810
  97.4 12.8 %collective-permute-start.13 = (bf16[96,3072]{1,0:T(8,128)(2,1)S(1)}, bf16[96,3072]{1,0:T(8,128)(2,1)S(1)}, u32[]{:S(2)}, u32[]{:S(2)}) collective-permute-start(bf16[96,3072]{1,0:T(8,128)(2,1)S(1)} %slice.121), channel_id=1, source_target_pairs={{0,4},{1,5},{2,6},{3,7},{4,0},{5,1},{6,2},{7,3},{8,12},{9,13},{10,... | collective-permute-start | bytes 1769480 | tf_op jit(solution)/shard_map/ppermute | solution.py:810
  99.5 20.2 %collective-permute-start.6 = (bf16[192,3456]{1,0:T(8,128)(2,1)}, bf16[192,3456]{1,0:T(8,128)(2,1)}, u32[]{:S(2)}, u32[]{:S(2)}) collective-permute-start(bf16[192,3456]{1,0:T(8,128)(2,1)} %collective-permute-done.1.refs_1_), channel_id=1, source_target_pairs={{0,1},{1,0},{2,3},{3,2},{4,5},{5,4},{6,7},{7,6},{8,9},{9,8},{10,11... | collective-permute-start | bytes 3981320 | tf_op jit(solution)/shard_map/ppermute | solution.py:810
  99.5 12.7 %collective-permute-start = (bf16[16,1536]{1,0:T(8,128)(2,1)S(1)}, bf16[16,1536]{1,0:T(8,128)(2,1)S(1)}, u32[]{:S(2)}, u32[]{:S(2)}) collective-permute-start(bf16[16,1536]{1,0:T(8,128)(2,1)S(1)} %slice_bitcast_fusion), channel_id=1, source_target_pairs={{0,8},{8,16},{16,24},{1,9},{9,17},{17,25},{2,10},{10,18},{18,26},{... | collective-permute-start | bytes 147464 | tf_op jit(solution)/shard_map/ppermute | solution.py:1228
  110.2 25.4 %collective-permute-start.20 = (bf16[384,1536]{1,0:T(8,128)(2,1)}, bf16[384,1536]{1,0:T(8,128)(2,1)}, u32[]{:S(2)}, u32[]{:S(2)}) collective-permute-start(bf16[384,1536]{1,0:T(8,128)(2,1)} %convert_element_type.40.refs_0_), channel_id=1, source_target_pairs={{0,4},{1,5},{2,6},{3,7},{4,0},{5,1},{6,2},{7,3},{8,12},{9,13},{10,... | collective-permute-start | bytes 3538952 | tf_op jit(solution)/shard_map/ppermute | solution.py:810
  111.9 25.1 %collective-permute-start.19 = (bf16[384,1536]{1,0:T(8,128)(2,1)}, bf16[384,1536]{1,0:T(8,128)(2,1)}, u32[]{:S(2)}, u32[]{:S(2)}) collective-permute-start(bf16[384,1536]{1,0:T(8,128)(2,1)} %convert_element_type.40.refs_0_), channel_id=1, source_target_pairs={{0,2},{1,3},{2,0},{3,1},{4,6},{5,7},{6,4},{7,5},{8,10},{9,11},{10,... | collective-permute-start | bytes 3538952 | tf_op jit(solution)/shard_map/ppermute | solution.py:810
  112.2 5.6 %collective-permute-start.8 = (bf16[96,3456]{1,0:T(8,128)(2,1)}, bf16[96,3456]{1,0:T(8,128)(2,1)}, u32[]{:S(2)}, u32[]{:S(2)}) collective-permute-start(bf16[96,3456]{1,0:T(8,128)(2,1)} %collective-permute-done.3.refs_3_), channel_id=1, source_target_pairs={{0,1},{1,0},{2,3},{3,2},{4,5},{5,4},{6,7},{7,6},{8,9},{9,8},{10,11... | collective-permute-start | bytes 1990664 | tf_op jit(solution)/shard_map/ppermute | solution.py:810
  112.2 6.2 %collective-permute-start.9 = (bf16[96,3456]{1,0:T(8,128)(2,1)}, bf16[96,3456]{1,0:T(8,128)(2,1)S(1)}, u32[]{:S(2)}, u32[]{:S(2)}) collective-permute-start(bf16[96,3456]{1,0:T(8,128)(2,1)} %collective-permute-done.4.refs_4_), channel_id=1, source_target_pairs={{0,1},{1,0},{2,3},{3,2},{4,5},{5,4},{6,7},{7,6},{8,9},{9,8},{10,11... | collective-permute-start | bytes 1990664 | tf_op jit(solution)/shard_map/ppermute | solution.py:810
  117.8 28.1 %collective-permute-start.7 = (bf16[192,3456]{1,0:T(8,128)(2,1)}, bf16[192,3456]{1,0:T(8,128)(2,1)}, u32[]{:S(2)}, u32[]{:S(2)}) collective-permute-start(bf16[192,3456]{1,0:T(8,128)(2,1)} %copy-done.13), channel_id=1, source_target_pairs={{0,1},{1,0},{2,3},{3,2},{4,5},{5,4},{6,7},{7,6},{8,9},{9,8},{10,11... | collective-permute-start | bytes 3981320 | tf_op jit(solution)/shard_map/ppermute | solution.py:810
  119.3 27.3 %collective-permute-start.14 = (bf16[192,3072]{1,0:T(8,128)(2,1)}, bf16[192,3072]{1,0:T(8,128)(2,1)}, u32[]{:S(2)}, u32[]{:S(2)}) collective-permute-start(bf16[192,3072]{1,0:T(8,128)(2,1)} %copy-done.9), channel_id=1, source_target_pairs={{0,1},{1,0},{2,3},{3,2},{4,5},{5,4},{6,7},{7,6},{8,9},{9,8},{10,11... | collective-permute-start | bytes 3538952 | tf_op jit(solution)/shard_map/ppermute | solution.py:810
  119.7 21.9 %copy-start.5 = (bf16[528,1536]{1,0:T(8,128)(2,1)}, bf16[528,1536]{1,0:T(8,128)(2,1)S(1)}, u32[]{:S(2)}) copy-start(bf16[528,1536]{1,0:T(8,128)(2,1)S(1)} %multiply_convert_fusion.left_ref) | copy-start | bytes 4866052
  119.8 69.6 %collective-permute-start.15 = (bf16[192,3072]{1,0:T(8,128)(2,1)}, bf16[192,3072]{1,0:T(8,128)(2,1)}, u32[]{:S(2)}, u32[]{:S(2)}) collective-permute-start(bf16[192,3072]{1,0:T(8,128)(2,1)} %copy-done.15), channel_id=1, source_target_pairs={{0,1},{1,0},{2,3},{3,2},{4,5},{5,4},{6,7},{7,6},{8,9},{9,8},{10,11... | collective-permute-start | bytes 3538952 | tf_op jit(solution)/shard_map/ppermute | solution.py:810
  135.5 54.4 %collective-permute-start.16 = (bf16[192,3072]{1,0:T(8,128)(2,1)}, bf16[192,3072]{1,0:T(8,128)(2,1)}, u32[]{:S(2)}, u32[]{:S(2)}) collective-permute-start(bf16[192,3072]{1,0:T(8,128)(2,1)} %copy-done.14), channel_id=1, source_target_pairs={{0,1},{1,0},{2,3},{3,2},{4,5},{5,4},{6,7},{7,6},{8,9},{9,8},{10,11... | collective-permute-start | bytes 3538952 | tf_op jit(solution)/shard_map/ppermute | solution.py:810
  136.9 10.0 %collective-permute-start.17 = (bf16[96,3072]{1,0:T(8,128)(2,1)}, bf16[96,3072]{1,0:T(8,128)(2,1)}, u32[]{:S(2)}, u32[]{:S(2)}) collective-permute-start(bf16[96,3072]{1,0:T(8,128)(2,1)} %collective-permute-done.12.refs_3_), channel_id=1, source_target_pairs={{0,1},{1,0},{2,3},{3,2},{4,5},{5,4},{6,7},{7,6},{8,9},{9,8},{10,11... | collective-permute-start | bytes 1769480 | tf_op jit(solution)/shard_map/ppermute | solution.py:810
  141.6 4.3 copy-start.37
  145.9 43.3 %collective-permute-start.18 = (bf16[96,3072]{1,0:T(8,128)(2,1)S(1)}, bf16[96,3072]{1,0:T(8,128)(2,1)S(1)}, u32[]{:S(2)}, u32[]{:S(2)}) collective-permute-start(bf16[96,3072]{1,0:T(8,128)(2,1)S(1)} %copy-done.37), channel_id=1, source_target_pairs={{0,1},{1,0},{2,3},{3,2},{4,5},{5,4},{6,7},{7,6},{8,9},{9,8},{10,11... | collective-permute-start | bytes 1769480 | tf_op jit(solution)/shard_map/ppermute | solution.py:810
  146.5 43.5 %collective-permute-start.21 = (bf16[192,1536]{1,0:T(8,128)(2,1)S(1)}, bf16[192,1536]{1,0:T(8,128)(2,1)S(1)}, u32[]{:S(2)}, u32[]{:S(2)}) collective-permute-start(bf16[192,1536]{1,0:T(8,128)(2,1)S(1)} %slice.122), channel_id=1, source_target_pairs={{0,2},{1,3},{2,0},{3,1},{4,6},{5,7},{6,4},{7,5},{8,10},{9,11},{10,... | collective-permute-start | bytes 1769480 | tf_op jit(solution)/shard_map/ppermute | solution.py:810
  146.9 43.5 %collective-permute-start.22 = (bf16[192,1536]{1,0:T(8,128)(2,1)S(1)}, bf16[192,1536]{1,0:T(8,128)(2,1)S(1)}, u32[]{:S(2)}, u32[]{:S(2)}) collective-permute-start(bf16[192,1536]{1,0:T(8,128)(2,1)S(1)} %slice.123), channel_id=1, source_target_pairs={{0,4},{1,5},{2,6},{3,7},{4,0},{5,1},{6,2},{7,3},{8,12},{9,13},{10,... | collective-permute-start | bytes 1769480 | tf_op jit(solution)/shard_map/ppermute | solution.py:810
  189.3 17.2 %copy-start.40 = (bf16[96,3072]{1,0:T(8,128)(2,1)}, bf16[96,3072]{1,0:T(8,128)(2,1)S(1)}, u32[]{:S(2)}) copy-start(bf16[96,3072]{1,0:T(8,128)(2,1)S(1)} %collective-permute-done.18.refs_9_) | copy-start | bytes 1769476
  189.3 31.0 %collective-permute-start.23 = (bf16[384,1536]{1,0:T(8,128)(2,1)}, bf16[384,1536]{1,0:T(8,128)(2,1)S(1)}, u32[]{:S(2)}, u32[]{:S(2)}) collective-permute-start(bf16[384,1536]{1,0:T(8,128)(2,1)} %convert_element_type.40.refs_0_), channel_id=1, source_target_pairs={{0,1},{1,0},{2,3},{3,2},{4,5},{5,4},{6,7},{7,6},{8,9},{9,8},{10,11... | collective-permute-start | bytes 3538952 | tf_op jit(solution)/shard_map/ppermute | solution.py:810
  189.4 31.0 %collective-permute-start.24 = (bf16[384,1536]{1,0:T(8,128)(2,1)}, bf16[384,1536]{1,0:T(8,128)(2,1)S(1)}, u32[]{:S(2)}, u32[]{:S(2)}) collective-permute-start(bf16[384,1536]{1,0:T(8,128)(2,1)} %collective-permute-done.19.refs_1_), channel_id=1, source_target_pairs={{0,1},{1,0},{2,3},{3,2},{4,5},{5,4},{6,7},{7,6},{8,9},{9,8},{10,11... | collective-permute-start | bytes 3538952 | tf_op jit(solution)/shard_map/ppermute | solution.py:810
  189.9 30.5 %collective-permute-start.25 = (bf16[384,1536]{1,0:T(8,128)(2,1)}, bf16[384,1536]{1,0:T(8,128)(2,1)S(1)}, u32[]{:S(2)}, u32[]{:S(2)}) collective-permute-start(bf16[384,1536]{1,0:T(8,128)(2,1)} %collective-permute-done.20.refs_2_), channel_id=1, source_target_pairs={{0,1},{1,0},{2,3},{3,2},{4,5},{5,4},{6,7},{7,6},{8,9},{9,8},{10,11... | collective-permute-start | bytes 3538952 | tf_op jit(solution)/shard_map/ppermute | solution.py:810
  190.0 16.5 %copy-start.38 = (bf16[192,1536]{1,0:T(8,128)(2,1)}, bf16[192,1536]{1,0:T(8,128)(2,1)S(1)}, u32[]{:S(2)}) copy-start(bf16[192,1536]{1,0:T(8,128)(2,1)S(1)} %collective-permute-done.21.refs_3_) | copy-start | bytes 1769476
  190.0 30.3 %collective-permute-start.26 = (bf16[192,1536]{1,0:T(8,128)(2,1)S(1)}, bf16[192,1536]{1,0:T(8,128)(2,1)S(1)}, u32[]{:S(2)}, u32[]{:S(2)}) collective-permute-start(bf16[192,1536]{1,0:T(8,128)(2,1)S(1)} %collective-permute-done.21.refs_3_), channel_id=1, source_target_pairs={{0,1},{1,0},{2,3},{3,2},{4,5},{5,4},{6,7},{7,6},{8,9},{9,8},{10,11... | collective-permute-start | bytes 1769480 | tf_op jit(solution)/shard_map/ppermute | solution.py:810
  190.4 16.1 %copy-start.39 = (bf16[192,1536]{1,0:T(8,128)(2,1)}, bf16[192,1536]{1,0:T(8,128)(2,1)S(1)}, u32[]{:S(2)}) copy-start(bf16[192,1536]{1,0:T(8,128)(2,1)S(1)} %collective-permute-done.22.refs_4_) | copy-start | bytes 1769476
  190.4 29.9 %collective-permute-start.27 = (bf16[192,1536]{1,0:T(8,128)(2,1)S(1)}, bf16[192,1536]{1,0:T(8,128)(2,1)S(1)}, u32[]{:S(2)}, u32[]{:S(2)}) collective-permute-start(bf16[192,1536]{1,0:T(8,128)(2,1)S(1)} %collective-permute-done.22.refs_4_), channel_id=1, source_target_pairs={{0,1},{1,0},{2,3},{3,2},{4,5},{5,4},{6,7},{7,6},{8,9},{9,8},{10,11... | collective-permute-start | bytes 1769480 | tf_op jit(solution)/shard_map/ppermute | solution.py:810
  237.9 18.2 %copy-start.6 = (bf16[1536,512]{1,0:T(8,128)(2,1)S(1)}, bf16[1536,512]{1,0:T(8,128)(2,1)}, u32[]{:S(2)}) copy-start(bf16[1536,512]{1,0:T(8,128)(2,1)} %copy.90) | copy-start | bytes 4718596
  475.8 3.9 copy-start
  479.7 10.5 %collective-permute-start.28 = (f32[21392]{0:T(1024)S(1)}, f32[21392]{0:T(1024)S(1)}, u32[]{:S(2)}, u32[]{:S(2)}) collective-permute-start(f32[21392]{0:T(1024)S(1)} %concatenate.20), channel_id=1, source_target_pairs={{0,1},{1,0},{2,3},{3,2},{4,5},{5,4},{6,7},{7,6},{8,9},{9,8},{10,11... | collective-permute-start | bytes 256712 | tf_op jit(solution)/shard_map/ppermute | solution.py:810
  479.7 17.0 %copy-start.2 = (f32[512,1536]{1,0:T(8,128)S(1)}, f32[512,1536]{1,0:T(8,128)}, u32[]{:S(2)}) copy-start(f32[512,1536]{1,0:T(8,128)} %get-tuple-element.96) | copy-start | bytes 9437188
  479.7 17.0 %copy-start.7 = (bf16[1,512,1536]{2,1,0:T(8,128)(2,1)S(1)}, bf16[1,512,1536]{2,1,0:T(8,128)(2,1)}, u32[]{:S(2)}) copy-start(bf16[1,512,1536]{2,1,0:T(8,128)(2,1)} %param.24) | copy-start | bytes 4718596
  490.2 5.0 collective-permute-start.29
  495.1 4.7 copy-start.10
  495.2 4.7 copy-start.11
  495.2 4.7 copy-start.12
  495.2 4.6 collective-permute-start.30
  499.7 4.6 collective-permute-start.31
  504.3 35.2 %collective-permute-start.32 = (f32[21392]{0:T(1024)S(1)}, f32[21392]{0:T(1024)S(1)}, u32[]{:S(2)}, u32[]{:S(2)}) collective-permute-start(f32[21392]{0:T(1024)S(1)} %add.134), channel_id=1, source_target_pairs={{0,16},{8,24},{16,0},{24,8},{1,17},{9,25},{17,1},{25,9},{2,18},{10... | collective-permute-start | bytes 256712 | tf_op jit(solution)/shard_map/ppermute | solution.py:810
  517.9 21.8 %copy-start.17 = (f32[5,416]{1,0:T(8,128)S(1)}, f32[5,416]{1,0:T(8,128)}, u32[]{:S(2)}) copy-start(f32[5,416]{1,0:T(8,128)} %param.30) | copy-start | bytes 24964
  517.9 21.8 %copy-start.20 = (f32[5,416]{1,0:T(8,128)S(1)}, f32[5,416]{1,0:T(8,128)}, u32[]{:S(2)}) copy-start(f32[5,416]{1,0:T(8,128)} %param.42) | copy-start | bytes 24964
  517.9 21.8 %copy-start.21 = (f32[5,416]{1,0:T(8,128)S(1)}, f32[5,416]{1,0:T(8,128)}, u32[]{:S(2)}) copy-start(f32[5,416]{1,0:T(8,128)} %param.43) | copy-start | bytes 24964
  517.9 22.5 %copy-start.22 = (f32[384]{0:T(512)S(1)}, f32[384]{0:T(512)}, u32[]{:S(2)}) copy-start(f32[384]{0:T(512)} %param.29) | copy-start | bytes 4612
  517.9 22.5 %copy-start.24 = (f32[384]{0:T(512)S(1)}, f32[384]{0:T(512)}, u32[]{:S(2)}) copy-start(f32[384]{0:T(512)} %param.40) | copy-start | bytes 4612
  517.9 22.4 %copy-start.25 = (f32[384]{0:T(512)S(1)}, f32[384]{0:T(512)}, u32[]{:S(2)}) copy-start(f32[384]{0:T(512)} %param.41) | copy-start | bytes 4612
  518.0 23.1 %copy-start.23 = (f32[3,6]{1,0:T(4,128)S(1)}, f32[3,6]{1,0:T(4,128)}, u32[]{:S(2)}) copy-start(f32[3,6]{1,0:T(4,128)} %param.31) | copy-start | bytes 220
  518.0 23.1 %copy-start.26 = (f32[3,6]{1,0:T(4,128)S(1)}, f32[3,6]{1,0:T(4,128)}, u32[]{:S(2)}) copy-start(f32[3,6]{1,0:T(4,128)} %param.44) | copy-start | bytes 220
  518.0 23.1 %copy-start.27 = (f32[3,6]{1,0:T(4,128)S(1)}, f32[3,6]{1,0:T(4,128)}, u32[]{:S(2)}) copy-start(f32[3,6]{1,0:T(4,128)} %param.45) | copy-start | bytes 220
  518.0 23.8 %copy-start.28 = (f32[192]{0:T(256)S(1)}, f32[192]{0:T(256)}, u32[]{:S(2)}) copy-start(f32[192]{0:T(256)} %param.28) | copy-start | bytes 2308
  518.0 23.8 %copy-start.29 = (f32[192]{0:T(256)S(1)}, f32[192]{0:T(256)}, u32[]{:S(2)}) copy-start(f32[192]{0:T(256)} %param.38) | copy-start | bytes 2308
  518.0 23.8 %copy-start.30 = (f32[192]{0:T(256)S(1)}, f32[192]{0:T(256)}, u32[]{:S(2)}) copy-start(f32[192]{0:T(256)} %param.39) | copy-start | bytes 2308
  (12 other events, 21.7 us)

commit v5 on v4

--- a/solution.py
+++ b/solution.py
@@ -100,33 +100,89 @@
     return rows >= cols if lower else rows <= cols
 
 
-def greet_along():
-    z = lax.axis_index("seq")
-    seq_count = lax.axis_size("seq")
-    barrier = pltpu.get_barrier_semaphore()
-
-    @pl.when(z > 0)
-    def _():
-        pl.semaphore_signal(barrier, inc=1, device_id={"seq": z - 1}, device_id_type=pl.DeviceIdType.MESH)
-
-    @pl.when(z < seq_count - 1)
-    def _():
-        pl.semaphore_signal(barrier, inc=1, device_id={"seq": z + 1}, device_id_type=pl.DeviceIdType.MESH)
-
-    pl.semaphore_wait(barrier, jnp.where(z > 0, 1, 0) + jnp.where(z < seq_count - 1, 1, 0))
-
-
-def states_kernel(
-    sig_ref, maps_ref, raw_ref, conv_ref, conv_maps_ref, head_ref,
-    x_ref, bc_ref, run_ref, lag_ref, run_t_ref, lag_t_ref, enter_ref, enter_all_ref, tail_ref, offs_ref,
-    states_ref, before_ref,
-    sig, in_t, ends, stage, land, sems,
+def gather_steps(count, own_ref, full_ref, far_sems, core_sems):
+    orders = part_orders(count)
+    bits = len(orders)
+    rows = own_ref.shape[0]
+    part = rows // bits
+    me = lax.axis_index("wsh")
+    mesh_id = pl.DeviceIdType.MESH
+
+    def copy(m, first, size, bit, sems, n):
+        start = lax.bitwise_xor(me, 2 * m) * rows + first
+        at = full_ref.at[pl.ds(pl.multiple_of(start, 16), size)]
+        return pltpu.make_async_remote_copy(
+            src_ref=at, dst_ref=at, send_sem=sems.at[0, n], recv_sem=sems.at[1, n],
+            device_id={"wsh": lax.bitwise_xor(me, bit)}, device_id_type=mesh_id,
+        )
+
+    far_spots = [
+        (q, m, p * part, part, 2 << order[q])
+        for q in range(bits)
+        for p, order in enumerate(orders)
+        for m in range(1 << bits)
+        if m & ~sum(1 << b for b in order[:q]) == 0
+    ]
+    core_spots = [(0, 0, 0, rows, 1)] + [
+        (q + 1, m, p * part, part, 1)
+        for q in range(bits)
+        for p, order in enumerate(orders)
+        for m in range(1 << bits)
+        if m >> order[q] & 1 and m & ~sum(1 << b for b in order[: q + 1]) == 0
+    ]
+    pick = lambda spots, sems, phase: [
+        copy(m, first, size, bit, sems, n)
+        for n, (q, m, first, size, bit) in enumerate(spots)
+        if phase is None or q == phase
+    ]
+
+    def start():
+        full_ref[pl.ds(pl.multiple_of(me * rows, 16), rows), :] = own_ref[...]
+        for item in pick(far_spots, far_sems, 0) + pick(core_spots, core_sems, 0):
+            item.start()
+
+    def advance(phase):
+        for item in pick(far_spots, far_sems, phase):
+            item.wait_recv()
+        later = pick(far_spots, far_sems, phase + 1) if phase + 1 < bits else []
+        for item in later + pick(core_spots, core_sems, phase + 1):
+            item.start()
+
+    def done():
+        for item in pick(core_spots, core_sems, None):
+            item.wait_recv()
+
+    def finish():
+        for item in pick(far_spots, far_sems, None) + pick(core_spots, core_sems, None):
+            item.wait_send()
+
+    return start, advance, done, finish
+
+
+def gather_sems(count):
+    bits = len(part_orders(count))
+    copies = bits * ((1 << bits) - 1)
+    return [pltpu.SemaphoreType.DMA((2, copies)), pltpu.SemaphoreType.DMA((2, copies + 1))]
+
+
+def forward_kernel(
+    count,
+    sig_ref, maps_ref, raw_ref, conv_ref, conv_maps_ref, head_ref, normed_ref, cot_ref, gate_own_ref, out_own_ref,
+    y_ref, bc_ref, lag_ref, run_t_ref, enter_ref, enter_all_ref, tail_ref, offs_ref, states_ref, before_ref,
+    gate_ref, back_ref, full_gate_ref, full_out_ref,
+    sig, in_t, inter, run, lag_t, ends, stage, land, sems, gate_full, out_full,
+    gate_far, gate_core, out_far, out_core, full_sems,
 ):
     step = pl.program_id(0)
-    rows = x_ref.shape[0]
+    rows = y_ref.shape[0]
     blocks = rows // BLOCK
     z = lax.axis_index("seq")
     seq_count = lax.axis_size("seq")
+    lower = triangle(True)
+    bits = len(part_orders(count))
+    gate_start, gate_advance, gate_done, gate_finish = gather_steps(count, gate_own_ref, gate_full, gate_far, gate_core)
+    out_start, out_advance, out_done, out_finish = gather_steps(count, out_own_ref, out_full, out_far, out_core)
+    gate_at, back_at = GROUPS + CHAIN_LAG, 2 * GROUPS + CHAIN_LAG
 
     def to_next(k):
         return pltpu.make_async_remote_copy(
@@ -136,7 +192,9 @@
 
     @pl.when(step == 0)
     def _():
-        greet_along()
+        greet()
+        gate_start()
+        out_start()
         sig[...] = maps_ref[...].astype(full_type)
         pre = convolve(sig, conv_maps_ref[...], rows)
         maps = pre * sigmoid(pre)
@@ -145,42 +203,68 @@
         step_sizes, _, rate = step_terms(raw_ref[HALO:, :].astype(full_type), head_ref[...])
         rates = step_sizes * rate * LOG2E
         log_steps = jnp.log2(step_sizes)
-        lower = jnp.where(triangle(True), 1.0, 0.0)
+        sums = jnp.where(lower, 1.0, 0.0)
         offset = jnp.zeros((1, LANES), full_type)
         offs_ref[...] = jnp.zeros(offs_ref.shape, full_type)
         for c in range(blocks):
             at = slice(c * BLOCK, (c + 1) * BLOCK)
-            run = dot(lower, rates[at], precision=highest)
-            lag = run - log_steps[at]
-            run_ref[at, :] = run
+            total = dot(sums, rates[at], precision=highest)
+            lag = total - log_steps[at]
+            run[at, :] = total
             lag_ref[at, :] = lag
-            run_t_ref[:, at] = run.T
-            lag_t_ref[:, at] = lag.T
-            enter_ref[at, :] = jnp.exp2(run)
-            enter_all_ref[at, :] = jnp.exp2(run + offset)
-            tail_ref[at, :] = jnp.exp2(run[BLOCK - 1 : BLOCK] - lag)
+            run_t_ref[:, at] = total.T
+            lag_t[:, at] = lag.T
+            enter_ref[at, :] = jnp.exp2(total)
+            enter_all_ref[at, :] = jnp.exp2(total + offset)
+            tail_ref[at, :] = jnp.exp2(total[BLOCK - 1 : BLOCK] - lag)
             offs_ref[c : c + 1, :] = offset
-            offset = offset + run[BLOCK - 1 : BLOCK]
+            offset = offset + total[BLOCK - 1 : BLOCK]
+            low_maps = maps[at].astype(low_type)
+            inter[c] = dot_nt(low_maps[:, STATE:], low_maps[:, :STATE])
         offs_ref[blocks : blocks + 1, :] = offset
 
+    pl.when(step == GROUPS // 2)(lambda: gate_advance(0))
+    pl.when(step == GROUPS)(lambda: out_advance(0))
+
     @pl.when(step < GROUPS)
     def _():
         sig[...] = sig_ref[...].astype(full_type)
-        pre = convolve(sig, conv_ref[...], rows)
-        x = pre * sigmoid(pre)
-        x_ref[...] = x
+        pre_all = convolve(sig, conv_ref[...], rows)
         tail = to_front(tail_ref[...], step)
         last = to_front(offs_ref[...], step)
+        run_all = to_front(run[...], step)
+        enter = to_front(enter_ref[...], step)
+        lag_rows = head_rows(lag_t, step)
+        skip = widen(to_front(head_ref[...], step)[2:3])
+        left = lane_ids((BLOCK, LANES)) < HEAD_DIM
         state = jnp.zeros((STATE, WIDE), full_type)
         for c in range(blocks):
             at = slice(c * BLOCK, (c + 1) * BLOCK)
-            weighted = (x[at] * widen(tail[at])).astype(low_type)
+            pre = pre_all[at]
+            x = pre * sigmoid(pre)
+            parts = []
+            for pair in range(2):
+                mixes = []
+                for i in range(2):
+                    h = 2 * pair + i
+                    power = jnp.where(lower, run_all[at, h : h + 1] - lag_rows[h : h + 1, at], -1e30)
+                    mixes.append((jnp.exp2(power) * inter[c]).astype(low_type))
+                half = x[:, pair * LANES : (pair + 1) * LANES].astype(low_type)
+                zero = jnp.zeros_like(half)
+                stacked = jnp.concatenate([jnp.where(left, half, zero), jnp.where(left, zero, half)], axis=0)
+                parts.append(dot(jnp.concatenate(mixes, axis=1), stacked))
+            y = jnp.concatenate(parts, axis=1) + skip * x
+            if c > 0:
+                out_map = bc_ref[at, STATE:].astype(low_type)
+                y = y + widen(enter[at]) * dot(out_map, state.astype(low_type))
+            y_ref[at, :] = y
+            weighted = (x * widen(tail[at])).astype(low_type)
             fade = jnp.exp2(widen(last[c + 1 : c + 2] - last[c : c + 1]))
             state = state * fade + dot(in_t[:, at], weighted)
             states_ref[c] = state.astype(low_type)
         ends[step] = state
 
-    @pl.when(step >= CHAIN_LAG)
+    @pl.when((step >= CHAIN_LAG) & (step < gate_at))
     def _():
         k = step - CHAIN_LAG
 
@@ -200,50 +284,44 @@
             stage[k] = (ends[k] + fade * land[k].astype(full_type)).astype(low_type)
             to_next(k).start()
 
-    @pl.when((step == GROUPS + CHAIN_LAG - 1) & (z < seq_count - 1))
-    def _():
-        for k in range(GROUPS):
-            to_next(k).wait_send()
-
-
-def outputs_kernel(x_ref, bc_ref, run_ref, lag_t_ref, enter_ref, states_ref, head_ref, y_ref, inter):
-    step = pl.program_id(0)
-    rows = x_ref.shape[0]
-    blocks = rows // BLOCK
-    lower = triangle(True)
-
-    @pl.when(step == 0)
-    def _():
-        for c in range(blocks):
-            at = slice(c * BLOCK, (c + 1) * BLOCK)
-            maps = bc_ref[at, :].astype(low_type)
-            inter[c] = dot_nt(maps[:, STATE:], maps[:, :STATE])
-
-    run = to_front(run_ref[...], step)
-    enter = to_front(enter_ref[...], step)
-    lag_rows = head_rows(lag_t_ref, step)
-    skip = widen(to_front(head_ref[...], step)[2:3])
-    left = lane_ids((BLOCK, LANES)) < HEAD_DIM
-    for c in range(blocks):
-        at = slice(c * BLOCK, (c + 1) * BLOCK)
-        x = x_ref[at, :]
-        parts = []
-        for pair in range(2):
-            mixes = []
-            for i in range(2):
-                h = 2 * pair + i
-                lag_row = lag_rows[h : h + 1, at]
-                power = jnp.where(lower, run[at, h : h + 1] - lag_row, -1e30)
-                mixes.append((jnp.exp2(power) * inter[c]).astype(low_type))
-            half = x[:, pair * LANES : (pair + 1) * LANES].astype(low_type)
-            zero = jnp.zeros_like(half)
-            stacked = jnp.concatenate([jnp.where(left, half, zero), jnp.where(left, zero, half)], axis=0)
-            parts.append(dot(jnp.concatenate(mixes, axis=1), stacked))
-        y = jnp.concatenate(parts, axis=1) + skip * x
-        if c > 0:
-            out_map = bc_ref[at, STATE:].astype(low_type)
-            y = y + widen(enter[at]) * dot(out_map, states_ref[c - 1])
-        y_ref[at, :] = y
+    gate_out = pltpu.make_async_copy(gate_full, full_gate_ref, full_sems.at[0])
+    out_out = pltpu.make_async_copy(out_full, full_out_ref, full_sems.at[1])
+
+    @pl.when(step == gate_at)
+    def _():
+        for q in range(1, bits):
+            gate_advance(q)
+        gate_done()
+        gate_out.start()
+
+    @pl.when((step >= gate_at) & (step < back_at))
+    def _():
+        col = pl.multiple_of((step - gate_at) * WIDE, WIDE)
+        gate_ref[...] = dot(normed_ref[...], gate_full[:, pl.ds(col, WIDE)])
+
+    @pl.when(step == back_at)
+    def _():
+        for q in range(1, bits):
+            out_advance(q)
+        out_done()
+        out_out.start()
+
+    @pl.when(step >= back_at)
+    def _():
+        row = pl.multiple_of((step - back_at) * WIDE, WIDE)
+        back_ref[...] = dot_nt(cot_ref[...], out_full[pl.ds(row, WIDE), :])
+
+    @pl.when(step == back_at + GROUPS - 1)
+    def _():
+        gate_finish()
+        out_finish()
+        gate_out.wait()
+        out_out.wait()
+
+        @pl.when(z < seq_count - 1)
+        def _():
+            for k in range(GROUPS):
+                to_next(k).wait_send()
 
 
 def norm_kernel(
@@ -592,83 +670,84 @@
         )
 
 
-def run_states(packed, conv, head):
+def run_forward(packed, conv, head, normed, cot, gate_own, out_own):
     rows = packed.shape[0] - HALO
     blocks = rows // BLOCK
-    last = lambda j: jnp.minimum(j, GROUPS - 1)
-    whole = lambda shape: pl.BlockSpec(shape, lambda j: (0,) * len(shape))
+    count = lax.axis_size("wsh")
+    gate_at, back_at = GROUPS + CHAIN_LAG, 2 * GROUPS + CHAIN_LAG
+    at = lambda first: lambda j: jnp.clip(j - first, 0, GROUPS - 1)
+    once = pl.Buffered(1)
+    whole = lambda shape: pl.BlockSpec(shape, lambda j: (0,) * len(shape), pipeline_mode=once)
+    kept = lambda shape: pl.BlockSpec(shape, lambda j: (0,) * len(shape))
+    cols = lambda height, first: pl.BlockSpec((height, WIDE), lambda j: (0, at(first)(j)))
+    anywhere = pl.BlockSpec(memory_space=pl.ANY)
     small = jax.ShapeDtypeStruct((rows, LANES), full_type)
     small_t = jax.ShapeDtypeStruct((LANES, rows), full_type)
+    wide = jax.ShapeDtypeStruct((rows, INNER), full_type)
+    vmem = pltpu.VMEM
     return pl.pallas_call(
-        states_kernel,
-        grid=(GROUPS + CHAIN_LAG,),
+        functools.partial(forward_kernel, count),
+        grid=(back_at + GROUPS,),
         in_specs=[
-            pl.BlockSpec((rows + HALO, WIDE), lambda j: (0, last(j))),
-            pl.BlockSpec((rows + HALO, WIDE), lambda j: (0, GROUPS)),
-            pl.BlockSpec((rows + HALO, LANES), lambda j: (0, CONV_CH // LANES)),
-            pl.BlockSpec((8, WIDE), lambda j: (0, last(j))),
-            pl.BlockSpec((8, WIDE), lambda j: (0, GROUPS)),
+            cols(rows + HALO, 0),
+            pl.BlockSpec((rows + HALO, WIDE), lambda j: (0, GROUPS), pipeline_mode=once),
+            pl.BlockSpec((rows + HALO, LANES), lambda j: (0, CONV_CH // LANES), pipeline_mode=once),
+            cols(8, 0),
+            pl.BlockSpec((8, WIDE), lambda j: (0, GROUPS), pipeline_mode=once),
             whole((8, LANES)),
+            whole(normed.shape),
+            whole(cot.shape),
+            whole(gate_own.shape),
+            whole(out_own.shape),
         ],
         out_specs=[
-            pl.BlockSpec((rows, WIDE), lambda j: (0, last(j))),
-            whole((rows, WIDE)),
-            whole((rows, LANES)),
-            whole((rows, LANES)),
-            whole((LANES, rows)),
-            whole((LANES, rows)),
-            whole((rows, LANES)),
-            whole((rows, LANES)),
-            whole((rows, LANES)),
-            whole((16, LANES)),
-            pl.BlockSpec((blocks, STATE, WIDE), lambda j: (0, 0, last(j))),
-            pl.BlockSpec((STATE, WIDE), lambda j: (0, jnp.maximum(j - CHAIN_LAG, 0))),
+            cols(rows, 0),
+            kept((rows, WIDE)),
+            kept((rows, LANES)),
+            kept((LANES, rows)),
+            kept((rows, LANES)),
+            kept((rows, LANES)),
+            kept((rows, LANES)),
+            kept((16, LANES)),
+            pl.BlockSpec((blocks, STATE, WIDE), lambda j: (0, 0, at(0)(j))),
+            cols(STATE, CHAIN_LAG),
+            cols(rows, gate_at),
+            cols(rows, back_at),
+            anywhere,
+            anywhere,
         ],
         out_shape=[
-            jax.ShapeDtypeStruct((rows, INNER), full_type),
+            wide,
             jax.ShapeDtypeStruct((rows, WIDE), full_type),
-            small, small, small_t, small_t, small, small, small,
+            small, small_t, small, small, small,
             jax.ShapeDtypeStruct((16, LANES), full_type),
             jax.ShapeDtypeStruct((blocks, STATE, INNER), low_type),
             jax.ShapeDtypeStruct((STATE, INNER), low_type),
+            wide,
+            wide,
+            jax.ShapeDtypeStruct((D, INNER), low_type),
+            jax.ShapeDtypeStruct((INNER, D), low_type),
         ],
         scratch_shapes=[
-            pltpu.VMEM((rows + HALO, WIDE), full_type),
-            pltpu.VMEM((STATE, rows), low_type),
-            pltpu.VMEM((GROUPS, STATE, WIDE), full_type),
-            pltpu.VMEM((GROUPS, STATE, WIDE), low_type),
-            pltpu.VMEM((GROUPS, STATE, WIDE), low_type),
+            vmem((rows + HALO, WIDE), full_type),
+            vmem((STATE, rows), low_type),
+            vmem((blocks, BLOCK, BLOCK), full_type),
+            vmem((rows, LANES), full_type),
+            vmem((LANES, rows), full_type),
+            vmem((GROUPS, STATE, WIDE), full_type),
+            vmem((GROUPS, STATE, WIDE), low_type),
+            vmem((GROUPS, STATE, WIDE), low_type),
             pltpu.SemaphoreType.DMA((2, GROUPS)),
+            vmem((D, INNER), low_type),
+            vmem((INNER, D), low_type),
+            *gather_sems(count),
+            *gather_sems(count),
+            pltpu.SemaphoreType.DMA((2,)),
         ],
         compiler_params=pltpu.CompilerParams(collective_id=1, has_side_effects=True, vmem_limit_bytes=VMEM_LIMIT),
-        cost_estimate=pl.CostEstimate(flops=10**9, bytes_accessed=15 * 10**6, transcendentals=10**6),
-        name="scan_states",
-    )(packed, packed, packed, conv, conv, head)
-
-
-def run_outputs(x, bc, run, lag_t, enter, states, head):
-    rows = x.shape[0]
-    blocks = rows // BLOCK
-    whole = lambda shape: pl.BlockSpec(shape, lambda j: (0,) * len(shape))
-    return pl.pallas_call(
-        outputs_kernel,
-        grid=(GROUPS,),
-        in_specs=[
-            pl.BlockSpec((rows, WIDE), lambda j: (0, j)),
-            whole((rows, WIDE)),
-            whole((rows, LANES)),
-            whole((LANES, rows)),
-            whole((rows, LANES)),
-            pl.BlockSpec((blocks, STATE, WIDE), lambda j: (0, 0, j)),
-            whole((8, LANES)),
-        ],
-        out_specs=pl.BlockSpec((rows, WIDE), lambda j: (0, j)),
-        out_shape=jax.ShapeDtypeStruct((rows, INNER), full_type),
-        scratch_shapes=[pltpu.VMEM((blocks, BLOCK, BLOCK), full_type)],
-        compiler_params=pltpu.CompilerParams(vmem_limit_bytes=VMEM_LIMIT),
-        cost_estimate=pl.CostEstimate(flops=10**10, bytes_accessed=15 * 10**6, transcendentals=3 * 10**6),
-        name="scan_outputs",
-    )(x, bc, run, lag_t, enter, states, head)
+        cost_estimate=pl.CostEstimate(flops=10**11, bytes_accessed=60 * 10**6, transcendentals=4 * 10**6),
+        name="forward_scan",
+    )(packed, packed, packed, conv, conv, head, normed, cot, gate_own, out_own)
 
 
 def run_norm(y, gate, back, gain, bc, enter, state):
@@ -862,55 +941,6 @@
     )(me, left, *[piece for _, _, piece in pieces])
 
 
-def back_kernel(spots, me_ref, left_ref, *refs):
-    sources, out_ref, whole_ref = refs[: len(spots)], refs[len(spots)], refs[len(spots) + 1]
-    step = pl.program_id(0)
-    for r in sorted({r for r, _ in spots}):
-
-        @pl.when(step == r)
-        def _():
-            for source, (other, first) in zip(sources, spots):
-                if other == r:
-                    whole_ref[first : first + source.shape[0], :] = source[...]
-            out_ref[...] = dot_nt(left_ref[...], whole_ref[...])
-
-
-def multiply_back(left, pieces, count, name):
-    rows, cols = pieces[0][2].shape
-    if rows % LANES:
-        whole = jnp.zeros((rows * count, cols), low_type)
-        for r, first, piece in pieces:
-            start = lax.bitwise_xor(lax.axis_index("wsh"), r) * rows + first
-            whole = lax.dynamic_update_slice_in_dim(whole, piece, start, 0)
-        return dot_nt(left, whole), whole
-    me = jnp.reshape(lax.axis_index("wsh"), (1,)).astype(jnp.int32)
-    spots = [(r, first) for r, first, _ in pieces]
-    once = pl.Buffered(1)
-    grid_spec = pltpu.PrefetchScalarGridSpec(
-        num_scalar_prefetch=1,
-        grid=(count,),
-        in_specs=[pl.BlockSpec(left.shape, lambda j, me: (0, 0), pipeline_mode=once)]
-        + [pl.BlockSpec(piece.shape, lambda j, me: (0, 0), pipeline_mode=once) for _, _, piece in pieces],
-        out_specs=[
-            pl.BlockSpec((left.shape[0], rows), lambda j, me: (0, lax.bitwise_xor(me[0], j))),
-            pl.BlockSpec((rows, cols), lambda j, me: (lax.bitwise_xor(me[0], j), 0)),
-        ],
-    )
-    return pl.pallas_call(
-        functools.partial(back_kernel, spots),
-        grid_spec=grid_spec,
-        out_shape=[
-            jax.ShapeDtypeStruct((left.shape[0], rows * count), full_type),
-            jax.ShapeDtypeStruct((rows * count, cols), low_type),
-        ],
-        compiler_params=pltpu.CompilerParams(vmem_limit_bytes=VMEM_LIMIT),
-        cost_estimate=pl.CostEstimate(
-            flops=2 * left.shape[0] * rows * count * cols, bytes_accessed=4 * rows * count * cols, transcendentals=0
-        ),
-        name=name,
-    )(me, left, *[piece for _, _, piece in pieces])
-
-
 def sum_small(vals):
     for axis in ("wsh", "seq"):
         bit = 1
@@ -1210,9 +1240,7 @@
     )
     small = lax.all_gather(flat, "wsh", axis=0)
     part_sig = after(part_sig, small)
-    sig_pieces, marks = gather_pieces(part_sig, wsh_count)
-    gate_pieces, marks = gather_pieces(after(w_in[:, :INNER].astype(low_type), *marks), wsh_count)
-    out_pieces, marks = gather_pieces(after(w_out.astype(low_type), *marks), wsh_count)
+    sig_pieces, _ = gather_pieces(part_sig, wsh_count)
     small = small.astype(full_type)
     ends = [rows_model, rows_model + rows_inner, rows_model + rows_inner + 5 * cols_conv]
     gain_in = small[:, : ends[0]].reshape(-1)
@@ -1234,10 +1262,9 @@
     inv_rms = inv_rms[HALO:]
     normed = normed_all[HALO:]
     normed_t = normed.T
-    x, bc, run, lag, run_t, lag_t, enter, enter_all, tail, offs, states, state_in = run_states(packed, conv, head)
-    y = run_outputs(x, bc, run, lag_t, enter, states, head)
-    gate_vals, full_gate = multiply_pieces(normed, gate_pieces, wsh_count, full_type, "project_gate")
-    back, full_out = multiply_back(cot_low, out_pieces, wsh_count, "project_back")
+    (
+        y, bc, lag, run_t, enter, enter_all, tail, offs, states, state_in, gate_vals, back, full_gate, full_out
+    ) = run_forward(packed, conv, head, normed, cot_low, w_in[:, :INNER].astype(low_type), w_out.astype(low_type))
     gain_rows = jnp.broadcast_to(gain_out, (8, INNER))
     normed_out, normed_out_t, grad_y, grad_gate, part_gnorm, grad_state = run_norm(
         y, gate_vals, back, gain_rows, bc, enter_all, state_in

time: 549 us -> 495 us (0.902)
  waiting for transfers between devices: 98 us -> 37.9 us
  Pallas kernels: 346 us -> 370 us
  starting transfers between devices: 23.6 us -> 11.4 us
    ppermute x32 -> x14, waiting for transfers between devices: 98 us -> 37.9 us  [swap(): lax.ppermute(vals, axis, [(i, i ^ bit) for i in range(lax.axis_size(axis))])]
    pallas_call x3 -> x1, Pallas kernels: 56.6 us -> 101 us  [run_forward(): pl.pallas_call(functools.partial(forward_kernel, count), grid=(back_at +...]
    pallas_call x2 -> x1, Pallas kernels: 28.7 us -> 14.9 us  [multiply_pieces(): pl.pallas_call(functools.partial(piece_kernel, spots, rows), grid=(pl.cdi...]
    ppermute x32 -> x14, starting transfers between devices: 20.1 us -> 7.88 us  [swap(): lax.ppermute(vals, axis, [(i, i ^ bit) for i in range(lax.axis_size(axis))])]
    pallas_call x1, Pallas kernels: 212 us -> 205 us  [run_backward(): pl.pallas_call(functools.partial(backward_kernel, (wsh_count, seq_count),...]
  transfers between devices with their start and end apart: 33 -> 15, of which waited for: 11 -> 6; matrix products, arithmetic and copies ran while one was open for 7% -> 8% of each run, Pallas kernels for 19% -> 6%
where the time goes in v5:
time: 495 us; the launch traced here: 493 us
  Pallas kernels  370 us (75%)
  waiting for transfers between devices  37.9 us (8%)
  other arithmetic  26.5 us (5%)
  local copies, waits for them, and re-layouts  25 us (5%)
  starting transfers between devices  11.4 us (2%)
  blocking collectives  10.7 us (2%)
  matrix products  10.4 us (2%)
    pallas_call x1, Pallas kernels, run_backward(): pl.pallas_call(functools.partial(backward_kernel, (wsh_count, seq_count),...  205 us
    pallas_call x1, Pallas kernels, run_forward(): pl.pallas_call(functools.partial(forward_kernel, count), grid=(back_at +...  101 us
    ppermute x14, waiting for transfers between devices, swap(): lax.ppermute(vals, axis, [(i, i ^ bit) for i in range(lax.axis_size(axis))])  37.9 us
    pallas_call x2, Pallas kernels, adam_chunks(): pl.pallas_call(functools.partial(adam_kernel, start, rate, decay), grid=(...  31.3 us
    pallas_call x1, Pallas kernels, run_norm(): pl.pallas_call(norm_kernel, grid=(rows // part,), in_specs=[by_rows(INNER...  18.2 us
    pallas_call x1, Pallas kernels, multiply_pieces(): pl.pallas_call(functools.partial(piece_kernel, spots, rows), grid=(pl.cdi...  14.9 us
    all_gather x1, blocking collectives, shards(): small = lax.all_gather(flat, 'wsh', axis=0)  10.7 us
    dot_general x1, matrix products, dot(): lax.dot_general(left_side, right_side, (dims, ((), ())), precision=precis...  10.4 us
  transfers between devices with their start and end apart: 15, of which 6 were waited for; matrix products, arithmetic and copies ran while one was open for 8% of the time, Pallas kernels for 6%

profile of v5, /device:TPU:0, one launch (start us, length us, event | category | flops | bytes accessed | tf_op | source)
XLA Modules:
  0.0 493.3 jit_solution(3747817378255767939)
XLA Ops:
  0.7 0.7 convert.21
  1.5 0.7 convert.22
  2.3 0.7 convert.20
  2.9 0.7 convert.19
  3.7 10.7 %all-gather.1 = bf16[8,1,2688]{2,1,0:T(2,128)(2,1)S(1)} all-gather(bf16[1,1,2688]{2,1,0:T(2,128)(2,1)S(1)} %reshape.137), channel_id=2, replica_groups=mesh['seq'=4,'wsh'=8] {'wsh'}, dimensions={0}, use_global_device_ids=true | all-gather | bytes 48384 | tf_op jit(solution)/shard_map/all_gather | solution.py:1241
  14.5 2.7 convert.23
  17.1 1.4 copy-done.3
  18.7 0.1 copy.87
  18.8 1.8 concatenate.18.refs_0_
  20.6 1.5 collective-permute-start.2
  22.1 0.5 collective-permute-start.1
  22.6 3.5 collective-permute-start
  26.4 2.4 slice.103.gate_own_ref
  28.8 0.7 copy.95
  30.0 0.7 pad.13.conv_ref.conv_maps_ref
  30.7 0.6 pad.14.head_ref
  31.3 2.8 convert_element_type.40.out_own_ref
  34.1 0.7 copy.91
  34.9 0.7 copy.93
  35.6 0.4 multiply_reduce_fusion
  36.0 16.3 %collective-permute-done.2.refs_2_ = bf16[192,3456]{1,0:T(8,128)(2,1)} collective-permute-done((bf16[192,3456]{1,0:T(8,128)(2,1)}, bf16[192,3456]{1,0:T(8,128)(2,1)}, u32[]{:S(2)}, u32[]{:S(2)}) %collective-permute-start.2) | collective-permute-done | bytes 1327136 | tf_op jit(solution)/shard_map/ppermute | solution.py:889
  52.3 1.1 slice.98
  53.4 1.6 collective-permute-start.3
  55.0 1.1 slice.99
  56.1 0.6 collective-permute-start.4
  56.7 0.7 slice.84
  57.4 0.5 collective-permute-start.7
  57.9 0.4 multiply_convert_fusion.left_ref
  58.4 11.6 %collective-permute-done.3.refs_3_ = bf16[96,3456]{1,0:T(8,128)(2,1)} collective-permute-done((bf16[96,3456]{1,0:T(8,128)(2,1)S(1)}, bf16[96,3456]{1,0:T(8,128)(2,1)}, u32[]{:S(2)}, u32[]{:S(2)}) %collective-permute-start.3) | collective-permute-done | bytes 663584 | tf_op jit(solution)/shard_map/ppermute | solution.py:889
  70.0 2.4 collective-permute-done.4.refs_4_
  72.4 1.9 slice_bitcast_fusion.3
  74.2 2.6 copy.90
  76.8 2.1 maximum_convert_fusion
  79.0 14.9 %project_signal.1 = (bf16[528,3456]{1,0:T(8,128)(2,1)}, bf16[1536,3456]{1,0:T(8,128)(2,1)}) custom-call(s32[1]{0:T(128)} %bitcast.2.me_ref, bf16[528,1536]{1,0:T(8,128)(2,1)} %copy-done.4, bf16[192,3456]{1,0:T(8,128)(2,1)} %concatenate.18.refs_0_, bf16[192,3456]{1,0:T(8,128)(2,1)} %collective-permute-done.1.refs_1_, ...), custom_call_target="tpu_custom_call" | custom-call | flops 5605687296 | bytes 21233664 | tf_op jit(solution)/shard_map/project_signal/pallas_call | solution.py:923
  93.9 101.2 %forward_scan.1 = (f32[512,3072]{1,0:T(8,128)}, f32[512,256]{1,0:T(8,128)}, f32[512,128]{1,0:T(8,128)}, f32[128,512]{1,0:T(8,128)}, f32[512,128]{1,0:T(8,128)}, ...) custom-call(bf16[528,3456]{1,0:T(8,128)(2,1)} %get-tuple-element.67., ...), custom_call_target="tpu_custom_call" | custom-call | flops 99999997952 | bytes 60000000 | tf_op jit(solution)/shard_map/forward_scan/pallas_call | solution.py:688
  195.1 0.6 broadcast_in_dim.20.gain_ref
  195.8 18.2 %gated_norm.1 = (bf16[512,3072]{1,0:T(8,128)(2,1)}, bf16[3072,512]{1,0:T(8,128)(2,1)}, bf16[512,3072]{1,0:T(8,128)(2,1)}, bf16[512,3072]{1,0:T(8,128)(2,1)}, f32[8,3072]{1,0:T(8,128)}, /*index=5*/f32[128,3072]{1,0:T(8,128)}) custom-call(f32[512,3072]{1,0:T(8,128)} %get-tuple-element.68.y_ref, f32[512,3072]{1,0:T(8,128)} %get-tuple-element.69.gate_ref, ...), custom_call_target="tpu_custom_call" | custom-call | flops 1000000000 | bytes 30000000 | tf_op jit(solution)/shard_map/gated_norm/pallas_call | solution.py:758
  214.0 4.4 pad_maximum_fusion.lefts_ref
  218.4 204.7 %scan_backward.1 = (f32[512,1536]{1,0:T(8,128)}, f32[8,3328]{1,0:T(8,128)}, f32[8,3072]{1,0:T(8,128)}, f32[8,128]{1,0:T(8,128)}, bf16[25,192,384]{2,1,0:T(8,128)(2,1)}) custom-call(bf16[528,3456]{1,0:T(8,128)(2,1)} %get-tuple-element.67.sig_ref.maps_ref.raw_ref, bf16[528,3456]{1,0:T(8,128)(2,1)} %get-tuple-element.67.sig_ref.maps_ref.raw_ref, ...), custom_call_target="tpu_custom_call" | custom-call | flops 99999997952 | bytes 20000000 | tf_op jit(solution)/shard_map/scan_backward/pallas_call | solution.py:801
  423.0 0.9 reshape.132
  423.9 0.9 slice_reduce_fusion
  424.9 0.1 reduce_sum.39
  425.1 0.7 slice_bitcast_fusion.1
  425.8 0.9 slice.86
  426.7 3.8 multiply_reduce_fusion.1
  430.6 10.4 %fusion.1 = bf16[1,512,1536]{2,1,0:T(8,128)(2,1)} fusion(bf16[512,3072]{1,0:T(8,128)(2,1)} %get-tuple-element.74, bf16[3072,1536]{1,0:T(8,128)(2,1)} %get-tuple-element.75, f32[528,1536]{1,0:T(8,128)S(1)} %copy-done), kind=kOutput, calls=%fused_computation.9 | convolution fusion | flops 4833411072 | bytes 17301504 | tf_op jit(solution)/shard_map/dot_general | solution.py:44
  441.1 1.5 collective-permute-start.11
  442.6 3.5 collective-permute-done.11
  446.1 1.5 collective-permute-start.12
  447.6 2.5 add_bitcast_fusion
  450.1 0.5 collective-permute-done.12
  450.8 0.9 multiply_subtract_fusion
  451.6 3.5 collective-permute-done.13
  455.3 0.8 bitcast_convert_fusion
  456.1 0.7 copy.97
  456.8 0.7 copy.98
  457.5 0.7 copy.99
  458.2 0.7 copy.96
  458.9 9.9 %adam_w_out.1 = (f32[384,1536]{1,0:T(8,128)}, f32[384,1536]{1,0:T(8,128)}, f32[384,1536]{1,0:T(8,128)}, f32[384,1536]{1,0:T(8,128)}) custom-call(bf16[25,192,384]{2,1,0:T(8,128)(2,1)} %get-tuple-element.89.refs_0_, f32[384,1536]{1,0:T(8,128)} %refs_1_.3, f32[384,1536]{1,0:T(8,128)} %refs_2_.3, f32[384,1536]{1,0:T(8,128)} %refs_3_.3), custom_call_target="tpu_custom_call" | custom-call | flops 11796480 | bytes 17694720 | tf_op jit(solution)/shard_map/adam_w_out/pallas_call | solution.py:1200
  468.9 21.4 %adam_w_in.1 = (f32[192,6400]{1,0:T(8,128)}, f32[192,6400]{1,0:T(8,128)}, f32[192,6400]{1,0:T(8,128)}, f32[192,6400]{1,0:T(8,128)}) custom-call(bf16[25,192,384]{2,1,0:T(8,128)(2,1)} %get-tuple-element.89.refs_0_, f32[192,6400]{1,0:T(8,128)} %refs_1_.2, f32[192,6400]{1,0:T(8,128)} %refs_2_.2, f32[192,6400]{1,0:T(8,128)} %refs_3_.2), custom_call_target="tpu_custom_call" | custom-call | flops 24576000 | bytes 36864000 | tf_op jit(solution)/shard_map/adam_w_in/pallas_call | solution.py:1200
  490.6 0.7 multiply_subtract_fusion.1
  491.3 0.7 multiply_subtract_fusion.2
  492.0 0.7 add_subtract_fusion
  492.7 0.7 multiply_subtract_fusion.3
  (108 shorter events, 1.9 us)
Async XLA Ops:
  14.5 4.2 copy-start.10
  17.1 1.4 copy-start.3
  18.6 4.0 copy-start.1
  20.6 31.7 %collective-permute-start.2 = (bf16[192,3456]{1,0:T(8,128)(2,1)}, bf16[192,3456]{1,0:T(8,128)(2,1)}, u32[]{:S(2)}, u32[]{:S(2)}) collective-permute-start(bf16[192,3456]{1,0:T(8,128)(2,1)} %concatenate.18.refs_0_), channel_id=1, source_target_pairs={{0,4},{1,5},{2,6},{3,7},{4,0},{5,1},{6,2},{7,3},{8,12},{9,13},{10,... | collective-permute-start | bytes 3981320 | tf_op jit(solution)/shard_map/ppermute | solution.py:889
  22.1 32.9 %collective-permute-start.1 = (bf16[192,3456]{1,0:T(8,128)(2,1)}, bf16[192,3456]{1,0:T(8,128)(2,1)}, u32[]{:S(2)}, u32[]{:S(2)}) collective-permute-start(bf16[192,3456]{1,0:T(8,128)(2,1)} %concatenate.18.refs_0_), channel_id=1, source_target_pairs={{0,2},{1,3},{2,0},{3,1},{4,6},{5,7},{6,4},{7,5},{8,10},{9,11},{10,... | collective-permute-start | bytes 3981320 | tf_op jit(solution)/shard_map/ppermute | solution.py:889
  22.6 13.0 %collective-permute-start = (bf16[16,1536]{1,0:T(8,128)(2,1)S(1)}, bf16[16,1536]{1,0:T(8,128)(2,1)S(1)}, u32[]{:S(2)}, u32[]{:S(2)}) collective-permute-start(bf16[16,1536]{1,0:T(8,128)(2,1)S(1)} %slice_bitcast_fusion), channel_id=1, source_target_pairs={{0,8},{8,16},{16,24},{1,9},{9,17},{17,25},{2,10},{10,18},{18,26},{... | collective-permute-start | bytes 147464 | tf_op jit(solution)/shard_map/ppermute | solution.py:1256
  26.1 52.9 %collective-permute-start.5 = (bf16[192,3456]{1,0:T(8,128)(2,1)}, bf16[192,3456]{1,0:T(8,128)(2,1)}, u32[]{:S(2)}, u32[]{:S(2)}) collective-permute-start(bf16[192,3456]{1,0:T(8,128)(2,1)} %concatenate.18.refs_0_), channel_id=1, source_target_pairs={{0,1},{1,0},{2,3},{3,2},{4,5},{5,4},{6,7},{7,6},{8,9},{9,8},{10,11... | collective-permute-start | bytes 3981320 | tf_op jit(solution)/shard_map/ppermute | solution.py:889
  26.3 7.8 %copy-start.14 = (f32[192,48]{0,1:T(8,128)S(1)}, f32[192,48]{0,1:T(8,128)}, u32[]{:S(2)}) copy-start(f32[192,48]{0,1:T(8,128)} %param.34) | copy-start | bytes 110596
  26.4 8.5 %copy-start.15 = (f32[192,48]{0,1:T(8,128)S(1)}, f32[192,48]{0,1:T(8,128)}, u32[]{:S(2)}) copy-start(f32[192,48]{0,1:T(8,128)} %param.35) | copy-start | bytes 110596
  29.6 28.3 %copy-start.11 = (f32[1536]{0:T(1024)}, f32[1536]{0:T(1024)S(1)}, u32[]{:S(2)}) copy-start(f32[1536]{0:T(1024)S(1)} %mul.234) | copy-start | bytes 18436
  53.4 16.5 %collective-permute-start.3 = (bf16[96,3456]{1,0:T(8,128)(2,1)S(1)}, bf16[96,3456]{1,0:T(8,128)(2,1)}, u32[]{:S(2)}, u32[]{:S(2)}) collective-permute-start(bf16[96,3456]{1,0:T(8,128)(2,1)S(1)} %slice.98), channel_id=1, source_target_pairs={{0,2},{1,3},{2,0},{3,1},{4,6},{5,7},{6,4},{7,5},{8,10},{9,11},{10,... | collective-permute-start | bytes 1990664 | tf_op jit(solution)/shard_map/ppermute | solution.py:889
  56.1 16.2 %collective-permute-start.4 = (bf16[96,3456]{1,0:T(8,128)(2,1)S(1)}, bf16[96,3456]{1,0:T(8,128)(2,1)}, u32[]{:S(2)}, u32[]{:S(2)}) collective-permute-start(bf16[96,3456]{1,0:T(8,128)(2,1)S(1)} %slice.99), channel_id=1, source_target_pairs={{0,4},{1,5},{2,6},{3,7},{4,0},{5,1},{6,2},{7,3},{8,12},{9,13},{10,... | collective-permute-start | bytes 1990664 | tf_op jit(solution)/shard_map/ppermute | solution.py:889
  57.4 21.6 %collective-permute-start.6 = (bf16[192,3456]{1,0:T(8,128)(2,1)}, bf16[192,3456]{1,0:T(8,128)(2,1)}, u32[]{:S(2)}, u32[]{:S(2)}) collective-permute-start(bf16[192,3456]{1,0:T(8,128)(2,1)} %collective-permute-done.1.refs_1_), channel_id=1, source_target_pairs={{0,1},{1,0},{2,3},{3,2},{4,5},{5,4},{6,7},{7,6},{8,9},{9,8},{10,11... | collective-permute-start | bytes 3981320 | tf_op jit(solution)/shard_map/ppermute | solution.py:889
  57.4 21.6 %collective-permute-start.7 = (bf16[192,3456]{1,0:T(8,128)(2,1)}, bf16[192,3456]{1,0:T(8,128)(2,1)}, u32[]{:S(2)}, u32[]{:S(2)}) collective-permute-start(bf16[192,3456]{1,0:T(8,128)(2,1)} %collective-permute-done.2.refs_2_), channel_id=1, source_target_pairs={{0,1},{1,0},{2,3},{3,2},{4,5},{5,4},{6,7},{7,6},{8,9},{9,8},{10,11... | collective-permute-start | bytes 3981320 | tf_op jit(solution)/shard_map/ppermute | solution.py:889
  58.3 18.5 %copy-start.4 = (bf16[528,1536]{1,0:T(8,128)(2,1)}, bf16[528,1536]{1,0:T(8,128)(2,1)S(1)}, u32[]{:S(2)}) copy-start(bf16[528,1536]{1,0:T(8,128)(2,1)S(1)} %multiply_convert_fusion.left_ref) | copy-start | bytes 4866052
  70.0 9.0 %collective-permute-start.8 = (bf16[96,3456]{1,0:T(8,128)(2,1)}, bf16[96,3456]{1,0:T(8,128)(2,1)}, u32[]{:S(2)}, u32[]{:S(2)}) collective-permute-start(bf16[96,3456]{1,0:T(8,128)(2,1)} %collective-permute-done.3.refs_3_), channel_id=1, source_target_pairs={{0,1},{1,0},{2,3},{3,2},{4,5},{5,4},{6,7},{7,6},{8,9},{9,8},{10,11... | collective-permute-start | bytes 1990664 | tf_op jit(solution)/shard_map/ppermute | solution.py:889
  72.4 6.6 %collective-permute-start.9 = (bf16[96,3456]{1,0:T(8,128)(2,1)}, bf16[96,3456]{1,0:T(8,128)(2,1)}, u32[]{:S(2)}, u32[]{:S(2)}) collective-permute-start(bf16[96,3456]{1,0:T(8,128)(2,1)} %collective-permute-done.4.refs_4_), channel_id=1, source_target_pairs={{0,1},{1,0},{2,3},{3,2},{4,5},{5,4},{6,7},{7,6},{8,9},{9,8},{10,11... | collective-permute-start | bytes 1990664 | tf_op jit(solution)/shard_map/ppermute | solution.py:889
  195.8 18.2 %copy-start.5 = (bf16[1536,512]{1,0:T(8,128)(2,1)S(1)}, bf16[1536,512]{1,0:T(8,128)(2,1)}, u32[]{:S(2)}) copy-start(bf16[1536,512]{1,0:T(8,128)(2,1)} %copy.90) | copy-start | bytes 4718596
  218.4 208.3 %copy-start.12 = (f32[1536]{0:T(1024)S(1)}, f32[1536]{0:T(1024)}, u32[]{:S(2)}) copy-start(f32[1536]{0:T(1024)} %copy-done.11) | copy-start | bytes 18436
  218.4 208.4 %copy-start.16 = (f32[512]{0:T(512)S(1)}, f32[512]{0:T(512)}, u32[]{:S(2)}) copy-start(f32[512]{0:T(512)} %slice.84) | copy-start | bytes 6148
  426.7 3.9 copy-start
  430.6 10.5 %collective-permute-start.10 = (f32[21392]{0:T(1024)S(1)}, f32[21392]{0:T(1024)S(1)}, u32[]{:S(2)}, u32[]{:S(2)}) collective-permute-start(f32[21392]{0:T(1024)S(1)} %concatenate.20), channel_id=1, source_target_pairs={{0,1},{1,0},{2,3},{3,2},{4,5},{5,4},{6,7},{7,6},{8,9},{9,8},{10,11... | collective-permute-start | bytes 256712 | tf_op jit(solution)/shard_map/ppermute | solution.py:889
  430.6 16.9 %copy-start.2 = (f32[512,1536]{1,0:T(8,128)S(1)}, f32[512,1536]{1,0:T(8,128)}, u32[]{:S(2)}) copy-start(f32[512,1536]{1,0:T(8,128)} %get-tuple-element.88) | copy-start | bytes 9437188
  430.6 16.9 %copy-start.6 = (bf16[1,512,1536]{2,1,0:T(8,128)(2,1)S(1)}, bf16[1,512,1536]{2,1,0:T(8,128)(2,1)}, u32[]{:S(2)}) copy-start(bf16[1,512,1536]{2,1,0:T(8,128)(2,1)} %param.24) | copy-start | bytes 4718596
  441.1 5.0 %collective-permute-start.11 = (f32[21392]{0:T(1024)S(1)}, f32[21392]{0:T(1024)S(1)}, u32[]{:S(2)}, u32[]{:S(2)}) collective-permute-start(f32[21392]{0:T(1024)S(1)} %add.131), channel_id=1, source_target_pairs={{0,2},{1,3},{2,0},{3,1},{4,6},{5,7},{6,4},{7,5},{8,10},{9,11},{10,... | collective-permute-start | bytes 256712 | tf_op jit(solution)/shard_map/ppermute | solution.py:889
  446.1 4.7 copy-start.7
  446.1 4.7 copy-start.8
  446.1 4.7 copy-start.9
  446.1 4.6 collective-permute-start.12
  450.6 4.6 collective-permute-start.13
  455.2 35.2 %collective-permute-start.14 = (f32[21392]{0:T(1024)S(1)}, f32[21392]{0:T(1024)S(1)}, u32[]{:S(2)}, u32[]{:S(2)}) collective-permute-start(f32[21392]{0:T(1024)S(1)} %add.134), channel_id=1, source_target_pairs={{0,16},{8,24},{16,0},{24,8},{1,17},{9,25},{17,1},{25,9},{2,18},{10... | collective-permute-start | bytes 256712 | tf_op jit(solution)/shard_map/ppermute | solution.py:889
  468.8 21.8 %copy-start.13 = (f32[5,416]{1,0:T(8,128)S(1)}, f32[5,416]{1,0:T(8,128)}, u32[]{:S(2)}) copy-start(f32[5,416]{1,0:T(8,128)} %param.30) | copy-start | bytes 24964
  468.8 21.8 %copy-start.17 = (f32[5,416]{1,0:T(8,128)S(1)}, f32[5,416]{1,0:T(8,128)}, u32[]{:S(2)}) copy-start(f32[5,416]{1,0:T(8,128)} %param.42) | copy-start | bytes 24964
  468.8 21.8 %copy-start.18 = (f32[5,416]{1,0:T(8,128)S(1)}, f32[5,416]{1,0:T(8,128)}, u32[]{:S(2)}) copy-start(f32[5,416]{1,0:T(8,128)} %param.43) | copy-start | bytes 24964
  468.8 22.5 %copy-start.19 = (f32[384]{0:T(512)S(1)}, f32[384]{0:T(512)}, u32[]{:S(2)}) copy-start(f32[384]{0:T(512)} %param.29) | copy-start | bytes 4612
  468.8 22.5 %copy-start.21 = (f32[384]{0:T(512)S(1)}, f32[384]{0:T(512)}, u32[]{:S(2)}) copy-start(f32[384]{0:T(512)} %param.40) | copy-start | bytes 4612
  468.8 22.4 %copy-start.22 = (f32[384]{0:T(512)S(1)}, f32[384]{0:T(512)}, u32[]{:S(2)}) copy-start(f32[384]{0:T(512)} %param.41) | copy-start | bytes 4612
  468.9 23.1 %copy-start.20 = (f32[3,6]{1,0:T(4,128)S(1)}, f32[3,6]{1,0:T(4,128)}, u32[]{:S(2)}) copy-start(f32[3,6]{1,0:T(4,128)} %param.31) | copy-start | bytes 220
  468.9 23.1 %copy-start.23 = (f32[3,6]{1,0:T(4,128)S(1)}, f32[3,6]{1,0:T(4,128)}, u32[]{:S(2)}) copy-start(f32[3,6]{1,0:T(4,128)} %param.44) | copy-start | bytes 220
  468.9 23.1 %copy-start.24 = (f32[3,6]{1,0:T(4,128)S(1)}, f32[3,6]{1,0:T(4,128)}, u32[]{:S(2)}) copy-start(f32[3,6]{1,0:T(4,128)} %param.45) | copy-start | bytes 220
  468.9 23.8 %copy-start.25 = (f32[192]{0:T(256)S(1)}, f32[192]{0:T(256)}, u32[]{:S(2)}) copy-start(f32[192]{0:T(256)} %param.28) | copy-start | bytes 2308
  468.9 23.8 %copy-start.26 = (f32[192]{0:T(256)S(1)}, f32[192]{0:T(256)}, u32[]{:S(2)}) copy-start(f32[192]{0:T(256)} %param.38) | copy-start | bytes 2308
  468.9 23.8 %copy-start.27 = (f32[192]{0:T(256)S(1)}, f32[192]{0:T(256)}, u32[]{:S(2)}) copy-start(f32[192]{0:T(256)} %param.39) | copy-start | bytes 2308

commit v6 on v5

--- a/solution.py
+++ b/solution.py
@@ -21,7 +21,7 @@
 HALO = 16
 GROUPS = INNER // WIDE
 CHAIN_LAG = 2
-AHEAD = 6
+CHAIN_PER = 2
 PACK = CONV_CH + LANES
 LOG2E = 1.4426950408889634
 VMEM_LIMIT = 56 * 1024 * 1024
@@ -100,17 +100,19 @@
     return rows >= cols if lower else rows <= cols
 
 
-def gather_steps(count, own_ref, full_ref, far_sems, core_sems):
+def gather_steps(count, own_ref, full_ref, far_sems, core_sems, cols=None, split=True):
     orders = part_orders(count)
     bits = len(orders)
+    orders = orders if split else orders[:1]
     rows = own_ref.shape[0]
-    part = rows // bits
+    part = rows // len(orders)
+    cols = cols or (0, own_ref.shape[1])
     me = lax.axis_index("wsh")
     mesh_id = pl.DeviceIdType.MESH
 
     def copy(m, first, size, bit, sems, n):
         start = lax.bitwise_xor(me, 2 * m) * rows + first
-        at = full_ref.at[pl.ds(pl.multiple_of(start, 16), size)]
+        at = full_ref.at[pl.ds(pl.multiple_of(start, 16), size), pl.ds(*cols)]
         return pltpu.make_async_remote_copy(
             src_ref=at, dst_ref=at, send_sem=sems.at[0, n], recv_sem=sems.at[1, n],
             device_id={"wsh": lax.bitwise_xor(me, bit)}, device_id_type=mesh_id,
@@ -137,7 +139,7 @@
     ]
 
     def start():
-        full_ref[pl.ds(pl.multiple_of(me * rows, 16), rows), :] = own_ref[...]
+        full_ref[pl.ds(pl.multiple_of(me * rows, 16), rows), pl.ds(*cols)] = own_ref[:, pl.ds(*cols)]
         for item in pick(far_spots, far_sems, 0) + pick(core_spots, core_sems, 0):
             item.start()
 
@@ -159,10 +161,108 @@
     return start, advance, done, finish
 
 
-def gather_sems(count):
+def gather_sems(count, split=True):
     bits = len(part_orders(count))
-    copies = bits * ((1 << bits) - 1)
+    copies = (bits if split else 1) * ((1 << bits) - 1)
     return [pltpu.SemaphoreType.DMA((2, copies)), pltpu.SemaphoreType.DMA((2, copies + 1))]
+
+
+def signal_kernel(
+    count, tokens_ref, own_ref, small_ref,
+    packed_ref, normed_ref, inv_ref, gain_in_ref, gain_out_ref, conv_ref, head_ref, full_ref,
+    normed, full, small_full, small_far, small_core, out_sems, *sems,
+):
+    bits = len(part_orders(count))
+    pieces = len(sems) // 2
+    width = own_ref.shape[1] // pieces
+    small_start, small_advance, small_done, small_finish = gather_steps(
+        count, small_ref, small_full, small_far, small_core, split=False
+    )
+    gathers = [
+        gather_steps(count, own_ref, full, sems[2 * c], sems[2 * c + 1], cols=(c * width, width)) for c in range(pieces)
+    ]
+    greet()
+    small_start()
+    for start, _, _, _ in gathers:
+        start()
+    for q in range(bits):
+        small_advance(q)
+    small_done()
+    height = small_ref.shape[0]
+    small = small_full[:height, :].astype(full_type)
+    for d in range(1, count):
+        small = small + small_full[d * height : (d + 1) * height, :].astype(full_type)
+    gain_in_ref[...] = jnp.broadcast_to(small[0:1, :D], gain_in_ref.shape)
+    gain_out_ref[...] = jnp.broadcast_to(small[1:2, :INNER], gain_out_ref.shape)
+    conv_ref[...] = jnp.concatenate([small[2:7], jnp.zeros((3, CONV_CH), full_type)], axis=0)
+    head_ref[...] = jnp.concatenate([small[7:10, :LANES], jnp.zeros((5, LANES), full_type)], axis=0)
+    gathers[0][1](0)
+    all_rows = tokens_ref.shape[0]
+    for first in range(0, all_rows, BLOCK):
+        size = min(BLOCK, all_rows - first)
+        tokens = tokens_ref[first : first + size, :].astype(full_type)
+        inv = lax.rsqrt(jnp.sum(tokens * tokens, axis=1, keepdims=True) * (1.0 / D) + norm_eps)
+        low = (tokens * inv * gain_in_ref[0:1, :]).astype(low_type)
+        normed[first : first + size, :] = low
+        skip = max(HALO - first, 0)
+        at = slice(first + skip - HALO, first + size - HALO)
+        normed_ref[at, :] = low[skip:]
+        inv_ref[at, :] = jnp.broadcast_to(inv[skip:], (size - skip, LANES))
+    for _, advance, _, _ in gathers[1:]:
+        advance(0)
+    outs = []
+    for c, (_, advance, done, _) in enumerate(gathers):
+        for q in range(1, bits):
+            advance(q)
+        done()
+        cols = pl.ds(c * width, width)
+        outs.append(pltpu.make_async_copy(full.at[:, cols], full_ref.at[:, cols], out_sems.at[c]))
+        outs[-1].start()
+
+        def multiply(t, carry, c=c):
+            col = pl.multiple_of(c * width + t * TILE, LANES)
+            packed_ref[:, pl.ds(col, TILE)] = dot(normed[...], full[:, pl.ds(col, TILE)]).astype(low_type)
+            return carry
+
+        lax.fori_loop(0, width // TILE, multiply, 0)
+    for out in outs:
+        out.wait()
+    small_finish()
+    for _, _, _, finish in gathers:
+        finish()
+
+
+def project_signal(tokens, own, small):
+    count = lax.axis_size("wsh")
+    all_rows = tokens.shape[0]
+    rows = all_rows - HALO
+    pieces = 3
+    vmem = pl.BlockSpec(memory_space=pltpu.VMEM)
+    wide = lambda cols: jax.ShapeDtypeStruct((8, cols), full_type)
+    sems = [sem for _ in range(pieces) for sem in gather_sems(count)]
+    return pl.pallas_call(
+        functools.partial(signal_kernel, count),
+        in_specs=[vmem] * 3,
+        out_specs=[vmem] * 7 + [pl.BlockSpec(memory_space=pl.ANY)],
+        out_shape=[
+            jax.ShapeDtypeStruct((all_rows, PACK), low_type),
+            jax.ShapeDtypeStruct((rows, D), low_type),
+            jax.ShapeDtypeStruct((rows, LANES), full_type),
+            wide(D), wide(INNER), wide(CONV_CH), wide(LANES),
+            jax.ShapeDtypeStruct((D, PACK), low_type),
+        ],
+        scratch_shapes=[
+            pltpu.VMEM((all_rows, D), low_type),
+            pltpu.VMEM((D, PACK), low_type),
+            pltpu.VMEM((count * small.shape[0], CONV_CH), low_type),
+            *gather_sems(count, split=False),
+            pltpu.SemaphoreType.DMA((pieces,)),
+            *sems,
+        ],
+        compiler_params=pltpu.CompilerParams(collective_id=0, has_side_effects=True, vmem_limit_bytes=VMEM_LIMIT),
+        cost_estimate=pl.CostEstimate(flops=6 * 10**10, bytes_accessed=30 * 10**6, transcendentals=0),
+        name="project_signal",
+    )(tokens, own, small)
 
 
 def forward_kernel(
@@ -325,8 +425,8 @@
 
 
 def norm_kernel(
-    y_ref, gate_ref, back_ref, gain_ref, bc_ref, enter_ref, state_ref,
-    normed_ref, normed_t_ref, grad_y_ref, grad_gate_ref, grad_gain_ref, grad_state_ref,
+    y_ref, gate_ref, back_ref, gain_ref, bc_ref, enter_ref, state_ref, inner_ref,
+    normed_ref, lefts_ref, grad_y_ref, grad_gate_ref, grad_gain_ref, grad_state_ref,
     gated, low_y,
 ):
     step = pl.program_id(0)
@@ -337,6 +437,8 @@
         grad_gain_ref[...] = jnp.zeros(grad_gain_ref.shape, full_type)
         grad_state_ref[...] = jnp.zeros(grad_state_ref.shape, full_type)
 
+    for j in range(D // WIDE):
+        lefts_ref[INNER + j * WIDE : INNER + (j + 1) * WIDE, :] = inner_ref[:, j * WIDE : (j + 1) * WIDE].T
     out_map = bc_ref[:, STATE:]
     out_low = out_map.astype(low_type)
     out_t = out_map.T.astype(low_type)
@@ -363,7 +465,7 @@
         scaled = vals * inv
         normed = (scaled * gain).astype(low_type)
         normed_ref[:, at] = normed
-        normed_t_ref[at, :] = normed.T
+        lefts_ref[at, :] = normed.T
         grad_gain_ref[0:1, at] += jnp.sum(back * scaled, axis=0, keepdims=True)
         grad_vals = back * gain * inv - vals * pull
         gate = gate_ref[:, at]
@@ -377,6 +479,10 @@
         grad_state_ref[:, at] += dot(out_t, (grad_y.astype(full_type) * enter).astype(low_type))
 
 
+def steps_ahead(seq_count):
+    return GROUPS // CHAIN_PER + seq_count - 1
+
+
 def backward_kernel(
     counts, spans,
     sig_ref, raw_ref, conv_ref, head_ref, grad_y_ref, bc_ref,
@@ -387,9 +493,10 @@
     stage, land, chain_sems, grad_pack, lasts, edges, edge_land, edge_sems, grad_normed, weights, weight_sems, done_sems,
     *scratch,
 ):
+    ahead = steps_ahead(counts[1])
     place = pl.program_id(0)
-    step = place - AHEAD
-    steps = GROUPS + 2 + AHEAD
+    step = place - ahead
+    steps = GROUPS + 2 + ahead
     rows = grad_y_ref.shape[0]
     blocks = rows // BLOCK
     z = lax.axis_index("seq")
@@ -405,22 +512,34 @@
             copy = pltpu.make_async_copy(ref.at[:, pl.ds(col, TILE)], weights.at[slot], weight_sems.at[slot])
             yield (k >= first) & (k < last), copy
 
-    def beside(k, tile):
+    def add_normed(k, right_ref, first):
+        col = pl.multiple_of((k - first) * TILE, LANES)
         for right, copy in weight_copies(k):
             pl.when(right)(copy.wait)
         for right, copy in weight_copies(k + 1):
             pl.when(right)(copy.start)
 
+        part = dot_nt(right_ref[:, pl.ds(col, TILE)], weights[lax.rem(k, 2)])
+
         @pl.when(k == first_gate)
         def _():
-            grad_normed[...] = dot_nt(tile[...], weights[lax.rem(k, 2)])
+            grad_normed[...] = part
 
         @pl.when(k > first_gate)
         def _():
-            grad_normed[...] += dot_nt(tile[...], weights[lax.rem(k, 2)])
+            grad_normed[...] += part
+
+    def late_turn(s, carry):
+        turn(s, 0)
+        per = -(-(chunks - first_gate) // (turns - early))
+        for i in range(per):
+            k = first_gate + (s - early) * per + i
+            pl.when(k < first_sig)(lambda k=k: add_normed(k, grad_gate_ref, first_gate))
+            pl.when((k >= first_sig) & (k < chunks))(lambda k=k: add_normed(k, grad_pack, first_sig))
+        return carry
 
     turns, turn, finish = reduce_turns(
-        *counts, spans, lefts_ref, [cot_ref, grad_gate_ref, grad_pack], sums_ref, scratch, beside
+        *counts, spans, lefts_ref, [cot_ref, grad_gate_ref, grad_pack], sums_ref, scratch
     )
 
     def to_previous(k):
@@ -466,6 +585,7 @@
     @pl.when(place == 0)
     def _():
         greet()
+        next(copy for _, copy in weight_copies(first_gate)).start()
 
     @pl.when((step >= 1) & (step <= GROUPS + 1))
     def _():
@@ -474,7 +594,7 @@
     early = chunks - 1
     for i in range(spans[2][1] - 1):
         at = next(p for p in range(steps) if (p + 1) * early // steps > first_sig + i)
-        assert AHEAD + ((i + 1) * TILE - 1) // WIDE + 1 <= at
+        assert ahead + ((i + 1) * TILE - 1) // WIDE + 1 <= at
 
     @pl.when(place < steps)
     def _():
@@ -482,14 +602,16 @@
 
     upper = triangle(False)
 
-    @pl.when(place < AHEAD)
-    def _():
-        for i in range(GROUPS // AHEAD):
-            chain(place * (GROUPS // AHEAD) + i)
+    turn_of = place - (seq_count - 1 - z)
+
+    @pl.when((turn_of >= 0) & (turn_of < GROUPS // CHAIN_PER))
+    def _():
+        for i in range(CHAIN_PER):
+            chain(turn_of * CHAIN_PER + i)
 
     @pl.when(place == steps)
     def _():
-        lax.fori_loop(early, turns, turn, 0)
+        lax.fori_loop(early, turns, late_turn, 0)
         normed_copy = pltpu.make_async_copy(grad_normed, grad_normed_ref, done_sems.at[0])
         normed_copy.start()
         finish()
@@ -750,7 +872,7 @@
     )(packed, packed, packed, conv, conv, head, normed, cot, gate_own, out_own)
 
 
-def run_norm(y, gate, back, gain, bc, enter, state):
+def run_norm(y, gate, back, gain, bc, enter, state, normed):
     rows = y.shape[0]
     part = BLOCK
     by_rows = lambda cols: pl.BlockSpec((part, cols), lambda i: (i, 0))
@@ -760,15 +882,15 @@
         grid=(rows // part,),
         in_specs=[
             by_rows(INNER), by_rows(INNER), by_rows(INNER), whole((8, INNER)),
-            by_rows(WIDE), by_rows(LANES), whole((STATE, INNER)),
+            by_rows(WIDE), by_rows(LANES), whole((STATE, INNER)), by_rows(D),
         ],
         out_specs=[
-            by_rows(INNER), pl.BlockSpec((INNER, part), lambda i: (0, i)), by_rows(INNER), by_rows(INNER),
+            by_rows(INNER), pl.BlockSpec((INNER + D, part), lambda i: (0, i)), by_rows(INNER), by_rows(INNER),
             whole((8, INNER)), whole((STATE, INNER)),
         ],
         out_shape=[
             jax.ShapeDtypeStruct((rows, INNER), low_type),
-            jax.ShapeDtypeStruct((INNER, rows), low_type),
+            jax.ShapeDtypeStruct((INNER + D, rows), low_type),
             jax.ShapeDtypeStruct((rows, INNER), low_type),
             jax.ShapeDtypeStruct((rows, INNER), low_type),
             jax.ShapeDtypeStruct((8, INNER), full_type),
@@ -778,7 +900,7 @@
         compiler_params=pltpu.CompilerParams(vmem_limit_bytes=VMEM_LIMIT),
         cost_estimate=pl.CostEstimate(flops=10**9, bytes_accessed=30 * 10**6, transcendentals=3 * 10**6),
         name="gated_norm",
-    )(y, gate, back, gain, bc, enter, state)
+    )(y, gate, back, gain, bc, enter, state, normed)
 
 
 def run_backward(
@@ -794,13 +916,14 @@
     spans = [(0, n_out, groups, 0), (first_gate, n_gate, 1, INNER), (first_sig, n_sig, 1, INNER)]
     chunks = first_sig + n_sig
     anywhere = pl.BlockSpec(memory_space=pl.ANY)
-    low_at = lambda j, top: jnp.clip(j - AHEAD, 0, top)
+    ahead = steps_ahead(seq_count)
+    low_at = lambda j, top: jnp.clip(j - ahead, 0, top)
     once = pl.Buffered(1)
     whole = lambda shape: pl.BlockSpec(shape, lambda j: (0,) * len(shape), pipeline_mode=once)
     kept = lambda shape: pl.BlockSpec(shape, lambda j: (0,) * len(shape))
     return pl.pallas_call(
         functools.partial(backward_kernel, (wsh_count, seq_count), spans),
-        grid=(GROUPS + 3 + AHEAD,),
+        grid=(GROUPS + 3 + ahead,),
         in_specs=[
             pl.BlockSpec((rows + HALO, WIDE), lambda j: (0, low_at(j, GROUPS))),
             pl.BlockSpec((rows + HALO, LANES), lambda j: (0, CONV_CH // LANES), pipeline_mode=once),
@@ -872,81 +995,25 @@
 
 def adam_update(weights, gradient, first_moment, second_moment, step_rate, decay_amount):
     next_first = beta_one * first_moment + (1.0 - beta_one) * gradient
-    next_second = beta_two * second_moment + (1.0 - beta_two) * gradient * gradient
-    corrected = (
-        next_first
-        / (1.0 - beta_one**STEP)
-        / (jnp.sqrt(next_second / (1.0 - beta_two**STEP)) + adam_eps)
-    )
-    return (weights - step_rate * (corrected + decay_amount * weights), next_first, next_second)
-
-
-def pad_rows(vals, rows):
-    return jnp.pad(vals, ((0, rows - vals.shape[0]), (0, 0)))
+    next_second = beta_two * second_moment + (1.0 - beta_two) * (gradient * gradient)
+    spread = jnp.sqrt(next_second * (1.0 / (1.0 - beta_two**STEP))) + adam_eps
+    change = next_first * (step_rate / (1.0 - beta_one**STEP)) / spread
+    return (weights * (1.0 - step_rate * decay_amount) - change, next_first, next_second)
 
 
 def swap(vals, bit, axis="wsh"):
     return lax.ppermute(vals, axis, [(i, i ^ bit) for i in range(lax.axis_size(axis))])
 
 
-def gather_pieces(own, count, also=None):
-    rows = own.shape[0]
-    far = [1 << b for b in range(1, count.bit_length() - 1)]
-    pieces = [(0, 0, own)]
-    if len(far) == 2:
-        one, two = far
-        half = rows // 2
-        by_one = swap(own, one)
-        by_two = swap(own, two)
-        pieces += [(one, 0, by_one), (two, 0, by_two)]
-        pieces += [(one | two, 0, swap(by_two[:half], one)), (one | two, half, swap(by_one[half:], two))]
-    else:
-        for bit in far:
-            pieces += [(r ^ bit, first, swap(piece, bit)) for r, first, piece in pieces]
-    marks = [piece for _, _, piece in pieces[-2:]]
-    return pieces + [(r ^ 1, first, swap(piece, 1)) for r, first, piece in pieces], marks
-
-
-def piece_kernel(spots, rows, me_ref, left_ref, *refs):
-    sources, out_ref, whole_ref = refs[: len(spots)], refs[len(spots)], refs[len(spots) + 1]
-    for source, (r, first) in zip(sources, spots):
-        start = lax.bitwise_xor(me_ref[0], r) * rows + first
-        whole_ref[pl.ds(pl.multiple_of(start, 16), source.shape[0]), :] = source[...]
-    out_ref[...] = dot(left_ref[...], whole_ref[...]).astype(out_ref.dtype)
-
-
-def multiply_pieces(left, pieces, count, out_type, name):
-    rows, cols = pieces[0][2].shape
-    tile = 512
-    me = jnp.reshape(lax.axis_index("wsh"), (1,)).astype(jnp.int32)
-    spots = [(r, first) for r, first, _ in pieces]
-    return pl.pallas_call(
-        functools.partial(piece_kernel, spots, rows),
-        grid=(pl.cdiv(cols, tile),),
-        in_specs=[pl.BlockSpec(memory_space=pltpu.SMEM), pl.BlockSpec(left.shape, lambda j: (0, 0))]
-        + [pl.BlockSpec((piece.shape[0], tile), lambda j: (0, j)) for _, _, piece in pieces],
-        out_specs=[
-            pl.BlockSpec((left.shape[0], tile), lambda j: (0, j)),
-            pl.BlockSpec((rows * count, tile), lambda j: (0, j)),
-        ],
-        out_shape=[
-            jax.ShapeDtypeStruct((left.shape[0], cols), out_type),
-            jax.ShapeDtypeStruct((rows * count, cols), low_type),
-        ],
-        compiler_params=pltpu.CompilerParams(vmem_limit_bytes=VMEM_LIMIT),
-        cost_estimate=pl.CostEstimate(
-            flops=2 * left.shape[0] * rows * count * cols, bytes_accessed=4 * rows * count * cols, transcendentals=0
-        ),
-        name=name,
-    )(me, left, *[piece for _, _, piece in pieces])
-
-
-def sum_small(vals):
-    for axis in ("wsh", "seq"):
-        bit = 1
-        while bit < lax.axis_size(axis):
-            vals = vals + swap(vals, bit, axis)
-            bit = 2 * bit
+def sum_small(vals, beside):
+    hops = [
+        (axis, 1 << b) for axis in ("wsh", "seq") for b in range(lax.axis_size(axis).bit_length() - 1)
+    ]
+    for i, (axis, bit) in enumerate(hops):
+        got = swap(vals, bit, axis)
+        if i < len(beside):
+            got = after(got, beside[i])
+        vals = vals + got
     return vals
 
 
@@ -990,7 +1057,7 @@
     pl.semaphore_wait(barrier, bits + along)
 
 
-def reduce_turns(wsh_count, seq_count, spans, left_ref, right_refs, out_ref, scratch, beside):
+def reduce_turns(wsh_count, seq_count, spans, left_ref, right_refs, out_ref, scratch):
     orders = part_orders(wsh_count)
     bits = len(orders)
     tile, stage, pair, *rest = scratch
@@ -1070,7 +1137,6 @@
         for b in range(blocks):
             stage[lax.rem(k, 2), b] = product(k, b, 1).astype(low_type)
         pair_copy(k).start()
-        beside(k, tile)
 
     def add_pair(k):
         take_tile(k)
@@ -1183,24 +1249,26 @@
     ]
 
 
-def adam_kernel(start, rate, decay, *refs):
-    share_ref, weight_ref, first_ref, second_ref, grad_ref, next_ref, next_first_ref, next_second_ref = refs
-    grad = share_ref[0].astype(full_type)
-    grad_ref[...] = grad
-    next_ref[...], next_first_ref[...], next_second_ref[...] = adam_update(
-        weight_ref[...], grad, first_ref[...], second_ref[...], rate, decay
-    )
+def adam_kernel(rate, decay, share_ref, weight_ref, first_ref, second_ref, *outs):
+    grad_ref, next_ref, next_first_ref, next_second_ref = outs
+    for i in range(share_ref.shape[0]):
+        at = slice(i * TILE, (i + 1) * TILE)
+        grad = share_ref[i].astype(full_type)
+        grad_ref[:, at] = grad
+        next_ref[:, at], next_first_ref[:, at], next_second_ref[:, at] = adam_update(
+            weight_ref[:, at], grad, first_ref[:, at], second_ref[:, at], rate, decay
+        )
 
 
 def adam_chunks(sums, start, weights, first_moment, second_moment, rate, decay, name):
     all_rows, cols = weights.shape
     rows = sums.shape[1]
-    tiles = pl.cdiv(cols, TILE)
-    block = pl.BlockSpec((rows, TILE), lambda i, j: (i, j))
+    tiles = pl.cdiv(cols, 2 * TILE)
+    block = pl.BlockSpec((rows, 2 * TILE), lambda i, j: (i, j))
     return pl.pallas_call(
-        functools.partial(adam_kernel, start, rate, decay),
+        functools.partial(adam_kernel, rate, decay),
         grid=(all_rows // rows, tiles),
-        in_specs=[pl.BlockSpec((1, rows, TILE), lambda i, j: (start + i * tiles + j, 0, 0))] + [block] * 3,
+        in_specs=[pl.BlockSpec((2, rows, TILE), lambda i, j: (start // 2 + i * tiles + j, 0, 0))] + [block] * 3,
         out_specs=[block] * 4,
         out_shape=[jax.ShapeDtypeStruct(weights.shape, full_type)] * 4,
         compiler_params=pltpu.CompilerParams(vmem_limit_bytes=VMEM_LIMIT),
@@ -1229,48 +1297,30 @@
     rows_inner = INNER // wsh_count
     cols_conv = CONV_CH // wsh_count
     cols_head = HEADS // wsh_count
-    flat = jnp.concatenate(
-        [gain_pre, gain_norm, conv_param.reshape(-1), head_param.reshape(-1)]
-    ).astype(low_type)
-    count = flat.shape[0]
-    flat = jnp.pad(flat, (0, -count % LANES))
+    small = jnp.zeros((16, CONV_CH), full_type)
+    for row, part in ((0, gain_pre[None]), (1, gain_norm[None]), (2, conv_param), (7, head_param)):
+        small = lax.dynamic_update_slice(small, part, (row, wsh_index * part.shape[1]))
     part_sig = jnp.concatenate(
         [w_in[:, INNER:].astype(low_type), w_dt.astype(low_type), jnp.zeros((rows_model, LANES - HEADS), low_type)],
         axis=1,
     )
-    small = lax.all_gather(flat, "wsh", axis=0)
-    part_sig = after(part_sig, small)
-    sig_pieces, _ = gather_pieces(part_sig, wsh_count)
-    small = small.astype(full_type)
-    ends = [rows_model, rows_model + rows_inner, rows_model + rows_inner + 5 * cols_conv]
-    gain_in = small[:, : ends[0]].reshape(-1)
-    gain_out = small[:, ends[0] : ends[1]].reshape(1, -1)
-    conv = small[:, ends[1] : ends[2]].reshape(wsh_count, 5, cols_conv).transpose(1, 0, 2).reshape(5, CONV_CH)
-    head = small[:, ends[2] : ends[2] + 3 * cols_head].reshape(wsh_count, 3, cols_head)
-    head = head.transpose(1, 0, 2).reshape(3, HEADS)
-    conv = pad_rows(conv, 8)
-    head = jnp.pad(head, ((0, 5), (0, LANES - HEADS)))
     tokens_low = inputs[0]
     cot_low = cotangent[0]
     rows = tokens_low.shape[0]
     before = lax.ppermute(tokens_low[rows - HALO :], "seq", [(i, i + 1) for i in range(seq_count - 1)])
-    tokens = jnp.concatenate([before, tokens_low], axis=0).astype(full_type)
-    inv_rms = lax.rsqrt(jnp.mean(tokens * tokens, axis=-1, keepdims=True) + norm_eps)
-    normed_all = (tokens * inv_rms * gain_in).astype(low_type)
-    packed, full_sig = multiply_pieces(normed_all, sig_pieces, wsh_count, low_type, "project_signal")
-    tokens = tokens[HALO:]
-    inv_rms = inv_rms[HALO:]
-    normed = normed_all[HALO:]
-    normed_t = normed.T
+    packed, normed, inv_wide, gain_in_rows, gain_rows, conv, head, full_sig = project_signal(
+        jnp.concatenate([before, tokens_low], axis=0), part_sig, small.astype(low_type)
+    )
+    tokens = tokens_low.astype(full_type)
+    inv_rms = inv_wide[:, :1]
+    gain_in = gain_in_rows[0]
     (
         y, bc, lag, run_t, enter, enter_all, tail, offs, states, state_in, gate_vals, back, full_gate, full_out
     ) = run_forward(packed, conv, head, normed, cot_low, w_in[:, :INNER].astype(low_type), w_out.astype(low_type))
-    gain_rows = jnp.broadcast_to(gain_out, (8, INNER))
-    normed_out, normed_out_t, grad_y, grad_gate, part_gnorm, grad_state = run_norm(
-        y, gate_vals, back, gain_rows, bc, enter_all, state_in
+    normed_out, lefts, grad_y, grad_gate, part_gnorm, grad_state = run_norm(
+        y, gate_vals, back, gain_rows, bc, enter_all, state_in, normed
     )
     block_out = (tokens + dot(normed_out, full_out)).astype(low_type)[None]
-    lefts = jnp.concatenate([normed_out_t, normed_t], axis=0)
     grad_normed, part_conv, part_skip, part_head, sums = run_backward(
         packed, conv, head, grad_y, bc, lag, run_t, enter, tail, offs, states, state_in, grad_state,
         lefts, cot_low, grad_gate, full_gate, full_sig,
@@ -1284,7 +1334,14 @@
     small_parts = [
         part_gpre, part_gnorm[0], part_conv[:5].reshape(-1), part_head[0, :HEADS], part_head[1, :HEADS], skip_sums
     ]
-    small_sums = sum_small(jnp.concatenate(small_parts))
+    tiles_out = (INNER // D) * (D // TILE)
+    grad_out, *new_out = adam_chunks(sums, 0, w_out, first_w_out, second_w_out, rate_matrix, weight_decay, "adam_w_out")
+    grad_in_w, *new_in = adam_chunks(
+        sums, tiles_out, w_in, first_w_in, second_w_in, rate_matrix, weight_decay, "adam_w_in"
+    )
+    at_dt = CONV_CH % TILE
+    grad_dt = sums[-1, :, at_dt : at_dt + HEADS].astype(full_type)
+    small_sums = sum_small(jnp.concatenate(small_parts), [block_out, new_out[0], new_in[0]])
     cuts = [D, D + INNER, D + INNER + 5 * CONV_CH]
     grad_gpre = lax.dynamic_slice_in_dim(small_sums[: cuts[0]], wsh_index * rows_model, rows_model, 0)
     grad_gnorm = lax.dynamic_slice_in_dim(small_sums[cuts[0] : cuts[1]], wsh_index * rows_inner, rows_inner, 0)
@@ -1294,13 +1351,6 @@
     grad_head = lax.dynamic_slice_in_dim(
         small_sums[cuts[2] :].reshape(3, HEADS), wsh_index * cols_head, cols_head, 1
     )
-    tiles_out = (INNER // D) * (D // TILE)
-    grad_out, *new_out = adam_chunks(sums, 0, w_out, first_w_out, second_w_out, rate_matrix, weight_decay, "adam_w_out")
-    grad_in_w, *new_in = adam_chunks(
-        sums, tiles_out, w_in, first_w_in, second_w_in, rate_matrix, weight_decay, "adam_w_in"
-    )
-    at_dt = CONV_CH % TILE
-    grad_dt = sums[-1, :, at_dt : at_dt + HEADS].astype(full_type)
     params = (w_in, w_dt, w_out, gain_pre, gain_norm, conv_param, head_param)
     gradients = (grad_in_w, grad_dt, grad_out, grad_gpre, grad_gnorm, grad_conv, grad_head)
     firsts = (first_w_in, first_w_dt, first_w_out, first_gain_pre, first_gain_norm, first_conv, first_head)

time: 495 us -> 451 us (0.911)
  waiting for transfers between devices: 37.9 us -> 5.9 us
  Pallas kernels: 370 us -> 390 us
  blocking collectives: 10.7 us -> 0 us
  other arithmetic: 26.5 us -> 17.5 us
  local copies, waits for them, and re-layouts: 25 us -> 18.1 us
    pallas_call x3, Pallas kernels: 46.2 us -> 89.2 us  [the longest x1 64.1 us: project_signal(): pl.pallas_call(functools.partial(signal_kernel, count), in_specs=[vmem] *...]
    ppermute x14 -> x5, waiting for transfers between devices: 37.9 us -> 5.9 us  [swap(): lax.ppermute(vals, axis, [(i, i ^ bit) for i in range(lax.axis_size(axis))])]
    pallas_call x1, Pallas kernels: 205 us -> 182 us  [run_backward(): pl.pallas_call(functools.partial(backward_kernel, (wsh_count, seq_count),...]
    all_gather x1 -> x0, blocking collectives: 10.7 us -> none  [shards(): small = lax.all_gather(flat, 'wsh', axis=0)]
    ppermute x14 -> x5, starting transfers between devices: 7.88 us -> 2.32 us  [swap(): lax.ppermute(vals, axis, [(i, i ^ bit) for i in range(lax.axis_size(axis))])]
  transfers between devices with their start and end apart: 15 -> 6, of which waited for: 6 -> 2; matrix products, arithmetic and copies ran while one was open for 8% -> 7% of each run, Pallas kernels for 6% -> 6%
where the time goes in v6:
time: 451 us; the launch traced here: 450 us
  Pallas kernels  390 us (86%)
  local copies, waits for them, and re-layouts  18.1 us (4%)
  other arithmetic  17.5 us (4%)
  matrix products  10.3 us (2%)
  starting transfers between devices  7.23 us (2%)
  waiting for transfers between devices  5.9 us (1%)
    pallas_call x1, Pallas kernels, run_backward(): pl.pallas_call(functools.partial(backward_kernel, (wsh_count, seq_count),...  182 us
    pallas_call x1, Pallas kernels, run_forward(): pl.pallas_call(functools.partial(forward_kernel, count), grid=(back_at +...  100 us
    pallas_call x1, Pallas kernels, project_signal(): pl.pallas_call(functools.partial(signal_kernel, count), in_specs=[vmem] *...  64.1 us
    pallas_call x2, Pallas kernels, adam_chunks(): pl.pallas_call(functools.partial(adam_kernel, rate, decay), grid=(all_row...  25.1 us
    pallas_call x1, Pallas kernels, run_norm(): pl.pallas_call(norm_kernel, grid=(rows // part,), in_specs=[by_rows(INNER...  18.7 us
    dot_general x1, matrix products, dot(): lax.dot_general(left_side, right_side, (dims, ((), ())), precision=precis...  10.3 us
  transfers between devices with their start and end apart: 6, of which 2 were waited for; matrix products, arithmetic and copies ran while one was open for 7% of the time, Pallas kernels for 6%

profile of v6, /device:TPU:0, one launch (start us, length us, event | category | flops | bytes accessed | tf_op | source)
XLA Modules:
  0.0 449.8 jit_solution(10907239347096399198)
XLA Ops:
  0.7 0.8 slice_bitcast_fusion
  1.5 4.9 %collective-permute-start = (bf16[16,1536]{1,0:T(8,128)(2,1)S(1)}, bf16[16,1536]{1,0:T(8,128)(2,1)S(1)}, u32[]{:S(2)}, u32[]{:S(2)}) collective-permute-start(bf16[16,1536]{1,0:T(8,128)(2,1)S(1)} %slice_bitcast_fusion), channel_id=1, source_target_pairs={{0,8},{8,16},{16,24},{1,9},{9,17},{17,25},{2,10},{10,18},{18,26},{... | collective-permute-start | bytes 147464 | tf_op jit(solution)/shard_map/ppermute | solution.py:1310
  6.4 0.8 convert_element_type.27
  7.2 1.5 copy.70
  8.7 2.6 convert.5
  11.4 0.0 copy-start.16
  11.4 0.0 copy-start.11
  11.4 0.0 copy-start.12
  11.4 1.2 slice.67.gate_own_ref
  12.6 0.1 slice.66
  12.7 0.1 copy.69
  12.8 0.7 copy.72
  13.5 0.7 copy.73
  14.3 2.9 convert_element_type.29.out_own_ref
  17.2 0.2 dynamic_update_slice.12
  17.5 1.8 concatenate.10.own_ref
  19.3 0.1 dynamic_update_slice.13
  19.4 0.6 dynamic_update_slice.14
  20.1 0.3 dynamic_update_slice.15.small_ref
  20.4 1.3 pad_maximum_fusion.tokens_ref
  21.7 64.1 %project_signal.1 = (bf16[528,3456]{1,0:T(8,128)(2,1)}, bf16[512,1536]{1,0:T(8,128)(2,1)}, f32[512,128]{1,0:T(8,128)}, f32[8,1536]{1,0:T(8,128)}, f32[8,3072]{1,...) custom-call(bf16[528,1536]{1,0:T(8,128)(2,1)} %pad_maximum_fusion.tokens_ref, ...), custom_call_target="tpu_custom_call" | custom-call | flops 60000002048 | bytes 30000000 | tf_op jit(solution)/shard_map/project_signal/pallas_call | solution.py:243
  85.8 1.7 slice_reduce_fusion
  87.5 1.4 slice_reduce_fusion.2
  88.9 100.2 %forward_scan.1 = (f32[512,3072]{1,0:T(8,128)}, f32[512,256]{1,0:T(8,128)}, f32[512,128]{1,0:T(8,128)}, f32[128,512]{1,0:T(8,128)}, f32[512,128]{1,0:T(8,128)}, ...) custom-call(bf16[528,3456]{1,0:T(8,128)(2,1)} %get-tuple-element.74., ...), custom_call_target="tpu_custom_call" | custom-call | flops 99999997952 | bytes 60000000 | tf_op jit(solution)/shard_map/forward_scan/pallas_call | solution.py:810
  189.1 18.7 %gated_norm.1 = (bf16[512,3072]{1,0:T(8,128)(2,1)}, bf16[4608,512]{1,0:T(8,128)(2,1)}, bf16[512,3072]{1,0:T(8,128)(2,1)}, bf16[512,3072]{1,0:T(8,128)(2,1)}, f32[8,3072]{1,0:T(8,128)}, /*index=5*/f32[128,3072]{1,0:T(8,128)}) custom-call(f32[512,3072]{1,0:T(8,128)} %get-tuple-element.78.y_ref, f32[512,3072]{1,0:T(8,128)} %get-tuple-element.79.gate_ref, ...), custom_call_target="tpu_custom_call" | custom-call | flops 1000000000 | bytes 30000000 | tf_op jit(solution)/shard_map/gated_norm/pallas_call | solution.py:880
  207.7 0.0 copy-start.1
  207.7 0.0 copy-start.8
  207.7 181.6 %scan_backward.1 = (f32[512,1536]{1,0:T(8,128)}, f32[8,3328]{1,0:T(8,128)}, f32[8,3072]{1,0:T(8,128)}, f32[8,128]{1,0:T(8,128)}, bf16[25,192,384]{2,1,0:T(8,128)(2,1)}) custom-call(bf16[528,3456]{1,0:T(8,128)(2,1)} %get-tuple-element.74.sig_ref.maps_ref.raw_ref, bf16[528,3456]{1,0:T(8,128)(2,1)} %get-tuple-element.74.sig_ref.maps_ref.raw_ref, ...), custom_call_target="tpu_custom_call" | custom-call | flops 99999997952 | bytes 20000000 | tf_op jit(solution)/shard_map/scan_backward/pallas_call | solution.py:924
  389.4 0.9 reshape.76
  390.3 0.8 slice_bitcast_fusion.1
  391.0 0.9 slice_reduce_fusion.1
  392.0 0.1 reshape_squeeze.3
  392.0 0.1 reduce_sum.29
  392.1 0.9 slice.57
  393.1 2.7 fusion.8
  395.8 0.1 concatenate.11
  395.9 0.0 collective-permute-start.1
  395.9 10.3 %fusion.10 = bf16[1,512,1536]{2,1,0:T(8,128)(2,1)} fusion(bf16[512,3072]{1,0:T(8,128)(2,1)} %get-tuple-element.85, bf16[3072,1536]{1,0:T(8,128)(2,1)} %get-tuple-element.86, bf16[1,512,1536]{2,1,0:T(8,128)(2,1)S(1)} %copy-done.1), kind=kOutput, calls=%fused_computation.12 | convolution fusion | flops 4834197504 | bytes 15728640 | tf_op jit(solution)/shard_map/dot_general | solution.py:44
  406.2 0.5 collective-permute-start.2
  406.7 8.6 %adam_w_out.1 = (f32[384,1536]{1,0:T(8,128)}, f32[384,1536]{1,0:T(8,128)}, f32[384,1536]{1,0:T(8,128)}, f32[384,1536]{1,0:T(8,128)}) custom-call(bf16[25,192,384]{2,1,0:T(8,128)(2,1)} %get-tuple-element.102.share_ref, f32[384,1536]{1,0:T(8,128)} %weight_ref.3, f32[384,1536]{1,0:T(8,128)} %first_ref.3, f32[384,1536]{1,0:T(8,128)} %second_ref.3), custom_call_target="tpu_custom_call" | custom-call | flops 11796480 | bytes 17694720 | tf_op jit(solution)/shard_map/adam_w_out/pallas_call | solution.py:1268
  415.4 1.6 collective-permute-start.3
  417.0 2.6 fusion.7
  419.6 0.0 copy-start.19
  419.6 0.0 copy-start.22
  419.7 0.0 copy-start.26
  419.7 0.0 copy-start.27
  419.7 0.0 copy-start.24
  419.7 0.0 copy-start.25
  419.7 16.5 %adam_w_in.1 = (f32[192,6400]{1,0:T(8,128)}, f32[192,6400]{1,0:T(8,128)}, f32[192,6400]{1,0:T(8,128)}, f32[192,6400]{1,0:T(8,128)}) custom-call(bf16[25,192,384]{2,1,0:T(8,128)(2,1)} %get-tuple-element.102.share_ref, f32[192,6400]{1,0:T(8,128)} %weight_ref.2, f32[192,6400]{1,0:T(8,128)} %first_ref.2, f32[192,6400]{1,0:T(8,128)} %second_ref.2), custom_call_target="tpu_custom_call" | custom-call | flops 24576000 | bytes 36864000 | tf_op jit(solution)/shard_map/adam_w_in/pallas_call | solution.py:1268
  436.3 0.1 collective-permute-start.4
  436.4 0.9 divide_subtract_fusion
  437.3 3.6 collective-permute-done.4
  440.8 0.1 collective-permute-start.5
  440.9 0.8 bitcast_convert_fusion
  441.7 0.7 copy.76
  442.4 0.7 copy.77
  443.1 0.7 copy.78
  443.8 0.7 copy.75
  444.5 2.3 collective-permute-done.5
  446.9 0.1 reshape.78
  447.0 0.7 divide_subtract_fusion.1
  447.8 0.7 divide_subtract_fusion.2
  448.4 0.7 divide_subtract_fusion.4
  449.1 0.7 divide_subtract_fusion.3
  (63 shorter events, 0.2 us)
Async XLA Ops:
  1.5 18.9 %collective-permute-start = (bf16[16,1536]{1,0:T(8,128)(2,1)S(1)}, bf16[16,1536]{1,0:T(8,128)(2,1)S(1)}, u32[]{:S(2)}, u32[]{:S(2)}) collective-permute-start(bf16[16,1536]{1,0:T(8,128)(2,1)S(1)} %slice_bitcast_fusion), channel_id=1, source_target_pairs={{0,8},{8,16},{16,24},{1,9},{9,17},{17,25},{2,10},{10,18},{18,26},{... | collective-permute-start | bytes 147464 | tf_op jit(solution)/shard_map/ppermute | solution.py:1310
  11.4 1.3 copy-start.16
  11.4 1.4 copy-start.11
  11.4 2.1 copy-start.12
  12.6 4.7 %copy-start.20 = (f32[192]{0:T(256)S(1)}, f32[192]{0:T(256)}, u32[]{:S(2)}) copy-start(f32[192]{0:T(256)} %param.28) | copy-start | bytes 2308
  14.3 5.1 %copy-start.9 = (f32[5,416]{1,0:T(8,128)S(1)}, f32[5,416]{1,0:T(8,128)}, u32[]{:S(2)}) copy-start(f32[5,416]{1,0:T(8,128)} %param.30) | copy-start | bytes 24964
  14.3 5.8 %copy-start.18 = (f32[3,6]{1,0:T(4,128)S(1)}, f32[3,6]{1,0:T(4,128)}, u32[]{:S(2)}) copy-start(f32[3,6]{1,0:T(4,128)} %param.31) | copy-start | bytes 220
  14.3 6.1 %copy-start = (bf16[1,512,1536]{2,1,0:T(8,128)(2,1)S(1)}, bf16[1,512,1536]{2,1,0:T(8,128)(2,1)}, u32[]{:S(2)}) copy-start(bf16[1,512,1536]{2,1,0:T(8,128)(2,1)} %param.23) | copy-start | bytes 4718596
  20.4 1.3 copy-start.7
  207.7 185.3 %copy-start.1 = (bf16[1,512,1536]{2,1,0:T(8,128)(2,1)S(1)}, bf16[1,512,1536]{2,1,0:T(8,128)(2,1)}, u32[]{:S(2)}) copy-start(bf16[1,512,1536]{2,1,0:T(8,128)(2,1)} %param.23) | copy-start | bytes 4718596
  207.7 185.3 %copy-start.8 = (f32[1536]{0:T(1024)S(1)}, f32[1536]{0:T(1024)}, u32[]{:S(2)}) copy-start(f32[1536]{0:T(1024)} %slice_reduce_fusion.2) | copy-start | bytes 18436
  207.7 185.3 %copy-start.13 = (f32[512]{0:T(512)S(1)}, f32[512]{0:T(512)}, u32[]{:S(2)}) copy-start(f32[512]{0:T(512)} %slice_reduce_fusion) | copy-start | bytes 6148
  395.9 10.3 %collective-permute-start.1 = (f32[21392]{0:T(1024)S(1)}, f32[21392]{0:T(1024)S(1)}, u32[]{:S(2)}, u32[]{:S(2)}) collective-permute-start(f32[21392]{0:T(1024)S(1)} %concatenate.11), channel_id=1, source_target_pairs={{0,1},{1,0},{2,3},{3,2},{4,5},{5,4},{6,7},{7,6},{8,9},{9,8},{10,11... | collective-permute-start | bytes 256712 | tf_op jit(solution)/shard_map/ppermute | solution.py:1005
  406.2 9.2 %collective-permute-start.2 = (f32[21392]{0:T(1024)S(1)}, f32[21392]{0:T(1024)S(1)}, u32[]{:S(2)}, u32[]{:S(2)}) collective-permute-start(f32[21392]{0:T(1024)S(1)} %add.106), channel_id=1, source_target_pairs={{0,2},{1,3},{2,0},{3,1},{4,6},{5,7},{6,4},{7,5},{8,10},{9,11},{10,... | collective-permute-start | bytes 256712 | tf_op jit(solution)/shard_map/ppermute | solution.py:1005
  406.7 10.3 %copy-start.2 = (f32[512,1536]{1,0:T(8,128)S(1)}, f32[512,1536]{1,0:T(8,128)}, u32[]{:S(2)}) copy-start(f32[512,1536]{1,0:T(8,128)} %get-tuple-element.100) | copy-start | bytes 9437188
  406.7 10.3 %copy-start.3 = (bf16[1,512,1536]{2,1,0:T(8,128)(2,1)S(1)}, bf16[1,512,1536]{2,1,0:T(8,128)(2,1)}, u32[]{:S(2)}) copy-start(bf16[1,512,1536]{2,1,0:T(8,128)(2,1)} %param.24) | copy-start | bytes 4718596
  415.4 20.8 %collective-permute-start.3 = (f32[21392]{0:T(1024)S(1)}, f32[21392]{0:T(1024)S(1)}, u32[]{:S(2)}, u32[]{:S(2)}) collective-permute-start(f32[21392]{0:T(1024)S(1)} %add.107), channel_id=1, source_target_pairs={{0,4},{1,5},{2,6},{3,7},{4,0},{5,1},{6,2},{7,3},{8,12},{9,13},{10,... | collective-permute-start | bytes 256712 | tf_op jit(solution)/shard_map/ppermute | solution.py:1005
  419.6 16.8 %copy-start.4 = (f32[192,48]{1,0:T(8,128)S(1)}, f32[192,48]{1,0:T(8,128)}, u32[]{:S(2)}) copy-start(f32[192,48]{1,0:T(8,128)} %copy.70) | copy-start | bytes 110596
  419.6 16.8 %copy-start.5 = (f32[192,48]{1,0:T(8,128)S(1)}, f32[192,48]{1,0:T(8,128)}, u32[]{:S(2)}) copy-start(f32[192,48]{1,0:T(8,128)} %copy.72) | copy-start | bytes 110596
  419.6 16.8 %copy-start.6 = (f32[192,48]{1,0:T(8,128)S(1)}, f32[192,48]{1,0:T(8,128)}, u32[]{:S(2)}) copy-start(f32[192,48]{1,0:T(8,128)} %copy.73) | copy-start | bytes 110596
  419.6 27.4 %copy-start.10 = (f32[5,416]{1,0:T(8,128)S(1)}, f32[5,416]{1,0:T(8,128)}, u32[]{:S(2)}) copy-start(f32[5,416]{1,0:T(8,128)} %param.30) | copy-start | bytes 24964
  419.6 27.4 %copy-start.14 = (f32[5,416]{1,0:T(8,128)S(1)}, f32[5,416]{1,0:T(8,128)}, u32[]{:S(2)}) copy-start(f32[5,416]{1,0:T(8,128)} %param.42) | copy-start | bytes 24964
  419.6 27.4 %copy-start.15 = (f32[5,416]{1,0:T(8,128)S(1)}, f32[5,416]{1,0:T(8,128)}, u32[]{:S(2)}) copy-start(f32[5,416]{1,0:T(8,128)} %param.43) | copy-start | bytes 24964
  419.6 28.1 %copy-start.19 = (f32[3,6]{1,0:T(4,128)S(1)}, f32[3,6]{1,0:T(4,128)}, u32[]{:S(2)}) copy-start(f32[3,6]{1,0:T(4,128)} %param.31) | copy-start | bytes 220
  419.6 28.1 %copy-start.22 = (f32[3,6]{1,0:T(4,128)S(1)}, f32[3,6]{1,0:T(4,128)}, u32[]{:S(2)}) copy-start(f32[3,6]{1,0:T(4,128)} %param.44) | copy-start | bytes 220
  419.6 28.1 %copy-start.23 = (f32[3,6]{1,0:T(4,128)S(1)}, f32[3,6]{1,0:T(4,128)}, u32[]{:S(2)}) copy-start(f32[3,6]{1,0:T(4,128)} %param.45) | copy-start | bytes 220
  419.7 28.8 %copy-start.21 = (f32[192]{0:T(256)S(1)}, f32[192]{0:T(256)}, u32[]{:S(2)}) copy-start(f32[192]{0:T(256)} %param.28) | copy-start | bytes 2308
  419.7 28.8 %copy-start.26 = (f32[192]{0:T(256)S(1)}, f32[192]{0:T(256)}, u32[]{:S(2)}) copy-start(f32[192]{0:T(256)} %param.38) | copy-start | bytes 2308
  419.7 28.8 %copy-start.27 = (f32[192]{0:T(256)S(1)}, f32[192]{0:T(256)}, u32[]{:S(2)}) copy-start(f32[192]{0:T(256)} %param.39) | copy-start | bytes 2308
  419.7 29.4 %copy-start.17 = (f32[384]{0:T(512)S(1)}, f32[384]{0:T(512)}, u32[]{:S(2)}) copy-start(f32[384]{0:T(512)} %param.29) | copy-start | bytes 4612
  419.7 29.4 %copy-start.24 = (f32[384]{0:T(512)S(1)}, f32[384]{0:T(512)}, u32[]{:S(2)}) copy-start(f32[384]{0:T(512)} %param.40) | copy-start | bytes 4612
  419.7 29.4 %copy-start.25 = (f32[384]{0:T(512)S(1)}, f32[384]{0:T(512)}, u32[]{:S(2)}) copy-start(f32[384]{0:T(512)} %param.41) | copy-start | bytes 4612
  436.3 4.6 %collective-permute-start.4 = (f32[21392]{0:T(1024)S(1)}, f32[21392]{0:T(1024)S(1)}, u32[]{:S(2)}, u32[]{:S(2)}) collective-permute-start(f32[21392]{0:T(1024)S(1)} %add.108), channel_id=1, source_target_pairs={{0,8},{8,0},{16,24},{24,16},{1,9},{9,1},{17,25},{25,17},{2,10},{10... | collective-permute-start | bytes 256712 | tf_op jit(solution)/shard_map/ppermute | solution.py:1005
  440.8 6.0 %collective-permute-start.5 = (f32[21392]{0:T(1024)S(1)}, f32[21392]{0:T(1024)S(1)}, u32[]{:S(2)}, u32[]{:S(2)}) collective-permute-start(f32[21392]{0:T(1024)S(1)} %add.109), channel_id=1, source_target_pairs={{0,16},{8,24},{16,0},{24,8},{1,17},{9,25},{17,1},{25,9},{2,18},{10... | collective-permute-start | bytes 256712 | tf_op jit(solution)/shard_map/ppermute | solution.py:1005

commit v7 on v6

--- a/solution.py
+++ b/solution.py
@@ -18,6 +18,7 @@
 BLOCK = 128
 LANES = 128
 WIDE = 256
+SIG_PIECES = 3
 HALO = 16
 GROUPS = INNER // WIDE
 CHAIN_LAG = 2
@@ -167,111 +168,15 @@
     return [pltpu.SemaphoreType.DMA((2, copies)), pltpu.SemaphoreType.DMA((2, copies + 1))]
 
 
-def signal_kernel(
-    count, tokens_ref, own_ref, small_ref,
-    packed_ref, normed_ref, inv_ref, gain_in_ref, gain_out_ref, conv_ref, head_ref, full_ref,
-    normed, full, small_full, small_far, small_core, out_sems, *sems,
-):
-    bits = len(part_orders(count))
-    pieces = len(sems) // 2
-    width = own_ref.shape[1] // pieces
-    small_start, small_advance, small_done, small_finish = gather_steps(
-        count, small_ref, small_full, small_far, small_core, split=False
-    )
-    gathers = [
-        gather_steps(count, own_ref, full, sems[2 * c], sems[2 * c + 1], cols=(c * width, width)) for c in range(pieces)
-    ]
-    greet()
-    small_start()
-    for start, _, _, _ in gathers:
-        start()
-    for q in range(bits):
-        small_advance(q)
-    small_done()
-    height = small_ref.shape[0]
-    small = small_full[:height, :].astype(full_type)
-    for d in range(1, count):
-        small = small + small_full[d * height : (d + 1) * height, :].astype(full_type)
-    gain_in_ref[...] = jnp.broadcast_to(small[0:1, :D], gain_in_ref.shape)
-    gain_out_ref[...] = jnp.broadcast_to(small[1:2, :INNER], gain_out_ref.shape)
-    conv_ref[...] = jnp.concatenate([small[2:7], jnp.zeros((3, CONV_CH), full_type)], axis=0)
-    head_ref[...] = jnp.concatenate([small[7:10, :LANES], jnp.zeros((5, LANES), full_type)], axis=0)
-    gathers[0][1](0)
-    all_rows = tokens_ref.shape[0]
-    for first in range(0, all_rows, BLOCK):
-        size = min(BLOCK, all_rows - first)
-        tokens = tokens_ref[first : first + size, :].astype(full_type)
-        inv = lax.rsqrt(jnp.sum(tokens * tokens, axis=1, keepdims=True) * (1.0 / D) + norm_eps)
-        low = (tokens * inv * gain_in_ref[0:1, :]).astype(low_type)
-        normed[first : first + size, :] = low
-        skip = max(HALO - first, 0)
-        at = slice(first + skip - HALO, first + size - HALO)
-        normed_ref[at, :] = low[skip:]
-        inv_ref[at, :] = jnp.broadcast_to(inv[skip:], (size - skip, LANES))
-    for _, advance, _, _ in gathers[1:]:
-        advance(0)
-    outs = []
-    for c, (_, advance, done, _) in enumerate(gathers):
-        for q in range(1, bits):
-            advance(q)
-        done()
-        cols = pl.ds(c * width, width)
-        outs.append(pltpu.make_async_copy(full.at[:, cols], full_ref.at[:, cols], out_sems.at[c]))
-        outs[-1].start()
-
-        def multiply(t, carry, c=c):
-            col = pl.multiple_of(c * width + t * TILE, LANES)
-            packed_ref[:, pl.ds(col, TILE)] = dot(normed[...], full[:, pl.ds(col, TILE)]).astype(low_type)
-            return carry
-
-        lax.fori_loop(0, width // TILE, multiply, 0)
-    for out in outs:
-        out.wait()
-    small_finish()
-    for _, _, _, finish in gathers:
-        finish()
-
-
-def project_signal(tokens, own, small):
-    count = lax.axis_size("wsh")
-    all_rows = tokens.shape[0]
-    rows = all_rows - HALO
-    pieces = 3
-    vmem = pl.BlockSpec(memory_space=pltpu.VMEM)
-    wide = lambda cols: jax.ShapeDtypeStruct((8, cols), full_type)
-    sems = [sem for _ in range(pieces) for sem in gather_sems(count)]
-    return pl.pallas_call(
-        functools.partial(signal_kernel, count),
-        in_specs=[vmem] * 3,
-        out_specs=[vmem] * 7 + [pl.BlockSpec(memory_space=pl.ANY)],
-        out_shape=[
-            jax.ShapeDtypeStruct((all_rows, PACK), low_type),
-            jax.ShapeDtypeStruct((rows, D), low_type),
-            jax.ShapeDtypeStruct((rows, LANES), full_type),
-            wide(D), wide(INNER), wide(CONV_CH), wide(LANES),
-            jax.ShapeDtypeStruct((D, PACK), low_type),
-        ],
-        scratch_shapes=[
-            pltpu.VMEM((all_rows, D), low_type),
-            pltpu.VMEM((D, PACK), low_type),
-            pltpu.VMEM((count * small.shape[0], CONV_CH), low_type),
-            *gather_sems(count, split=False),
-            pltpu.SemaphoreType.DMA((pieces,)),
-            *sems,
-        ],
-        compiler_params=pltpu.CompilerParams(collective_id=0, has_side_effects=True, vmem_limit_bytes=VMEM_LIMIT),
-        cost_estimate=pl.CostEstimate(flops=6 * 10**10, bytes_accessed=30 * 10**6, transcendentals=0),
-        name="project_signal",
-    )(tokens, own, small)
-
-
 def forward_kernel(
     count,
-    sig_ref, maps_ref, raw_ref, conv_ref, conv_maps_ref, head_ref, normed_ref, cot_ref, gate_own_ref, out_own_ref,
+    tokens_ref, sig_own_ref, small_ref, cot_ref, gate_own_ref, out_own_ref,
+    packed_ref, normed_ref, inv_ref, gain_in_ref, gain_out_ref, conv_ref, head_ref, full_sig_ref,
     y_ref, bc_ref, lag_ref, run_t_ref, enter_ref, enter_all_ref, tail_ref, offs_ref, states_ref, before_ref,
     gate_ref, back_ref, full_gate_ref, full_out_ref,
     sig, in_t, inter, run, lag_t, ends, stage, land, sems, gate_full, out_full,
     gate_far, gate_core, out_far, out_core, full_sems,
+    packed, normed, sig_full, small_full, small_far, small_core, *sig_sems,
 ):
     step = pl.program_id(0)
     rows = y_ref.shape[0]
@@ -283,6 +188,61 @@
     gate_start, gate_advance, gate_done, gate_finish = gather_steps(count, gate_own_ref, gate_full, gate_far, gate_core)
     out_start, out_advance, out_done, out_finish = gather_steps(count, out_own_ref, out_full, out_far, out_core)
     gate_at, back_at = GROUPS + CHAIN_LAG, 2 * GROUPS + CHAIN_LAG
+    small_start, small_advance, small_done, small_finish = gather_steps(
+        count, small_ref, small_full, small_far, small_core, split=False
+    )
+    width = PACK // SIG_PIECES
+    gathers = [
+        gather_steps(count, sig_own_ref, sig_full, sig_sems[2 * c], sig_sems[2 * c + 1], cols=(c * width, width))
+        for c in range(SIG_PIECES)
+    ]
+    sig_out = pltpu.make_async_copy(sig_full, full_sig_ref, full_sems.at[2])
+    packed_out = pltpu.make_async_copy(packed, packed_ref, full_sems.at[3])
+    normed_out = pltpu.make_async_copy(normed.at[pl.ds(HALO, rows)], normed_ref, full_sems.at[4])
+
+    def project_signal():
+        small_start()
+        for start, _, _, _ in gathers:
+            start()
+        for q in range(bits):
+            small_advance(q)
+        small_done()
+        height = small_ref.shape[0]
+        small = small_full[:height, :].astype(full_type)
+        for d in range(1, count):
+            small = small + small_full[d * height : (d + 1) * height, :].astype(full_type)
+        gain_in_ref[...] = jnp.broadcast_to(small[0:1, :D], gain_in_ref.shape)
+        gain_out_ref[...] = jnp.broadcast_to(small[1:2, :INNER], gain_out_ref.shape)
+        conv_ref[...] = jnp.concatenate([small[2:7], jnp.zeros((3, CONV_CH), full_type)], axis=0)
+        head_ref[...] = jnp.concatenate([small[7:10, :LANES], jnp.zeros((5, LANES), full_type)], axis=0)
+        gathers[0][1](0)
+        all_rows = tokens_ref.shape[0]
+        for first in range(0, all_rows, BLOCK):
+            size = min(BLOCK, all_rows - first)
+            tokens = tokens_ref[first : first + size, :].astype(full_type)
+            inv = lax.rsqrt(jnp.sum(tokens * tokens, axis=1, keepdims=True) * (1.0 / D) + norm_eps)
+            normed[first : first + size, :] = (tokens * inv * gain_in_ref[0:1, :]).astype(low_type)
+            skip = max(HALO - first, 0)
+            at = slice(first + skip - HALO, first + size - HALO)
+            inv_ref[at, :] = jnp.broadcast_to(inv[skip:], (size - skip, LANES))
+        normed_out.start()
+        for _, advance, _, _ in gathers[1:]:
+            advance(0)
+        gate_start()
+        out_start()
+        for c, (_, advance, done, _) in enumerate(gathers):
+            for q in range(1, bits):
+                advance(q)
+            done()
+
+            def multiply(t, carry, c=c):
+                col = pl.multiple_of(c * width + t * TILE, LANES)
+                packed[:, pl.ds(col, TILE)] = dot(normed[...], sig_full[:, pl.ds(col, TILE)]).astype(low_type)
+                return carry
+
+            lax.fori_loop(0, width // TILE, multiply, 0)
+        sig_out.start()
+        packed_out.start()
 
     def to_next(k):
         return pltpu.make_async_remote_copy(
@@ -293,14 +253,13 @@
     @pl.when(step == 0)
     def _():
         greet()
-        gate_start()
-        out_start()
-        sig[...] = maps_ref[...].astype(full_type)
-        pre = convolve(sig, conv_maps_ref[...], rows)
+        project_signal()
+        sig[...] = packed[:, INNER:CONV_CH].astype(full_type)
+        pre = convolve(sig, conv_ref[:, INNER:], rows)
         maps = pre * sigmoid(pre)
         bc_ref[...] = maps
         in_t[...] = maps[:, :STATE].T.astype(low_type)
-        step_sizes, _, rate = step_terms(raw_ref[HALO:, :].astype(full_type), head_ref[...])
+        step_sizes, _, rate = step_terms(packed[HALO:, CONV_CH:].astype(full_type), head_ref[...])
         rates = step_sizes * rate * LOG2E
         log_steps = jnp.log2(step_sizes)
         sums = jnp.where(lower, 1.0, 0.0)
@@ -328,8 +287,9 @@
 
     @pl.when(step < GROUPS)
     def _():
-        sig[...] = sig_ref[...].astype(full_type)
-        pre_all = convolve(sig, conv_ref[...], rows)
+        cols = pl.ds(pl.multiple_of(step * WIDE, WIDE), WIDE)
+        sig[...] = packed[:, cols].astype(full_type)
+        pre_all = convolve(sig, conv_ref[:, cols], rows)
         tail = to_front(tail_ref[...], step)
         last = to_front(offs_ref[...], step)
         run_all = to_front(run[...], step)
@@ -397,7 +357,7 @@
     @pl.when((step >= gate_at) & (step < back_at))
     def _():
         col = pl.multiple_of((step - gate_at) * WIDE, WIDE)
-        gate_ref[...] = dot(normed_ref[...], gate_full[:, pl.ds(col, WIDE)])
+        gate_ref[...] = dot(normed[HALO:, :], gate_full[:, pl.ds(col, WIDE)])
 
     @pl.when(step == back_at)
     def _():
@@ -413,8 +373,14 @@
 
     @pl.when(step == back_at + GROUPS - 1)
     def _():
+        for _, _, _, end in gathers:
+            end()
+        small_finish()
         gate_finish()
         out_finish()
+        sig_out.wait()
+        packed_out.wait()
+        normed_out.wait()
         gate_out.wait()
         out_out.wait()
 
@@ -792,8 +758,9 @@
         )
 
 
-def run_forward(packed, conv, head, normed, cot, gate_own, out_own):
-    rows = packed.shape[0] - HALO
+def run_forward(tokens, sig_own, small, cot, gate_own, out_own):
+    all_rows = tokens.shape[0]
+    rows = all_rows - HALO
     blocks = rows // BLOCK
     count = lax.axis_size("wsh")
     gate_at, back_at = GROUPS + CHAIN_LAG, 2 * GROUPS + CHAIN_LAG
@@ -803,26 +770,24 @@
     kept = lambda shape: pl.BlockSpec(shape, lambda j: (0,) * len(shape))
     cols = lambda height, first: pl.BlockSpec((height, WIDE), lambda j: (0, at(first)(j)))
     anywhere = pl.BlockSpec(memory_space=pl.ANY)
-    small = jax.ShapeDtypeStruct((rows, LANES), full_type)
+    small_out = jax.ShapeDtypeStruct((rows, LANES), full_type)
+    eight = lambda width: jax.ShapeDtypeStruct((8, width), full_type)
     small_t = jax.ShapeDtypeStruct((LANES, rows), full_type)
     wide = jax.ShapeDtypeStruct((rows, INNER), full_type)
     vmem = pltpu.VMEM
     return pl.pallas_call(
         functools.partial(forward_kernel, count),
         grid=(back_at + GROUPS,),
-        in_specs=[
-            cols(rows + HALO, 0),
-            pl.BlockSpec((rows + HALO, WIDE), lambda j: (0, GROUPS), pipeline_mode=once),
-            pl.BlockSpec((rows + HALO, LANES), lambda j: (0, CONV_CH // LANES), pipeline_mode=once),
-            cols(8, 0),
-            pl.BlockSpec((8, WIDE), lambda j: (0, GROUPS), pipeline_mode=once),
-            whole((8, LANES)),
-            whole(normed.shape),
-            whole(cot.shape),
-            whole(gate_own.shape),
-            whole(out_own.shape),
-        ],
+        in_specs=[whole(item.shape) for item in (tokens, sig_own, small, cot, gate_own, out_own)],
         out_specs=[
+            anywhere,
+            anywhere,
+            kept((rows, LANES)),
+            kept((8, D)),
+            kept((8, INNER)),
+            kept((8, CONV_CH)),
+            kept((8, LANES)),
+            anywhere,
             cols(rows, 0),
             kept((rows, WIDE)),
             kept((rows, LANES)),
@@ -839,9 +804,14 @@
             anywhere,
         ],
         out_shape=[
+            jax.ShapeDtypeStruct((all_rows, PACK), low_type),
+            jax.ShapeDtypeStruct((rows, D), low_type),
+            small_out,
+            eight(D), eight(INNER), eight(CONV_CH), eight(LANES),
+            jax.ShapeDtypeStruct((D, PACK), low_type),
             wide,
             jax.ShapeDtypeStruct((rows, WIDE), full_type),
-            small, small_t, small, small, small,
+            small_out, small_t, small_out, small_out, small_out,
             jax.ShapeDtypeStruct((16, LANES), full_type),
             jax.ShapeDtypeStruct((blocks, STATE, INNER), low_type),
             jax.ShapeDtypeStruct((STATE, INNER), low_type),
@@ -864,12 +834,18 @@
             vmem((INNER, D), low_type),
             *gather_sems(count),
             *gather_sems(count),
-            pltpu.SemaphoreType.DMA((2,)),
+            pltpu.SemaphoreType.DMA((5,)),
+            vmem((all_rows, PACK), low_type),
+            vmem((all_rows, D), low_type),
+            vmem((D, PACK), low_type),
+            vmem((count * small.shape[0], CONV_CH), low_type),
+            *gather_sems(count, split=False),
+            *[sem for _ in range(SIG_PIECES) for sem in gather_sems(count)],
         ],
-        compiler_params=pltpu.CompilerParams(collective_id=1, has_side_effects=True, vmem_limit_bytes=VMEM_LIMIT),
+        compiler_params=pltpu.CompilerParams(collective_id=1, has_side_effects=True, vmem_limit_bytes=61 * 1024 * 1024),
         cost_estimate=pl.CostEstimate(flops=10**11, bytes_accessed=60 * 10**6, transcendentals=4 * 10**6),
         name="forward_scan",
-    )(packed, packed, packed, conv, conv, head, normed, cot, gate_own, out_own)
+    )(tokens, sig_own, small, cot, gate_own, out_own)
 
 
 def run_norm(y, gate, back, gain, bc, enter, state, normed):
@@ -1308,15 +1284,16 @@
     cot_low = cotangent[0]
     rows = tokens_low.shape[0]
     before = lax.ppermute(tokens_low[rows - HALO :], "seq", [(i, i + 1) for i in range(seq_count - 1)])
-    packed, normed, inv_wide, gain_in_rows, gain_rows, conv, head, full_sig = project_signal(
-        jnp.concatenate([before, tokens_low], axis=0), part_sig, small.astype(low_type)
+    (
+        packed, normed, inv_wide, gain_in_rows, gain_rows, conv, head, full_sig,
+        y, bc, lag, run_t, enter, enter_all, tail, offs, states, state_in, gate_vals, back, full_gate, full_out,
+    ) = run_forward(
+        jnp.concatenate([before, tokens_low], axis=0), part_sig, small.astype(low_type), cot_low,
+        w_in[:, :INNER].astype(low_type), w_out.astype(low_type),
     )
     tokens = tokens_low.astype(full_type)
     inv_rms = inv_wide[:, :1]
     gain_in = gain_in_rows[0]
-    (
-        y, bc, lag, run_t, enter, enter_all, tail, offs, states, state_in, gate_vals, back, full_gate, full_out
-    ) = run_forward(packed, conv, head, normed, cot_low, w_in[:, :INNER].astype(low_type), w_out.astype(low_type))
     normed_out, lefts, grad_y, grad_gate, part_gnorm, grad_state = run_norm(
         y, gate_vals, back, gain_rows, bc, enter_all, state_in, normed
     )

time: 451 us -> 440 us (0.976)
  Pallas kernels: 390 us -> 381 us
    pallas_call x1 -> x0, Pallas kernels: 64.1 us -> none  [project_signal(): pl.pallas_call(functools.partial(signal_kernel, count), in_specs=[vmem] *...]
    pallas_call x1, Pallas kernels: 100 us -> 154 us  [run_forward(): pl.pallas_call(functools.partial(forward_kernel, count), grid=(back_at +...]
where the time goes in v7:
time: 440 us; the launch traced here: 439 us
  Pallas kernels  381 us (87%)
  other arithmetic  16.8 us (4%)
  local copies, waits for them, and re-layouts  16.5 us (4%)
  matrix products  10.3 us (2%)
  starting transfers between devices  7.23 us (2%)
  waiting for transfers between devices  5.9 us (1%)
    pallas_call x1, Pallas kernels, run_backward(): pl.pallas_call(functools.partial(backward_kernel, (wsh_count, seq_count),...  183 us
    pallas_call x1, Pallas kernels, run_forward(): pl.pallas_call(functools.partial(forward_kernel, count), grid=(back_at +...  154 us
    pallas_call x2, Pallas kernels, adam_chunks(): pl.pallas_call(functools.partial(adam_kernel, rate, decay), grid=(all_row...  25.1 us
    pallas_call x1, Pallas kernels, run_norm(): pl.pallas_call(norm_kernel, grid=(rows // part,), in_specs=[by_rows(INNER...  18.7 us
    dot_general x1, matrix products, dot(): lax.dot_general(left_side, right_side, (dims, ((), ())), precision=precis...  10.3 us
  transfers between devices with their start and end apart: 6, of which 2 were waited for; matrix products, arithmetic and copies ran while one was open for 7% of the time, Pallas kernels for 6%

profile of v7, /device:TPU:0, one launch (start us, length us, event | category | flops | bytes accessed | tf_op | source)
XLA Modules:
  0.0 438.8 jit_solution(13920420870535401104)
XLA Ops:
  0.7 0.8 slice_bitcast_fusion
  1.5 4.9 %collective-permute-start = (bf16[16,1536]{1,0:T(8,128)(2,1)S(1)}, bf16[16,1536]{1,0:T(8,128)(2,1)S(1)}, u32[]{:S(2)}, u32[]{:S(2)}) collective-permute-start(bf16[16,1536]{1,0:T(8,128)(2,1)S(1)} %slice_bitcast_fusion), channel_id=1, source_target_pairs={{0,8},{8,16},{16,24},{1,9},{9,17},{17,25},{2,10},{10,18},{18,26},{... | collective-permute-start | bytes 147464 | tf_op jit(solution)/shard_map/ppermute | solution.py:1286
  6.4 2.6 convert.5
  9.1 0.0 copy-start.3
  9.1 0.0 copy-start.9
  9.1 0.0 copy-start.17
  9.1 1.4 copy-done.3
  10.5 1.2 slice.67.gate_own_ref
  11.7 0.7 copy.70
  12.4 0.1 copy.69
  12.5 0.0 copy-start.19
  12.5 0.0 copy-start
  12.6 2.9 convert_element_type.29.out_own_ref
  15.5 0.7 copy.72
  16.2 0.7 copy.73
  17.0 0.2 dynamic_update_slice.12
  17.3 1.8 concatenate.10.sig_own_ref
  19.0 0.1 dynamic_update_slice.13
  19.2 0.6 dynamic_update_slice.14
  19.8 0.3 dynamic_update_slice.15.small_ref
  20.2 0.0 copy-start.10
  20.2 1.3 pad_maximum_fusion.tokens_ref
  21.5 153.9 %forward_scan.1 = (bf16[528,3456]{1,0:T(8,128)(2,1)}, bf16[512,1536]{1,0:T(8,128)(2,1)}, f32[512,128]{1,0:T(8,128)}, f32[8,1536]{1,0:T(8,128)}, f32[8,3072]{1,0:...) custom-call(bf16[528,1536]{1,0:T(8,128)(2,1)} %pad_maximum_fusion.to, ...), custom_call_target="tpu_custom_call" | custom-call | flops 99999997952 | bytes 60000000 | tf_op jit(solution)/shard_map/forward_scan/pallas_call | solution.py:778
  175.3 18.7 %gated_norm.1 = (bf16[512,3072]{1,0:T(8,128)(2,1)}, bf16[4608,512]{1,0:T(8,128)(2,1)}, bf16[512,3072]{1,0:T(8,128)(2,1)}, bf16[512,3072]{1,0:T(8,128)(2,1)}, f32[8,3072]{1,0:T(8,128)}, /*index=5*/f32[128,3072]{1,0:T(8,128)}) custom-call(f32[512,3072]{1,0:T(8,128)} %get-tuple-element.74.y_ref, f32[512,3072]{1,0:T(8,128)} %get-tuple-element.75.gate_ref, ...), custom_call_target="tpu_custom_call" | custom-call | flops 1000000000 | bytes 30000000 | tf_op jit(solution)/shard_map/gated_norm/pallas_call | solution.py:856
  194.0 0.0 copy-start.1
  194.0 183.3 %scan_backward.1 = (f32[512,1536]{1,0:T(8,128)}, f32[8,3328]{1,0:T(8,128)}, f32[8,3072]{1,0:T(8,128)}, f32[8,128]{1,0:T(8,128)}, bf16[25,192,384]{2,1,0:T(8,128)(2,1)}) custom-call(bf16[528,3456]{1,0:T(8,128)(2,1)} %get-tuple-element.85.sig_ref.raw_ref, bf16[528,3456]{1,0:T(8,128)(2,1)} %get-tuple-element.85.sig_ref.raw_ref, ...), custom_call_target="tpu_custom_call" | custom-call | flops 99999997952 | bytes 20000000 | tf_op jit(solution)/shard_map/scan_backward/pallas_call | solution.py:900
  377.3 0.9 reshape.76
  378.2 0.9 slice_reduce_fusion.1
  379.1 0.1 reshape_squeeze.3
  379.2 0.1 reduce_sum.29
  379.3 0.8 slice_reduce_fusion.2
  380.2 0.1 slice_reduce_fusion
  380.3 0.8 slice_bitcast_fusion.1
  381.1 0.9 slice.57
  382.0 2.8 fusion.8
  384.8 0.1 concatenate.11
  384.8 0.0 collective-permute-start.1
  384.9 10.3 %fusion.10 = bf16[1,512,1536]{2,1,0:T(8,128)(2,1)} fusion(bf16[512,3072]{1,0:T(8,128)(2,1)} %get-tuple-element.82, bf16[3072,1536]{1,0:T(8,128)(2,1)} %get-tuple-element.83, bf16[1,512,1536]{2,1,0:T(8,128)(2,1)S(1)} %copy-done.1), kind=kOutput, calls=%fused_computation.12 | convolution fusion | flops 4834197504 | bytes 15728640 | tf_op jit(solution)/shard_map/dot_general | solution.py:45
  395.2 0.5 collective-permute-start.2
  395.6 8.6 %adam_w_out.1 = (f32[384,1536]{1,0:T(8,128)}, f32[384,1536]{1,0:T(8,128)}, f32[384,1536]{1,0:T(8,128)}, f32[384,1536]{1,0:T(8,128)}) custom-call(bf16[25,192,384]{2,1,0:T(8,128)(2,1)} %get-tuple-element.102.share_ref, f32[384,1536]{1,0:T(8,128)} %weight_ref.3, f32[384,1536]{1,0:T(8,128)} %first_ref.3, f32[384,1536]{1,0:T(8,128)} %second_ref.3), custom_call_target="tpu_custom_call" | custom-call | flops 11796480 | bytes 17694720 | tf_op jit(solution)/shard_map/adam_w_out/pallas_call | solution.py:1244
  404.3 1.7 collective-permute-start.3
  406.0 2.6 fusion.7
  408.6 0.0 copy-start.16
  408.6 0.0 copy-start.18
  408.6 0.0 copy-start.20
  408.6 0.0 copy-start.25
  408.7 0.0 copy-start.27
  408.7 0.0 copy-start.28
  408.7 16.5 %adam_w_in.1 = (f32[192,6400]{1,0:T(8,128)}, f32[192,6400]{1,0:T(8,128)}, f32[192,6400]{1,0:T(8,128)}, f32[192,6400]{1,0:T(8,128)}) custom-call(bf16[25,192,384]{2,1,0:T(8,128)(2,1)} %get-tuple-element.102.share_ref, f32[192,6400]{1,0:T(8,128)} %weight_ref.2, f32[192,6400]{1,0:T(8,128)} %first_ref.2, f32[192,6400]{1,0:T(8,128)} %second_ref.2), custom_call_target="tpu_custom_call" | custom-call | flops 24576000 | bytes 36864000 | tf_op jit(solution)/shard_map/adam_w_in/pallas_call | solution.py:1244
  425.2 0.1 collective-permute-start.4
  425.3 0.9 divide_subtract_fusion
  426.2 3.6 collective-permute-done.4
  429.8 0.1 collective-permute-start.5
  429.9 0.8 bitcast_convert_fusion
  430.7 0.7 copy.76
  431.4 0.7 copy.77
  432.1 0.7 copy.78
  432.8 0.7 copy.75
  433.5 2.3 collective-permute-done.5
  435.9 0.1 reshape.78
  436.0 0.7 divide_subtract_fusion.1
  436.7 0.7 divide_subtract_fusion.3
  437.4 0.7 divide_subtract_fusion.2
  438.1 0.7 divide_subtract_fusion.4
  (65 shorter events, 0.2 us)
Async XLA Ops:
  1.5 18.7 %collective-permute-start = (bf16[16,1536]{1,0:T(8,128)(2,1)S(1)}, bf16[16,1536]{1,0:T(8,128)(2,1)S(1)}, u32[]{:S(2)}, u32[]{:S(2)}) collective-permute-start(bf16[16,1536]{1,0:T(8,128)(2,1)S(1)} %slice_bitcast_fusion), channel_id=1, source_target_pairs={{0,8},{8,16},{16,24},{1,9},{9,17},{17,25},{2,10},{10,18},{18,26},{... | collective-permute-start | bytes 147464 | tf_op jit(solution)/shard_map/ppermute | solution.py:1286
  9.1 1.4 copy-start.3
  9.1 2.6 copy-start.9
  9.1 3.3 copy-start.17
  10.5 5.0 %copy-start.13 = (f32[192,48]{0,1:T(8,128)S(1)}, f32[192,48]{0,1:T(8,128)}, u32[]{:S(2)}) copy-start(f32[192,48]{0,1:T(8,128)} %param.34) | copy-start | bytes 110596
  10.5 5.7 %copy-start.14 = (f32[192,48]{0,1:T(8,128)S(1)}, f32[192,48]{0,1:T(8,128)}, u32[]{:S(2)}) copy-start(f32[192,48]{0,1:T(8,128)} %param.35) | copy-start | bytes 110596
  10.5 6.5 %copy-start.21 = (f32[192]{0:T(256)S(1)}, f32[192]{0:T(256)}, u32[]{:S(2)}) copy-start(f32[192]{0:T(256)} %param.28) | copy-start | bytes 2308
  11.7 5.6 %slice-start = ((bf16[192,6400]{1,0:T(8,128)(2,1)}), bf16[192,3328]{1,0:T(8,128)(2,1)S(1)}, s32[]{:S(2)}) async-start(bf16[192,6400]{1,0:T(8,128)(2,1)} %copy-done.3), calls=%async_computation | async-start | bytes 2555904 | tf_op jit(solution)/shard_map/slice | solution.py:1280
  12.5 6.7 %copy-start.11 = (f32[5,416]{1,0:T(8,128)S(1)}, f32[5,416]{1,0:T(8,128)}, u32[]{:S(2)}) copy-start(f32[5,416]{1,0:T(8,128)} %param.30) | copy-start | bytes 24964
  12.5 7.3 %copy-start.19 = (f32[3,6]{1,0:T(4,128)S(1)}, f32[3,6]{1,0:T(4,128)}, u32[]{:S(2)}) copy-start(f32[3,6]{1,0:T(4,128)} %param.31) | copy-start | bytes 220
  12.5 7.6 %copy-start = (bf16[1,512,1536]{2,1,0:T(8,128)(2,1)S(1)}, bf16[1,512,1536]{2,1,0:T(8,128)(2,1)}, u32[]{:S(2)}) copy-start(bf16[1,512,1536]{2,1,0:T(8,128)(2,1)} %param.23) | copy-start | bytes 4718596
  20.2 1.3 copy-start.10
  194.0 186.2 %copy-start.8 = (f32[512,128]{1,0:T(8,128)S(1)}, f32[512,128]{1,0:T(8,128)}, u32[]{:S(2)}) copy-start(f32[512,128]{1,0:T(8,128)} %get-tuple-element.84) | copy-start | bytes 786436
  194.0 188.0 %copy-start.1 = (bf16[1,512,1536]{2,1,0:T(8,128)(2,1)S(1)}, bf16[1,512,1536]{2,1,0:T(8,128)(2,1)}, u32[]{:S(2)}) copy-start(bf16[1,512,1536]{2,1,0:T(8,128)(2,1)} %param.23) | copy-start | bytes 4718596
  384.8 10.3 %collective-permute-start.1 = (f32[21392]{0:T(1024)S(1)}, f32[21392]{0:T(1024)S(1)}, u32[]{:S(2)}, u32[]{:S(2)}) collective-permute-start(f32[21392]{0:T(1024)S(1)} %concatenate.11), channel_id=1, source_target_pairs={{0,1},{1,0},{2,3},{3,2},{4,5},{5,4},{6,7},{7,6},{8,9},{9,8},{10,11... | collective-permute-start | bytes 256712 | tf_op jit(solution)/shard_map/ppermute | solution.py:981
  395.2 9.1 %collective-permute-start.2 = (f32[21392]{0:T(1024)S(1)}, f32[21392]{0:T(1024)S(1)}, u32[]{:S(2)}, u32[]{:S(2)}) collective-permute-start(f32[21392]{0:T(1024)S(1)} %add.106), channel_id=1, source_target_pairs={{0,2},{1,3},{2,0},{3,1},{4,6},{5,7},{6,4},{7,5},{8,10},{9,11},{10,... | collective-permute-start | bytes 256712 | tf_op jit(solution)/shard_map/ppermute | solution.py:981
  395.6 10.4 %copy-start.2 = (f32[512,1536]{1,0:T(8,128)S(1)}, f32[512,1536]{1,0:T(8,128)}, u32[]{:S(2)}) copy-start(f32[512,1536]{1,0:T(8,128)} %get-tuple-element.100) | copy-start | bytes 9437188
  395.6 10.4 %copy-start.4 = (bf16[1,512,1536]{2,1,0:T(8,128)(2,1)S(1)}, bf16[1,512,1536]{2,1,0:T(8,128)(2,1)}, u32[]{:S(2)}) copy-start(bf16[1,512,1536]{2,1,0:T(8,128)(2,1)} %param.24) | copy-start | bytes 4718596
  404.3 20.9 %collective-permute-start.3 = (f32[21392]{0:T(1024)S(1)}, f32[21392]{0:T(1024)S(1)}, u32[]{:S(2)}, u32[]{:S(2)}) collective-permute-start(f32[21392]{0:T(1024)S(1)} %add.107), channel_id=1, source_target_pairs={{0,4},{1,5},{2,6},{3,7},{4,0},{5,1},{6,2},{7,3},{8,12},{9,13},{10,... | collective-permute-start | bytes 256712 | tf_op jit(solution)/shard_map/ppermute | solution.py:981
  408.5 16.8 %copy-start.5 = (f32[192,48]{1,0:T(8,128)S(1)}, f32[192,48]{1,0:T(8,128)}, u32[]{:S(2)}) copy-start(f32[192,48]{1,0:T(8,128)} %copy.70) | copy-start | bytes 110596
  408.6 16.8 %copy-start.6 = (f32[192,48]{1,0:T(8,128)S(1)}, f32[192,48]{1,0:T(8,128)}, u32[]{:S(2)}) copy-start(f32[192,48]{1,0:T(8,128)} %copy.72) | copy-start | bytes 110596
  408.6 16.8 %copy-start.7 = (f32[192,48]{1,0:T(8,128)S(1)}, f32[192,48]{1,0:T(8,128)}, u32[]{:S(2)}) copy-start(f32[192,48]{1,0:T(8,128)} %copy.73) | copy-start | bytes 110596
  408.6 27.4 %copy-start.12 = (f32[5,416]{1,0:T(8,128)S(1)}, f32[5,416]{1,0:T(8,128)}, u32[]{:S(2)}) copy-start(f32[5,416]{1,0:T(8,128)} %param.30) | copy-start | bytes 24964
  408.6 27.4 %copy-start.15 = (f32[5,416]{1,0:T(8,128)S(1)}, f32[5,416]{1,0:T(8,128)}, u32[]{:S(2)}) copy-start(f32[5,416]{1,0:T(8,128)} %param.42) | copy-start | bytes 24964
  408.6 27.4 %copy-start.16 = (f32[5,416]{1,0:T(8,128)S(1)}, f32[5,416]{1,0:T(8,128)}, u32[]{:S(2)}) copy-start(f32[5,416]{1,0:T(8,128)} %param.43) | copy-start | bytes 24964
  408.6 28.1 %copy-start.18 = (f32[384]{0:T(512)S(1)}, f32[384]{0:T(512)}, u32[]{:S(2)}) copy-start(f32[384]{0:T(512)} %param.29) | copy-start | bytes 4612
  408.6 28.1 %copy-start.23 = (f32[384]{0:T(512)S(1)}, f32[384]{0:T(512)}, u32[]{:S(2)}) copy-start(f32[384]{0:T(512)} %param.40) | copy-start | bytes 4612
  408.6 28.1 %copy-start.24 = (f32[384]{0:T(512)S(1)}, f32[384]{0:T(512)}, u32[]{:S(2)}) copy-start(f32[384]{0:T(512)} %param.41) | copy-start | bytes 4612
  408.6 28.8 %copy-start.20 = (f32[3,6]{1,0:T(4,128)S(1)}, f32[3,6]{1,0:T(4,128)}, u32[]{:S(2)}) copy-start(f32[3,6]{1,0:T(4,128)} %param.31) | copy-start | bytes 220
  408.6 28.8 %copy-start.25 = (f32[3,6]{1,0:T(4,128)S(1)}, f32[3,6]{1,0:T(4,128)}, u32[]{:S(2)}) copy-start(f32[3,6]{1,0:T(4,128)} %param.44) | copy-start | bytes 220
  408.6 28.8 %copy-start.26 = (f32[3,6]{1,0:T(4,128)S(1)}, f32[3,6]{1,0:T(4,128)}, u32[]{:S(2)}) copy-start(f32[3,6]{1,0:T(4,128)} %param.45) | copy-start | bytes 220
  408.7 29.4 %copy-start.22 = (f32[192]{0:T(256)S(1)}, f32[192]{0:T(256)}, u32[]{:S(2)}) copy-start(f32[192]{0:T(256)} %param.28) | copy-start | bytes 2308
  408.7 29.4 %copy-start.27 = (f32[192]{0:T(256)S(1)}, f32[192]{0:T(256)}, u32[]{:S(2)}) copy-start(f32[192]{0:T(256)} %param.38) | copy-start | bytes 2308
  408.7 29.4 %copy-start.28 = (f32[192]{0:T(256)S(1)}, f32[192]{0:T(256)}, u32[]{:S(2)}) copy-start(f32[192]{0:T(256)} %param.39) | copy-start | bytes 2308
  425.2 4.6 %collective-permute-start.4 = (f32[21392]{0:T(1024)S(1)}, f32[21392]{0:T(1024)S(1)}, u32[]{:S(2)}, u32[]{:S(2)}) collective-permute-start(f32[21392]{0:T(1024)S(1)} %add.108), channel_id=1, source_target_pairs={{0,8},{8,0},{16,24},{24,16},{1,9},{9,1},{17,25},{25,17},{2,10},{10... | collective-permute-start | bytes 256712 | tf_op jit(solution)/shard_map/ppermute | solution.py:981
  429.8 6.0 %collective-permute-start.5 = (f32[21392]{0:T(1024)S(1)}, f32[21392]{0:T(1024)S(1)}, u32[]{:S(2)}, u32[]{:S(2)}) collective-permute-start(f32[21392]{0:T(1024)S(1)} %add.109), channel_id=1, source_target_pairs={{0,16},{8,24},{16,0},{24,8},{1,17},{9,25},{17,1},{25,9},{2,18},{10... | collective-permute-start | bytes 256712 | tf_op jit(solution)/shard_map/ppermute | solution.py:981
